TPU v7x, 256 devices: a whole 4x4x8 slice. The times are simulated.
256 devices in a mesh: rans: 64 (over z, y, core), pitch: 2 (over x_hi), span: 2 (over x_lo).
Axes of the slice: x: 4 (x_hi: 2, x_lo: 2; x = x_hi * 2 + x_lo), y: 4, z: 8, core: 2. Of those that a mesh axis runs over, the one named last changes fastest.
Arguments:
- solution: bfloat16 [5, 64, 393216], P(None, None, ('rans', 'pitch', 'span')), may hold values from -6 to 6
- volume_ops: bfloat16 [3, 64, 64], replicated, may hold values from -0.4375 to 0.4375
- flux_jacobian: float32 [3, 5, 5], replicated, may hold values from -2.5 to 2.5
- lift_matrix: bfloat16 [64, 96], replicated, may hold values from -1.5 to 1.5
- filter_matrix: bfloat16 [64, 64], replicated
- wall_matrix: bfloat16 [64, 64], replicated, may hold values from -0.75 to 0.75
- pinched_map: int32 [393216], P(('rans', 'pitch', 'span')), may hold values from 0 to 1, as said below
- mode_rows: int32 [2, 2, 16384, 64], P('pitch', 'span', 'rans'), may hold values from 0 to 2047
- mode_seeds: int32 [2, 2, 16384], P('pitch', 'span', 'rans'), may hold values from 0 to 31
- mode_shape: float32 [2, 2, 16384, 64], P('pitch', 'span', 'rans'), may hold values from 0.2 to 1
- mean_inflow: float32 [2, 2, 5, 2048], P('pitch', 'span'), may hold values from -6 to 6
- eddy_amplitude: float32 [2, 2, 5, 2048], P('pitch', 'span'), may hold values from 0.3 to 3
Outputs:
- new_solution: bfloat16 [5, 64, 393216], P(None, None, ('rans', 'pitch', 'span'))
Inputs may be any that keep to these rules, and one draw needn't show every extreme that they name: pinched_map is 1 only for elements in the last 4 element layers of the whole domain along span, hence only on devices with the last span index; one device holds at most 192 ones, and some devices hold exactly 192.
All inputs are finite; a program needn't handle non-finite values.
Results may differ from a plain program's by a relative error of at most 0.0042.
The roundings to bfloat16 on the way count: a program that leaves them out, or rounds other values in their place, can miss the bound.
Values may be sent and summed in bfloat16 or wider, within the bound.
No kernel may reach another device: no remote copies, remote signals or barrier semaphores. Data moves between devices by JAX's collectives and lax.ppermute only.
A program may use at most 128 MiB of HBM per device.

v0:
```python
import jax
import jax.numpy as jnp
from jax import lax
from jax.sharding import PartitionSpec as P

EX = 12
EY = 4
EZ = 32


time_step = 0.4
upwind_speed = 1.0
highest = lax.Precision.HIGHEST


def with_halo(block, sides, width, periodic):
    for axis, dim in sides:
        count = lax.axis_size(axis)
        forward = [(i, i + 1) for i in range(count - 1)]
        if periodic:
            forward.append((count - 1, 0))
        backward = [(target, source) for source, target in forward]
        low = lax.ppermute(
            lax.slice_in_dim(block, block.shape[dim] - width, None, axis=dim), axis, forward
        )
        high = lax.ppermute(lax.slice_in_dim(block, 0, width, axis=dim), axis, backward)
        block = jnp.concatenate([low, block, high], axis=dim)
    return block


def face_term(flux_jacobian, direction, normal_sign, inner_trace, outer_trace):
    identity = jnp.eye(5, dtype=jnp.float32)
    matrix = 0.5 * normal_sign * flux_jacobian[direction] - 0.5 * upwind_speed * identity
    difference = outer_trace.astype(jnp.float32) - inner_trace.astype(jnp.float32)
    mixed_jump = jnp.einsum("fh,h...->f...", matrix, difference, precision=highest)
    return mixed_jump.reshape(5, 16, -1)


def phase_rate(current, volume_ops, flux_jacobian, lift_matrix, wall_matrix, pinched_map, inflow):
    elements = current.shape[2]
    plane_cells = EY * EZ
    rans_index = lax.axis_index("rans")
    span_index = lax.axis_index("span")
    last_rans = lax.axis_size("rans") - 1
    last_span = lax.axis_size("span") - 1
    nodal = current.reshape(5, 4, 4, 4, elements)
    low_stream = nodal[:, 0, :, :, :plane_cells]
    high_stream = nodal[:, 3, :, :, elements - plane_cells :]
    stream_own = jnp.stack([low_stream.reshape(-1), high_stream.reshape(-1)])
    stream_ext = with_halo(stream_own, (("rans", 0),), 1, False)
    from_below = stream_ext[0].reshape(5, 4, 4, plane_cells).astype(jnp.float32)
    from_above = stream_ext[3].reshape(5, 4, 4, plane_cells)
    lower_edge = jnp.where(rans_index == 0, inflow, from_below)
    upper_edge = jnp.where(rans_index == last_rans, high_stream, from_above)
    stream_low = jnp.concatenate(
        [lower_edge, nodal[:, 3, :, :, : elements - plane_cells].astype(jnp.float32)], axis=-1
    )
    stream_high = jnp.concatenate([nodal[:, 0, :, :, plane_cells:], upper_edge], axis=-1)
    jumps_stream_low = face_term(flux_jacobian, 0, -1.0, nodal[:, 0], stream_low).astype(
        jnp.bfloat16
    )
    jumps_stream_high = face_term(flux_jacobian, 0, 1.0, nodal[:, 3], stream_high).astype(
        jnp.bfloat16
    )
    pitch_view = current.reshape(5, 4, 4, 4, EX, plane_cells)
    pitch_low_trace = pitch_view[:, :, 0, :, :, :EZ]
    pitch_high_trace = pitch_view[:, :, 3, :, :, plane_cells - EZ :]
    pitch_own = jnp.stack([pitch_low_trace.reshape(-1), pitch_high_trace.reshape(-1)])
    pitch_ext = with_halo(pitch_own, (("pitch", 0),), 1, True)
    pitch_below = pitch_ext[0].reshape(5, 4, 4, EX, EZ)
    pitch_above = pitch_ext[3].reshape(5, 4, 4, EX, EZ)
    pitch_low = jnp.concatenate(
        [pitch_below, pitch_view[:, :, 3, :, :, : plane_cells - EZ]], axis=-1
    )
    pitch_high = jnp.concatenate([pitch_view[:, :, 0, :, :, EZ:], pitch_above], axis=-1)
    jumps_pitch_low = face_term(flux_jacobian, 1, -1.0, pitch_view[:, :, 0], pitch_low).astype(
        jnp.bfloat16
    )
    jumps_pitch_high = face_term(flux_jacobian, 1, 1.0, pitch_view[:, :, 3], pitch_high).astype(
        jnp.bfloat16
    )
    span_view = current.reshape(5, 4, 4, 4, EX * EY, EZ)
    span_low_trace = span_view[:, :, :, 0, :, 0]
    span_high_trace = span_view[:, :, :, 3, :, EZ - 1]
    span_own = jnp.stack([span_low_trace.reshape(-1), span_high_trace.reshape(-1)])
    span_ext = with_halo(span_own, (("span", 0),), 1, False)
    span_below = jnp.where(span_index == 0, span_low_trace, span_ext[0].reshape(5, 4, 4, EX * EY))
    span_above = jnp.where(
        span_index == last_span, span_high_trace, span_ext[3].reshape(5, 4, 4, EX * EY)
    )
    layer_c = jnp.arange(elements, dtype=jnp.int32) % EZ
    edge_cell = jnp.zeros((5, 4, 4, 1), jnp.bfloat16)
    below_fill = jnp.broadcast_to(span_below[..., None], (5, 4, 4, EX * EY, EZ)).reshape(
        5, 4, 4, elements
    )
    above_fill = jnp.broadcast_to(span_above[..., None], (5, 4, 4, EX * EY, EZ)).reshape(
        5, 4, 4, elements
    )
    span_low = jnp.where(
        layer_c == 0,
        below_fill,
        jnp.concatenate([edge_cell, nodal[:, :, :, 3, : elements - 1]], axis=-1),
    )
    span_high = jnp.where(
        layer_c == EZ - 1, above_fill, jnp.concatenate([nodal[:, :, :, 0, 1:], edge_cell], axis=-1)
    )
    jumps_span_low = face_term(flux_jacobian, 2, -1.0, nodal[:, :, :, 0], span_low).astype(
        jnp.bfloat16
    )
    jumps_span_high = face_term(flux_jacobian, 2, 1.0, nodal[:, :, :, 3], span_high).astype(
        jnp.bfloat16
    )
    face_jumps = jnp.concatenate(
        [
            jumps_stream_low,
            jumps_stream_high,
            jumps_pitch_low,
            jumps_pitch_high,
            jumps_span_low,
            jumps_span_high,
        ],
        axis=1,
    )
    fluxes = jnp.einsum(
        "dfg,gne->dfne", flux_jacobian, current.astype(jnp.float32), precision=highest
    ).astype(jnp.bfloat16)
    volume = jnp.einsum("dnm,dfme->fne", volume_ops, fluxes, preferred_element_type=jnp.float32)
    surface = jnp.einsum("nq,fqe->fne", lift_matrix, face_jumps, preferred_element_type=jnp.float32)
    wall_term = jnp.einsum("nm,fme->fne", wall_matrix, current, preferred_element_type=jnp.float32)
    wall_term = wall_term * pinched_map.astype(jnp.float32)
    return -(volume + surface + wall_term)


def body(
    solution,
    volume_ops,
    flux_jacobian,
    lift_matrix,
    filter_matrix,
    wall_matrix,
    pinched_map,
    mode_rows,
    mode_seeds,
    mode_shape,
    mean_inflow,
    eddy_amplitude,
):
    plane_rows = mean_inflow.shape[3]
    powers = 2 ** jnp.arange(5, dtype=jnp.int32)
    parity = mode_seeds[0, 0][None, :] // powers[:, None] % 2
    mode_signs = (2 * parity - 1).astype(jnp.float32)
    shapes = mode_shape[0, 0]
    normalizer = (plane_rows / (shapes.shape[0] * lax.axis_size("rans") * shapes.shape[1])) ** 0.5
    contrib = mode_signs[:, :, None] * shapes[None, :, :] * normalizer
    partial_plane = jax.ops.segment_sum(
        contrib.reshape(5, -1).T, mode_rows[0, 0].reshape(-1), num_segments=plane_rows
    ).T
    fluctuation = lax.psum(partial_plane, "rans")
    inflow = (mean_inflow[0, 0] + eddy_amplitude[0, 0] * fluctuation).reshape(5, 4, 4, EY * EZ)
    rate_one = phase_rate(
        solution, volume_ops, flux_jacobian, lift_matrix, wall_matrix, pinched_map, inflow
    )
    trial_one = (solution.astype(jnp.float32) + time_step * rate_one).astype(jnp.bfloat16)
    phase_one = jnp.einsum(
        "nm,fme->fne", filter_matrix, trial_one, preferred_element_type=jnp.float32
    ).astype(jnp.bfloat16)
    rate_two = phase_rate(
        phase_one, volume_ops, flux_jacobian, lift_matrix, wall_matrix, pinched_map, inflow
    )
    trial_two = (
        0.5 * (solution.astype(jnp.float32) + phase_one.astype(jnp.float32) + time_step * rate_two)
    ).astype(jnp.bfloat16)
    return jnp.einsum(
        "nm,fme->fne", filter_matrix, trial_two, preferred_element_type=jnp.float32
    ).astype(jnp.bfloat16)


def solution(mesh):
    in_specs = (
        P(None, None, ("rans", "pitch", "span")),
        P(),
        P(),
        P(),
        P(),
        P(),
        P(("rans", "pitch", "span")),
        P("pitch", "span", "rans", None),
        P("pitch", "span", "rans"),
        P("pitch", "span", "rans", None),
        P("pitch", "span", None, None),
        P("pitch", "span", None, None),
    )
    out_specs = P(None, None, ("rans", "pitch", "span"))
    return jax.shard_map(body, mesh=mesh, in_specs=in_specs, out_specs=out_specs, check_vma=False)
```

profile of v0, /device:TPU:1, one launch (start us, length us, event | category | flops | bytes accessed | tf_op | source)
XLA Modules:
  0.0 578.2 jit_solution(6772849689493679791)
XLA Ops:
  2.6 4.6 collective-permute-start
  18.6 3.9 reshape.326
  22.5 3.5 slice_reduce_fusion.2
  26.7 3.3 collective-permute-start.4
  37.6 8.4 %convolution_convert_fusion.1 = bf16[3,5,64,1536]{3,0,2,1:T(4,128)(2,1)} fusion(bf16[5,64,1536]{2,1,0:T(8,128)(2,1)S(1)} %copy-done.1, f32[3,5,5]{2,0,1:T(4,128)S(1)} %copy-done.21), kind=kOutput, calls=%fused_computation.6 | convolution fusion | flops 89948160 | bytes 3932460 | tf_op jit(solution)/shard_map/dfg,gne->dfne/dot_general | solution.py:124
  55.2 5.6 fusion.2
  60.8 80.7 %scatter_custom_fusion = f32[2048,5]{1,0:T(8,128)} fusion(s32[16384]{0:T(1024)} %reshape.352, f32[5,16384]{0,1:T(8,128)} %fusion.2, f32[]{:T(128)} %constant.42.clone.1), kind=kCustom, calls=%fused_computation.1 | custom fusion | flops 81920 | bytes 8430080 | tf_op jit(solution)/shard_map/scatter-add | solution.py:155
  141.5 258.0 %psum.7 = f32[5,2048]{0,1:T(8,128)} all-reduce(f32[5,2048]{0,1:T(8,128)} %bitcast.324), channel_id=1, replica_groups=mesh['rans'=64,'pitch'=2,'span'=2] {'rans'}, use_global_device_ids=true, to_apply=%region_1.2 | all-reduce | flops 10240 | bytes 81920 | tf_op jit(solution)/shard_map/psum | solution.py:158
  403.8 4.4 fusion.22
  424.9 2.7 reshape.327
  432.6 3.1 reshape.328
  451.9 2.5 fusion.57
  463.6 4.2 convolution_add_fusion.1
  470.1 4.0 reshape.331
  484.8 2.9 slice_reduce_fusion
  489.7 6.6 %fusion.3 = bf16[3,5,64,1536]{3,0,1,2:T(4,128)(2,1)S(1)} fusion(bf16[5,64,1536,1]{2,1,0,3:T(8,128)(2,1)S(1)} %bitcast.323, f32[3,5,5]{2,0,1:T(4,128)S(1)} %copy-done.22), kind=kOutput, calls=%fused_computation.7 | convolution fusion | flops 89948160 | bytes 3932460 | tf_op jit(solution)/shard_map/dfg,gne->dfne/dot_general | solution.py:124
  500.6 5.7 collective-permute-start.10
  516.2 9.5 %collective-permute-start.7 = (bf16[1,10240]{1,0:T(2,128)(2,1)}, bf16[1,10240]{1,0:T(2,128)(2,1)}, u32[]{:S(2)}, u32[]{:S(2)}) collective-permute-start(bf16[1,10240]{1,0:T(2,128)(2,1)} %stack_reshape_squeeze.43), channel_id=1, source_target_pairs={{4,0},{8,4},{12,8},{16,12},{20,16},{24,20},{28,24},{32,28},{36,32}... | collective-permute-start | bytes 61448 | tf_op jit(solution)/shard_map/ppermute | solution.py:26
  532.7 2.7 reshape.333
  537.8 2.9 reshape.332
  557.3 2.8 fusion.55
  566.1 2.7 fusion.29
  570.3 4.2 convolution_add_fusion
  574.5 3.5 fusion.27
  (197 shorter events, 144.9 us)
Async XLA Ops:
  0.0 403.8 %copy-start = (bf16[3,64,64]{2,1,0:T(8,128)(2,1)S(1)}, bf16[3,64,64]{2,1,0:T(8,128)(2,1)}, u32[]{:S(2)}) copy-start(bf16[3,64,64]{2,1,0:T(8,128)(2,1)} %param.13) | copy-start | bytes 73732
  0.0 10.2 %copy-start.1 = (bf16[5,64,1536]{2,1,0:T(8,128)(2,1)S(1)}, bf16[5,64,1536]{2,1,0:T(8,128)(2,1)}, u32[]{:S(2)}) copy-start(bf16[5,64,1536]{2,1,0:T(8,128)(2,1)} %param.12) | copy-start | bytes 2949124
  2.6 439.8 %collective-permute-start = (bf16[1,10240]{1,0:T(2,128)(2,1)}, bf16[1,10240]{1,0:T(2,128)(2,1)}, u32[]{:S(2)}, u32[]{:S(2)}) collective-permute-start(bf16[1,10240]{1,0:T(2,128)(2,1)} %stack_reshape_squeeze.36), channel_id=1, source_target_pairs={{0,4},{4,8},{8,12},{12,16},{16,20},{20,24},{24,28},{28,32},{32,36}... | collective-permute-start | bytes 61448 | tf_op jit(solution)/shard_map/ppermute | solution.py:23
  7.8 432.3 %collective-permute-start.1 = (bf16[1,10240]{1,0:T(2,128)(2,1)}, bf16[1,10240]{1,0:T(2,128)(2,1)}, u32[]{:S(2)}, u32[]{:S(2)}) collective-permute-start(bf16[1,10240]{1,0:T(2,128)(2,1)} %stack_reshape_squeeze.37), channel_id=1, source_target_pairs={{4,0},{8,4},{12,8},{16,12},{20,16},{24,20},{28,24},{32,28},{36,32}... | collective-permute-start | bytes 61448 | tf_op jit(solution)/shard_map/ppermute | solution.py:26
  13.8 434.4 %collective-permute-start.2 = (bf16[1,30720]{1,0:T(2,128)(2,1)}, bf16[1,30720]{1,0:T(2,128)(2,1)}, u32[]{:S(2)}, u32[]{:S(2)}) collective-permute-start(bf16[1,30720]{1,0:T(2,128)(2,1)} %stack_reshape_squeeze.38), channel_id=1, source_target_pairs={{0,2},{2,0},{1,3},{3,1},{4,6},{6,4},{5,7},{7,5},{8,10},{10,8},{9,1... | collective-permute-start | bytes 184328 | tf_op jit(solution)/shard_map/ppermute | solution.py:23
  17.9 431.8 %collective-permute-start.3 = (bf16[1,30720]{1,0:T(2,128)(2,1)}, bf16[1,30720]{1,0:T(2,128)(2,1)}, u32[]{:S(2)}, u32[]{:S(2)}) collective-permute-start(bf16[1,30720]{1,0:T(2,128)(2,1)} %stack_reshape_squeeze.39), channel_id=1, source_target_pairs={{2,0},{0,2},{3,1},{1,3},{6,4},{4,6},{7,5},{5,7},{10,8},{8,10},{11,... | collective-permute-start | bytes 184328 | tf_op jit(solution)/shard_map/ppermute | solution.py:26
  26.7 391.8 %collective-permute-start.4 = (bf16[1,3840]{1,0:T(2,128)(2,1)}, bf16[1,3840]{1,0:T(2,128)(2,1)}, u32[]{:S(2)}, u32[]{:S(2)}) collective-permute-start(bf16[1,3840]{1,0:T(2,128)(2,1)} %stack_reshape_squeeze.40), channel_id=1, source_target_pairs={{0,1},{2,3},{4,5},{6,7},{8,9},{10,11},{12,13},{14,15},{16,17},{18,... | collective-permute-start | bytes 23048 | tf_op jit(solution)/shard_map/ppermute | solution.py:23
  37.6 8.4 %copy-start.33 = (s32[1,1,256]{2,1,0:T(1,128)S(1)}, s32[1,1,256]{2,1,0:T(1,128)}, u32[]{:S(2)}) copy-start(s32[1,1,256]{2,1,0:T(1,128)} %param.20) | copy-start | bytes 3076
  418.6 9.0 %collective-permute-start.5 = (bf16[1,3840]{1,0:T(2,128)(2,1)}, bf16[1,3840]{1,0:T(2,128)(2,1)}, u32[]{:S(2)}, u32[]{:S(2)}) collective-permute-start(bf16[1,3840]{1,0:T(2,128)(2,1)} %stack_reshape_squeeze.41), channel_id=1, source_target_pairs={{1,0},{3,2},{5,4},{7,6},{9,8},{11,10},{13,12},{15,14},{17,16},{19,... | collective-permute-start | bytes 23048 | tf_op jit(solution)/shard_map/ppermute | solution.py:26
  444.9 7.0 %copy-start.14 = (bf16[5,4,4,12,96]{4,3,2,1,0:T(8,128)(2,1)S(1)}, bf16[5,4,4,12,96]{4,3,2,1,0:T(8,128)(2,1)}, u32[]{:S(2)}) copy-start(bf16[5,4,4,12,96]{4,3,2,1,0:T(8,128)(2,1)} %get-tuple-element.17) | copy-start | bytes 552964
  444.9 7.0 %copy-start.15 = (bf16[5,4,4,12,96]{4,3,2,1,0:T(8,128)(2,1)S(1)}, bf16[5,4,4,12,96]{4,3,2,1,0:T(8,128)(2,1)}, u32[]{:S(2)}) copy-start(bf16[5,4,4,12,96]{4,3,2,1,0:T(8,128)(2,1)} %get-tuple-element.18) | copy-start | bytes 552964
  456.9 6.7 %copy-start.4 = (f32[5,1536,64]{1,2,0:T(8,128)S(1)}, f32[5,1536,64]{1,2,0:T(8,128)}, u32[]{:S(2)}) copy-start(f32[5,1536,64]{1,2,0:T(8,128)} %fusion.22) | copy-start | bytes 5898244
  481.8 7.9 %copy-start.22 = (f32[3,5,5]{2,0,1:T(4,128)S(1)}, f32[3,5,5]{2,0,1:T(4,128)}, u32[]{:S(2)}) copy-start(f32[3,5,5]{2,0,1:T(4,128)} %param.14) | copy-start | bytes 904
  488.4 38.6 %collective-permute-start.11 = (bf16[1,3840]{1,0:T(2,128)(2,1)}, bf16[1,3840]{1,0:T(2,128)(2,1)}, u32[]{:S(2)}, u32[]{:S(2)}) collective-permute-start(bf16[1,3840]{1,0:T(2,128)(2,1)} %stack_reshape_squeeze.47), channel_id=1, source_target_pairs={{1,0},{3,2},{5,4},{7,6},{9,8},{11,10},{13,12},{15,14},{17,16},{19,... | collective-permute-start | bytes 23048 | tf_op jit(solution)/shard_map/ppermute | solution.py:26
  500.6 34.8 %collective-permute-start.10 = (bf16[1,3840]{1,0:T(2,128)(2,1)}, bf16[1,3840]{1,0:T(2,128)(2,1)}, u32[]{:S(2)}, u32[]{:S(2)}) collective-permute-start(bf16[1,3840]{1,0:T(2,128)(2,1)} %stack_reshape_squeeze.46), channel_id=1, source_target_pairs={{0,1},{2,3},{4,5},{6,7},{8,9},{10,11},{12,13},{14,15},{16,17},{18,... | collective-permute-start | bytes 23048 | tf_op jit(solution)/shard_map/ppermute | solution.py:23
  510.0 42.9 %collective-permute-start.8 = (bf16[1,30720]{1,0:T(2,128)(2,1)}, bf16[1,30720]{1,0:T(2,128)(2,1)}, u32[]{:S(2)}, u32[]{:S(2)}) collective-permute-start(bf16[1,30720]{1,0:T(2,128)(2,1)} %stack_reshape_squeeze.44), channel_id=1, source_target_pairs={{0,2},{2,0},{1,3},{3,1},{4,6},{6,4},{5,7},{7,5},{8,10},{10,8},{9,1... | collective-permute-start | bytes 184328 | tf_op jit(solution)/shard_map/ppermute | solution.py:23
  514.4 40.7 %collective-permute-start.9 = (bf16[1,30720]{1,0:T(2,128)(2,1)}, bf16[1,30720]{1,0:T(2,128)(2,1)}, u32[]{:S(2)}, u32[]{:S(2)}) collective-permute-start(bf16[1,30720]{1,0:T(2,128)(2,1)} %stack_reshape_squeeze.45), channel_id=1, source_target_pairs={{2,0},{0,2},{3,1},{1,3},{6,4},{4,6},{7,5},{5,7},{10,8},{8,10},{11,... | collective-permute-start | bytes 184328 | tf_op jit(solution)/shard_map/ppermute | solution.py:26
  516.2 29.8 %collective-permute-start.7 = (bf16[1,10240]{1,0:T(2,128)(2,1)}, bf16[1,10240]{1,0:T(2,128)(2,1)}, u32[]{:S(2)}, u32[]{:S(2)}) collective-permute-start(bf16[1,10240]{1,0:T(2,128)(2,1)} %stack_reshape_squeeze.43), channel_id=1, source_target_pairs={{4,0},{8,4},{12,8},{16,12},{20,16},{24,20},{28,24},{32,28},{36,32}... | collective-permute-start | bytes 61448 | tf_op jit(solution)/shard_map/ppermute | solution.py:26
  527.1 13.7 %copy-start.31 = (pred[1536]{0:T(1024)(128)(4,1)S(1)}, pred[1536]{0:T(1024)(128)(4,1)}, u32[]{:S(2)}) copy-start(pred[1536]{0:T(1024)(128)(4,1)} %fusion.89) | copy-start | bytes 4612
  527.1 19.8 %collective-permute-start.6 = (bf16[1,10240]{1,0:T(2,128)(2,1)}, bf16[1,10240]{1,0:T(2,128)(2,1)}, u32[]{:S(2)}, u32[]{:S(2)}) collective-permute-start(bf16[1,10240]{1,0:T(2,128)(2,1)} %stack_reshape_squeeze.42), channel_id=1, source_target_pairs={{0,4},{4,8},{8,12},{12,16},{16,20},{20,24},{24,28},{28,32},{32,36}... | collective-permute-start | bytes 61448 | tf_op jit(solution)/shard_map/ppermute | solution.py:23
  532.7 9.5 %copy-start.32 = (pred[1536]{0:T(1024)(128)(4,1)S(1)}, pred[1536]{0:T(1024)(128)(4,1)}, u32[]{:S(2)}) copy-start(pred[1536]{0:T(1024)(128)(4,1)} %fusion.90) | copy-start | bytes 4612
  549.6 7.7 %copy-start.2 = (bf16[5,4,4,4,12,128]{5,4,3,2,1,0:T(8,128)(2,1)S(1)}, bf16[5,4,4,4,12,128]{5,4,3,2,1,0:T(8,128)(2,1)}, u32[]{:S(2)}) copy-start(bf16[5,4,4,4,12,128]{5,4,3,2,1,0:T(8,128)(2,1)} %reshape.330) | copy-start | bytes 2949124
  562.5 7.8 %copy-start.3 = (f32[5,1536,64]{1,2,0:T(8,128)S(1)}, f32[5,1536,64]{1,2,0:T(8,128)}, u32[]{:S(2)}) copy-start(f32[5,1536,64]{1,2,0:T(8,128)} %fusion.19) | copy-start | bytes 5898244
  562.5 7.8 %copy-start.26 = (bf16[64,96]{1,0:T(8,128)(2,1)S(1)}, bf16[64,96]{1,0:T(8,128)(2,1)}, u32[]{:S(2)}) copy-start(bf16[64,96]{1,0:T(8,128)(2,1)} %param.15) | copy-start | bytes 36868
  (22 other events, 94.8 us)
where the time goes:
time: 585 us; the launch traced here: 578 us
  blocking collectives  258 us (44%)
  other arithmetic  126 us (22%)
  local copies, waits for them, and re-layouts  104 us (18%)
  matrix products  53.3 us (9%)
  starting transfers between devices  36 us (6%)
    psum x1, blocking collectives, body(): fluctuation = lax.psum(partial_plane, 'rans')  258 us
    scatter-add x1, other arithmetic, body(): jax.ops.segment_sum(contrib.reshape(5, -1).T, mode_rows[0, 0].reshape(-1)...  80.7 us
    ppermute x6, starting transfers between devices, with_halo(): lax.ppermute(lax.slice_in_dim(block, block.shape[dim] - width, None, axis...  20.2 us
    dot_general x12, matrix products, face_term(): jnp.einsum('fh,h...->f...', matrix, difference, precision=highest)  17.6 us
    unnamed x76, local copies, waits for them, and re-layouts  16.8 us
    ppermute x6, starting transfers between devices, with_halo(): lax.ppermute(lax.slice_in_dim(block, 0, width, axis=dim), axis, backward)  15.7 us
    dot_general x2, matrix products, phase_rate(): jnp.einsum('dfg,gne->dfne', flux_jacobian, current.astype(jnp.float32), p...  15 us
    dot_general x7, other arithmetic, face_term(): jnp.einsum('fh,h...->f...', matrix, difference, precision=highest)  13 us
  transfers between devices with their start and end apart: 12, of which 0 were waited for; matrix products, arithmetic and copies ran while one was open for 37% of the time, Pallas kernels for 0%

commit v1 on v0

v1 whole, which is shorter than its diff:
```python
import functools

import jax
import jax.numpy as jnp
import numpy as np
from jax import lax
from jax.experimental import pallas as pl
from jax.experimental.pallas import tpu as pltpu
from jax.sharding import PartitionSpec as P

FIELDS = 5
NODES = 64
EX = 12
CELLS = 128
SPAN_CELLS = 32
PAIR = 2 * CELLS
MIXED = 352
TIME_STEP = 0.4
f32 = jnp.float32
bf16 = jnp.bfloat16


def trace_selector():
    pick = np.zeros((64, 64), np.float32)
    for first in range(4):
        for second in range(4):
            w = 4 * first + second
            pick[w, 16 * first + second] = 1
            pick[16 + w, 16 * first + 12 + second] = 1
            pick[32 + w, 16 * first + 4 * second] = 1
            pick[48 + w, 16 * first + 4 * second + 3] = 1
    return jnp.asarray(pick, bf16)


def dot(a, b):
    return jnp.dot(a, b, preferred_element_type=f32)


def lanes():
    return lax.broadcasted_iota(jnp.int32, (16, CELLS), 1)


def plane_kernel(rows_ref, seeds_ref, shape_ref, plane_ref, rows_t, shape_t, *, normalizer):
    rows_t[...] = rows_ref[...].T
    shape_t[...] = shape_ref[...].T
    seeds = seeds_ref[...]
    signs = [(2 * ((seeds >> f) & 1) - 1).astype(f32) for f in range(FIELDS)]
    signs = [jnp.broadcast_to(s, (32, s.shape[1])).astype(bf16) for s in signs]
    eddies = rows_ref.shape[0]
    high_row = lax.broadcasted_iota(jnp.int32, (16, eddies), 0)
    low_row = lax.broadcasted_iota(jnp.int32, (CELLS, eddies), 0)

    def chunk(i, total):
        start = pl.multiple_of(i * 8, 8)
        rows = rows_t[pl.ds(start, 8), :]
        shapes = shape_t[pl.ds(start, 8), :]
        for q in range(8):
            row, shape = rows[q : q + 1], shapes[q : q + 1]
            placed = jnp.where((row >> 7) == high_row, shape, 0.0)
            coarse = placed.astype(bf16)
            fine = (placed - coarse.astype(f32)).astype(bf16)
            both = jnp.concatenate([coarse, fine], axis=0)
            signed = jnp.concatenate([both * s for s in signs], axis=0)
            hot = jnp.where((row & 127) == low_row, 1.0, 0.0).astype(bf16)
            total = total + lax.dot_general(
                signed, hot, (((1,), (1,)), ((), ())), preferred_element_type=f32
            )
        return total

    total = lax.fori_loop(0, rows_ref.shape[1] // 8, chunk, jnp.zeros((160, CELLS), f32))
    for f in range(FIELDS):
        plane_ref[f] = (total[32 * f : 32 * f + 16] + total[32 * f + 16 : 32 * f + 32]) * normalizer


def pack_pitch(traces, lane):
    (low0, high0), (low1, high1) = traces
    return jnp.where(
        lane < 32,
        low0,
        jnp.where(
            lane < 64,
            pltpu.roll(low1, 32, 1),
            jnp.where(lane < 96, pltpu.roll(high0, 96, 1), high1),
        ),
    )


def pack_span(held, low, high, layer, first_span, lane):
    edge = jnp.where(first_span, high, low)
    shift = lax.rem(layer + jnp.where(first_span, 97, 0), 128)
    return jnp.where((lane & 31) == layer, pltpu.roll(edge, shift, 1), held)


def pack_pair(values, pair, pick, first_span, lane, pitch_ref, span_held):
    for f in range(FIELDS):
        trace = dot(pick, values[f])
        halves = [trace[:, :CELLS], trace[:, CELLS:]]
        packed = pack_pitch([(h[0:16], h[16:32]) for h in halves], lane)
        at = pl.multiple_of(pair * CELLS, CELLS)
        pitch_ref[f, :, pl.ds(at, CELLS)] = packed.astype(bf16)
        held = span_held[f]
        for h in range(2):
            held = pack_span(
                held, halves[h][32:48], halves[h][48:64], 2 * pair + h, first_span, lane
            )
        span_held[f] = held


def pack_kernel(v_ref, pick_ref, up_ref, down_ref, pitch_ref, span_ref, span_held):
    first_span = lax.axis_index("span") == 0
    lane = lanes()
    pick = pick_ref[...]
    span_held[...] = jnp.zeros_like(span_held)

    def step(pair, _):
        at = pl.multiple_of(pair * PAIR, PAIR)
        values = [v_ref[f, :, pl.ds(at, PAIR)] for f in range(FIELDS)]
        pack_pair(values, pair, pick, first_span, lane, pitch_ref, span_held)
        return 0

    lax.fori_loop(0, EX // 2, step, 0)
    span_ref[...] = span_held[...].astype(bf16)
    up_ref[...] = v_ref[:, 48:64, (EX - 1) * CELLS :]
    down_ref[...] = v_ref[:, 0:16, 0:CELLS]


def mix(coefs, base, arrays):
    total = coefs[base] * arrays[0]
    for g in range(1, FIELDS):
        total = total + coefs[base + g] * arrays[g]
    return total


def advance(
    width, read, lower, upper, pitch, span, pinned, layers, coefs, weights, pick, smooth, mixed,
    first_span, lane, base=None,
):
    for r in range(0, NODES, 16):
        rows = [read(f, r, r + 16).astype(f32) for f in range(FIELDS)]
        for d in range(3):
            for f in range(FIELDS):
                mixed[f, 64 * d + r : 64 * d + r + 16, 0:width] = mix(
                    coefs, 25 * d + 5 * f, rows
                ).astype(bf16)
    jumps = [[None] * FIELDS for _ in range(6)]
    for f in range(FIELDS):
        jumps[0][f] = lower(f) - read(f, 0, 16).astype(f32)
        jumps[1][f] = upper(f) - read(f, 48, 64).astype(f32)
        trace = dot(pick, read(f, 0, 64))
        near, far = pitch(f), span(f)
        parts = [[], [], [], []]
        for h, layer in enumerate(layers):
            t = trace[:, h * CELLS : (h + 1) * CELLS]
            pl_low, pl_high, sp_low, sp_high = t[0:16], t[16:32], t[32:48], t[48:64]
            below = jnp.where(
                lane < 32, pltpu.roll(near, 64 if h == 0 else 32, 1), pltpu.roll(pl_high, 32, 1)
            )
            above = jnp.where(
                lane >= 96, pltpu.roll(near, 96 if h == 0 else 64, 1), pltpu.roll(pl_low, 96, 1)
            )
            shift = lax.rem(jnp.where(first_span, 31, 128) - layer, 128)
            arrived = pltpu.roll(far, shift, 1)
            left = jnp.where(
                (lane & 31) == 0, jnp.where(first_span, sp_low, arrived), pltpu.roll(sp_high, 1, 1)
            )
            right = jnp.where(
                (lane & 31) == 31,
                jnp.where(first_span, arrived, sp_high),
                pltpu.roll(sp_low, 127, 1),
            )
            for held, now in zip(
                parts, (below - pl_low, above - pl_high, left - sp_low, right - sp_high)
            ):
                held.append(now)
        for t in range(4):
            p = parts[t]
            jumps[2 + t][f] = p[0] if len(p) == 1 else jnp.concatenate(p, axis=1)
    for t in range(6):
        for f in range(FIELDS):
            mixed[f, 192 + 16 * t : 208 + 16 * t, 0:width] = mix(
                coefs, 75 + 25 * t + 5 * f, jumps[t]
            ).astype(bf16)
    out = []
    for f in range(FIELDS):
        v = read(f, 0, 64).astype(f32)
        mixed[f, 288:352, 0:width] = (v * pinned).astype(bf16)
        rate = dot(weights, mixed[f, :, 0:width])
        if base is None:
            trial = v - TIME_STEP * rate
        else:
            trial = 0.5 * (base(f).astype(f32) + v - TIME_STEP * rate)
        out.append(dot(smooth, trial.astype(bf16)).astype(bf16))
    return out


def fill_stream(v_ref, from_below, from_above, lower_all, upper_all):
    rans = lax.axis_index("rans")
    last = rans == lax.axis_size("rans") - 1
    lower_all[:, :, CELLS:] = v_ref[:, 48:64, : (EX - 1) * CELLS]
    lower_all[:, :, :CELLS] = from_below[...]
    upper_all[:, :, : (EX - 1) * CELLS] = v_ref[:, 0:16, CELLS:]
    edge = v_ref[:, 48:64, (EX - 1) * CELLS :]
    upper_all[:, :, (EX - 1) * CELLS :] = jnp.where(last, edge, from_above[...])


def phase_kernel(
    *refs, second
):
    if second:
        (v_ref, base_ref, below_ref, above_ref, near_ref, far_ref, pin_ref, coefs, weights_ref,
         pick_ref, smooth_ref, out_ref, mixed, lower_all, upper_all) = refs
    else:
        (v_ref, below_ref, above_ref, near_ref, far_ref, pin_ref, coefs, weights_ref, pick_ref,
         smooth_ref, out_ref, up_ref, down_ref, pitch_ref, span_ref, mixed, lower_all, upper_all,
         span_held) = refs
    first_span = lax.axis_index("span") == 0
    lane = lanes()
    fill_stream(v_ref, below_ref, above_ref, lower_all, upper_all)
    pick, weights, smooth = pick_ref[...], weights_ref[...], smooth_ref[...]
    if not second:
        span_held[...] = jnp.zeros_like(span_held)

    def step(pair, _):
        at = pl.ds(pl.multiple_of(pair * PAIR, PAIR), PAIR)
        near_at = pl.ds(pl.multiple_of(pair * CELLS, CELLS), CELLS)
        values = advance(
            PAIR,
            lambda f, r0, r1: v_ref[f, r0:r1, at],
            lambda f: lower_all[f, :, at].astype(f32),
            lambda f: upper_all[f, :, at].astype(f32),
            lambda f: near_ref[f, :, near_at].astype(f32),
            lambda f: far_ref[f].astype(f32),
            pin_ref[:, at].astype(f32),
            [2 * pair, 2 * pair + 1],
            coefs, weights, pick, smooth, mixed, first_span, lane,
            base=(lambda f: base_ref[f, :, at]) if second else None,
        )
        for f in range(FIELDS):
            out_ref[f, :, at] = values[f]
        if not second:
            pack_pair(values, pair, pick, first_span, lane, pitch_ref, span_held)
        return 0

    lax.fori_loop(0, EX // 2, step, 0)
    if not second:
        span_ref[...] = span_held[...].astype(bf16)
        up_ref[...] = out_ref[:, 48:64, (EX - 1) * CELLS :]
        down_ref[...] = out_ref[:, 0:16, 0:CELLS]


def inflow_of(mean_ref, amp_ref, plane_ref):
    return lambda f: mean_ref[f] + amp_ref[f] * plane_ref[f]


def first_fix_kernel(
    v_ref, mean_ref, amp_ref, plane_ref, near_ref, far_ref, pin_ref, coefs, weights_ref, pick_ref,
    smooth_ref, out_ref, pitch_ref, span_ref, mixed,
):
    first_span = lax.axis_index("span") == 0
    lane = lanes()

    @pl.when(lax.axis_index("rans") == 0)
    def _():
        pick = pick_ref[...]
        values = advance(
            CELLS,
            lambda f, r0, r1: v_ref[f, r0:r1, 0:CELLS],
            inflow_of(mean_ref, amp_ref, plane_ref),
            lambda f: v_ref[f, 0:16, CELLS:PAIR].astype(f32),
            lambda f: near_ref[f, :, 0:CELLS].astype(f32),
            lambda f: far_ref[f].astype(f32),
            pin_ref[:, 0:CELLS].astype(f32),
            [0],
            coefs, weights_ref[...], pick, smooth_ref[...], mixed, first_span, lane,
        )
        for f in range(FIELDS):
            out_ref[f] = values[f]
            t = dot(pick, values[f])
            pitch_ref[f] = jnp.where(lane < 32, t[0:16], pltpu.roll(t[16:32], 96, 1)).astype(bf16)
            span_ref[f] = pack_span(
                jnp.zeros((16, CELLS), f32), t[32:48], t[48:64], 0, first_span, lane
            ).astype(bf16)


def second_fix_kernel(
    held_ref, base_ref, v0_ref, v_ref, mean_ref, amp_ref, plane_ref, near0_ref, far0_ref, near_ref,
    far_ref, pin_ref, coefs, weights_ref, pick_ref, smooth_ref, out_ref, mixed, joined,
):
    first_span = lax.axis_index("span") == 0
    lane = lanes()
    first_rans = lax.axis_index("rans") == 0

    @pl.when(first_rans)
    def _():
        joined[:, :, 0:CELLS] = v0_ref[...]
        joined[:, :, CELLS:] = v_ref[:, :, CELLS : 3 * CELLS]
        inflow = inflow_of(mean_ref, amp_ref, plane_ref)

        def near(f):
            return jnp.where(
                (lane & 63) < 32, near0_ref[f].astype(f32), near_ref[f, :, 0:CELLS].astype(f32)
            )

        def far(f):
            return jnp.where((lane & 31) == 0, far0_ref[f].astype(f32), far_ref[f].astype(f32))

        values = advance(
            PAIR,
            lambda f, r0, r1: joined[f, r0:r1, 0:PAIR],
            lambda f: jnp.concatenate(
                [inflow(f), joined[f, 48:64, 0:CELLS].astype(f32)], axis=1
            ),
            lambda f: joined[f, 0:16, CELLS : 3 * CELLS].astype(f32),
            near,
            far,
            pin_ref[:, 0:PAIR].astype(f32),
            [0, 1],
            coefs, weights_ref[...], pick_ref[...], smooth_ref[...], mixed, first_span, lane,
            base=lambda f: base_ref[f],
        )
        for f in range(FIELDS):
            out_ref[f] = values[f]

    @pl.when(jnp.logical_not(first_rans))
    def _():
        out_ref[...] = held_ref[...]


VMEM = pl.BlockSpec(memory_space=pltpu.VMEM)
SMEM = pl.BlockSpec(memory_space=pltpu.SMEM)
PARAMS = pltpu.CompilerParams(vmem_limit_bytes=40 * 2**20)


def shape_of(*dims, dtype=bf16):
    return jax.ShapeDtypeStruct(dims, dtype)


def front(*dims):
    return pl.BlockSpec(dims, lambda i: (0,) * len(dims))


def cost(us):
    return pl.CostEstimate(flops=int(us * 1e8), bytes_accessed=int(us * 3e6), transcendentals=0)


def body(
    solution, volume_ops, flux_jacobian, lift_matrix, filter_matrix, wall_matrix, pinched_map,
    mode_rows, mode_seeds, mode_shape, mean_inflow, eddy_amplitude,
):
    ranks = lax.axis_size("rans")
    eddies, foot = mode_shape.shape[2:]
    plane_rows = mean_inflow.shape[3]
    faces = shape_of(FIELDS, 16, CELLS)
    pick = trace_selector()

    plane = pl.pallas_call(
        functools.partial(
            plane_kernel, normalizer=float((plane_rows / (eddies * ranks * foot)) ** 0.5)
        ),
        out_shape=shape_of(FIELDS, 16, CELLS, dtype=f32),
        in_specs=[VMEM] * 3,
        out_specs=VMEM,
        scratch_shapes=[pltpu.VMEM((foot, eddies), jnp.int32), pltpu.VMEM((foot, eddies), f32)],
        compiler_params=PARAMS,
        cost_estimate=cost(4),
        name="eddy_plane",
    )(mode_rows.reshape(eddies, foot), mode_seeds.reshape(1, eddies), mode_shape.reshape(eddies, foot))

    def gather_sum(value, offsets, roots):
        parts = [lax.ppermute(value, "rans", [(r + o, r) for r in roots]) for o in offsets]
        for part in parts:
            value = value + part
        return value

    plane = gather_sum(plane, (2, 4, 6), [8 * z + c for z in range(8) for c in range(2)])
    plane = gather_sum(plane, (1, 8, 9), [0, 16, 32, 48])
    plane = gather_sum(plane, (16, 32, 48), [0])

    weights = jnp.concatenate(
        [volume_ops[0], volume_ops[1], volume_ops[2], lift_matrix, wall_matrix], axis=1
    )
    identity = jnp.eye(FIELDS, dtype=f32)
    sides = jnp.array([-1.0, 1.0], f32)
    face_coefs = (
        0.5 * sides[None, :, None, None] * flux_jacobian[:, None] - 0.5 * identity
    ).reshape(-1)
    coefs = jnp.concatenate([flux_jacobian.reshape(-1), face_coefs])
    pins = pinched_map.reshape(1, -1)
    fixed = (pins, coefs, weights, pick, filter_matrix)
    fixed_specs = [VMEM, SMEM, VMEM, VMEM, VMEM]
    elements = solution.shape[2]
    sends = (faces, faces, shape_of(FIELDS, 16, EX // 2 * CELLS), faces)

    def exchange(up, down, pitch, span):
        rise = [(i, i + 1) for i in range(ranks - 1)]
        swap = [(0, 1), (1, 0)]
        return (
            lax.ppermute(up, "rans", rise),
            lax.ppermute(down, "rans", [(b, a) for a, b in rise]),
            lax.ppermute(pitch, "pitch", swap),
            lax.ppermute(span, "span", swap),
        )

    span_scratch = pltpu.VMEM((FIELDS, 16, CELLS), f32)
    sent = pl.pallas_call(
        pack_kernel,
        out_shape=sends,
        in_specs=[VMEM] * 2,
        out_specs=(VMEM,) * 4,
        scratch_shapes=[span_scratch],
        compiler_params=PARAMS,
        cost_estimate=cost(2),
        name="pack_faces",
    )(solution, pick)
    halo_one = exchange(*sent)

    scratch = [
        pltpu.VMEM((FIELDS, MIXED, PAIR), bf16),
        pltpu.VMEM((FIELDS, 16, elements), bf16),
        pltpu.VMEM((FIELDS, 16, elements), bf16),
    ]
    phase_one, *sent = pl.pallas_call(
        functools.partial(phase_kernel, second=False),
        out_shape=(shape_of(*solution.shape),) + sends,
        in_specs=[VMEM] * 5 + fixed_specs,
        out_specs=(VMEM,) * 5,
        scratch_shapes=scratch + [span_scratch],
        compiler_params=PARAMS,
        cost_estimate=cost(8),
        name="phase_one",
    )(solution, *halo_one, *fixed)
    halo_two = exchange(*sent)
    result = pl.pallas_call(
        functools.partial(phase_kernel, second=True),
        out_shape=shape_of(*solution.shape),
        in_specs=[VMEM] * 6 + fixed_specs,
        out_specs=VMEM,
        scratch_shapes=scratch,
        compiler_params=PARAMS,
        cost_estimate=cost(8),
        name="phase_two",
    )(phase_one, solution, *halo_two, *fixed)

    mean = mean_inflow.reshape(FIELDS, 16, CELLS)
    amplitude = eddy_amplitude.reshape(FIELDS, 16, CELLS)
    block = front(FIELDS, NODES, PAIR)
    face_block = front(FIELDS, 16, CELLS)
    fixed_blocks = [front(1, PAIR), SMEM, front(NODES, MIXED), front(64, 64), front(64, 64)]
    edge, *sent = pl.pallas_call(
        first_fix_kernel,
        grid=(1,),
        out_shape=(shape_of(FIELDS, NODES, CELLS), faces, faces),
        in_specs=[block] + [face_block] * 5 + fixed_blocks,
        out_specs=(front(FIELDS, NODES, CELLS), face_block, face_block),
        scratch_shapes=[pltpu.VMEM((FIELDS, MIXED, CELLS), bf16)],
        compiler_params=PARAMS,
        cost_estimate=cost(1),
        name="inflow_phase_one",
    )(solution, mean, amplitude, plane, halo_one[2], halo_one[3], *fixed)
    axes = ("rans", "pitch", "span")
    near0 = lax.ppermute(sent[0], axes, [(0, 2), (2, 0), (1, 3), (3, 1)])
    far0 = lax.ppermute(sent[1], axes, [(0, 1), (1, 0), (2, 3), (3, 2)])
    return pl.pallas_call(
        second_fix_kernel,
        grid=(1,),
        out_shape=shape_of(*solution.shape),
        in_specs=[block, block, front(FIELDS, NODES, CELLS), front(FIELDS, NODES, 3 * CELLS)]
        + [face_block] * 7
        + fixed_blocks,
        out_specs=block,
        scratch_shapes=[
            pltpu.VMEM((FIELDS, MIXED, PAIR), bf16),
            pltpu.VMEM((FIELDS, NODES, 3 * CELLS), bf16),
        ],
        input_output_aliases={0: 0},
        compiler_params=PARAMS,
        cost_estimate=cost(2),
        name="inflow_phase_two",
    )(
        result, solution, edge, phase_one, mean, amplitude, plane, near0, far0, halo_two[2],
        halo_two[3], *fixed,
    )


def solution(mesh):
    spread = P(None, None, ("rans", "pitch", "span"))
    in_specs = (
        spread,
        P(),
        P(),
        P(),
        P(),
        P(),
        P(("rans", "pitch", "span")),
        P("pitch", "span", "rans", None),
        P("pitch", "span", "rans"),
        P("pitch", "span", "rans", None),
        P("pitch", "span", None, None),
        P("pitch", "span", None, None),
    )
    return jax.shard_map(body, mesh=mesh, in_specs=in_specs, out_specs=spread, check_vma=False)
```

time: 585 us -> 73.6 us (0.13)
  the two profiles are of different devices: /device:TPU:1 before, /device:TPU:128 now
where the time goes in v1:
time: 73.6 us; the launch traced here: 73.1 us
  starting transfers between devices  38.3 us (52%)
  Pallas kernels  26.6 us (36%)
  waiting for transfers between devices  3.94 us (5%)
  local copies, waits for them, and re-layouts  3.62 us (5%)
    ppermute x2, starting transfers between devices, exchange(): lax.ppermute(down, 'rans', [(b, a) for a, b in rise])  13.9 us
    ppermute x9, starting transfers between devices, gather_sum(): lax.ppermute(value, 'rans', [(r + o, r) for r in roots])  10.4 us
    pallas_call x1, Pallas kernels, body(): pl.pallas_call(functools.partial(phase_kernel, second=False), out_shape=(...  10.2 us
    pallas_call x1, Pallas kernels, body(): pl.pallas_call(functools.partial(phase_kernel, second=True), out_shape=sh...  9.81 us
    ppermute x2, starting transfers between devices, exchange(): lax.ppermute(pitch, 'pitch', swap)  5.75 us
    ppermute x2, starting transfers between devices, exchange(): lax.ppermute(up, 'rans', rise)  3.84 us
    unnamed x27, local copies, waits for them, and re-layouts  3.32 us
    ppermute x2, starting transfers between devices, exchange(): lax.ppermute(span, 'span', swap)  3.08 us
  transfers between devices with their start and end apart: 19, of which 4 were waited for; matrix products, arithmetic and copies ran while one was open for 1% of the time, Pallas kernels for 30%

profile of v1, /device:TPU:128, one launch (start us, length us, event | category | flops | bytes accessed | tf_op | source)
XLA Modules:
  0.0 73.1 jit_solution(15261735550214484010)
XLA Ops:
  0.0 1.0 %copy.22 = s32[1,1,256,64]{3,2,1,0:T(8,128)S(1)} copy(s32[1,1,256,64]{2,3,1,0:T(8,128)} %param.21) | data formatting | bytes 131072 | tf_op args[7]
  1.0 0.9 %copy.23 = f32[1,1,256,64]{3,2,1,0:T(8,128)S(1)} copy(f32[1,1,256,64]{2,3,1,0:T(8,128)} %param.23) | data formatting | bytes 131072 | tf_op args[9]
  2.6 2.9 %eddy_plane.1 = f32[5,16,128]{2,1,0:T(8,128)S(1)} custom-call(s32[256,64]{1,0:T(8,128)S(1)} %bitcast.15, s32[1,256]{1,0:T(1,128)S(1)} %bitcast.17, f32[256,64]{1,0:T(8,128)S(1)} %bitcast.16), custom_call_target="tpu_custom_call" | custom-call | flops 400000000 | bytes 12000000 | tf_op jit(solution)/shard_map/eddy_plane/pallas_call | solution.py:356
  5.6 1.3 %collective-permute-start.10 = (f32[5,16,128]{2,1,0:T(8,128)S(1)}, f32[5,16,128]{2,1,0:T(8,128)S(1)}, u32[]{:S(2)}, u32[]{:S(2)}) collective-permute-start(f32[5,16,128]{2,1,0:T(8,128)S(1)} %eddy_plane.1), channel_id=1, source_target_pairs={{24,0},{28,4},{56,32},{60,36},{88,64},{92,68},{120,96},{124,100},{... | collective-permute-start | bytes 122888 | tf_op jit(solution)/shard_map/ppermute | solution.py:370
  6.9 1.3 %collective-permute-start.9 = (f32[5,16,128]{2,1,0:T(8,128)S(1)}, f32[5,16,128]{2,1,0:T(8,128)S(1)}, u32[]{:S(2)}, u32[]{:S(2)}) collective-permute-start(f32[5,16,128]{2,1,0:T(8,128)S(1)} %eddy_plane.1), channel_id=1, source_target_pairs={{16,0},{20,4},{48,32},{52,36},{80,64},{84,68},{112,96},{116,100},{... | collective-permute-start | bytes 122888 | tf_op jit(solution)/shard_map/ppermute | solution.py:370
  8.2 1.3 %collective-permute-start.8 = (f32[5,16,128]{2,1,0:T(8,128)S(1)}, f32[5,16,128]{2,1,0:T(8,128)S(1)}, u32[]{:S(2)}, u32[]{:S(2)}) collective-permute-start(f32[5,16,128]{2,1,0:T(8,128)S(1)} %eddy_plane.1), channel_id=1, source_target_pairs={{8,0},{12,4},{40,32},{44,36},{72,64},{76,68},{104,96},{108,100},{1... | collective-permute-start | bytes 122888 | tf_op jit(solution)/shard_map/ppermute | solution.py:370
  9.5 1.5 %pack_faces.1 = (bf16[5,16,128]{2,1,0:T(8,128)(2,1)S(1)}, bf16[5,16,128]{2,1,0:T(8,128)(2,1)S(1)}, bf16[5,16,768]{2,1,0:T(8,128)(2,1)S(1)}, bf16[5,16,128]{2,1,0:T(8,128)(2,1)S(1)}) custom-call(bf16[5,64,1536]{2,1,0:T(8,128)(2,1)S(1)} %copy-done, bf16[64,64]{1,0:T(8,128)(2,1)S(1)} %copy-done.1), custom_call_target="tpu_custom_call" | custom-call | flops 200000000 | bytes 6000000 | tf_op jit(solution)/shard_map/pack_faces/pallas_call | solution.py:405
  11.0 1.9 %collective-permute-start = (bf16[5,16,128]{2,1,0:T(8,128)(2,1)S(1)}, bf16[5,16,128]{2,1,0:T(8,128)(2,1)S(1)}, u32[]{:S(2)}, u32[]{:S(2)}) collective-permute-start(bf16[5,16,128]{2,1,0:T(8,128)(2,1)S(1)} %get-tuple-element.17), channel_id=1, source_target_pairs={{0,4},{4,8},{8,12},{12,16},{16,20},{20,24},{24,28},{28,32},{32,36}... | collective-permute-start | bytes 61448 | tf_op jit(solution)/shard_map/ppermute | solution.py:398
  13.0 7.0 %collective-permute-start.1 = (bf16[5,16,128]{2,1,0:T(8,128)(2,1)S(1)}, bf16[5,16,128]{2,1,0:T(8,128)(2,1)S(1)}, u32[]{:S(2)}, u32[]{:S(2)}) collective-permute-start(bf16[5,16,128]{2,1,0:T(8,128)(2,1)S(1)} %get-tuple-element.18), channel_id=1, source_target_pairs={{4,0},{8,4},{12,8},{16,12},{20,16},{24,20},{28,24},{32,28},{36,32}... | collective-permute-start | bytes 61448 | tf_op jit(solution)/shard_map/ppermute | solution.py:399
  21.0 1.3 %collective-permute-start.13 = (f32[5,16,128]{2,1,0:T(8,128)S(1)}, f32[5,16,128]{2,1,0:T(8,128)S(1)}, u32[]{:S(2)}, u32[]{:S(2)}) collective-permute-start(f32[5,16,128]{2,1,0:T(8,128)S(1)} %add_add_fusion.2), channel_id=1, source_target_pairs={{36,0},{100,64},{164,128},{228,192},{37,1},{101,65},{165,129},{229... | collective-permute-start | bytes 122888 | tf_op jit(solution)/shard_map/ppermute | solution.py:370
  22.3 1.3 %collective-permute-start.12 = (f32[5,16,128]{2,1,0:T(8,128)S(1)}, f32[5,16,128]{2,1,0:T(8,128)S(1)}, u32[]{:S(2)}, u32[]{:S(2)}) collective-permute-start(f32[5,16,128]{2,1,0:T(8,128)S(1)} %add_add_fusion.2), channel_id=1, source_target_pairs={{32,0},{96,64},{160,128},{224,192},{33,1},{97,65},{161,129},{225,1... | collective-permute-start | bytes 122888 | tf_op jit(solution)/shard_map/ppermute | solution.py:370
  23.6 1.3 %collective-permute-start.11 = (f32[5,16,128]{2,1,0:T(8,128)S(1)}, f32[5,16,128]{2,1,0:T(8,128)S(1)}, u32[]{:S(2)}, u32[]{:S(2)}) collective-permute-start(f32[5,16,128]{2,1,0:T(8,128)S(1)} %add_add_fusion.2), channel_id=1, source_target_pairs={{4,0},{68,64},{132,128},{196,192},{5,1},{69,65},{133,129},{197,193... | collective-permute-start | bytes 122888 | tf_op jit(solution)/shard_map/ppermute | solution.py:370
  25.1 1.2 %collective-permute-done.13 = f32[5,16,128]{2,1,0:T(8,128)S(1)} collective-permute-done((f32[5,16,128]{2,1,0:T(8,128)S(1)}, f32[5,16,128]{2,1,0:T(8,128)S(1)}, u32[]{:S(2)}, u32[]{:S(2)}) %collective-permute-start.13) | collective-permute-done | bytes 40992 | tf_op jit(solution)/shard_map/ppermute | solution.py:370
  26.3 1.5 %collective-permute-start.3 = (bf16[5,16,128]{2,1,0:T(8,128)(2,1)S(1)}, bf16[5,16,128]{2,1,0:T(8,128)(2,1)S(1)}, u32[]{:S(2)}, u32[]{:S(2)}) collective-permute-start(bf16[5,16,128]{2,1,0:T(8,128)(2,1)S(1)} %get-tuple-element.20), channel_id=1, source_target_pairs={{0,1},{1,0},{2,3},{3,2},{4,5},{5,4},{6,7},{7,6},{8,9},{9,8},{10,11... | collective-permute-start | bytes 61448 | tf_op jit(solution)/shard_map/ppermute | solution.py:401
  28.2 3.0 %collective-permute-start.2 = (bf16[5,16,768]{2,1,0:T(8,128)(2,1)S(1)}, bf16[5,16,768]{2,1,0:T(8,128)(2,1)S(1)}, u32[]{:S(2)}, u32[]{:S(2)}) collective-permute-start(bf16[5,16,768]{2,1,0:T(8,128)(2,1)S(1)} %get-tuple-element.19), channel_id=1, source_target_pairs={{0,2},{2,0},{1,3},{3,1},{4,6},{6,4},{5,7},{7,5},{8,10},{10,8},{9,1... | collective-permute-start | bytes 368648 | tf_op jit(solution)/shard_map/ppermute | solution.py:400
  31.9 1.3 %collective-permute-start.15 = (f32[5,16,128]{2,1,0:T(8,128)S(1)}, f32[5,16,128]{2,1,0:T(8,128)S(1)}, u32[]{:S(2)}, u32[]{:S(2)}) collective-permute-start(f32[5,16,128]{2,1,0:T(8,128)S(1)} %add_add_fusion.1), channel_id=1, source_target_pairs={{128,0},{129,1},{130,2},{131,3}} | collective-permute-start | bytes 122888 | tf_op jit(solution)/shard_map/ppermute | solution.py:370
  34.6 10.2 %phase_one.1 = (bf16[5,64,1536]{2,1,0:T(8,128)(2,1)S(1)}, bf16[5,16,128]{2,1,0:T(8,128)(2,1)S(1)}, bf16[5,16,128]{2,1,0:T(8,128)(2,1)S(1)}, bf16[5,16,768]{2,1,0:T(8,128)(2,1)S(1)}, bf16[5,16,128]{2,1,0:T(8,128)(2,1)S(1)}) custom-call(bf16[5,64,1536]{2,1,0:T(8,128)(2,1)S(1)} %copy-done, bf16[5,16,128]{2,1,0:T(8,128)(2,1)S(1)} %collective-permute-done.refs_1_, ...), custom_call_target="tpu_custom_call" | custom-call | flops 800000000 | bytes 24000000 | tf_op jit(solution)/shard_map/phase_one/pallas_call | solution.py:422
  44.7 1.9 %collective-permute-start.4 = (bf16[5,16,128]{2,1,0:T(8,128)(2,1)S(1)}, bf16[5,16,128]{2,1,0:T(8,128)(2,1)S(1)}, u32[]{:S(2)}, u32[]{:S(2)}) collective-permute-start(bf16[5,16,128]{2,1,0:T(8,128)(2,1)S(1)} %get-tuple-element.22), channel_id=1, source_target_pairs={{0,4},{4,8},{8,12},{12,16},{16,20},{20,24},{24,28},{28,32},{32,36}... | collective-permute-start | bytes 61448 | tf_op jit(solution)/shard_map/ppermute | solution.py:398
  46.7 7.0 %collective-permute-start.5 = (bf16[5,16,128]{2,1,0:T(8,128)(2,1)S(1)}, bf16[5,16,128]{2,1,0:T(8,128)(2,1)S(1)}, u32[]{:S(2)}, u32[]{:S(2)}) collective-permute-start(bf16[5,16,128]{2,1,0:T(8,128)(2,1)S(1)} %get-tuple-element.23), channel_id=1, source_target_pairs={{4,0},{8,4},{12,8},{16,12},{20,16},{24,20},{28,24},{32,28},{36,32}... | collective-permute-start | bytes 61448 | tf_op jit(solution)/shard_map/ppermute | solution.py:399
  53.7 1.6 %collective-permute-start.7 = (bf16[5,16,128]{2,1,0:T(8,128)(2,1)S(1)}, bf16[5,16,128]{2,1,0:T(8,128)(2,1)S(1)}, u32[]{:S(2)}, u32[]{:S(2)}) collective-permute-start(bf16[5,16,128]{2,1,0:T(8,128)(2,1)S(1)} %get-tuple-element.25), channel_id=1, source_target_pairs={{0,1},{1,0},{2,3},{3,2},{4,5},{5,4},{6,7},{7,6},{8,9},{9,8},{10,11... | collective-permute-start | bytes 61448 | tf_op jit(solution)/shard_map/ppermute | solution.py:401
  55.2 2.7 %collective-permute-start.6 = (bf16[5,16,768]{2,1,0:T(8,128)(2,1)S(1)}, bf16[5,16,768]{2,1,0:T(8,128)(2,1)S(1)}, u32[]{:S(2)}, u32[]{:S(2)}) collective-permute-start(bf16[5,16,768]{2,1,0:T(8,128)(2,1)S(1)} %get-tuple-element.24), channel_id=1, source_target_pairs={{0,2},{2,0},{1,3},{3,1},{4,6},{6,4},{5,7},{7,5},{8,10},{10,8},{9,1... | collective-permute-start | bytes 368648 | tf_op jit(solution)/shard_map/ppermute | solution.py:400
  60.0 1.7 %collective-permute-done.6.refs_4_.near_ref = bf16[5,16,768]{2,1,0:T(8,128)(2,1)S(1)} collective-permute-done((bf16[5,16,768]{2,1,0:T(8,128)(2,1)S(1)}, bf16[5,16,768]{2,1,0:T(8,128)(2,1)S(1)}, u32[]{:S(2)}, u32[]{:S(2)}) %collective-permute-start.6) | collective-permute-done | bytes 122912 | tf_op jit(solution)/shard_map/ppermute | solution.py:400
  61.6 9.8 %phase_two.1.held_ref = bf16[5,64,1536]{2,1,0:T(8,128)(2,1)} custom-call(bf16[5,64,1536]{2,1,0:T(8,128)(2,1)S(1)} %get-tuple-element.21.refs_0_.v_ref, bf16[5,64,1536]{2,1,0:T(8,128)(2,1)S(1)} %copy-done, bf16[5,16,128]{2,1,0:T(8,128)(2,1)S(1)} %collective-permute-done.4.refs_2_, bf16[5,16,128]{2,1,0:T(8,128)(2,1)S(1)} %collective-permute-done.5.refs_3_, ...), custom_call_target="tpu_custom_call" | custom-call | flops 800000000 | bytes 24000000 | tf_op jit(solution)/shard_map/phase_two/pallas_call | solution.py:433
  71.4 1.6 %inflow_phase_two.1 = bf16[5,64,1536]{2,1,0:T(8,128)(2,1)} custom-call(bf16[5,64,1536]{2,1,0:T(8,128)(2,1)} %phase_two.1.held_ref, bf16[5,64,1536]{2,1,0:T(8,128)(2,1)S(1)} %copy-done, bf16[5,64,128]{2,1,0:T(8,128)(2,1)S(1)} %get-tuple-element.26.v0_ref, bf16[5,64,1536]{2,1,0:T(8,128)(2,1)S(1)} %get-tuple-element.21.refs_0_.v_ref, ...), custom_call_target="tpu_custom_call", output_to_operand_aliasing={{}: (0, {})} | custom-call | flops 200000000 | bytes 6000000 | tf_op jit(solution)/shard_map/inflow_phase_two/pallas_call | solution.py:463
  (58 shorter events, 6.2 us)
Async XLA Ops:
  0.0 9.5 %copy-start = (bf16[5,64,1536]{2,1,0:T(8,128)(2,1)S(1)}, bf16[5,64,1536]{2,1,0:T(8,128)(2,1)}, u32[]{:S(2)}) copy-start(bf16[5,64,1536]{2,1,0:T(8,128)(2,1)} %base_ref.1) | copy-start | bytes 2949124
  2.6 6.8 %copy-start.1 = (bf16[64,64]{1,0:T(8,128)(2,1)S(1)}, bf16[64,64]{1,0:T(8,128)(2,1)}, u32[]{:S(2)}) copy-start(bf16[64,64]{1,0:T(8,128)(2,1)} %constant.9.clone.pick_ref.refs_8_.refs_9_) | copy-start | bytes 24580
  5.6 15.4 %collective-permute-start.10 = (f32[5,16,128]{2,1,0:T(8,128)S(1)}, f32[5,16,128]{2,1,0:T(8,128)S(1)}, u32[]{:S(2)}, u32[]{:S(2)}) collective-permute-start(f32[5,16,128]{2,1,0:T(8,128)S(1)} %eddy_plane.1), channel_id=1, source_target_pairs={{24,0},{28,4},{56,32},{60,36},{88,64},{92,68},{120,96},{124,100},{... | collective-permute-start | bytes 122888 | tf_op jit(solution)/shard_map/ppermute | solution.py:370
  6.9 14.1 %collective-permute-start.9 = (f32[5,16,128]{2,1,0:T(8,128)S(1)}, f32[5,16,128]{2,1,0:T(8,128)S(1)}, u32[]{:S(2)}, u32[]{:S(2)}) collective-permute-start(f32[5,16,128]{2,1,0:T(8,128)S(1)} %eddy_plane.1), channel_id=1, source_target_pairs={{16,0},{20,4},{48,32},{52,36},{80,64},{84,68},{112,96},{116,100},{... | collective-permute-start | bytes 122888 | tf_op jit(solution)/shard_map/ppermute | solution.py:370
  8.2 12.8 %collective-permute-start.8 = (f32[5,16,128]{2,1,0:T(8,128)S(1)}, f32[5,16,128]{2,1,0:T(8,128)S(1)}, u32[]{:S(2)}, u32[]{:S(2)}) collective-permute-start(f32[5,16,128]{2,1,0:T(8,128)S(1)} %eddy_plane.1), channel_id=1, source_target_pairs={{8,0},{12,4},{40,32},{44,36},{72,64},{76,68},{104,96},{108,100},{1... | collective-permute-start | bytes 122888 | tf_op jit(solution)/shard_map/ppermute | solution.py:370
  9.5 10.5 %copy-start.9 = (f32[3,5,5]{2,0,1:T(4,128)S(1)}, f32[3,5,5]{2,0,1:T(4,128)}, u32[]{:S(2)}) copy-start(f32[3,5,5]{2,0,1:T(4,128)} %param.16) | copy-start | bytes 904
  9.5 10.5 %copy-start.6 = (bf16[3,64,64]{2,1,0:T(8,128)(2,1)S(1)}, bf16[3,64,64]{2,1,0:T(8,128)(2,1)}, u32[]{:S(2)}) copy-start(bf16[3,64,64]{2,1,0:T(8,128)(2,1)} %param.15) | copy-start | bytes 73732
  11.0 20.9 %collective-permute-start = (bf16[5,16,128]{2,1,0:T(8,128)(2,1)S(1)}, bf16[5,16,128]{2,1,0:T(8,128)(2,1)S(1)}, u32[]{:S(2)}, u32[]{:S(2)}) collective-permute-start(bf16[5,16,128]{2,1,0:T(8,128)(2,1)S(1)} %get-tuple-element.17), channel_id=1, source_target_pairs={{0,4},{4,8},{8,12},{12,16},{16,20},{20,24},{24,28},{28,32},{32,36}... | collective-permute-start | bytes 61448 | tf_op jit(solution)/shard_map/ppermute | solution.py:398
  13.0 20.3 %collective-permute-start.1 = (bf16[5,16,128]{2,1,0:T(8,128)(2,1)S(1)}, bf16[5,16,128]{2,1,0:T(8,128)(2,1)S(1)}, u32[]{:S(2)}, u32[]{:S(2)}) collective-permute-start(bf16[5,16,128]{2,1,0:T(8,128)(2,1)S(1)} %get-tuple-element.18), channel_id=1, source_target_pairs={{4,0},{8,4},{12,8},{16,12},{20,16},{24,20},{28,24},{32,28},{36,32}... | collective-permute-start | bytes 61448 | tf_op jit(solution)/shard_map/ppermute | solution.py:399
  21.0 5.3 %collective-permute-start.13 = (f32[5,16,128]{2,1,0:T(8,128)S(1)}, f32[5,16,128]{2,1,0:T(8,128)S(1)}, u32[]{:S(2)}, u32[]{:S(2)}) collective-permute-start(f32[5,16,128]{2,1,0:T(8,128)S(1)} %add_add_fusion.2), channel_id=1, source_target_pairs={{36,0},{100,64},{164,128},{228,192},{37,1},{101,65},{165,129},{229... | collective-permute-start | bytes 122888 | tf_op jit(solution)/shard_map/ppermute | solution.py:370
  22.3 5.9 %collective-permute-start.12 = (f32[5,16,128]{2,1,0:T(8,128)S(1)}, f32[5,16,128]{2,1,0:T(8,128)S(1)}, u32[]{:S(2)}, u32[]{:S(2)}) collective-permute-start(f32[5,16,128]{2,1,0:T(8,128)S(1)} %add_add_fusion.2), channel_id=1, source_target_pairs={{32,0},{96,64},{160,128},{224,192},{33,1},{97,65},{161,129},{225,1... | collective-permute-start | bytes 122888 | tf_op jit(solution)/shard_map/ppermute | solution.py:370
  23.6 7.6 %collective-permute-start.11 = (f32[5,16,128]{2,1,0:T(8,128)S(1)}, f32[5,16,128]{2,1,0:T(8,128)S(1)}, u32[]{:S(2)}, u32[]{:S(2)}) collective-permute-start(f32[5,16,128]{2,1,0:T(8,128)S(1)} %add_add_fusion.2), channel_id=1, source_target_pairs={{4,0},{68,64},{132,128},{196,192},{5,1},{69,65},{133,129},{197,193... | collective-permute-start | bytes 122888 | tf_op jit(solution)/shard_map/ppermute | solution.py:370
  26.3 7.6 %collective-permute-start.3 = (bf16[5,16,128]{2,1,0:T(8,128)(2,1)S(1)}, bf16[5,16,128]{2,1,0:T(8,128)(2,1)S(1)}, u32[]{:S(2)}, u32[]{:S(2)}) collective-permute-start(bf16[5,16,128]{2,1,0:T(8,128)(2,1)S(1)} %get-tuple-element.20), channel_id=1, source_target_pairs={{0,1},{1,0},{2,3},{3,2},{4,5},{5,4},{6,7},{7,6},{8,9},{9,8},{10,11... | collective-permute-start | bytes 61448 | tf_op jit(solution)/shard_map/ppermute | solution.py:401
  28.2 6.4 %copy-start.4 = (bf16[64,64]{1,0:T(8,128)(2,1)S(1)}, bf16[64,64]{1,0:T(8,128)(2,1)}, u32[]{:S(2)}) copy-start(bf16[64,64]{1,0:T(8,128)(2,1)} %smooth_ref.3) | copy-start | bytes 24580
  28.2 6.4 %collective-permute-start.2 = (bf16[5,16,768]{2,1,0:T(8,128)(2,1)S(1)}, bf16[5,16,768]{2,1,0:T(8,128)(2,1)S(1)}, u32[]{:S(2)}, u32[]{:S(2)}) collective-permute-start(bf16[5,16,768]{2,1,0:T(8,128)(2,1)S(1)} %get-tuple-element.19), channel_id=1, source_target_pairs={{0,2},{2,0},{1,3},{3,1},{4,6},{6,4},{5,7},{7,5},{8,10},{10,8},{9,1... | collective-permute-start | bytes 368648 | tf_op jit(solution)/shard_map/ppermute | solution.py:400
  31.2 22.4 %collective-permute-start.16 = (f32[5,16,128]{2,1,0:T(8,128)S(1)}, f32[5,16,128]{2,1,0:T(8,128)S(1)}, u32[]{:S(2)}, u32[]{:S(2)}) collective-permute-start(f32[5,16,128]{2,1,0:T(8,128)S(1)} %add_add_fusion.1), channel_id=1, source_target_pairs={{192,0},{193,1},{194,2},{195,3}} | collective-permute-start | bytes 122888 | tf_op jit(solution)/shard_map/ppermute | solution.py:370
  31.9 23.3 %collective-permute-start.15 = (f32[5,16,128]{2,1,0:T(8,128)S(1)}, f32[5,16,128]{2,1,0:T(8,128)S(1)}, u32[]{:S(2)}, u32[]{:S(2)}) collective-permute-start(f32[5,16,128]{2,1,0:T(8,128)S(1)} %add_add_fusion.1), channel_id=1, source_target_pairs={{128,0},{129,1},{130,2},{131,3}} | collective-permute-start | bytes 122888 | tf_op jit(solution)/shard_map/ppermute | solution.py:370
  33.2 24.7 %collective-permute-start.14 = (f32[5,16,128]{2,1,0:T(8,128)S(1)}, f32[5,16,128]{2,1,0:T(8,128)S(1)}, u32[]{:S(2)}, u32[]{:S(2)}) collective-permute-start(f32[5,16,128]{2,1,0:T(8,128)S(1)} %add_add_fusion.1), channel_id=1, source_target_pairs={{64,0},{65,1},{66,2},{67,3}} | collective-permute-start | bytes 122888 | tf_op jit(solution)/shard_map/ppermute | solution.py:370
  44.7 14.5 %collective-permute-start.4 = (bf16[5,16,128]{2,1,0:T(8,128)(2,1)S(1)}, bf16[5,16,128]{2,1,0:T(8,128)(2,1)S(1)}, u32[]{:S(2)}, u32[]{:S(2)}) collective-permute-start(bf16[5,16,128]{2,1,0:T(8,128)(2,1)S(1)} %get-tuple-element.22), channel_id=1, source_target_pairs={{0,4},{4,8},{8,12},{12,16},{16,20},{20,24},{24,28},{28,32},{32,36}... | collective-permute-start | bytes 61448 | tf_op jit(solution)/shard_map/ppermute | solution.py:398
  46.7 13.3 %collective-permute-start.5 = (bf16[5,16,128]{2,1,0:T(8,128)(2,1)S(1)}, bf16[5,16,128]{2,1,0:T(8,128)(2,1)S(1)}, u32[]{:S(2)}, u32[]{:S(2)}) collective-permute-start(bf16[5,16,128]{2,1,0:T(8,128)(2,1)S(1)} %get-tuple-element.23), channel_id=1, source_target_pairs={{4,0},{8,4},{12,8},{16,12},{20,16},{24,20},{28,24},{32,28},{36,32}... | collective-permute-start | bytes 61448 | tf_op jit(solution)/shard_map/ppermute | solution.py:399
  53.7 6.3 %collective-permute-start.7 = (bf16[5,16,128]{2,1,0:T(8,128)(2,1)S(1)}, bf16[5,16,128]{2,1,0:T(8,128)(2,1)S(1)}, u32[]{:S(2)}, u32[]{:S(2)}) collective-permute-start(bf16[5,16,128]{2,1,0:T(8,128)(2,1)S(1)} %get-tuple-element.25), channel_id=1, source_target_pairs={{0,1},{1,0},{2,3},{3,2},{4,5},{5,4},{6,7},{7,6},{8,9},{9,8},{10,11... | collective-permute-start | bytes 61448 | tf_op jit(solution)/shard_map/ppermute | solution.py:401
  55.2 6.4 %collective-permute-start.6 = (bf16[5,16,768]{2,1,0:T(8,128)(2,1)S(1)}, bf16[5,16,768]{2,1,0:T(8,128)(2,1)S(1)}, u32[]{:S(2)}, u32[]{:S(2)}) collective-permute-start(bf16[5,16,768]{2,1,0:T(8,128)(2,1)S(1)} %get-tuple-element.24), channel_id=1, source_target_pairs={{0,2},{2,0},{1,3},{3,1},{4,6},{6,4},{5,7},{7,5},{8,10},{10,8},{9,1... | collective-permute-start | bytes 368648 | tf_op jit(solution)/shard_map/ppermute | solution.py:400
  58.6 12.8 %collective-permute-start.17 = (bf16[5,16,128]{2,1,0:T(8,128)(2,1)S(1)}, bf16[5,16,128]{2,1,0:T(8,128)(2,1)S(1)}, u32[]{:S(2)}, u32[]{:S(2)}) collective-permute-start(bf16[5,16,128]{2,1,0:T(8,128)(2,1)S(1)} %get-tuple-element.27), channel_id=1, source_target_pairs={{0,2},{2,0},{1,3},{3,1}} | collective-permute-start | bytes 61448 | tf_op jit(solution)/shard_map/ppermute | solution.py:461
  59.3 12.2 %collective-permute-start.18 = (bf16[5,16,128]{2,1,0:T(8,128)(2,1)S(1)}, bf16[5,16,128]{2,1,0:T(8,128)(2,1)S(1)}, u32[]{:S(2)}, u32[]{:S(2)}) collective-permute-start(bf16[5,16,128]{2,1,0:T(8,128)(2,1)S(1)} %get-tuple-element.28), channel_id=1, source_target_pairs={{0,1},{1,0},{2,3},{3,2}} | collective-permute-start | bytes 61448 | tf_op jit(solution)/shard_map/ppermute | solution.py:462
  (7 other events, 19.0 us)

commit v2 on v1

v2 whole, which is shorter than its diff:
```python
import functools

import jax
import jax.numpy as jnp
import numpy as np
from jax import lax
from jax.experimental import pallas as pl
from jax.experimental.pallas import tpu as pltpu
from jax.sharding import PartitionSpec as P

FIELDS = 5
NODES = 64
EX = 12
CELLS = 128
SPAN_CELLS = 32
PAIR = 2 * CELLS
MIXED = 352
TIME_STEP = 0.4
f32 = jnp.float32
bf16 = jnp.bfloat16


def trace_selector():
    pick = np.zeros((64, 64), np.float32)
    for first in range(4):
        for second in range(4):
            w = 4 * first + second
            pick[w, 16 * first + second] = 1
            pick[16 + w, 16 * first + 12 + second] = 1
            pick[32 + w, 16 * first + 4 * second] = 1
            pick[48 + w, 16 * first + 4 * second + 3] = 1
    return jnp.asarray(pick, bf16)


def dot(a, b):
    return jnp.dot(a, b, preferred_element_type=f32)


def lanes():
    return lax.broadcasted_iota(jnp.int32, (16, CELLS), 1)


def plane_kernel(rows_ref, seeds_ref, shape_ref, plane_ref, *, normalizer):
    seeds = seeds_ref[...]
    signs = [(2 * ((seeds >> f) & 1) - 1).astype(f32) for f in range(FIELDS)]
    signs = [jnp.broadcast_to(s, (32, s.shape[1])).astype(bf16) for s in signs]
    eddies = rows_ref.shape[1]
    high_row = lax.broadcasted_iota(jnp.int32, (16, eddies), 0)
    low_row = lax.broadcasted_iota(jnp.int32, (CELLS, eddies), 0)

    def chunk(i, total):
        start = pl.multiple_of(i * 8, 8)
        rows = rows_ref[pl.ds(start, 8), :]
        shapes = shape_ref[pl.ds(start, 8), :]
        for q in range(8):
            row, shape = rows[q : q + 1], shapes[q : q + 1]
            placed = jnp.where((row >> 7) == high_row, shape, 0.0)
            coarse = placed.astype(bf16)
            fine = (placed - coarse.astype(f32)).astype(bf16)
            both = jnp.concatenate([coarse, fine], axis=0)
            signed = jnp.concatenate([both * s for s in signs], axis=0)
            hot = jnp.where((row & 127) == low_row, 1.0, 0.0).astype(bf16)
            total = total + lax.dot_general(
                signed, hot, (((1,), (1,)), ((), ())), preferred_element_type=f32
            )
        return total

    total = lax.fori_loop(0, rows_ref.shape[0] // 8, chunk, jnp.zeros((160, CELLS), f32))
    for f in range(FIELDS):
        plane_ref[f] = (total[32 * f : 32 * f + 16] + total[32 * f + 16 : 32 * f + 32]) * normalizer


def pack_pitch(traces, lane):
    (low0, high0), (low1, high1) = traces
    return jnp.where(
        lane < 32,
        low0,
        jnp.where(
            lane < 64,
            pltpu.roll(low1, 32, 1),
            jnp.where(lane < 96, pltpu.roll(high0, 96, 1), high1),
        ),
    )


def pack_span(held, low, high, layer, first_span, lane):
    edge = jnp.where(first_span, high, low)
    shift = lax.rem(layer + jnp.where(first_span, 97, 0), 128)
    return jnp.where((lane & 31) == layer, pltpu.roll(edge, shift, 1), held)


def pack_pair(traces, pair, first_span, lane, pitch_ref, span_held):
    for f in range(FIELDS):
        halves = [traces[f][:, :CELLS], traces[f][:, CELLS:]]
        packed = pack_pitch([(h[0:16], h[16:32]) for h in halves], lane)
        pitch_ref[f, :, pair * CELLS : (pair + 1) * CELLS] = packed.astype(bf16)
        held = span_held[f]
        for h in range(2):
            held = pack_span(
                held, halves[h][32:48], halves[h][48:64], 2 * pair + h, first_span, lane
            )
        span_held[f] = held


def pack_kernel(
    v_ref, pick_ref, trace_ref, up_ref, down_ref, pitch_ref, span_ref, span_held
):
    first_span = lax.axis_index("span") == 0
    lane = lanes()
    pick = pick_ref[...]
    span_held[...] = jnp.zeros_like(span_held)
    for pair in range(EX // 2):
        at = slice(pair * PAIR, (pair + 1) * PAIR)
        traces = [dot(pick, v_ref[f, :, at]) for f in range(FIELDS)]
        for f in range(FIELDS):
            trace_ref[f, :, at] = traces[f].astype(bf16)
        pack_pair(traces, pair, first_span, lane, pitch_ref, span_held)
    span_ref[...] = span_held[...].astype(bf16)
    up_ref[...] = v_ref[:, 48:64, (EX - 1) * CELLS :]
    down_ref[...] = v_ref[:, 0:16, 0:CELLS]


def mix(coefs, base, arrays):
    total = coefs[base] * arrays[0]
    for g in range(1, FIELDS):
        total = total + coefs[base + g] * arrays[g]
    return total


def advance(
    read, trace, lower, upper, pitch, span, pinned, layers, coefs, weights, smooth, mixed,
    first_span, lane, base=None,
):
    for r in range(0, NODES, 16):
        rows = [read(f, r, r + 16).astype(f32) for f in range(FIELDS)]
        for d in range(3):
            for f in range(FIELDS):
                mixed[f, 64 * d + r : 64 * d + r + 16, :] = mix(
                    coefs, 25 * d + 5 * f, rows
                ).astype(bf16)
    jumps = [[None] * FIELDS for _ in range(6)]
    for f in range(FIELDS):
        jumps[0][f] = lower(f) - read(f, 0, 16).astype(f32)
        jumps[1][f] = upper(f) - read(f, 48, 64).astype(f32)
        own = trace(f).astype(f32)
        near, far = pitch(f), span(f)
        parts = [[], [], [], []]
        for h, layer in enumerate(layers):
            t = own[:, h * CELLS : (h + 1) * CELLS]
            pl_low, pl_high, sp_low, sp_high = t[0:16], t[16:32], t[32:48], t[48:64]
            below = jnp.where(
                lane < 32, pltpu.roll(near, 64 if h == 0 else 32, 1), pltpu.roll(pl_high, 32, 1)
            )
            above = jnp.where(
                lane >= 96, pltpu.roll(near, 96 if h == 0 else 64, 1), pltpu.roll(pl_low, 96, 1)
            )
            shift = lax.rem(jnp.where(first_span, 31, 128) - layer, 128)
            arrived = pltpu.roll(far, shift, 1)
            left = jnp.where(
                (lane & 31) == 0, jnp.where(first_span, sp_low, arrived), pltpu.roll(sp_high, 1, 1)
            )
            right = jnp.where(
                (lane & 31) == 31,
                jnp.where(first_span, arrived, sp_high),
                pltpu.roll(sp_low, 127, 1),
            )
            for held, now in zip(
                parts, (below - pl_low, above - pl_high, left - sp_low, right - sp_high)
            ):
                held.append(now)
        for t in range(4):
            p = parts[t]
            jumps[2 + t][f] = p[0] if len(p) == 1 else jnp.concatenate(p, axis=1)
    for t in range(6):
        for f in range(FIELDS):
            mixed[f, 192 + 16 * t : 208 + 16 * t, :] = mix(
                coefs, 75 + 25 * t + 5 * f, jumps[t]
            ).astype(bf16)
    out = []
    for f in range(FIELDS):
        v = read(f, 0, 64).astype(f32)
        mixed[f, 288:352, :] = (v * pinned).astype(bf16)
        rate = dot(weights, mixed[f])
        if base is None:
            trial = v - TIME_STEP * rate
        else:
            trial = 0.5 * (base(f).astype(f32) + v - TIME_STEP * rate)
        out.append(dot(smooth, trial.astype(bf16)))
    return out


def phase_kernel(*refs, second):
    if second:
        (v_ref, trace_ref, base_ref, mean_ref, amp_ref, plane_ref, below_ref, above_ref, near_ref,
         far_ref, pin_ref, coefs, weights_ref, smooth_ref, out_ref, mixed) = refs
    else:
        (v_ref, trace_ref, below_ref, above_ref, near_ref, far_ref, pin_ref, coefs, weights_ref,
         smooth_ref, out_ref, out_trace_ref, up_ref, down_ref, pitch_ref, span_ref, mixed,
         span_held) = refs
    first_span = lax.axis_index("span") == 0
    rans = lax.axis_index("rans")
    last_rans = rans == lax.axis_size("rans") - 1
    lane = lanes()
    weights, smooth = weights_ref[...], smooth_ref[...]
    if not second:
        span_held[...] = jnp.zeros_like(span_held)

    def lower(f, pair):
        if pair:
            return v_ref[f, 48:64, pair * PAIR - CELLS : (pair + 1) * PAIR - CELLS].astype(f32)
        edge = below_ref[f].astype(f32)
        if second:
            edge = jnp.where(rans == 0, inflow_of(mean_ref, amp_ref, plane_ref)(f), edge)
        return jnp.concatenate([edge, v_ref[f, 48:64, 0:CELLS].astype(f32)], axis=1)

    def upper(f, pair):
        first = pair * PAIR + CELLS
        if pair < EX // 2 - 1:
            return v_ref[f, 0:16, first : first + PAIR].astype(f32)
        edge = jnp.where(
            last_rans, v_ref[f, 48:64, first : first + CELLS].astype(f32), above_ref[f].astype(f32)
        )
        return jnp.concatenate([v_ref[f, 0:16, first : first + CELLS].astype(f32), edge], axis=1)

    for pair in range(EX // 2):
        at = slice(pair * PAIR, (pair + 1) * PAIR)
        values = advance(
            lambda f, r0, r1: v_ref[f, r0:r1, at],
            lambda f: trace_ref[f, :, at],
            lambda f: lower(f, pair),
            lambda f: upper(f, pair),
            lambda f: near_ref[f, :, pair * CELLS : (pair + 1) * CELLS].astype(f32),
            lambda f: far_ref[f].astype(f32),
            pin_ref[:, at].astype(f32),
            [2 * pair, 2 * pair + 1],
            coefs, weights, smooth, mixed.at[pair % mixed.shape[0]], first_span, lane,
            base=(lambda f: base_ref[f, :, at]) if second else None,
        )
        for f in range(FIELDS):
            out_ref[f, :, at] = values[f][0:64].astype(bf16)
        if not second:
            for f in range(FIELDS):
                out_trace_ref[f, :, at] = values[f][64:128].astype(bf16)
            pack_pair(
                [values[f][64:128] for f in range(FIELDS)], pair, first_span, lane, pitch_ref,
                span_held,
            )
    if not second:
        span_ref[...] = span_held[...].astype(bf16)
        up_ref[...] = out_ref[:, 48:64, (EX - 1) * CELLS :]
        down_ref[...] = out_ref[:, 0:16, 0:CELLS]


def inflow_of(mean_ref, amp_ref, plane_ref):
    return lambda f: mean_ref[f] + amp_ref[f] * plane_ref[f]


def inflow_kernel(
    held_ref, held_trace_ref, held_pitch_ref, held_span_ref, v_ref, trace_ref, mean_ref, amp_ref,
    plane_ref, near_ref, far_ref, pin_ref, coefs, weights_ref, smooth_ref, out_ref, out_trace_ref,
    pitch_ref, span_ref, mixed,
):
    first_span = lax.axis_index("span") == 0
    first_rans = lax.axis_index("rans") == 0
    lane = lanes()

    @pl.when(first_rans)
    def _():
        values = advance(
            lambda f, r0, r1: v_ref[f, r0:r1, 0:CELLS],
            lambda f: trace_ref[f],
            inflow_of(mean_ref, amp_ref, plane_ref),
            lambda f: v_ref[f, 0:16, CELLS:PAIR].astype(f32),
            lambda f: near_ref[f].astype(f32),
            lambda f: far_ref[f].astype(f32),
            pin_ref[...].astype(f32),
            [0],
            coefs, weights_ref[...], smooth_ref[...], mixed, first_span, lane,
        )
        for f in range(FIELDS):
            out_ref[f] = values[f][0:64].astype(bf16)
            t = values[f][64:128]
            out_trace_ref[f] = t.astype(bf16)
            pitch = jnp.where(lane < 32, t[0:16], pltpu.roll(t[16:32], 96, 1))
            pitch_ref[f] = jnp.where(
                (lane & 63) < 32, pitch, held_pitch_ref[f].astype(f32)
            ).astype(bf16)
            span_ref[f] = pack_span(
                held_span_ref[f].astype(f32), t[32:48], t[48:64], 0, first_span, lane
            ).astype(bf16)

    @pl.when(jnp.logical_not(first_rans))
    def _():
        out_ref[...] = held_ref[...]
        out_trace_ref[...] = held_trace_ref[...]
        pitch_ref[...] = held_pitch_ref[...]
        span_ref[...] = held_span_ref[...]


VMEM = pl.BlockSpec(memory_space=pltpu.VMEM)
SMEM = pl.BlockSpec(memory_space=pltpu.SMEM)
PARAMS = pltpu.CompilerParams(vmem_limit_bytes=40 * 2**20)
SLOTS = 2


def shape_of(*dims, dtype=bf16):
    return jax.ShapeDtypeStruct(dims, dtype)


def front(*dims):
    return pl.BlockSpec(dims, lambda i: (0,) * len(dims))


def cost(us):
    return pl.CostEstimate(flops=int(us * 1e8), bytes_accessed=int(us * 3e6), transcendentals=0)


def body(
    solution, volume_ops, flux_jacobian, lift_matrix, filter_matrix, wall_matrix, pinched_map,
    mode_rows, mode_seeds, mode_shape, mean_inflow, eddy_amplitude,
):
    ranks = lax.axis_size("rans")
    eddies, foot = mode_shape.shape[2:]
    plane_rows = mean_inflow.shape[3]
    faces = shape_of(FIELDS, 16, CELLS)
    pick = trace_selector()

    plane = pl.pallas_call(
        functools.partial(
            plane_kernel, normalizer=float((plane_rows / (eddies * ranks * foot)) ** 0.5)
        ),
        out_shape=shape_of(FIELDS, 16, CELLS, dtype=f32),
        in_specs=[VMEM] * 3,
        out_specs=VMEM,
        compiler_params=PARAMS,
        cost_estimate=cost(3),
        name="eddy_plane",
    )(mode_rows[0, 0].T, mode_seeds.reshape(1, eddies), mode_shape[0, 0].T)

    def gather_sum(value, offsets, roots):
        parts = [lax.ppermute(value, "rans", [(r + o, r) for r in roots]) for o in offsets]
        for part in parts:
            value = value + part
        return value

    plane = gather_sum(plane, (2, 4, 6), [8 * z + c for z in range(8) for c in range(2)])
    plane = gather_sum(plane, (1, 8, 9), [0, 16, 32, 48])
    plane = gather_sum(plane, (16, 32, 48), [0])

    weights = jnp.concatenate(
        [volume_ops[0], volume_ops[1], volume_ops[2], lift_matrix, wall_matrix], axis=1
    )
    identity = jnp.eye(FIELDS, dtype=f32)
    sides = jnp.array([-1.0, 1.0], f32)
    face_coefs = (
        0.5 * sides[None, :, None, None] * flux_jacobian[:, None] - 0.5 * identity
    ).reshape(-1)
    coefs = jnp.concatenate([flux_jacobian.reshape(-1), face_coefs])
    pins = pinched_map.reshape(1, -1)
    rows = filter_matrix.reshape(4, 4, 4, NODES)
    smooth = jnp.concatenate(
        [filter_matrix]
        + [part.reshape(16, NODES) for part in (rows[:, 0], rows[:, 3], rows[:, :, 0], rows[:, :, 3])]
    )
    fixed_specs = [VMEM, SMEM, VMEM, VMEM]
    elements = solution.shape[2]
    traces = shape_of(FIELDS, NODES, elements)
    sends = (faces, faces, shape_of(FIELDS, 16, EX // 2 * CELLS), faces)
    rise = [(i, i + 1) for i in range(ranks - 1)]
    fall = [(b, a) for a, b in rise]
    swap = [(0, 1), (1, 0)]

    span_scratch = pltpu.VMEM((FIELDS, 16, CELLS), f32)
    trace, up, down, pitch, span = pl.pallas_call(
        pack_kernel,
        out_shape=(traces,) + sends,
        in_specs=[VMEM] * 2,
        out_specs=(VMEM,) * 5,
        scratch_shapes=[span_scratch],
        compiler_params=PARAMS,
        cost_estimate=cost(2),
        name="pack_faces",
    )(solution, pick)
    below = lax.ppermute(up, "rans", rise)
    above = lax.ppermute(down, "rans", fall)
    near = lax.ppermute(pitch, "pitch", swap)
    far = lax.ppermute(span, "span", swap)

    scratch = [pltpu.VMEM((SLOTS, FIELDS, MIXED, PAIR), bf16)]
    phase_one, trace_one, up, down, pitch, span = pl.pallas_call(
        functools.partial(phase_kernel, second=False),
        out_shape=(traces, traces) + sends,
        in_specs=[VMEM] * 6 + fixed_specs,
        out_specs=(VMEM,) * 6,
        scratch_shapes=scratch + [span_scratch],
        compiler_params=PARAMS,
        cost_estimate=cost(6),
        name="phase_one",
    )(solution, trace, below, above, near, far, pins, coefs, weights, smooth)
    below = lax.ppermute(up, "rans", rise)
    above = lax.ppermute(down, "rans", fall)

    mean = mean_inflow.reshape(FIELDS, 16, CELLS)
    amplitude = eddy_amplitude.reshape(FIELDS, 16, CELLS)
    layer = front(FIELDS, NODES, CELLS)
    face = front(FIELDS, 16, CELLS)
    phase_one, trace_one, pitch, span = pl.pallas_call(
        inflow_kernel,
        grid=(1,),
        out_shape=(traces, traces, sends[2], sends[3]),
        in_specs=[layer, layer, face, face, front(FIELDS, NODES, PAIR), layer]
        + [face] * 5
        + [front(1, CELLS), SMEM, front(NODES, MIXED), front(2 * NODES, NODES)],
        out_specs=(layer, layer, face, face),
        scratch_shapes=[pltpu.VMEM((FIELDS, MIXED, CELLS), bf16)],
        input_output_aliases={0: 0, 1: 1, 2: 2, 3: 3},
        compiler_params=PARAMS,
        cost_estimate=cost(1),
        name="inflow_layer",
    )(
        phase_one, trace_one, pitch, span, solution, trace, mean, amplitude, plane, near, far,
        pins, coefs, weights, smooth,
    )
    near = lax.ppermute(pitch, "pitch", swap)
    far = lax.ppermute(span, "span", swap)
    return pl.pallas_call(
        functools.partial(phase_kernel, second=True),
        out_shape=traces,
        in_specs=[VMEM] * 10 + fixed_specs,
        out_specs=VMEM,
        scratch_shapes=scratch,
        compiler_params=PARAMS,
        cost_estimate=cost(6),
        name="phase_two",
    )(
        phase_one, trace_one, solution, mean, amplitude, plane, below, above, near, far, pins,
        coefs, weights, filter_matrix,
    )


def solution(mesh):
    spread = P(None, None, ("rans", "pitch", "span"))
    in_specs = (
        spread,
        P(),
        P(),
        P(),
        P(),
        P(),
        P(("rans", "pitch", "span")),
        P("pitch", "span", "rans", None),
        P("pitch", "span", "rans"),
        P("pitch", "span", "rans", None),
        P("pitch", "span", None, None),
        P("pitch", "span", None, None),
    )
    return jax.shard_map(body, mesh=mesh, in_specs=in_specs, out_specs=spread, check_vma=False)
```

time: 73.6 us -> 71 us (0.965)
  the two profiles are of different devices: /device:TPU:128 before, /device:TPU:1 now
where the time goes in v2:
time: 71 us; the launch traced here: 70.5 us
  starting transfers between devices  42.4 us (60%)
  Pallas kernels  18.6 us (26%)
  waiting for transfers between devices  4.64 us (7%)
  local copies, waits for them, and re-layouts  4.23 us (6%)
    ppermute x2, starting transfers between devices, body(): above = lax.ppermute(down, 'rans', fall)  18.3 us
    ppermute x2, starting transfers between devices, body(): below = lax.ppermute(up, 'rans', rise)  11.7 us
    ppermute x9, starting transfers between devices, gather_sum(): lax.ppermute(value, 'rans', [(r + o, r) for r in roots])  8.49 us
    pallas_call x1, Pallas kernels, body(): pl.pallas_call(functools.partial(phase_kernel, second=True), out_shape=tr...  7.77 us
    pallas_call x1, Pallas kernels, body(): pl.pallas_call(functools.partial(phase_kernel, second=False), out_shape=(...  6.89 us
    unnamed x35, local copies, waits for them, and re-layouts  3.9 us
    ppermute x2, starting transfers between devices, body(): near = lax.ppermute(pitch, 'pitch', swap)  3.81 us
    pallas_call x1, Pallas kernels, body(): pl.pallas_call(functools.partial(plane_kernel, normalizer=float((plane_ro...  2.81 us
  transfers between devices with their start and end apart: 17, of which 4 were waited for; matrix products, arithmetic and copies ran while one was open for 1% of the time, Pallas kernels for 1%

profile of v2, /device:TPU:1, one launch (start us, length us, event | category | flops | bytes accessed | tf_op | source)
XLA Modules:
  0.0 70.5 jit_solution(12592410009005831547)
XLA Ops:
  0.0 0.9 %copy-done.5 = s32[1,1,256,64]{2,3,1,0:T(8,128)S(1)} copy-done((s32[1,1,256,64]{2,3,1,0:T(8,128)S(1)}, s32[1,1,256,64]{2,3,1,0:T(8,128)}, u32[]{:S(2)}) %copy-start.5) | copy-done | bytes 65560
  0.9 0.8 %copy-done.6 = f32[1,1,256,64]{2,3,1,0:T(8,128)S(1)} copy-done((f32[1,1,256,64]{2,3,1,0:T(8,128)S(1)}, f32[1,1,256,64]{2,3,1,0:T(8,128)}, u32[]{:S(2)}) %copy-start.6) | copy-done | bytes 65560
  1.8 0.7 copy-done.7
  2.4 2.8 %eddy_plane.1 = f32[5,16,128]{2,1,0:T(8,128)S(1)} custom-call(s32[64,256]{1,0:T(8,128)S(1)} %bitcast.30, s32[1,256]{1,0:T(1,128)S(1)} %bitcast.32, f32[64,256]{1,0:T(8,128)S(1)} %bitcast.31), custom_call_target="tpu_custom_call" | custom-call | flops 300000000 | bytes 9000000 | tf_op jit(solution)/shard_map/eddy_plane/pallas_call | solution.py:328
  5.3 1.3 %collective-permute-start.6 = (f32[5,16,128]{2,1,0:T(8,128)S(1)}, f32[5,16,128]{2,1,0:T(8,128)S(1)}, u32[]{:S(2)}, u32[]{:S(2)}) collective-permute-start(f32[5,16,128]{2,1,0:T(8,128)S(1)} %eddy_plane.1), channel_id=1, source_target_pairs={{24,0},{28,4},{56,32},{60,36},{88,64},{92,68},{120,96},{124,100},{... | collective-permute-start | bytes 122888 | tf_op jit(solution)/shard_map/ppermute | solution.py:341
  6.6 1.3 %collective-permute-start.5 = (f32[5,16,128]{2,1,0:T(8,128)S(1)}, f32[5,16,128]{2,1,0:T(8,128)S(1)}, u32[]{:S(2)}, u32[]{:S(2)}) collective-permute-start(f32[5,16,128]{2,1,0:T(8,128)S(1)} %eddy_plane.1), channel_id=1, source_target_pairs={{16,0},{20,4},{48,32},{52,36},{80,64},{84,68},{112,96},{116,100},{... | collective-permute-start | bytes 122888 | tf_op jit(solution)/shard_map/ppermute | solution.py:341
  7.9 1.3 %collective-permute-start.4 = (f32[5,16,128]{2,1,0:T(8,128)S(1)}, f32[5,16,128]{2,1,0:T(8,128)S(1)}, u32[]{:S(2)}, u32[]{:S(2)}) collective-permute-start(f32[5,16,128]{2,1,0:T(8,128)S(1)} %eddy_plane.1), channel_id=1, source_target_pairs={{8,0},{12,4},{40,32},{44,36},{72,64},{76,68},{104,96},{108,100},{1... | collective-permute-start | bytes 122888 | tf_op jit(solution)/shard_map/ppermute | solution.py:341
  9.7 7.4 %collective-permute-start = (bf16[5,16,128]{2,1,0:T(8,128)(2,1)S(1)}, bf16[5,16,128]{2,1,0:T(8,128)(2,1)S(1)}, u32[]{:S(2)}, u32[]{:S(2)}) collective-permute-start(bf16[5,16,128]{2,1,0:T(8,128)(2,1)S(1)} %get-tuple-element.21), channel_id=1, source_target_pairs={{0,4},{4,8},{8,12},{12,16},{16,20},{20,24},{24,28},{28,32},{32,36}... | collective-permute-start | bytes 61448 | tf_op jit(solution)/shard_map/ppermute | solution.py:384
  17.1 1.9 %collective-permute-start.1 = (bf16[5,16,128]{2,1,0:T(8,128)(2,1)S(1)}, bf16[5,16,128]{2,1,0:T(8,128)(2,1)S(1)}, u32[]{:S(2)}, u32[]{:S(2)}) collective-permute-start(bf16[5,16,128]{2,1,0:T(8,128)(2,1)S(1)} %get-tuple-element.22), channel_id=1, source_target_pairs={{4,0},{8,4},{12,8},{16,12},{20,16},{24,20},{28,24},{32,28},{36,32}... | collective-permute-start | bytes 61448 | tf_op jit(solution)/shard_map/ppermute | solution.py:385
  19.1 0.7 copy-done.11
  20.6 0.7 collective-permute-start.9
  21.3 0.7 collective-permute-start.8
  22.0 1.3 %collective-permute-start.7 = (f32[5,16,128]{2,1,0:T(8,128)S(1)}, f32[5,16,128]{2,1,0:T(8,128)S(1)}, u32[]{:S(2)}, u32[]{:S(2)}) collective-permute-start(f32[5,16,128]{2,1,0:T(8,128)S(1)} %add_add_fusion.2), channel_id=1, source_target_pairs={{4,0},{68,64},{132,128},{196,192},{5,1},{69,65},{133,129},{197,193... | collective-permute-start | bytes 122888 | tf_op jit(solution)/shard_map/ppermute | solution.py:341
  24.2 0.7 collective-permute-start.12
  24.8 0.7 collective-permute-start.11
  25.5 0.7 collective-permute-start.10
  26.5 1.9 %collective-permute-start.2 = (bf16[5,16,768]{2,1,0:T(8,128)(2,1)S(1)}, bf16[5,16,768]{2,1,0:T(8,128)(2,1)S(1)}, u32[]{:S(2)}, u32[]{:S(2)}) collective-permute-start(bf16[5,16,768]{2,1,0:T(8,128)(2,1)S(1)} %get-tuple-element.23), channel_id=1, source_target_pairs={{0,2},{2,0},{1,3},{3,1},{4,6},{6,4},{5,7},{7,5},{8,10},{10,8},{9,1... | collective-permute-start | bytes 368648 | tf_op jit(solution)/shard_map/ppermute | solution.py:386
  29.1 2.7 %collective-permute-done.2.refs_4_.near_ref = bf16[5,16,768]{2,1,0:T(8,128)(2,1)S(1)} collective-permute-done((bf16[5,16,768]{2,1,0:T(8,128)(2,1)S(1)}, bf16[5,16,768]{2,1,0:T(8,128)(2,1)S(1)}, u32[]{:S(2)}, u32[]{:S(2)}) %collective-permute-start.2) | collective-permute-done | bytes 122912 | tf_op jit(solution)/shard_map/ppermute | solution.py:386
  31.8 6.9 %phase_one.1 = (bf16[5,64,1536]{2,1,0:T(8,128)(2,1)S(1)}, bf16[5,64,1536]{2,1,0:T(8,128)(2,1)S(1)}, bf16[5,16,128]{2,1,0:T(8,128)(2,1)S(1)}, bf16[5,16,128]{2,1,...) custom-call(bf16[5,64,1536]{2,1,0:T(8,128)(2,1)S(1)} %copy-done, ...), custom_call_target="tpu_custom_call" | custom-call | flops 600000000 | bytes 18000000 | tf_op jit(solution)/shard_map/phase_one/pallas_call | solution.py:390
  38.8 0.7 inflow_layer.1
  39.5 1.9 %collective-permute-start.15 = (bf16[5,16,768]{2,1,0:T(8,128)(2,1)S(1)}, bf16[5,16,768]{2,1,0:T(8,128)(2,1)S(1)}, u32[]{:S(2)}, u32[]{:S(2)}) collective-permute-start(bf16[5,16,768]{2,1,0:T(8,128)(2,1)S(1)} %get-tuple-element.33), channel_id=1, source_target_pairs={{0,2},{2,0},{1,3},{3,1},{4,6},{6,4},{5,7},{7,5},{8,10},{10,8},{9,1... | collective-permute-start | bytes 368648 | tf_op jit(solution)/shard_map/ppermute | solution.py:424
  41.4 4.3 %collective-permute-start.13 = (bf16[5,16,128]{2,1,0:T(8,128)(2,1)S(1)}, bf16[5,16,128]{2,1,0:T(8,128)(2,1)S(1)}, u32[]{:S(2)}, u32[]{:S(2)}) collective-permute-start(bf16[5,16,128]{2,1,0:T(8,128)(2,1)S(1)} %get-tuple-element.31), channel_id=1, source_target_pairs={{0,4},{4,8},{8,12},{12,16},{16,20},{20,24},{24,28},{28,32},{32,36}... | collective-permute-start | bytes 61448 | tf_op jit(solution)/shard_map/ppermute | solution.py:400
  45.7 16.3 %collective-permute-start.14 = (bf16[5,16,128]{2,1,0:T(8,128)(2,1)S(1)}, bf16[5,16,128]{2,1,0:T(8,128)(2,1)S(1)}, u32[]{:S(2)}, u32[]{:S(2)}) collective-permute-start(bf16[5,16,128]{2,1,0:T(8,128)(2,1)S(1)} %get-tuple-element.32), channel_id=1, source_target_pairs={{4,0},{8,4},{12,8},{16,12},{20,16},{24,20},{28,24},{32,28},{36,32}... | collective-permute-start | bytes 61448 | tf_op jit(solution)/shard_map/ppermute | solution.py:401
  62.7 7.8 %phase_two.1 = bf16[5,64,1536]{2,1,0:T(8,128)(2,1)} custom-call(bf16[5,64,1536]{2,1,0:T(8,128)(2,1)S(1)} %get-tuple-element.29.refs_0_, bf16[5,64,1536]{2,1,0:T(8,128)(2,1)S(1)} %get-tuple-element.30.refs_1_, bf16[5,64,1536]{2,1,0:T(8,128)(2,1)S(1)} %copy-done, f32[5,16,128]{2,1,0:T(8,128)S(1)} %bitcast.27, f32[5,16,128]{2,1,0:T(8,128)S(1)} %bitcast.29, ...), custom_call_target="tpu_custom_call" | custom-call | flops 600000000 | bytes 18000000 | tf_op jit(solution)/shard_map/phase_two/pallas_call | solution.py:426
  (64 shorter events, 3.8 us)
Async XLA Ops:
  0.0 9.2 %copy-start = (bf16[5,64,1536]{2,1,0:T(8,128)(2,1)S(1)}, bf16[5,64,1536]{2,1,0:T(8,128)(2,1)}, u32[]{:S(2)}) copy-start(bf16[5,64,1536]{2,1,0:T(8,128)(2,1)} %refs_2_.1) | copy-start | bytes 2949124
  2.4 6.7 %copy-start.4 = (bf16[64,64]{1,0:T(8,128)(2,1)S(1)}, bf16[64,64]{1,0:T(8,128)(2,1)}, u32[]{:S(2)}) copy-start(bf16[64,64]{1,0:T(8,128)(2,1)} %constant.9.clone.pick_ref) | copy-start | bytes 24580
  5.3 13.7 %copy-start.1 = (bf16[64,64]{1,0:T(8,128)(2,1)S(1)}, bf16[64,64]{1,0:T(8,128)(2,1)}, u32[]{:S(2)}) copy-start(bf16[64,64]{1,0:T(8,128)(2,1)} %refs_13_.1) | copy-start | bytes 24580
  5.3 15.3 %collective-permute-start.6 = (f32[5,16,128]{2,1,0:T(8,128)S(1)}, f32[5,16,128]{2,1,0:T(8,128)S(1)}, u32[]{:S(2)}, u32[]{:S(2)}) collective-permute-start(f32[5,16,128]{2,1,0:T(8,128)S(1)} %eddy_plane.1), channel_id=1, source_target_pairs={{24,0},{28,4},{56,32},{60,36},{88,64},{92,68},{120,96},{124,100},{... | collective-permute-start | bytes 122888 | tf_op jit(solution)/shard_map/ppermute | solution.py:341
  6.6 14.0 %collective-permute-start.5 = (f32[5,16,128]{2,1,0:T(8,128)S(1)}, f32[5,16,128]{2,1,0:T(8,128)S(1)}, u32[]{:S(2)}, u32[]{:S(2)}) collective-permute-start(f32[5,16,128]{2,1,0:T(8,128)S(1)} %eddy_plane.1), channel_id=1, source_target_pairs={{16,0},{20,4},{48,32},{52,36},{80,64},{84,68},{112,96},{116,100},{... | collective-permute-start | bytes 122888 | tf_op jit(solution)/shard_map/ppermute | solution.py:341
  7.9 12.7 %collective-permute-start.4 = (f32[5,16,128]{2,1,0:T(8,128)S(1)}, f32[5,16,128]{2,1,0:T(8,128)S(1)}, u32[]{:S(2)}, u32[]{:S(2)}) collective-permute-start(f32[5,16,128]{2,1,0:T(8,128)S(1)} %eddy_plane.1), channel_id=1, source_target_pairs={{8,0},{12,4},{40,32},{44,36},{72,64},{76,68},{104,96},{108,100},{1... | collective-permute-start | bytes 122888 | tf_op jit(solution)/shard_map/ppermute | solution.py:341
  9.7 18.8 %collective-permute-start = (bf16[5,16,128]{2,1,0:T(8,128)(2,1)S(1)}, bf16[5,16,128]{2,1,0:T(8,128)(2,1)S(1)}, u32[]{:S(2)}, u32[]{:S(2)}) collective-permute-start(bf16[5,16,128]{2,1,0:T(8,128)(2,1)S(1)} %get-tuple-element.21), channel_id=1, source_target_pairs={{0,4},{4,8},{8,12},{12,16},{16,20},{20,24},{24,28},{28,32},{32,36}... | collective-permute-start | bytes 61448 | tf_op jit(solution)/shard_map/ppermute | solution.py:384
  17.1 11.4 %collective-permute-start.1 = (bf16[5,16,128]{2,1,0:T(8,128)(2,1)S(1)}, bf16[5,16,128]{2,1,0:T(8,128)(2,1)S(1)}, u32[]{:S(2)}, u32[]{:S(2)}) collective-permute-start(bf16[5,16,128]{2,1,0:T(8,128)(2,1)S(1)} %get-tuple-element.22), channel_id=1, source_target_pairs={{4,0},{8,4},{12,8},{16,12},{20,16},{24,20},{28,24},{32,28},{36,32}... | collective-permute-start | bytes 61448 | tf_op jit(solution)/shard_map/ppermute | solution.py:385
  20.6 2.9 %collective-permute-start.9 = (f32[5,16,128]{2,1,0:T(8,128)S(1)}, f32[5,16,128]{2,1,0:T(8,128)S(1)}, u32[]{:S(2)}, u32[]{:S(2)}) collective-permute-start(f32[5,16,128]{2,1,0:T(8,128)S(1)} %add_add_fusion.2), channel_id=1, source_target_pairs={{36,0},{100,64},{164,128},{228,192},{37,1},{101,65},{165,129},{229... | collective-permute-start | bytes 122888 | tf_op jit(solution)/shard_map/ppermute | solution.py:341
  21.3 2.2 %collective-permute-start.8 = (f32[5,16,128]{2,1,0:T(8,128)S(1)}, f32[5,16,128]{2,1,0:T(8,128)S(1)}, u32[]{:S(2)}, u32[]{:S(2)}) collective-permute-start(f32[5,16,128]{2,1,0:T(8,128)S(1)} %add_add_fusion.2), channel_id=1, source_target_pairs={{32,0},{96,64},{160,128},{224,192},{33,1},{97,65},{161,129},{225,1... | collective-permute-start | bytes 122888 | tf_op jit(solution)/shard_map/ppermute | solution.py:341
  22.0 2.2 %collective-permute-start.7 = (f32[5,16,128]{2,1,0:T(8,128)S(1)}, f32[5,16,128]{2,1,0:T(8,128)S(1)}, u32[]{:S(2)}, u32[]{:S(2)}) collective-permute-start(f32[5,16,128]{2,1,0:T(8,128)S(1)} %add_add_fusion.2), channel_id=1, source_target_pairs={{4,0},{68,64},{132,128},{196,192},{5,1},{69,65},{133,129},{197,193... | collective-permute-start | bytes 122888 | tf_op jit(solution)/shard_map/ppermute | solution.py:341
  23.5 2.8 %copy-start.12 = (s32[1536]{0:T(1024)S(1)}, s32[1536]{0:T(1024)}, u32[]{:S(2)}) copy-start(s32[1536]{0:T(1024)} %param.20) | copy-start | bytes 18436
  24.1 2.1 %copy-start.10 = (bf16[64,64]{1,0:T(8,128)(2,1)S(1)}, bf16[64,64]{1,0:T(8,128)(2,1)}, u32[]{:S(2)}) copy-start(bf16[64,64]{1,0:T(8,128)(2,1)} %param.19) | copy-start | bytes 24580
  24.2 2.2 %collective-permute-start.12 = (f32[5,16,128]{2,1,0:T(8,128)S(1)}, f32[5,16,128]{2,1,0:T(8,128)S(1)}, u32[]{:S(2)}, u32[]{:S(2)}) collective-permute-start(f32[5,16,128]{2,1,0:T(8,128)S(1)} %add_add_fusion.1), channel_id=1, source_target_pairs={{192,0},{193,1},{194,2},{195,3}} | collective-permute-start | bytes 122888 | tf_op jit(solution)/shard_map/ppermute | solution.py:341
  24.8 1.7 %collective-permute-start.11 = (f32[5,16,128]{2,1,0:T(8,128)S(1)}, f32[5,16,128]{2,1,0:T(8,128)S(1)}, u32[]{:S(2)}, u32[]{:S(2)}) collective-permute-start(f32[5,16,128]{2,1,0:T(8,128)S(1)} %add_add_fusion.1), channel_id=1, source_target_pairs={{128,0},{129,1},{130,2},{131,3}} | collective-permute-start | bytes 122888 | tf_op jit(solution)/shard_map/ppermute | solution.py:341
  25.5 2.9 %collective-permute-start.10 = (f32[5,16,128]{2,1,0:T(8,128)S(1)}, f32[5,16,128]{2,1,0:T(8,128)S(1)}, u32[]{:S(2)}, u32[]{:S(2)}) collective-permute-start(f32[5,16,128]{2,1,0:T(8,128)S(1)} %add_add_fusion.1), channel_id=1, source_target_pairs={{64,0},{65,1},{66,2},{67,3}} | collective-permute-start | bytes 122888 | tf_op jit(solution)/shard_map/ppermute | solution.py:341
  26.4 2.7 %collective-permute-start.3 = (bf16[5,16,128]{2,1,0:T(8,128)(2,1)S(1)}, bf16[5,16,128]{2,1,0:T(8,128)(2,1)S(1)}, u32[]{:S(2)}, u32[]{:S(2)}) collective-permute-start(bf16[5,16,128]{2,1,0:T(8,128)(2,1)S(1)} %get-tuple-element.24), channel_id=1, source_target_pairs={{0,1},{1,0},{2,3},{3,2},{4,5},{5,4},{6,7},{7,6},{8,9},{9,8},{10,11... | collective-permute-start | bytes 61448 | tf_op jit(solution)/shard_map/ppermute | solution.py:387
  26.5 5.3 %collective-permute-start.2 = (bf16[5,16,768]{2,1,0:T(8,128)(2,1)S(1)}, bf16[5,16,768]{2,1,0:T(8,128)(2,1)S(1)}, u32[]{:S(2)}, u32[]{:S(2)}) collective-permute-start(bf16[5,16,768]{2,1,0:T(8,128)(2,1)S(1)} %get-tuple-element.23), channel_id=1, source_target_pairs={{0,2},{2,0},{1,3},{3,1},{4,6},{6,4},{5,7},{7,5},{8,10},{10,8},{9,1... | collective-permute-start | bytes 368648 | tf_op jit(solution)/shard_map/ppermute | solution.py:386
  31.8 6.9 %copy-start.2 = (f32[1,1,5,2048]{3,1,2,0:T(1,128)S(1)}, f32[1,1,5,2048]{3,1,2,0:T(1,128)}, u32[]{:S(2)}) copy-start(f32[1,1,5,2048]{3,1,2,0:T(1,128)} %param.24) | copy-start | bytes 122884
  31.8 6.9 %copy-start.3 = (f32[1,1,5,2048]{3,1,2,0:T(1,128)S(1)}, f32[1,1,5,2048]{3,1,2,0:T(1,128)}, u32[]{:S(2)}) copy-start(f32[1,1,5,2048]{3,1,2,0:T(1,128)} %param.25) | copy-start | bytes 122884
  39.5 23.3 %collective-permute-start.15 = (bf16[5,16,768]{2,1,0:T(8,128)(2,1)S(1)}, bf16[5,16,768]{2,1,0:T(8,128)(2,1)S(1)}, u32[]{:S(2)}, u32[]{:S(2)}) collective-permute-start(bf16[5,16,768]{2,1,0:T(8,128)(2,1)S(1)} %get-tuple-element.33), channel_id=1, source_target_pairs={{0,2},{2,0},{1,3},{3,1},{4,6},{6,4},{5,7},{7,5},{8,10},{10,8},{9,1... | collective-permute-start | bytes 368648 | tf_op jit(solution)/shard_map/ppermute | solution.py:424
  41.4 20.7 %collective-permute-start.16 = (bf16[5,16,128]{2,1,0:T(8,128)(2,1)S(1)}, bf16[5,16,128]{2,1,0:T(8,128)(2,1)S(1)}, u32[]{:S(2)}, u32[]{:S(2)}) collective-permute-start(bf16[5,16,128]{2,1,0:T(8,128)(2,1)S(1)} %get-tuple-element.34), channel_id=1, source_target_pairs={{0,1},{1,0},{2,3},{3,2},{4,5},{5,4},{6,7},{7,6},{8,9},{9,8},{10,11... | collective-permute-start | bytes 61448 | tf_op jit(solution)/shard_map/ppermute | solution.py:425
  41.4 20.7 %collective-permute-start.13 = (bf16[5,16,128]{2,1,0:T(8,128)(2,1)S(1)}, bf16[5,16,128]{2,1,0:T(8,128)(2,1)S(1)}, u32[]{:S(2)}, u32[]{:S(2)}) collective-permute-start(bf16[5,16,128]{2,1,0:T(8,128)(2,1)S(1)} %get-tuple-element.31), channel_id=1, source_target_pairs={{0,4},{4,8},{8,12},{12,16},{16,20},{20,24},{24,28},{28,32},{32,36}... | collective-permute-start | bytes 61448 | tf_op jit(solution)/shard_map/ppermute | solution.py:400
  45.7 17.0 %collective-permute-start.14 = (bf16[5,16,128]{2,1,0:T(8,128)(2,1)S(1)}, bf16[5,16,128]{2,1,0:T(8,128)(2,1)S(1)}, u32[]{:S(2)}, u32[]{:S(2)}) collective-permute-start(bf16[5,16,128]{2,1,0:T(8,128)(2,1)S(1)} %get-tuple-element.32), channel_id=1, source_target_pairs={{4,0},{8,4},{12,8},{16,12},{20,16},{24,20},{28,24},{32,28},{36,32}... | collective-permute-start | bytes 61448 | tf_op jit(solution)/shard_map/ppermute | solution.py:401
  (7 other events, 6.7 us)

commit v3 on v2

--- a/solution.py
+++ b/solution.py
@@ -15,6 +15,7 @@
 SPAN_CELLS = 32
 PAIR = 2 * CELLS
 MIXED = 352
+INNER = 224
 TIME_STEP = 0.4
 f32 = jnp.float32
 bf16 = jnp.bfloat16
@@ -89,17 +90,14 @@
     return jnp.where((lane & 31) == layer, pltpu.roll(edge, shift, 1), held)
 
 
-def pack_pair(traces, pair, first_span, lane, pitch_ref, span_held):
-    for f in range(FIELDS):
-        halves = [traces[f][:, :CELLS], traces[f][:, CELLS:]]
-        packed = pack_pitch([(h[0:16], h[16:32]) for h in halves], lane)
-        pitch_ref[f, :, pair * CELLS : (pair + 1) * CELLS] = packed.astype(bf16)
-        held = span_held[f]
-        for h in range(2):
-            held = pack_span(
-                held, halves[h][32:48], halves[h][48:64], 2 * pair + h, first_span, lane
-            )
-        span_held[f] = held
+def pack_field(f, trace, pair, first_span, lane, pitch_ref, span_held):
+    halves = [trace[:, :CELLS], trace[:, CELLS:]]
+    packed = pack_pitch([(h[0:16], h[16:32]) for h in halves], lane)
+    pitch_ref[f, :, pair * CELLS : (pair + 1) * CELLS] = packed.astype(bf16)
+    held = span_held[f]
+    for h in range(2):
+        held = pack_span(held, halves[h][32:48], halves[h][48:64], 2 * pair + h, first_span, lane)
+    span_held[f] = held
 
 
 def pack_kernel(
@@ -114,7 +112,7 @@
         traces = [dot(pick, v_ref[f, :, at]) for f in range(FIELDS)]
         for f in range(FIELDS):
             trace_ref[f, :, at] = traces[f].astype(bf16)
-        pack_pair(traces, pair, first_span, lane, pitch_ref, span_held)
+            pack_field(f, traces[f], pair, first_span, lane, pitch_ref, span_held)
     span_ref[...] = span_held[...].astype(bf16)
     up_ref[...] = v_ref[:, 48:64, (EX - 1) * CELLS :]
     down_ref[...] = v_ref[:, 0:16, 0:CELLS]
@@ -127,94 +125,174 @@
     return total
 
 
-def advance(
-    read, trace, lower, upper, pitch, span, pinned, layers, coefs, weights, smooth, mixed,
-    first_span, lane, base=None,
-):
-    for r in range(0, NODES, 16):
-        rows = [read(f, r, r + 16).astype(f32) for f in range(FIELDS)]
-        for d in range(3):
-            for f in range(FIELDS):
-                mixed[f, 64 * d + r : 64 * d + r + 16, :] = mix(
-                    coefs, 25 * d + 5 * f, rows
-                ).astype(bf16)
-    jumps = [[None] * FIELDS for _ in range(6)]
+def mix_fluxes(read, coefs, mixed):
+    def rows_step(r):
+        def run():
+            rows = [read(f, r, r + 16).astype(f32) for f in range(FIELDS)]
+            for d in range(3):
+                for f in range(FIELDS):
+                    mixed[f, 64 * d + r : 64 * d + r + 16, :] = mix(
+                        coefs, 25 * d + 5 * f, rows
+                    ).astype(bf16)
+
+        return run
+
+    return [rows_step(r) for r in range(0, NODES, 16)]
+
+
+def write_jumps(t, jumps, coefs, mixed, first_row):
     for f in range(FIELDS):
-        jumps[0][f] = lower(f) - read(f, 0, 16).astype(f32)
-        jumps[1][f] = upper(f) - read(f, 48, 64).astype(f32)
-        own = trace(f).astype(f32)
-        near, far = pitch(f), span(f)
-        parts = [[], [], [], []]
-        for h, layer in enumerate(layers):
-            t = own[:, h * CELLS : (h + 1) * CELLS]
-            pl_low, pl_high, sp_low, sp_high = t[0:16], t[16:32], t[32:48], t[48:64]
-            below = jnp.where(
-                lane < 32, pltpu.roll(near, 64 if h == 0 else 32, 1), pltpu.roll(pl_high, 32, 1)
-            )
-            above = jnp.where(
-                lane >= 96, pltpu.roll(near, 96 if h == 0 else 64, 1), pltpu.roll(pl_low, 96, 1)
-            )
-            shift = lax.rem(jnp.where(first_span, 31, 128) - layer, 128)
-            arrived = pltpu.roll(far, shift, 1)
-            left = jnp.where(
-                (lane & 31) == 0, jnp.where(first_span, sp_low, arrived), pltpu.roll(sp_high, 1, 1)
-            )
-            right = jnp.where(
-                (lane & 31) == 31,
-                jnp.where(first_span, arrived, sp_high),
-                pltpu.roll(sp_low, 127, 1),
-            )
-            for held, now in zip(
-                parts, (below - pl_low, above - pl_high, left - sp_low, right - sp_high)
-            ):
-                held.append(now)
-        for t in range(4):
-            p = parts[t]
-            jumps[2 + t][f] = p[0] if len(p) == 1 else jnp.concatenate(p, axis=1)
-    for t in range(6):
+        mixed[f, first_row : first_row + 16, :] = mix(coefs, 75 + 25 * t + 5 * f, jumps).astype(bf16)
+
+
+def mix_stream(read, lower, upper, coefs, mixed, row):
+    def low():
+        jumps = [lower(f) - read(f, 0, 16).astype(f32) for f in range(FIELDS)]
+        write_jumps(0, jumps, coefs, mixed, row)
+
+    def high():
+        jumps = [upper(f) - read(f, 48, 64).astype(f32) for f in range(FIELDS)]
+        write_jumps(1, jumps, coefs, mixed, row + 16)
+
+    return [low, high]
+
+
+def mix_sides(trace, pitch, span, layers, coefs, mixed, row, first_span, lane):
+    def halves(f, r):
+        own = trace(f, r, r + 16)
+        return [own[:, h * CELLS : (h + 1) * CELLS] for h in range(len(layers))]
+
+    def join(parts):
+        return parts[0] if len(parts) == 1 else jnp.concatenate(parts, axis=1)
+
+    def pitch_low():
+        jumps = []
         for f in range(FIELDS):
-            mixed[f, 192 + 16 * t : 208 + 16 * t, :] = mix(
-                coefs, 75 + 25 * t + 5 * f, jumps[t]
-            ).astype(bf16)
-    out = []
-    for f in range(FIELDS):
+            near, low, high = pitch(f), halves(f, 0), halves(f, 16)
+            jumps.append(join([
+                jnp.where(
+                    lane < 32, pltpu.roll(near, 64 if h == 0 else 32, 1), pltpu.roll(high[h], 32, 1)
+                ) - low[h]
+                for h in range(len(layers))
+            ]))
+        write_jumps(2, jumps, coefs, mixed, row)
+
+    def pitch_high():
+        jumps = []
+        for f in range(FIELDS):
+            near, low, high = pitch(f), halves(f, 0), halves(f, 16)
+            jumps.append(join([
+                jnp.where(
+                    lane >= 96, pltpu.roll(near, 96 if h == 0 else 64, 1), pltpu.roll(low[h], 96, 1)
+                ) - high[h]
+                for h in range(len(layers))
+            ]))
+        write_jumps(3, jumps, coefs, mixed, row + 16)
+
+    def arrived(f, layer):
+        return pltpu.roll(span(f), lax.rem(jnp.where(first_span, 31, 128) - layer, 128), 1)
+
+    def span_low():
+        jumps = []
+        for f in range(FIELDS):
+            low, high = halves(f, 32), halves(f, 48)
+            jumps.append(join([
+                jnp.where(
+                    (lane & 31) == 0,
+                    jnp.where(first_span, low[h], arrived(f, layer)),
+                    pltpu.roll(high[h], 1, 1),
+                ) - low[h]
+                for h, layer in enumerate(layers)
+            ]))
+        write_jumps(4, jumps, coefs, mixed, row + 32)
+
+    def span_high():
+        jumps = []
+        for f in range(FIELDS):
+            low, high = halves(f, 32), halves(f, 48)
+            jumps.append(join([
+                jnp.where(
+                    (lane & 31) == 31,
+                    jnp.where(first_span, arrived(f, layer), high[h]),
+                    pltpu.roll(low[h], 127, 1),
+                ) - high[h]
+                for h, layer in enumerate(layers)
+            ]))
+        write_jumps(5, jumps, coefs, mixed, row + 48)
+
+    return [pitch_low, pitch_high, span_low, span_high]
+
+
+def mix_wall(read, pinned, mixed, row):
+    def run():
+        for f in range(FIELDS):
+            mixed[f, row : row + 64, :] = (read(f, 0, 64).astype(f32) * pinned()).astype(bf16)
+
+    return [run]
+
+
+def staggered(stages):
+    held = [None] * FIELDS
+    steps = []
+
+    def step(stage, f):
+        def run():
+            held[f] = stage(f, held[f])
+
+        return run
+
+    for turn in range(FIELDS + len(stages) - 1):
+        for k, stage in enumerate(stages):
+            if 0 <= turn - k < FIELDS:
+                steps.append(step(stage, turn - k))
+    return steps
+
+
+def interleave(first, second):
+    count = max(len(first), len(second))
+    for i in range(count):
+        for steps in (first, second):
+            for step in steps[i * len(steps) // count : (i + 1) * len(steps) // count]:
+                step()
+
+
+def pipeline(vector, matrix):
+    for step in vector[0]:
+        step()
+    for p in range(len(matrix)):
+        interleave(matrix[p], vector[p + 1] if p + 1 < len(vector) else [])
+
+
+def finish(read, base, smooth):
+    def trial(f, rate):
         v = read(f, 0, 64).astype(f32)
-        mixed[f, 288:352, :] = (v * pinned).astype(bf16)
-        rate = dot(weights, mixed[f])
         if base is None:
-            trial = v - TIME_STEP * rate
+            now = v - TIME_STEP * rate
         else:
-            trial = 0.5 * (base(f).astype(f32) + v - TIME_STEP * rate)
-        out.append(dot(smooth, trial.astype(bf16)))
-    return out
-
-
-def phase_kernel(*refs, second):
-    if second:
-        (v_ref, trace_ref, base_ref, mean_ref, amp_ref, plane_ref, below_ref, above_ref, near_ref,
-         far_ref, pin_ref, coefs, weights_ref, smooth_ref, out_ref, mixed) = refs
-    else:
-        (v_ref, trace_ref, below_ref, above_ref, near_ref, far_ref, pin_ref, coefs, weights_ref,
-         smooth_ref, out_ref, out_trace_ref, up_ref, down_ref, pitch_ref, span_ref, mixed,
-         span_held) = refs
-    first_span = lax.axis_index("span") == 0
-    rans = lax.axis_index("rans")
-    last_rans = rans == lax.axis_size("rans") - 1
-    lane = lanes()
-    weights, smooth = weights_ref[...], smooth_ref[...]
-    if not second:
-        span_held[...] = jnp.zeros_like(span_held)
-
-    def lower(f, pair):
+            now = 0.5 * (base(f).astype(f32) + v - TIME_STEP * rate)
+        return dot(smooth, now.astype(bf16))
+
+    return trial
+
+
+def place(pair):
+    return slice(pair * PAIR, (pair + 1) * PAIR)
+
+
+def lower_pair(v_ref, edge, pair):
+    def lower(f):
         if pair:
             return v_ref[f, 48:64, pair * PAIR - CELLS : (pair + 1) * PAIR - CELLS].astype(f32)
-        edge = below_ref[f].astype(f32)
-        if second:
-            edge = jnp.where(rans == 0, inflow_of(mean_ref, amp_ref, plane_ref)(f), edge)
-        return jnp.concatenate([edge, v_ref[f, 48:64, 0:CELLS].astype(f32)], axis=1)
-
-    def upper(f, pair):
-        first = pair * PAIR + CELLS
+        return jnp.concatenate([edge(f), v_ref[f, 48:64, 0:CELLS].astype(f32)], axis=1)
+
+    return lower
+
+
+def upper_pair(v_ref, above_ref, pair):
+    first = pair * PAIR + CELLS
+    last_rans = lax.axis_index("rans") == lax.axis_size("rans") - 1
+
+    def upper(f):
         if pair < EX // 2 - 1:
             return v_ref[f, 0:16, first : first + PAIR].astype(f32)
         edge = jnp.where(
@@ -222,33 +300,135 @@
         )
         return jnp.concatenate([v_ref[f, 0:16, first : first + CELLS].astype(f32), edge], axis=1)
 
+    return upper
+
+
+def phase_one_kernel(
+    v_ref, trace_ref, below_ref, above_ref, near_ref, far_ref, pin_ref, coefs, weights_ref,
+    smooth_ref, out_ref, out_trace_ref, up_ref, down_ref, pitch_ref, span_ref, mixed, span_held,
+):
+    first_span = lax.axis_index("span") == 0
+    lane = lanes()
+    weights, smooth = weights_ref[...], smooth_ref[...]
+    span_held[...] = jnp.zeros_like(span_held)
+    vector, matrix = [], []
+
+    def add(pair):
+        at = place(pair)
+        rows = mixed.at[pair % 2]
+
+        def read(f, r0, r1):
+            return v_ref[f, r0:r1, at]
+
+        def store(f, value):
+            out_ref[f, :, at] = value[0:64].astype(bf16)
+            trace = value[64:128]
+            out_trace_ref[f, :, at] = trace.astype(bf16)
+            pack_field(f, trace, pair, first_span, lane, pitch_ref, span_held)
+
+        vector.append(
+            mix_fluxes(read, coefs, rows)
+            + mix_stream(
+                read,
+                lower_pair(v_ref, lambda f: below_ref[f].astype(f32), pair),
+                upper_pair(v_ref, above_ref, pair),
+                coefs, rows, 192,
+            )
+            + mix_sides(
+                lambda f, r0, r1: trace_ref[f, r0:r1, at].astype(f32),
+                lambda f: near_ref[f, :, pair * CELLS : (pair + 1) * CELLS].astype(f32),
+                lambda f: far_ref[f].astype(f32),
+                [2 * pair, 2 * pair + 1], coefs, rows, 224, first_span, lane,
+            )
+            + mix_wall(read, lambda: pin_ref[:, at].astype(f32), rows, 288)
+        )
+        matrix.append(
+            staggered([lambda f, _: dot(weights, rows[f]), finish(read, None, smooth), store])
+        )
+
     for pair in range(EX // 2):
-        at = slice(pair * PAIR, (pair + 1) * PAIR)
-        values = advance(
-            lambda f, r0, r1: v_ref[f, r0:r1, at],
-            lambda f: trace_ref[f, :, at],
-            lambda f: lower(f, pair),
-            lambda f: upper(f, pair),
-            lambda f: near_ref[f, :, pair * CELLS : (pair + 1) * CELLS].astype(f32),
-            lambda f: far_ref[f].astype(f32),
-            pin_ref[:, at].astype(f32),
-            [2 * pair, 2 * pair + 1],
-            coefs, weights, smooth, mixed.at[pair % mixed.shape[0]], first_span, lane,
-            base=(lambda f: base_ref[f, :, at]) if second else None,
-        )
-        for f in range(FIELDS):
-            out_ref[f, :, at] = values[f][0:64].astype(bf16)
-        if not second:
-            for f in range(FIELDS):
-                out_trace_ref[f, :, at] = values[f][64:128].astype(bf16)
-            pack_pair(
-                [values[f][64:128] for f in range(FIELDS)], pair, first_span, lane, pitch_ref,
-                span_held,
+        add(pair)
+    pipeline(vector, matrix)
+    span_ref[...] = span_held[...].astype(bf16)
+    up_ref[...] = out_ref[:, 48:64, (EX - 1) * CELLS :]
+    down_ref[...] = out_ref[:, 0:16, 0:CELLS]
+
+
+def inner_two_kernel(
+    v_ref, mean_ref, amp_ref, plane_ref, below_ref, above_ref, coefs, weights_ref, part_ref, mixed
+):
+    first_rans = lax.axis_index("rans") == 0
+    weights = weights_ref[...]
+    vector, matrix = [], []
+
+    def edge(f):
+        return jnp.where(
+            first_rans, inflow_of(mean_ref, amp_ref, plane_ref)(f), below_ref[f].astype(f32)
+        )
+
+    def add(pair):
+        at = place(pair)
+        rows = mixed.at[pair % 2]
+
+        def read(f, r0, r1):
+            return v_ref[f, r0:r1, at]
+
+        def store(f, value):
+            part_ref[f, :, at] = value
+
+        vector.append(
+            mix_fluxes(read, coefs, rows)
+            + mix_stream(
+                read, lower_pair(v_ref, edge, pair), upper_pair(v_ref, above_ref, pair), coefs, rows,
+                192,
             )
-    if not second:
-        span_ref[...] = span_held[...].astype(bf16)
-        up_ref[...] = out_ref[:, 48:64, (EX - 1) * CELLS :]
-        down_ref[...] = out_ref[:, 0:16, 0:CELLS]
+        )
+        matrix.append(staggered([lambda f, _: dot(weights, rows[f]), store]))
+
+    for pair in range(EX // 2):
+        add(pair)
+    pipeline(vector, matrix)
+
+
+def outer_two_kernel(
+    v_ref, trace_ref, base_ref, part_ref, near_ref, far_ref, pin_ref, coefs, weights_ref,
+    smooth_ref, out_ref, mixed,
+):
+    first_span = lax.axis_index("span") == 0
+    lane = lanes()
+    weights, smooth = weights_ref[...], smooth_ref[...]
+    vector, matrix = [], []
+
+    def add(pair):
+        at = place(pair)
+        rows = mixed.at[pair % 2]
+
+        def read(f, r0, r1):
+            return v_ref[f, r0:r1, at]
+
+        def store(f, value):
+            out_ref[f, :, at] = value.astype(bf16)
+
+        vector.append(
+            mix_sides(
+                lambda f, r0, r1: trace_ref[f, r0:r1, at].astype(f32),
+                lambda f: near_ref[f, :, pair * CELLS : (pair + 1) * CELLS].astype(f32),
+                lambda f: far_ref[f].astype(f32),
+                [2 * pair, 2 * pair + 1], coefs, rows, 0, first_span, lane,
+            )
+            + mix_wall(read, lambda: pin_ref[:, at].astype(f32), rows, 64)
+        )
+        matrix.append(
+            staggered([
+                lambda f, _: dot(weights, rows[f]) + part_ref[f, :, at],
+                finish(read, lambda f: base_ref[f, :, at], smooth),
+                store,
+            ])
+        )
+
+    for pair in range(EX // 2):
+        add(pair)
+    pipeline(vector, matrix)
 
 
 def inflow_of(mean_ref, amp_ref, plane_ref):
@@ -266,20 +446,14 @@
 
     @pl.when(first_rans)
     def _():
-        values = advance(
-            lambda f, r0, r1: v_ref[f, r0:r1, 0:CELLS],
-            lambda f: trace_ref[f],
-            inflow_of(mean_ref, amp_ref, plane_ref),
-            lambda f: v_ref[f, 0:16, CELLS:PAIR].astype(f32),
-            lambda f: near_ref[f].astype(f32),
-            lambda f: far_ref[f].astype(f32),
-            pin_ref[...].astype(f32),
-            [0],
-            coefs, weights_ref[...], smooth_ref[...], mixed, first_span, lane,
-        )
-        for f in range(FIELDS):
-            out_ref[f] = values[f][0:64].astype(bf16)
-            t = values[f][64:128]
+        weights, smooth = weights_ref[...], smooth_ref[...]
+
+        def read(f, r0, r1):
+            return v_ref[f, r0:r1, 0:CELLS]
+
+        def store(f, value):
+            out_ref[f] = value[0:64].astype(bf16)
+            t = value[64:128]
             out_trace_ref[f] = t.astype(bf16)
             pitch = jnp.where(lane < 32, t[0:16], pltpu.roll(t[16:32], 96, 1))
             pitch_ref[f] = jnp.where(
@@ -289,6 +463,27 @@
                 held_span_ref[f].astype(f32), t[32:48], t[48:64], 0, first_span, lane
             ).astype(bf16)
 
+        vector = (
+            mix_stream(
+                read,
+                inflow_of(mean_ref, amp_ref, plane_ref),
+                lambda f: v_ref[f, 0:16, CELLS:PAIR].astype(f32),
+                coefs, mixed, 192,
+            )
+            + mix_sides(
+                lambda f, r0, r1: trace_ref[f, r0:r1].astype(f32),
+                lambda f: near_ref[f].astype(f32),
+                lambda f: far_ref[f].astype(f32),
+                [0], coefs, mixed, 224, first_span, lane,
+            )
+            + mix_fluxes(read, coefs, mixed)
+            + mix_wall(read, lambda: pin_ref[...].astype(f32), mixed, 288)
+        )
+        matrix = staggered(
+            [lambda f, _: dot(weights, mixed[f]), finish(read, None, smooth), store]
+        )
+        pipeline([vector], [matrix])
+
     @pl.when(jnp.logical_not(first_rans))
     def _():
         out_ref[...] = held_ref[...]
@@ -300,7 +495,6 @@
 VMEM = pl.BlockSpec(memory_space=pltpu.VMEM)
 SMEM = pl.BlockSpec(memory_space=pltpu.SMEM)
 PARAMS = pltpu.CompilerParams(vmem_limit_bytes=40 * 2**20)
-SLOTS = 2
 
 
 def shape_of(*dims, dtype=bf16):
@@ -342,10 +536,6 @@
         for part in parts:
             value = value + part
         return value
-
-    plane = gather_sum(plane, (2, 4, 6), [8 * z + c for z in range(8) for c in range(2)])
-    plane = gather_sum(plane, (1, 8, 9), [0, 16, 32, 48])
-    plane = gather_sum(plane, (16, 32, 48), [0])
 
     weights = jnp.concatenate(
         [volume_ops[0], volume_ops[1], volume_ops[2], lift_matrix, wall_matrix], axis=1
@@ -381,24 +571,30 @@
         cost_estimate=cost(2),
         name="pack_faces",
     )(solution, pick)
+    plane = gather_sum(plane, (2, 6, 4), [8 * z + c for z in range(8) for c in range(2)])
+    near = lax.ppermute(pitch, "pitch", swap)
+    far = lax.ppermute(span, "span", swap)
+    plane, near, far, up, down = lax.optimization_barrier((plane, near, far, up, down))
+    plane = gather_sum(plane, (1, 8, 9), [0, 16, 32, 48])
     below = lax.ppermute(up, "rans", rise)
     above = lax.ppermute(down, "rans", fall)
-    near = lax.ppermute(pitch, "pitch", swap)
-    far = lax.ppermute(span, "span", swap)
-
-    scratch = [pltpu.VMEM((SLOTS, FIELDS, MIXED, PAIR), bf16)]
+    plane, near, far, below, above = lax.optimization_barrier((plane, near, far, below, above))
+    plane = gather_sum(plane, (16, 48, 32), [0])
+
     phase_one, trace_one, up, down, pitch, span = pl.pallas_call(
-        functools.partial(phase_kernel, second=False),
+        phase_one_kernel,
         out_shape=(traces, traces) + sends,
         in_specs=[VMEM] * 6 + fixed_specs,
         out_specs=(VMEM,) * 6,
-        scratch_shapes=scratch + [span_scratch],
+        scratch_shapes=[pltpu.VMEM((2, FIELDS, MIXED, PAIR), bf16), span_scratch],
         compiler_params=PARAMS,
         cost_estimate=cost(6),
         name="phase_one",
     )(solution, trace, below, above, near, far, pins, coefs, weights, smooth)
     below = lax.ppermute(up, "rans", rise)
     above = lax.ppermute(down, "rans", fall)
+
+    plane, below, above = lax.optimization_barrier((plane, below, above))
 
     mean = mean_inflow.reshape(FIELDS, 16, CELLS)
     amplitude = eddy_amplitude.reshape(FIELDS, 16, CELLS)
@@ -423,18 +619,28 @@
     )
     near = lax.ppermute(pitch, "pitch", swap)
     far = lax.ppermute(span, "span", swap)
+    part = pl.pallas_call(
+        inner_two_kernel,
+        out_shape=shape_of(FIELDS, NODES, elements, dtype=f32),
+        in_specs=[VMEM] * 6 + [SMEM, VMEM],
+        out_specs=VMEM,
+        scratch_shapes=[pltpu.VMEM((2, FIELDS, INNER, PAIR), bf16)],
+        compiler_params=PARAMS,
+        cost_estimate=cost(3),
+        name="inner_two",
+    )(phase_one, mean, amplitude, plane, below, above, coefs, weights[:, :INNER])
     return pl.pallas_call(
-        functools.partial(phase_kernel, second=True),
+        outer_two_kernel,
         out_shape=traces,
-        in_specs=[VMEM] * 10 + fixed_specs,
+        in_specs=[VMEM] * 7 + fixed_specs[1:],
         out_specs=VMEM,
-        scratch_shapes=scratch,
+        scratch_shapes=[pltpu.VMEM((2, FIELDS, MIXED - INNER, PAIR), bf16)],
         compiler_params=PARAMS,
-        cost_estimate=cost(6),
-        name="phase_two",
+        cost_estimate=cost(4),
+        name="outer_two",
     )(
-        phase_one, trace_one, solution, mean, amplitude, plane, below, above, near, far, pins,
-        coefs, weights, filter_matrix,
+        phase_one, trace_one, solution, part, near, far, pins, coefs, weights[:, INNER:],
+        filter_matrix,
     )
 
 

time: 71 us -> 66.7 us (0.939)
  the two profiles are of different devices: /device:TPU:1 before, /device:TPU:123 now
where the time goes in v3:
time: 66.7 us; the launch traced here: 66.3 us
  starting transfers between devices  28.7 us (43%)
  Pallas kernels  16.3 us (24%)
  waiting for transfers between devices  15.6 us (23%)
  local copies, waits for them, and re-layouts  4.78 us (7%)
    ppermute x2, waiting for transfers between devices, body(): above = lax.ppermute(down, 'rans', fall)  12.9 us
    ppermute x2, starting transfers between devices, body(): below = lax.ppermute(up, 'rans', rise)  10.8 us
    ppermute x9, starting transfers between devices, gather_sum(): lax.ppermute(value, 'rans', [(r + o, r) for r in roots])  7.76 us
    pallas_call x1, Pallas kernels, body(): pl.pallas_call(phase_one_kernel, out_shape=(traces, traces) + sends, in_s...  5.28 us
    unnamed x37, local copies, waits for them, and re-layouts  4.45 us
    ppermute x2, starting transfers between devices, body(): near = lax.ppermute(pitch, 'pitch', swap)  4.23 us
    ppermute x2, starting transfers between devices, body(): above = lax.ppermute(down, 'rans', fall)  3.84 us
    pallas_call x1, Pallas kernels, body(): pl.pallas_call(outer_two_kernel, out_shape=traces, in_specs=[VMEM] * 7 +...  3.81 us
  transfers between devices with their start and end apart: 17, of which 3 were waited for; matrix products, arithmetic and copies ran while one was open for 1% of the time, Pallas kernels for 14%

profile of v3, /device:TPU:123, one launch (start us, length us, event | category | flops | bytes accessed | tf_op | source)
XLA Modules:
  0.0 66.3 jit_solution(14098087986534482615)
XLA Ops:
  0.0 0.9 %copy-done.6 = s32[1,1,256,64]{2,3,1,0:T(8,128)S(1)} copy-done((s32[1,1,256,64]{2,3,1,0:T(8,128)S(1)}, s32[1,1,256,64]{2,3,1,0:T(8,128)}, u32[]{:S(2)}) %copy-start.6) | copy-done | bytes 65560
  0.9 0.8 %copy-done.7 = f32[1,1,256,64]{2,3,1,0:T(8,128)S(1)} copy-done((f32[1,1,256,64]{2,3,1,0:T(8,128)S(1)}, f32[1,1,256,64]{2,3,1,0:T(8,128)}, u32[]{:S(2)}) %copy-start.7) | copy-done | bytes 65560
  1.8 0.7 %copy-done.8 = s32[1,1,256]{2,1,0:T(1,128)S(1)} copy-done((s32[1,1,256]{2,1,0:T(1,128)S(1)}, s32[1,1,256]{2,1,0:T(1,128)}, u32[]{:S(2)}) %copy-start.8) | copy-done | bytes 1048
  2.5 2.8 %eddy_plane.1 = f32[5,16,128]{2,1,0:T(8,128)S(1)} custom-call(s32[64,256]{1,0:T(8,128)S(1)} %bitcast.30, s32[1,256]{1,0:T(1,128)S(1)} %bitcast.32, f32[64,256]{1,0:T(8,128)S(1)} %bitcast.31), custom_call_target="tpu_custom_call" | custom-call | flops 300000000 | bytes 9000000 | tf_op jit(solution)/shard_map/eddy_plane/pallas_call | solution.py:522
  5.3 0.7 %collective-permute-start.2 = (f32[5,16,128]{2,1,0:T(8,128)S(1)}, f32[5,16,128]{2,1,0:T(8,128)S(1)}, u32[]{:S(2)}, u32[]{:S(2)}) collective-permute-start(f32[5,16,128]{2,1,0:T(8,128)S(1)} %eddy_plane.1), channel_id=1, source_target_pairs={{16,0},{20,4},{48,32},{52,36},{80,64},{84,68},{112,96},{116,100},{... | collective-permute-start | bytes 122888 | tf_op jit(solution)/shard_map/ppermute | solution.py:535
  6.0 2.5 %collective-permute-start.1 = (f32[5,16,128]{2,1,0:T(8,128)S(1)}, f32[5,16,128]{2,1,0:T(8,128)S(1)}, u32[]{:S(2)}, u32[]{:S(2)}) collective-permute-start(f32[5,16,128]{2,1,0:T(8,128)S(1)} %eddy_plane.1), channel_id=1, source_target_pairs={{24,0},{28,4},{56,32},{60,36},{88,64},{92,68},{120,96},{124,100},{... | collective-permute-start | bytes 122888 | tf_op jit(solution)/shard_map/ppermute | solution.py:535
  9.1 1.2 %copy-done = bf16[5,64,1536]{2,1,0:T(8,128)(2,1)S(1)} copy-done((bf16[5,64,1536]{2,1,0:T(8,128)(2,1)S(1)}, bf16[5,64,1536]{2,1,0:T(8,128)(2,1)}, u32[]{:S(2)}) %copy-start) | copy-done | bytes 983064
  10.3 0.7 %copy-done.5 = bf16[64,64]{1,0:T(8,128)(2,1)S(1)} copy-done((bf16[64,64]{1,0:T(8,128)(2,1)S(1)}, bf16[64,64]{1,0:T(8,128)(2,1)}, u32[]{:S(2)}) %copy-start.5) | copy-done | bytes 8216
  11.9 2.1 %collective-permute-start.3 = (bf16[5,16,768]{2,1,0:T(8,128)(2,1)S(1)}, bf16[5,16,768]{2,1,0:T(8,128)(2,1)S(1)}, u32[]{:S(2)}, u32[]{:S(2)}) collective-permute-start(bf16[5,16,768]{2,1,0:T(8,128)(2,1)S(1)} %get-tuple-element.34), channel_id=1, source_target_pairs={{0,2},{2,0},{1,3},{3,1},{4,6},{6,4},{5,7},{7,5},{8,10},{10,8},{9,1... | collective-permute-start | bytes 368648 | tf_op jit(solution)/shard_map/ppermute | solution.py:575
  14.6 2.7 %collective-permute-done.3.near_ref = bf16[5,16,768]{2,1,0:T(8,128)(2,1)S(1)} collective-permute-done((bf16[5,16,768]{2,1,0:T(8,128)(2,1)S(1)}, bf16[5,16,768]{2,1,0:T(8,128)(2,1)S(1)}, u32[]{:S(2)}, u32[]{:S(2)}) %collective-permute-start.3) | collective-permute-done | bytes 122912 | tf_op jit(solution)/shard_map/ppermute | solution.py:575
  18.7 0.7 %collective-permute-start.5 = (f32[5,16,128]{2,1,0:T(8,128)S(1)}, f32[5,16,128]{2,1,0:T(8,128)S(1)}, u32[]{:S(2)}, u32[]{:S(2)}) collective-permute-start(f32[5,16,128]{2,1,0:T(8,128)S(1)} %add_add_fusion.2), channel_id=1, source_target_pairs={{4,0},{68,64},{132,128},{196,192},{5,1},{69,65},{133,129},{197,193... | collective-permute-start | bytes 122888 | tf_op jit(solution)/shard_map/ppermute | solution.py:535
  19.6 8.2 %collective-permute-start.8 = (bf16[5,16,128]{2,1,0:T(8,128)(2,1)S(1)}, bf16[5,16,128]{2,1,0:T(8,128)(2,1)S(1)}, u32[]{:S(2)}, u32[]{:S(2)}) collective-permute-start(bf16[5,16,128]{2,1,0:T(8,128)(2,1)S(1)} %get-tuple-element.41), channel_id=1, source_target_pairs={{0,4},{4,8},{8,12},{12,16},{16,20},{20,24},{24,28},{28,32},{32,36}... | collective-permute-start | bytes 61448 | tf_op jit(solution)/shard_map/ppermute | solution.py:579
  27.8 1.9 %collective-permute-start.9 = (bf16[5,16,128]{2,1,0:T(8,128)(2,1)S(1)}, bf16[5,16,128]{2,1,0:T(8,128)(2,1)S(1)}, u32[]{:S(2)}, u32[]{:S(2)}) collective-permute-start(bf16[5,16,128]{2,1,0:T(8,128)(2,1)S(1)} %get-tuple-element.42), channel_id=1, source_target_pairs={{4,0},{8,4},{12,8},{16,12},{20,16},{24,20},{28,24},{32,28},{36,32}... | collective-permute-start | bytes 61448 | tf_op jit(solution)/shard_map/ppermute | solution.py:580
  29.8 6.4 %collective-permute-done.9.above_ref = bf16[5,16,128]{2,1,0:T(8,128)(2,1)S(1)} collective-permute-done((bf16[5,16,128]{2,1,0:T(8,128)(2,1)S(1)}, bf16[5,16,128]{2,1,0:T(8,128)(2,1)S(1)}, u32[]{:S(2)}, u32[]{:S(2)}) %collective-permute-start.9) | collective-permute-done | bytes 20512 | tf_op jit(solution)/shard_map/ppermute | solution.py:580
  37.6 0.7 %collective-permute-start.10 = (f32[5,16,128]{2,1,0:T(8,128)S(1)}, f32[5,16,128]{2,1,0:T(8,128)S(1)}, u32[]{:S(2)}, u32[]{:S(2)}) collective-permute-start(f32[5,16,128]{2,1,0:T(8,128)S(1)} %add_add_fusion.1), channel_id=1, source_target_pairs={{64,0},{65,1},{66,2},{67,3}} | collective-permute-start | bytes 122888 | tf_op jit(solution)/shard_map/ppermute | solution.py:535
  38.3 5.3 %phase_one.1 = (bf16[5,64,1536]{2,1,0:T(8,128)(2,1)S(1)}, bf16[5,64,1536]{2,1,0:T(8,128)(2,1)S(1)}, bf16[5,16,128]{2,1,0:T(8,128)(2,1)S(1)}, bf16[5,16,128]{2,1,...) custom-call(bf16[5,64,1536]{2,1,0:T(8,128)(2,1)S(1)} %copy-done.1, ...), custom_call_target="tpu_custom_call" | custom-call | flops 600000000 | bytes 18000000 | tf_op jit(solution)/shard_map/phase_one/pallas_call | solution.py:584
  43.5 2.6 %collective-permute-start.13 = (bf16[5,16,128]{2,1,0:T(8,128)(2,1)S(1)}, bf16[5,16,128]{2,1,0:T(8,128)(2,1)S(1)}, u32[]{:S(2)}, u32[]{:S(2)}) collective-permute-start(bf16[5,16,128]{2,1,0:T(8,128)(2,1)S(1)} %get-tuple-element.52), channel_id=1, source_target_pairs={{0,4},{4,8},{8,12},{12,16},{16,20},{20,24},{24,28},{28,32},{32,36}... | collective-permute-start | bytes 61448 | tf_op jit(solution)/shard_map/ppermute | solution.py:594
  46.1 1.9 %collective-permute-start.14 = (bf16[5,16,128]{2,1,0:T(8,128)(2,1)S(1)}, bf16[5,16,128]{2,1,0:T(8,128)(2,1)S(1)}, u32[]{:S(2)}, u32[]{:S(2)}) collective-permute-start(bf16[5,16,128]{2,1,0:T(8,128)(2,1)S(1)} %get-tuple-element.53), channel_id=1, source_target_pairs={{4,0},{8,4},{12,8},{16,12},{20,16},{24,20},{28,24},{32,28},{36,32}... | collective-permute-start | bytes 61448 | tf_op jit(solution)/shard_map/ppermute | solution.py:595
  48.1 6.4 %collective-permute-done.14.above_ref = bf16[5,16,128]{2,1,0:T(8,128)(2,1)S(1)} collective-permute-done((bf16[5,16,128]{2,1,0:T(8,128)(2,1)S(1)}, bf16[5,16,128]{2,1,0:T(8,128)(2,1)S(1)}, u32[]{:S(2)}, u32[]{:S(2)}) %collective-permute-start.14) | collective-permute-done | bytes 20512 | tf_op jit(solution)/shard_map/ppermute | solution.py:595
  54.5 0.7 %inflow_layer.1 = (bf16[5,64,1536]{2,1,0:T(8,128)(2,1)S(1)}, bf16[5,64,1536]{2,1,0:T(8,128)(2,1)S(1)}, bf16[5,16,768]{2,1,0:T(8,128)(2,1)S(1)}, bf16[5,16,128]{2,1,0:T(8,128)(2,1)S(1)}) custom-call(bf16[5,64,1536]{2,1,0:T(8,128)(2,1)S(1)} %get-tuple-element.47.held_ref, ...), custom_call_target="tpu_custom_call", output_to_operand_aliasing={{0}: (0, {}), {1}: (1, {}), {2}: (2, {}), {3}: (3, {})} | custom-call | flops 100000000 | bytes 3000000 | tf_op jit(solution)/shard_map/inflow_layer/pallas_call | solution.py:603
  55.2 2.1 %collective-permute-start.15 = (bf16[5,16,768]{2,1,0:T(8,128)(2,1)S(1)}, bf16[5,16,768]{2,1,0:T(8,128)(2,1)S(1)}, u32[]{:S(2)}, u32[]{:S(2)}) collective-permute-start(bf16[5,16,768]{2,1,0:T(8,128)(2,1)S(1)} %get-tuple-element.59), channel_id=1, source_target_pairs={{0,2},{2,0},{1,3},{3,1},{4,6},{6,4},{5,7},{7,5},{8,10},{10,8},{9,1... | collective-permute-start | bytes 368648 | tf_op jit(solution)/shard_map/ppermute | solution.py:620
  57.4 1.8 %collective-permute-start.16 = (bf16[5,16,128]{2,1,0:T(8,128)(2,1)S(1)}, bf16[5,16,128]{2,1,0:T(8,128)(2,1)S(1)}, u32[]{:S(2)}, u32[]{:S(2)}) collective-permute-start(bf16[5,16,128]{2,1,0:T(8,128)(2,1)S(1)} %get-tuple-element.60), channel_id=1, source_target_pairs={{0,1},{1,0},{2,3},{3,2},{4,5},{5,4},{6,7},{7,6},{8,9},{9,8},{10,11... | collective-permute-start | bytes 61448 | tf_op jit(solution)/shard_map/ppermute | solution.py:621
  59.2 3.3 %inner_two.1.part_ref = f32[5,64,1536]{2,1,0:T(8,128)S(1)} custom-call(bf16[5,64,1536]{2,1,0:T(8,128)(2,1)S(1)} %get-tuple-element.55.v_ref, f32[5,16,128]{2,1,0:T(8,128)S(1)} %bitcast.27, f32[5,16,128]{2,1,0:T(8,128)S(1)} %bitcast.29, f32[5,16,128]{2,1,0:T(8,128)S(1)} %add_add_fusion.plane_ref, bf16[5,16,128]{2,1,0:T(8,128)(2,1)S(1)} %collective-permute-done.13.below_ref, ...), custom_call_target="tpu_custom_call" | custom-call | flops 300000000 | bytes 9000000 | tf_op jit(solution)/shard_map/inner_two/pallas_call | solution.py:622
  62.5 3.8 %outer_two.1 = bf16[5,64,1536]{2,1,0:T(8,128)(2,1)} custom-call(bf16[5,64,1536]{2,1,0:T(8,128)(2,1)S(1)} %get-tuple-element.55.v_ref, bf16[5,64,1536]{2,1,0:T(8,128)(2,1)S(1)} %get-tuple-element.56.trace_ref, bf16[5,64,1536]{2,1,0:T(8,128)(2,1)S(1)} %copy-done.1, f32[5,64,1536]{2,1,0:T(8,128)S(1)} %inner_two.1.part_ref, ...), custom_call_target="tpu_custom_call" | custom-call | flops 400000000 | bytes 12000000 | tf_op jit(solution)/shard_map/outer_two/pallas_call | solution.py:632
  (69 shorter events, 5.0 us)
Async XLA Ops:
  0.0 38.3 %copy-start.1 = (bf16[5,64,1536]{2,1,0:T(8,128)(2,1)S(1)}, bf16[5,64,1536]{2,1,0:T(8,128)(2,1)}, u32[]{:S(2)}) copy-start(bf16[5,64,1536]{2,1,0:T(8,128)(2,1)} %base_ref.1) | copy-start | bytes 2949124
  0.0 14.0 %copy-start.2 = (bf16[64,64]{1,0:T(8,128)(2,1)S(1)}, bf16[64,64]{1,0:T(8,128)(2,1)}, u32[]{:S(2)}) copy-start(bf16[64,64]{1,0:T(8,128)(2,1)} %smooth_ref.1) | copy-start | bytes 24580
  2.5 11.8 %copy-start.9 = (bf16[64,96]{1,0:T(8,128)(2,1)S(1)}, bf16[64,96]{1,0:T(8,128)(2,1)}, u32[]{:S(2)}) copy-start(bf16[64,96]{1,0:T(8,128)(2,1)} %param.17) | copy-start | bytes 36868
  2.5 17.0 %copy-start.13 = (s32[1536]{0:T(1024)S(1)}, s32[1536]{0:T(1024)}, u32[]{:S(2)}) copy-start(s32[1536]{0:T(1024)} %param.20) | copy-start | bytes 18436
  2.5 17.0 %copy-start.10 = (bf16[64,64]{1,0:T(8,128)(2,1)S(1)}, bf16[64,64]{1,0:T(8,128)(2,1)}, u32[]{:S(2)}) copy-start(bf16[64,64]{1,0:T(8,128)(2,1)} %param.19) | copy-start | bytes 24580
  5.3 9.3 %collective-permute-start.2 = (f32[5,16,128]{2,1,0:T(8,128)S(1)}, f32[5,16,128]{2,1,0:T(8,128)S(1)}, u32[]{:S(2)}, u32[]{:S(2)}) collective-permute-start(f32[5,16,128]{2,1,0:T(8,128)S(1)} %eddy_plane.1), channel_id=1, source_target_pairs={{16,0},{20,4},{48,32},{52,36},{80,64},{84,68},{112,96},{116,100},{... | collective-permute-start | bytes 122888 | tf_op jit(solution)/shard_map/ppermute | solution.py:535
  6.0 8.6 %collective-permute-start.1 = (f32[5,16,128]{2,1,0:T(8,128)S(1)}, f32[5,16,128]{2,1,0:T(8,128)S(1)}, u32[]{:S(2)}, u32[]{:S(2)}) collective-permute-start(f32[5,16,128]{2,1,0:T(8,128)S(1)} %eddy_plane.1), channel_id=1, source_target_pairs={{24,0},{28,4},{56,32},{60,36},{88,64},{92,68},{120,96},{124,100},{... | collective-permute-start | bytes 122888 | tf_op jit(solution)/shard_map/ppermute | solution.py:535
  8.5 6.1 %collective-permute-start = (f32[5,16,128]{2,1,0:T(8,128)S(1)}, f32[5,16,128]{2,1,0:T(8,128)S(1)}, u32[]{:S(2)}, u32[]{:S(2)}) collective-permute-start(f32[5,16,128]{2,1,0:T(8,128)S(1)} %eddy_plane.1), channel_id=1, source_target_pairs={{8,0},{12,4},{40,32},{44,36},{72,64},{76,68},{104,96},{108,100},{1... | collective-permute-start | bytes 122888 | tf_op jit(solution)/shard_map/ppermute | solution.py:535
  11.5 43.0 %copy-start.3 = (f32[1,1,5,2048]{3,1,2,0:T(1,128)S(1)}, f32[1,1,5,2048]{3,1,2,0:T(1,128)}, u32[]{:S(2)}) copy-start(f32[1,1,5,2048]{3,1,2,0:T(1,128)} %param.24) | copy-start | bytes 122884
  11.5 43.0 %copy-start.4 = (f32[1,1,5,2048]{3,1,2,0:T(1,128)S(1)}, f32[1,1,5,2048]{3,1,2,0:T(1,128)}, u32[]{:S(2)}) copy-start(f32[1,1,5,2048]{3,1,2,0:T(1,128)} %param.25) | copy-start | bytes 122884
  11.6 3.1 %collective-permute-start.4 = (bf16[5,16,128]{2,1,0:T(8,128)(2,1)S(1)}, bf16[5,16,128]{2,1,0:T(8,128)(2,1)S(1)}, u32[]{:S(2)}, u32[]{:S(2)}) collective-permute-start(bf16[5,16,128]{2,1,0:T(8,128)(2,1)S(1)} %get-tuple-element.35), channel_id=1, source_target_pairs={{0,1},{1,0},{2,3},{3,2},{4,5},{5,4},{6,7},{7,6},{8,9},{9,8},{10,11... | collective-permute-start | bytes 61448 | tf_op jit(solution)/shard_map/ppermute | solution.py:576
  11.9 5.5 %collective-permute-start.3 = (bf16[5,16,768]{2,1,0:T(8,128)(2,1)S(1)}, bf16[5,16,768]{2,1,0:T(8,128)(2,1)S(1)}, u32[]{:S(2)}, u32[]{:S(2)}) collective-permute-start(bf16[5,16,768]{2,1,0:T(8,128)(2,1)S(1)} %get-tuple-element.34), channel_id=1, source_target_pairs={{0,2},{2,0},{1,3},{3,1},{4,6},{6,4},{5,7},{7,5},{8,10},{10,8},{9,1... | collective-permute-start | bytes 368648 | tf_op jit(solution)/shard_map/ppermute | solution.py:575
  17.4 12.4 %collective-permute-start.7 = (f32[5,16,128]{2,1,0:T(8,128)S(1)}, f32[5,16,128]{2,1,0:T(8,128)S(1)}, u32[]{:S(2)}, u32[]{:S(2)}) collective-permute-start(f32[5,16,128]{2,1,0:T(8,128)S(1)} %add_add_fusion.2), channel_id=1, source_target_pairs={{36,0},{100,64},{164,128},{228,192},{37,1},{101,65},{165,129},{229... | collective-permute-start | bytes 122888 | tf_op jit(solution)/shard_map/ppermute | solution.py:535
  18.0 11.7 %collective-permute-start.6 = (f32[5,16,128]{2,1,0:T(8,128)S(1)}, f32[5,16,128]{2,1,0:T(8,128)S(1)}, u32[]{:S(2)}, u32[]{:S(2)}) collective-permute-start(f32[5,16,128]{2,1,0:T(8,128)S(1)} %add_add_fusion.2), channel_id=1, source_target_pairs={{32,0},{96,64},{160,128},{224,192},{33,1},{97,65},{161,129},{225,1... | collective-permute-start | bytes 122888 | tf_op jit(solution)/shard_map/ppermute | solution.py:535
  18.7 11.1 %collective-permute-start.5 = (f32[5,16,128]{2,1,0:T(8,128)S(1)}, f32[5,16,128]{2,1,0:T(8,128)S(1)}, u32[]{:S(2)}, u32[]{:S(2)}) collective-permute-start(f32[5,16,128]{2,1,0:T(8,128)S(1)} %add_add_fusion.2), channel_id=1, source_target_pairs={{4,0},{68,64},{132,128},{196,192},{5,1},{69,65},{133,129},{197,193... | collective-permute-start | bytes 122888 | tf_op jit(solution)/shard_map/ppermute | solution.py:535
  19.6 10.2 %collective-permute-start.8 = (bf16[5,16,128]{2,1,0:T(8,128)(2,1)S(1)}, bf16[5,16,128]{2,1,0:T(8,128)(2,1)S(1)}, u32[]{:S(2)}, u32[]{:S(2)}) collective-permute-start(bf16[5,16,128]{2,1,0:T(8,128)(2,1)S(1)} %get-tuple-element.41), channel_id=1, source_target_pairs={{0,4},{4,8},{8,12},{12,16},{16,20},{20,24},{24,28},{28,32},{32,36}... | collective-permute-start | bytes 61448 | tf_op jit(solution)/shard_map/ppermute | solution.py:579
  27.8 8.4 %collective-permute-start.9 = (bf16[5,16,128]{2,1,0:T(8,128)(2,1)S(1)}, bf16[5,16,128]{2,1,0:T(8,128)(2,1)S(1)}, u32[]{:S(2)}, u32[]{:S(2)}) collective-permute-start(bf16[5,16,128]{2,1,0:T(8,128)(2,1)S(1)} %get-tuple-element.42), channel_id=1, source_target_pairs={{4,0},{8,4},{12,8},{16,12},{20,16},{24,20},{28,24},{32,28},{36,32}... | collective-permute-start | bytes 61448 | tf_op jit(solution)/shard_map/ppermute | solution.py:580
  36.2 11.8 %collective-permute-start.12 = (f32[5,16,128]{2,1,0:T(8,128)S(1)}, f32[5,16,128]{2,1,0:T(8,128)S(1)}, u32[]{:S(2)}, u32[]{:S(2)}) collective-permute-start(f32[5,16,128]{2,1,0:T(8,128)S(1)} %add_add_fusion.1), channel_id=1, source_target_pairs={{128,0},{129,1},{130,2},{131,3}} | collective-permute-start | bytes 122888 | tf_op jit(solution)/shard_map/ppermute | solution.py:535
  36.9 11.1 %collective-permute-start.11 = (f32[5,16,128]{2,1,0:T(8,128)S(1)}, f32[5,16,128]{2,1,0:T(8,128)S(1)}, u32[]{:S(2)}, u32[]{:S(2)}) collective-permute-start(f32[5,16,128]{2,1,0:T(8,128)S(1)} %add_add_fusion.1), channel_id=1, source_target_pairs={{192,0},{193,1},{194,2},{195,3}} | collective-permute-start | bytes 122888 | tf_op jit(solution)/shard_map/ppermute | solution.py:535
  37.6 10.5 %collective-permute-start.10 = (f32[5,16,128]{2,1,0:T(8,128)S(1)}, f32[5,16,128]{2,1,0:T(8,128)S(1)}, u32[]{:S(2)}, u32[]{:S(2)}) collective-permute-start(f32[5,16,128]{2,1,0:T(8,128)S(1)} %add_add_fusion.1), channel_id=1, source_target_pairs={{64,0},{65,1},{66,2},{67,3}} | collective-permute-start | bytes 122888 | tf_op jit(solution)/shard_map/ppermute | solution.py:535
  43.5 4.6 %collective-permute-start.13 = (bf16[5,16,128]{2,1,0:T(8,128)(2,1)S(1)}, bf16[5,16,128]{2,1,0:T(8,128)(2,1)S(1)}, u32[]{:S(2)}, u32[]{:S(2)}) collective-permute-start(bf16[5,16,128]{2,1,0:T(8,128)(2,1)S(1)} %get-tuple-element.52), channel_id=1, source_target_pairs={{0,4},{4,8},{8,12},{12,16},{16,20},{20,24},{24,28},{28,32},{32,36}... | collective-permute-start | bytes 61448 | tf_op jit(solution)/shard_map/ppermute | solution.py:594
  46.1 8.4 %collective-permute-start.14 = (bf16[5,16,128]{2,1,0:T(8,128)(2,1)S(1)}, bf16[5,16,128]{2,1,0:T(8,128)(2,1)S(1)}, u32[]{:S(2)}, u32[]{:S(2)}) collective-permute-start(bf16[5,16,128]{2,1,0:T(8,128)(2,1)S(1)} %get-tuple-element.53), channel_id=1, source_target_pairs={{4,0},{8,4},{12,8},{16,12},{20,16},{24,20},{28,24},{32,28},{36,32}... | collective-permute-start | bytes 61448 | tf_op jit(solution)/shard_map/ppermute | solution.py:595
  55.2 7.2 %collective-permute-start.15 = (bf16[5,16,768]{2,1,0:T(8,128)(2,1)S(1)}, bf16[5,16,768]{2,1,0:T(8,128)(2,1)S(1)}, u32[]{:S(2)}, u32[]{:S(2)}) collective-permute-start(bf16[5,16,768]{2,1,0:T(8,128)(2,1)S(1)} %get-tuple-element.59), channel_id=1, source_target_pairs={{0,2},{2,0},{1,3},{3,1},{4,6},{6,4},{5,7},{7,5},{8,10},{10,8},{9,1... | collective-permute-start | bytes 368648 | tf_op jit(solution)/shard_map/ppermute | solution.py:620
  57.4 5.0 %collective-permute-start.16 = (bf16[5,16,128]{2,1,0:T(8,128)(2,1)S(1)}, bf16[5,16,128]{2,1,0:T(8,128)(2,1)S(1)}, u32[]{:S(2)}, u32[]{:S(2)}) collective-permute-start(bf16[5,16,128]{2,1,0:T(8,128)(2,1)S(1)} %get-tuple-element.60), channel_id=1, source_target_pairs={{0,1},{1,0},{2,3},{3,2},{4,5},{5,4},{6,7},{7,6},{8,9},{9,8},{10,11... | collective-permute-start | bytes 61448 | tf_op jit(solution)/shard_map/ppermute | solution.py:621
  (8 other events, 39.4 us)

commit v4 on v3

--- a/solution.py
+++ b/solution.py
@@ -2,7 +2,6 @@
 
 import jax
 import jax.numpy as jnp
-import numpy as np
 from jax import lax
 from jax.experimental import pallas as pl
 from jax.experimental.pallas import tpu as pltpu
@@ -22,15 +21,13 @@
 
 
 def trace_selector():
-    pick = np.zeros((64, 64), np.float32)
-    for first in range(4):
-        for second in range(4):
-            w = 4 * first + second
-            pick[w, 16 * first + second] = 1
-            pick[16 + w, 16 * first + 12 + second] = 1
-            pick[32 + w, 16 * first + 4 * second] = 1
-            pick[48 + w, 16 * first + 4 * second + 3] = 1
-    return jnp.asarray(pick, bf16)
+    row = lax.broadcasted_iota(jnp.int32, (64, 64), 0)
+    node = lax.broadcasted_iota(jnp.int32, (64, 64), 1)
+    face, first, second = row >> 4, (row >> 2) & 3, row & 3
+    on_pitch = second + jnp.where(face == 1, 12, 0)
+    on_span = 4 * second + jnp.where(face == 3, 3, 0)
+    source = 16 * first + jnp.where(face < 2, on_pitch, on_span)
+    return jnp.where(node == source, 1.0, 0.0).astype(bf16)
 
 
 def dot(a, b):
@@ -41,7 +38,7 @@
     return lax.broadcasted_iota(jnp.int32, (16, CELLS), 1)
 
 
-def plane_kernel(rows_ref, seeds_ref, shape_ref, plane_ref, *, normalizer):
+def sum_eddies(rows_ref, seeds_ref, shape_ref, plane_ref, normalizer):
     seeds = seeds_ref[...]
     signs = [(2 * ((seeds >> f) & 1) - 1).astype(f32) for f in range(FIELDS)]
     signs = [jnp.broadcast_to(s, (32, s.shape[1])).astype(bf16) for s in signs]
@@ -100,13 +97,46 @@
     span_held[f] = held
 
 
-def pack_kernel(
-    v_ref, pick_ref, trace_ref, up_ref, down_ref, pitch_ref, span_ref, span_held
+def is_even():
+    return (lax.axis_index("rans") & 1) == 0
+
+
+def store_stream(up, down, near_chip_ref, far_chip_ref):
+    even = is_even()
+    near_chip_ref[...] = jnp.where(even, up, down)
+    far_chip_ref[...] = jnp.where(even, down, up)
+
+
+def from_below(near_chip_ref, far_chip_ref):
+    even = is_even()
+    return lambda f: jnp.where(even, far_chip_ref[f].astype(f32), near_chip_ref[f].astype(f32))
+
+
+def from_above(near_chip_ref, far_chip_ref):
+    even = is_even()
+    return lambda f: jnp.where(even, near_chip_ref[f].astype(f32), far_chip_ref[f].astype(f32))
+
+
+def prepare_kernel(
+    rows_hbm, seeds_hbm, shape_hbm, v_hbm, plane_ref, trace_ref, core_ref, chip_ref, pitch_ref,
+    span_ref, rows_ref, seeds_ref, shape_ref, v_ref, span_held, sems, *, normalizer,
 ):
+    copies = [
+        pltpu.make_async_copy(source, target, sems.at[i])
+        for i, (source, target) in enumerate([
+            (rows_hbm, rows_ref), (seeds_hbm, seeds_ref), (shape_hbm, shape_ref), (v_hbm, v_ref)
+        ])
+    ]
+    for copy in copies:
+        copy.start()
     first_span = lax.axis_index("span") == 0
     lane = lanes()
-    pick = pick_ref[...]
+    pick = trace_selector()
     span_held[...] = jnp.zeros_like(span_held)
+    for copy in copies[:3]:
+        copy.wait()
+    sum_eddies(rows_ref, seeds_ref, shape_ref, plane_ref, normalizer)
+    copies[3].wait()
     for pair in range(EX // 2):
         at = slice(pair * PAIR, (pair + 1) * PAIR)
         traces = [dot(pick, v_ref[f, :, at]) for f in range(FIELDS)]
@@ -114,8 +144,9 @@
             trace_ref[f, :, at] = traces[f].astype(bf16)
             pack_field(f, traces[f], pair, first_span, lane, pitch_ref, span_held)
     span_ref[...] = span_held[...].astype(bf16)
-    up_ref[...] = v_ref[:, 48:64, (EX - 1) * CELLS :]
-    down_ref[...] = v_ref[:, 0:16, 0:CELLS]
+    store_stream(
+        v_ref[:, 48:64, (EX - 1) * CELLS :], v_ref[:, 0:16, 0:CELLS], core_ref, chip_ref
+    )
 
 
 def mix(coefs, base, arrays):
@@ -288,7 +319,7 @@
     return lower
 
 
-def upper_pair(v_ref, above_ref, pair):
+def upper_pair(v_ref, above, pair):
     first = pair * PAIR + CELLS
     last_rans = lax.axis_index("rans") == lax.axis_size("rans") - 1
 
@@ -296,7 +327,7 @@
         if pair < EX // 2 - 1:
             return v_ref[f, 0:16, first : first + PAIR].astype(f32)
         edge = jnp.where(
-            last_rans, v_ref[f, 48:64, first : first + CELLS].astype(f32), above_ref[f].astype(f32)
+            last_rans, v_ref[f, 48:64, first : first + CELLS].astype(f32), above(f)
         )
         return jnp.concatenate([v_ref[f, 0:16, first : first + CELLS].astype(f32), edge], axis=1)
 
@@ -304,13 +335,14 @@
 
 
 def phase_one_kernel(
-    v_ref, trace_ref, below_ref, above_ref, near_ref, far_ref, pin_ref, coefs, weights_ref,
-    smooth_ref, out_ref, out_trace_ref, up_ref, down_ref, pitch_ref, span_ref, mixed, span_held,
+    v_ref, trace_ref, from_core_ref, from_chip_ref, near_ref, far_ref, pin_ref, coefs, weights_ref,
+    smooth_ref, out_ref, out_trace_ref, core_ref, chip_ref, pitch_ref, span_ref, mixed, span_held,
 ):
     first_span = lax.axis_index("span") == 0
     lane = lanes()
     weights, smooth = weights_ref[...], smooth_ref[...]
     span_held[...] = jnp.zeros_like(span_held)
+    below, above = from_below(from_core_ref, from_chip_ref), from_above(from_core_ref, from_chip_ref)
     vector, matrix = [], []
 
     def add(pair):
@@ -330,8 +362,8 @@
             mix_fluxes(read, coefs, rows)
             + mix_stream(
                 read,
-                lower_pair(v_ref, lambda f: below_ref[f].astype(f32), pair),
-                upper_pair(v_ref, above_ref, pair),
+                lower_pair(v_ref, below, pair),
+                upper_pair(v_ref, above, pair),
                 coefs, rows, 192,
             )
             + mix_sides(
@@ -350,21 +382,22 @@
         add(pair)
     pipeline(vector, matrix)
     span_ref[...] = span_held[...].astype(bf16)
-    up_ref[...] = out_ref[:, 48:64, (EX - 1) * CELLS :]
-    down_ref[...] = out_ref[:, 0:16, 0:CELLS]
+    store_stream(
+        out_ref[:, 48:64, (EX - 1) * CELLS :], out_ref[:, 0:16, 0:CELLS], core_ref, chip_ref
+    )
 
 
 def inner_two_kernel(
-    v_ref, mean_ref, amp_ref, plane_ref, below_ref, above_ref, coefs, weights_ref, part_ref, mixed
+    v_ref, mean_ref, amp_ref, plane_ref, from_core_ref, from_chip_ref, coefs, weights_ref, part_ref,
+    mixed,
 ):
     first_rans = lax.axis_index("rans") == 0
     weights = weights_ref[...]
+    below, above = from_below(from_core_ref, from_chip_ref), from_above(from_core_ref, from_chip_ref)
     vector, matrix = [], []
 
     def edge(f):
-        return jnp.where(
-            first_rans, inflow_of(mean_ref, amp_ref, plane_ref)(f), below_ref[f].astype(f32)
-        )
+        return jnp.where(first_rans, inflow_of(mean_ref, amp_ref, plane_ref)(f), below(f))
 
     def add(pair):
         at = place(pair)
@@ -379,8 +412,7 @@
         vector.append(
             mix_fluxes(read, coefs, rows)
             + mix_stream(
-                read, lower_pair(v_ref, edge, pair), upper_pair(v_ref, above_ref, pair), coefs, rows,
-                192,
+                read, lower_pair(v_ref, edge, pair), upper_pair(v_ref, above, pair), coefs, rows, 192,
             )
         )
         matrix.append(staggered([lambda f, _: dot(weights, rows[f]), store]))
@@ -517,20 +549,6 @@
     eddies, foot = mode_shape.shape[2:]
     plane_rows = mean_inflow.shape[3]
     faces = shape_of(FIELDS, 16, CELLS)
-    pick = trace_selector()
-
-    plane = pl.pallas_call(
-        functools.partial(
-            plane_kernel, normalizer=float((plane_rows / (eddies * ranks * foot)) ** 0.5)
-        ),
-        out_shape=shape_of(FIELDS, 16, CELLS, dtype=f32),
-        in_specs=[VMEM] * 3,
-        out_specs=VMEM,
-        compiler_params=PARAMS,
-        cost_estimate=cost(3),
-        name="eddy_plane",
-    )(mode_rows[0, 0].T, mode_seeds.reshape(1, eddies), mode_shape[0, 0].T)
-
     def gather_sum(value, offsets, roots):
         parts = [lax.ppermute(value, "rans", [(r + o, r) for r in roots]) for o in offsets]
         for part in parts:
@@ -556,32 +574,44 @@
     elements = solution.shape[2]
     traces = shape_of(FIELDS, NODES, elements)
     sends = (faces, faces, shape_of(FIELDS, 16, EX // 2 * CELLS), faces)
-    rise = [(i, i + 1) for i in range(ranks - 1)]
-    fall = [(b, a) for a, b in rise]
     swap = [(0, 1), (1, 0)]
+    same_chip = [(i, i ^ 1) for i in range(ranks)]
+    next_chip = [(a + 1, b + 1) for a, b in same_chip if max(a, b) + 1 < ranks]
 
     span_scratch = pltpu.VMEM((FIELDS, 16, CELLS), f32)
-    trace, up, down, pitch, span = pl.pallas_call(
-        pack_kernel,
-        out_shape=(traces,) + sends,
-        in_specs=[VMEM] * 2,
-        out_specs=(VMEM,) * 5,
-        scratch_shapes=[span_scratch],
-        compiler_params=PARAMS,
-        cost_estimate=cost(2),
-        name="pack_faces",
-    )(solution, pick)
+    plane, trace, core, chip, pitch, span = pl.pallas_call(
+        functools.partial(
+            prepare_kernel, normalizer=float((plane_rows / (eddies * ranks * foot)) ** 0.5)
+        ),
+        out_shape=(shape_of(FIELDS, 16, CELLS, dtype=f32), traces) + sends,
+        in_specs=[pl.BlockSpec(memory_space=pltpu.HBM)] * 4,
+        out_specs=(VMEM,) * 6,
+        scratch_shapes=[
+            pltpu.VMEM((foot, eddies), jnp.int32),
+            pltpu.VMEM((1, eddies), jnp.int32),
+            pltpu.VMEM((foot, eddies), f32),
+            pltpu.VMEM(solution.shape, bf16),
+            span_scratch,
+            pltpu.SemaphoreType.DMA((4,)),
+        ],
+        compiler_params=pltpu.CompilerParams(vmem_limit_bytes=60 * 2**20),
+        cost_estimate=cost(5),
+        name="prepare",
+    )(mode_rows[0, 0].T, mode_seeds.reshape(1, eddies), mode_shape[0, 0].T, solution)
     plane = gather_sum(plane, (2, 6, 4), [8 * z + c for z in range(8) for c in range(2)])
     near = lax.ppermute(pitch, "pitch", swap)
+    from_chip = lax.ppermute(chip, "rans", next_chip)
+    plane, core, span = lax.optimization_barrier((plane, core, span))
+    plane = gather_sum(plane, (1, 8, 9), [0, 16, 32, 48])
+    core, span, near, from_chip = lax.optimization_barrier((core, span, near, from_chip))
     far = lax.ppermute(span, "span", swap)
-    plane, near, far, up, down = lax.optimization_barrier((plane, near, far, up, down))
-    plane = gather_sum(plane, (1, 8, 9), [0, 16, 32, 48])
-    below = lax.ppermute(up, "rans", rise)
-    above = lax.ppermute(down, "rans", fall)
-    plane, near, far, below, above = lax.optimization_barrier((plane, near, far, below, above))
+    from_core = lax.ppermute(core, "rans", same_chip)
+    plane, near, far, from_core, from_chip = lax.optimization_barrier(
+        (plane, near, far, from_core, from_chip)
+    )
     plane = gather_sum(plane, (16, 48, 32), [0])
 
-    phase_one, trace_one, up, down, pitch, span = pl.pallas_call(
+    phase_one, trace_one, core, chip, pitch, span = pl.pallas_call(
         phase_one_kernel,
         out_shape=(traces, traces) + sends,
         in_specs=[VMEM] * 6 + fixed_specs,
@@ -590,11 +620,10 @@
         compiler_params=PARAMS,
         cost_estimate=cost(6),
         name="phase_one",
-    )(solution, trace, below, above, near, far, pins, coefs, weights, smooth)
-    below = lax.ppermute(up, "rans", rise)
-    above = lax.ppermute(down, "rans", fall)
-
-    plane, below, above = lax.optimization_barrier((plane, below, above))
+    )(solution, trace, from_core, from_chip, near, far, pins, coefs, weights, smooth)
+    from_core = lax.ppermute(core, "rans", same_chip)
+    from_chip = lax.ppermute(chip, "rans", next_chip)
+    plane, from_core, from_chip = lax.optimization_barrier((plane, from_core, from_chip))
 
     mean = mean_inflow.reshape(FIELDS, 16, CELLS)
     amplitude = eddy_amplitude.reshape(FIELDS, 16, CELLS)
@@ -628,7 +657,7 @@
         compiler_params=PARAMS,
         cost_estimate=cost(3),
         name="inner_two",
-    )(phase_one, mean, amplitude, plane, below, above, coefs, weights[:, :INNER])
+    )(phase_one, mean, amplitude, plane, from_core, from_chip, coefs, weights[:, :INNER])
     return pl.pallas_call(
         outer_two_kernel,
         out_shape=traces,

time: 66.7 us -> 58 us (0.87)
  the two profiles are of different devices: /device:TPU:123 before, /device:TPU:224 now
where the time goes in v4:
time: 58 us; the launch traced here: 57.5 us
  starting transfers between devices  23.7 us (41%)
  Pallas kernels  18.3 us (32%)
  waiting for transfers between devices  9.45 us (16%)
  local copies, waits for them, and re-layouts  4.53 us (8%)
  other arithmetic  1.15 us (2%)
    ppermute x9, starting transfers between devices, gather_sum(): lax.ppermute(value, 'rans', [(r + o, r) for r in roots])  10.9 us
    ppermute x2, starting transfers between devices, body(): from_chip = lax.ppermute(chip, 'rans', next_chip)  6.66 us
    pallas_call x1, Pallas kernels, body(): pl.pallas_call(phase_one_kernel, out_shape=(traces, traces) + sends, in_s...  5.3 us
    ppermute x2, waiting for transfers between devices, body(): from_chip = lax.ppermute(chip, 'rans', next_chip)  5.22 us
    pallas_call x1, Pallas kernels, body(): pl.pallas_call(functools.partial(prepare_kernel, normalizer=float((plane_...  5.21 us
    pallas_call x1, Pallas kernels, body(): pl.pallas_call(outer_two_kernel, out_shape=traces, in_specs=[VMEM] * 7 +...  3.8 us
    ppermute x2, starting transfers between devices, body(): near = lax.ppermute(pitch, 'pitch', swap)  3.77 us
    ppermute x2, waiting for transfers between devices, body(): far = lax.ppermute(span, 'span', swap)  3.31 us
  transfers between devices with their start and end apart: 17, of which 4 were waited for; matrix products, arithmetic and copies ran while one was open for 8% of the time, Pallas kernels for 15%

profile of v4, /device:TPU:224, one launch (start us, length us, event | category | flops | bytes accessed | tf_op | source)
XLA Modules:
  0.0 57.5 jit_solution(5220429354323339021)
XLA Ops:
  0.0 5.2 %prepare.1 = (f32[5,16,128]{2,1,0:T(8,128)}, bf16[5,64,1536]{2,1,0:T(8,128)(2,1)}, bf16[5,16,128]{2,1,0:T(8,128)(2,1)}, bf16[5,16,128]{2,1,0:T(8,128)(2,1)}, bf1...) custom-call(s32[64,256]{1,0:T(8,128)} %bitcast.34, s32[1,256]{1,0:T(1,128)} %bitcast.36, f32[64,256]{1,0:T(8,128)} %bitcast.35, ...), custom_call_target="tpu_custom_call" | custom-call | flops 500000000 | bytes 15000000 | tf_op jit(solution)/shard_map/prepare/pallas_call | solution.py:582
  5.3 1.4 %collective-permute-start.2 = (f32[5,16,128]{2,1,0:T(8,128)}, f32[5,16,128]{2,1,0:T(8,128)S(1)}, u32[]{:S(2)}, u32[]{:S(2)}) collective-permute-start(f32[5,16,128]{2,1,0:T(8,128)} %get-tuple-element.37), channel_id=1, source_target_pairs={{16,0},{20,4},{48,32},{52,36},{80,64},{84,68},{112,96},{116,100},{... | collective-permute-start | bytes 122888 | tf_op jit(solution)/shard_map/ppermute | solution.py:553
  6.7 1.3 %collective-permute-start.1 = (f32[5,16,128]{2,1,0:T(8,128)}, f32[5,16,128]{2,1,0:T(8,128)S(1)}, u32[]{:S(2)}, u32[]{:S(2)}) collective-permute-start(f32[5,16,128]{2,1,0:T(8,128)} %get-tuple-element.37), channel_id=1, source_target_pairs={{24,0},{28,4},{56,32},{60,36},{88,64},{92,68},{120,96},{124,100},{... | collective-permute-start | bytes 122888 | tf_op jit(solution)/shard_map/ppermute | solution.py:553
  8.0 1.3 %collective-permute-start = (f32[5,16,128]{2,1,0:T(8,128)}, f32[5,16,128]{2,1,0:T(8,128)S(1)}, u32[]{:S(2)}, u32[]{:S(2)}) collective-permute-start(f32[5,16,128]{2,1,0:T(8,128)} %get-tuple-element.37), channel_id=1, source_target_pairs={{8,0},{12,4},{40,32},{44,36},{72,64},{76,68},{104,96},{108,100},{1... | collective-permute-start | bytes 122888 | tf_op jit(solution)/shard_map/ppermute | solution.py:553
  9.3 4.7 %collective-permute-start.7 = (bf16[5,16,128]{2,1,0:T(8,128)(2,1)}, bf16[5,16,128]{2,1,0:T(8,128)(2,1)S(1)}, u32[]{:S(2)}, u32[]{:S(2)}) collective-permute-start(bf16[5,16,128]{2,1,0:T(8,128)(2,1)} %get-tuple-element.44), channel_id=1, source_target_pairs={{4,8},{8,4},{12,16},{16,12},{20,24},{24,20},{28,32},{32,28},{36,40... | collective-permute-start | bytes 61448 | tf_op jit(solution)/shard_map/ppermute | solution.py:603
  14.1 3.1 %collective-permute-start.6 = (bf16[5,16,768]{2,1,0:T(8,128)(2,1)}, bf16[5,16,768]{2,1,0:T(8,128)(2,1)S(1)}, u32[]{:S(2)}, u32[]{:S(2)}) collective-permute-start(bf16[5,16,768]{2,1,0:T(8,128)(2,1)} %get-tuple-element.43), channel_id=1, source_target_pairs={{0,2},{2,0},{1,3},{3,1},{4,6},{6,4},{5,7},{7,5},{8,10},{10,8},{9,1... | collective-permute-start | bytes 368648 | tf_op jit(solution)/shard_map/ppermute | solution.py:602
  17.2 0.7 %fusion.2 = (bf16[4,1,4,64]{3,2,1,0:T(4,128)(2,1)S(1)}, bf16[4,1,4,64]{3,2,1,0:T(4,128)(2,1)S(1)}) fusion(bf16[4,4,4,64]{3,2,1,0:T(4,128)(2,1)} %bitcast.24), kind=kLoop, calls=%fused_computation.20 | loop fusion | bytes 8192 | tf_op jit(solution)/shard_map/slice | solution.py:571
  17.9 0.8 %fusion.1 = (bf16[4,4,1,64]{3,2,1,0:T(2,128)(2,1)S(1)}, bf16[4,4,1,64]{3,2,1,0:T(2,128)(2,1)S(1)}) fusion(bf16[4,4,4,64]{3,2,1,0:T(4,128)(2,1)} %bitcast.25), kind=kLoop, calls=%fused_computation.19 | loop fusion | bytes 8192 | tf_op jit(solution)/shard_map/slice | solution.py:571
  18.7 0.7 %constant_dynamic-update-slice_fusion.4 = bf16[128,64]{1,0:T(8,128)(2,1)S(1)} fusion(bf16[64,64]{1,0:T(8,128)(2,1)} %smooth_ref.1), kind=kLoop, calls=%fused_computation.15 | loop fusion | bytes 24576
  19.4 0.7 %copy.24 = f32[3,5,5]{2,1,0:T(8,128)S(1)} copy(f32[3,5,5]{2,0,1:T(4,128)} %param.15) | data formatting | bytes 600 | tf_op args[2]
  20.6 0.8 %add_add_fusion.2 = f32[5,16,128]{2,1,0:T(8,128)S(1)} fusion(f32[5,16,128]{2,1,0:T(8,128)S(1)} %collective-permute-done.2, f32[5,16,128]{2,1,0:T(8,128)S(1)} %collective-permute-done.1, f32[5,16,128]{2,1,0:T(8,128)} %get-tuple-element.37, f32[5,16,128]{2,1,0:T(8,128)S(1)} %collective-permute-done), kind=kLoop, calls=%fused_computation.2 | loop fusion | flops 30720 | bytes 204800 | tf_op jit(solution)/shard_map/add | solution.py:555
  21.4 0.7 %collective-permute-start.5 = (f32[5,16,128]{2,1,0:T(8,128)S(1)}, f32[5,16,128]{2,1,0:T(8,128)S(1)}, u32[]{:S(2)}, u32[]{:S(2)}) collective-permute-start(f32[5,16,128]{2,1,0:T(8,128)S(1)} %add_add_fusion.2), channel_id=1, source_target_pairs={{36,0},{100,64},{164,128},{228,192},{37,1},{101,65},{165,129},{229... | collective-permute-start | bytes 122888 | tf_op jit(solution)/shard_map/ppermute | solution.py:553
  22.1 3.6 %collective-permute-start.4 = (f32[5,16,128]{2,1,0:T(8,128)S(1)}, f32[5,16,128]{2,1,0:T(8,128)S(1)}, u32[]{:S(2)}, u32[]{:S(2)}) collective-permute-start(f32[5,16,128]{2,1,0:T(8,128)S(1)} %add_add_fusion.2), channel_id=1, source_target_pairs={{32,0},{96,64},{160,128},{224,192},{33,1},{97,65},{161,129},{225,1... | collective-permute-start | bytes 122888 | tf_op jit(solution)/shard_map/ppermute | solution.py:553
  26.5 0.7 %collective-permute-start.8 = (bf16[5,16,128]{2,1,0:T(8,128)(2,1)}, bf16[5,16,128]{2,1,0:T(8,128)(2,1)S(1)}, u32[]{:S(2)}, u32[]{:S(2)}) collective-permute-start(bf16[5,16,128]{2,1,0:T(8,128)(2,1)} %get-tuple-element.46), channel_id=1, source_target_pairs={{0,1},{1,0},{2,3},{3,2},{4,5},{5,4},{6,7},{7,6},{8,9},{9,8},{10,11... | collective-permute-start | bytes 61448 | tf_op jit(solution)/shard_map/ppermute | solution.py:607
  27.3 3.3 %collective-permute-done.8.far_ref = bf16[5,16,128]{2,1,0:T(8,128)(2,1)S(1)} collective-permute-done((bf16[5,16,128]{2,1,0:T(8,128)(2,1)}, bf16[5,16,128]{2,1,0:T(8,128)(2,1)S(1)}, u32[]{:S(2)}, u32[]{:S(2)}) %collective-permute-start.8) | collective-permute-done | bytes 20512 | tf_op jit(solution)/shard_map/ppermute | solution.py:607
  32.7 1.2 %copy-done.1 = bf16[5,64,1536]{2,1,0:T(8,128)(2,1)S(1)} copy-done((bf16[5,64,1536]{2,1,0:T(8,128)(2,1)S(1)}, bf16[5,64,1536]{2,1,0:T(8,128)(2,1)}, u32[]{:S(2)}) %copy-start.1) | copy-done | bytes 983064
  33.9 5.3 %phase_one.1 = (bf16[5,64,1536]{2,1,0:T(8,128)(2,1)S(1)}, bf16[5,64,1536]{2,1,0:T(8,128)(2,1)S(1)}, bf16[5,16,128]{2,1,0:T(8,128)(2,1)S(1)}, bf16[5,16,128]{2,1,...) custom-call(bf16[5,64,1536]{2,1,0:T(8,128)(2,1)S(1)} %copy-done, ...), custom_call_target="tpu_custom_call" | custom-call | flops 600000000 | bytes 18000000 | tf_op jit(solution)/shard_map/phase_one/pallas_call | solution.py:614
  39.3 1.9 %collective-permute-start.14 = (bf16[5,16,128]{2,1,0:T(8,128)(2,1)S(1)}, bf16[5,16,128]{2,1,0:T(8,128)(2,1)S(1)}, u32[]{:S(2)}, u32[]{:S(2)}) collective-permute-start(bf16[5,16,128]{2,1,0:T(8,128)(2,1)S(1)} %get-tuple-element.59), channel_id=1, source_target_pairs={{4,8},{8,4},{12,16},{16,12},{20,24},{24,20},{28,32},{32,28},{36,40... | collective-permute-start | bytes 61448 | tf_op jit(solution)/shard_map/ppermute | solution.py:625
  41.2 5.2 %collective-permute-done.14.from_chip_ref = bf16[5,16,128]{2,1,0:T(8,128)(2,1)S(1)} collective-permute-done((bf16[5,16,128]{2,1,0:T(8,128)(2,1)S(1)}, bf16[5,16,128]{2,1,0:T(8,128)(2,1)S(1)}, u32[]{:S(2)}, u32[]{:S(2)}) %collective-permute-start.14) | collective-permute-done | bytes 20512 | tf_op jit(solution)/shard_map/ppermute | solution.py:625
  46.5 0.7 %inflow_layer.1 = (bf16[5,64,1536]{2,1,0:T(8,128)(2,1)S(1)}, bf16[5,64,1536]{2,1,0:T(8,128)(2,1)S(1)}, bf16[5,16,768]{2,1,0:T(8,128)(2,1)S(1)}, bf16[5,16,128]{2,1,0:T(8,128)(2,1)S(1)}) custom-call(bf16[5,64,1536]{2,1,0:T(8,128)(2,1)S(1)} %get-tuple-element.53.held_ref, ...), custom_call_target="tpu_custom_call", output_to_operand_aliasing={{0}: (0, {}), {1}: (1, {}), {2}: (2, {}), {3}: (3, {})} | custom-call | flops 100000000 | bytes 3000000 | tf_op jit(solution)/shard_map/inflow_layer/pallas_call | solution.py:632
  47.9 1.6 %collective-permute-start.16 = (bf16[5,16,128]{2,1,0:T(8,128)(2,1)S(1)}, bf16[5,16,128]{2,1,0:T(8,128)(2,1)S(1)}, u32[]{:S(2)}, u32[]{:S(2)}) collective-permute-start(bf16[5,16,128]{2,1,0:T(8,128)(2,1)S(1)} %get-tuple-element.66), channel_id=1, source_target_pairs={{0,1},{1,0},{2,3},{3,2},{4,5},{5,4},{6,7},{7,6},{8,9},{9,8},{10,11... | collective-permute-start | bytes 61448 | tf_op jit(solution)/shard_map/ppermute | solution.py:650
  49.6 3.3 %inner_two.1.part_ref = f32[5,64,1536]{2,1,0:T(8,128)S(1)} custom-call(bf16[5,64,1536]{2,1,0:T(8,128)(2,1)S(1)} %get-tuple-element.61.v_ref, f32[5,16,128]{2,1,0:T(8,128)S(1)} %bitcast.27, f32[5,16,128]{2,1,0:T(8,128)S(1)} %bitcast.29, f32[5,16,128]{2,1,0:T(8,128)S(1)} %add_add_fusion.plane_ref, ...), custom_call_target="tpu_custom_call" | custom-call | flops 300000000 | bytes 9000000 | tf_op jit(solution)/shard_map/inner_two/pallas_call | solution.py:651
  52.9 0.8 %collective-permute-done.15.near_ref = bf16[5,16,768]{2,1,0:T(8,128)(2,1)S(1)} collective-permute-done((bf16[5,16,768]{2,1,0:T(8,128)(2,1)S(1)}, bf16[5,16,768]{2,1,0:T(8,128)(2,1)S(1)}, u32[]{:S(2)}, u32[]{:S(2)}) %collective-permute-start.15) | collective-permute-done | bytes 122912 | tf_op jit(solution)/shard_map/ppermute | solution.py:649
  53.7 3.8 %outer_two.1 = bf16[5,64,1536]{2,1,0:T(8,128)(2,1)} custom-call(bf16[5,64,1536]{2,1,0:T(8,128)(2,1)S(1)} %get-tuple-element.61.v_ref, bf16[5,64,1536]{2,1,0:T(8,128)(2,1)S(1)} %get-tuple-element.62.trace_ref, bf16[5,64,1536]{2,1,0:T(8,128)(2,1)S(1)} %copy-done, f32[5,64,1536]{2,1,0:T(8,128)S(1)} %inner_two.1.part_ref, ...), custom_call_target="tpu_custom_call" | custom-call | flops 400000000 | bytes 12000000 | tf_op jit(solution)/shard_map/outer_two/pallas_call | solution.py:661
  (60 shorter events, 4.3 us)
Async XLA Ops:
  0.0 32.6 %copy-start = (bf16[5,64,1536]{2,1,0:T(8,128)(2,1)S(1)}, bf16[5,64,1536]{2,1,0:T(8,128)(2,1)}, u32[]{:S(2)}) copy-start(bf16[5,64,1536]{2,1,0:T(8,128)(2,1)} %base_ref.1) | copy-start | bytes 2949124
  0.0 20.3 %copy-start.6 = (bf16[64,96]{1,0:T(8,128)(2,1)S(1)}, bf16[64,96]{1,0:T(8,128)(2,1)}, u32[]{:S(2)}) copy-start(bf16[64,96]{1,0:T(8,128)(2,1)} %param.16) | copy-start | bytes 36868
  0.0 26.4 %copy-start.9 = (s32[1536]{0:T(1024)S(1)}, s32[1536]{0:T(1024)}, u32[]{:S(2)}) copy-start(s32[1536]{0:T(1024)} %param.19) | copy-start | bytes 18436
  0.0 26.4 %copy-start.7 = (bf16[64,64]{1,0:T(8,128)(2,1)S(1)}, bf16[64,64]{1,0:T(8,128)(2,1)}, u32[]{:S(2)}) copy-start(bf16[64,64]{1,0:T(8,128)(2,1)} %param.18) | copy-start | bytes 24580
  0.0 46.4 %copy-start.5 = (f32[1,1,5,2048]{3,1,2,0:T(1,128)S(1)}, f32[1,1,5,2048]{3,1,2,0:T(1,128)}, u32[]{:S(2)}) copy-start(f32[1,1,5,2048]{3,1,2,0:T(1,128)} %param.24) | copy-start | bytes 122884
  5.3 41.2 %copy-start.2 = (bf16[5,64,1536]{2,1,0:T(8,128)(2,1)S(1)}, bf16[5,64,1536]{2,1,0:T(8,128)(2,1)}, u32[]{:S(2)}) copy-start(bf16[5,64,1536]{2,1,0:T(8,128)(2,1)} %get-tuple-element.36.trace_ref) | copy-start | bytes 2949124
  5.3 41.2 %copy-start.4 = (f32[1,1,5,2048]{3,1,2,0:T(1,128)S(1)}, f32[1,1,5,2048]{3,1,2,0:T(1,128)}, u32[]{:S(2)}) copy-start(f32[1,1,5,2048]{3,1,2,0:T(1,128)} %param.23) | copy-start | bytes 122884
  5.3 15.3 %collective-permute-start.2 = (f32[5,16,128]{2,1,0:T(8,128)}, f32[5,16,128]{2,1,0:T(8,128)S(1)}, u32[]{:S(2)}, u32[]{:S(2)}) collective-permute-start(f32[5,16,128]{2,1,0:T(8,128)} %get-tuple-element.37), channel_id=1, source_target_pairs={{16,0},{20,4},{48,32},{52,36},{80,64},{84,68},{112,96},{116,100},{... | collective-permute-start | bytes 122888 | tf_op jit(solution)/shard_map/ppermute | solution.py:553
  6.7 13.9 %collective-permute-start.1 = (f32[5,16,128]{2,1,0:T(8,128)}, f32[5,16,128]{2,1,0:T(8,128)S(1)}, u32[]{:S(2)}, u32[]{:S(2)}) collective-permute-start(f32[5,16,128]{2,1,0:T(8,128)} %get-tuple-element.37), channel_id=1, source_target_pairs={{24,0},{28,4},{56,32},{60,36},{88,64},{92,68},{120,96},{124,100},{... | collective-permute-start | bytes 122888 | tf_op jit(solution)/shard_map/ppermute | solution.py:553
  8.0 12.6 %collective-permute-start = (f32[5,16,128]{2,1,0:T(8,128)}, f32[5,16,128]{2,1,0:T(8,128)S(1)}, u32[]{:S(2)}, u32[]{:S(2)}) collective-permute-start(f32[5,16,128]{2,1,0:T(8,128)} %get-tuple-element.37), channel_id=1, source_target_pairs={{8,0},{12,4},{40,32},{44,36},{72,64},{76,68},{104,96},{108,100},{1... | collective-permute-start | bytes 122888 | tf_op jit(solution)/shard_map/ppermute | solution.py:553
  9.3 17.2 %collective-permute-start.7 = (bf16[5,16,128]{2,1,0:T(8,128)(2,1)}, bf16[5,16,128]{2,1,0:T(8,128)(2,1)S(1)}, u32[]{:S(2)}, u32[]{:S(2)}) collective-permute-start(bf16[5,16,128]{2,1,0:T(8,128)(2,1)} %get-tuple-element.44), channel_id=1, source_target_pairs={{4,8},{8,4},{12,16},{16,12},{20,24},{24,20},{28,32},{32,28},{36,40... | collective-permute-start | bytes 61448 | tf_op jit(solution)/shard_map/ppermute | solution.py:603
  14.1 12.5 %collective-permute-start.6 = (bf16[5,16,768]{2,1,0:T(8,128)(2,1)}, bf16[5,16,768]{2,1,0:T(8,128)(2,1)S(1)}, u32[]{:S(2)}, u32[]{:S(2)}) collective-permute-start(bf16[5,16,768]{2,1,0:T(8,128)(2,1)} %get-tuple-element.43), channel_id=1, source_target_pairs={{0,2},{2,0},{1,3},{3,1},{4,6},{6,4},{5,7},{7,5},{8,10},{10,8},{9,1... | collective-permute-start | bytes 368648 | tf_op jit(solution)/shard_map/ppermute | solution.py:602
  21.4 5.8 %collective-permute-start.5 = (f32[5,16,128]{2,1,0:T(8,128)S(1)}, f32[5,16,128]{2,1,0:T(8,128)S(1)}, u32[]{:S(2)}, u32[]{:S(2)}) collective-permute-start(f32[5,16,128]{2,1,0:T(8,128)S(1)} %add_add_fusion.2), channel_id=1, source_target_pairs={{36,0},{100,64},{164,128},{228,192},{37,1},{101,65},{165,129},{229... | collective-permute-start | bytes 122888 | tf_op jit(solution)/shard_map/ppermute | solution.py:553
  22.1 5.2 %collective-permute-start.4 = (f32[5,16,128]{2,1,0:T(8,128)S(1)}, f32[5,16,128]{2,1,0:T(8,128)S(1)}, u32[]{:S(2)}, u32[]{:S(2)}) collective-permute-start(f32[5,16,128]{2,1,0:T(8,128)S(1)} %add_add_fusion.2), channel_id=1, source_target_pairs={{32,0},{96,64},{160,128},{224,192},{33,1},{97,65},{161,129},{225,1... | collective-permute-start | bytes 122888 | tf_op jit(solution)/shard_map/ppermute | solution.py:553
  25.6 1.7 %collective-permute-start.3 = (f32[5,16,128]{2,1,0:T(8,128)S(1)}, f32[5,16,128]{2,1,0:T(8,128)S(1)}, u32[]{:S(2)}, u32[]{:S(2)}) collective-permute-start(f32[5,16,128]{2,1,0:T(8,128)S(1)} %add_add_fusion.2), channel_id=1, source_target_pairs={{4,0},{68,64},{132,128},{196,192},{5,1},{69,65},{133,129},{197,193... | collective-permute-start | bytes 122888 | tf_op jit(solution)/shard_map/ppermute | solution.py:553
  26.5 4.1 %collective-permute-start.8 = (bf16[5,16,128]{2,1,0:T(8,128)(2,1)}, bf16[5,16,128]{2,1,0:T(8,128)(2,1)S(1)}, u32[]{:S(2)}, u32[]{:S(2)}) collective-permute-start(bf16[5,16,128]{2,1,0:T(8,128)(2,1)} %get-tuple-element.46), channel_id=1, source_target_pairs={{0,1},{1,0},{2,3},{3,2},{4,5},{5,4},{6,7},{7,6},{8,9},{9,8},{10,11... | collective-permute-start | bytes 61448 | tf_op jit(solution)/shard_map/ppermute | solution.py:607
  27.2 3.4 %collective-permute-start.9 = (bf16[5,16,128]{2,1,0:T(8,128)(2,1)}, bf16[5,16,128]{2,1,0:T(8,128)(2,1)S(1)}, u32[]{:S(2)}, u32[]{:S(2)}) collective-permute-start(bf16[5,16,128]{2,1,0:T(8,128)(2,1)} %get-tuple-element.47), channel_id=1, source_target_pairs={{0,4},{4,0},{8,12},{12,8},{16,20},{20,16},{24,28},{28,24},{32,36},... | collective-permute-start | bytes 61448 | tf_op jit(solution)/shard_map/ppermute | solution.py:608
  30.6 10.6 %collective-permute-start.12 = (f32[5,16,128]{2,1,0:T(8,128)S(1)}, f32[5,16,128]{2,1,0:T(8,128)S(1)}, u32[]{:S(2)}, u32[]{:S(2)}) collective-permute-start(f32[5,16,128]{2,1,0:T(8,128)S(1)} %add_add_fusion.1), channel_id=1, source_target_pairs={{128,0},{129,1},{130,2},{131,3}} | collective-permute-start | bytes 122888 | tf_op jit(solution)/shard_map/ppermute | solution.py:553
  31.3 9.9 %collective-permute-start.11 = (f32[5,16,128]{2,1,0:T(8,128)S(1)}, f32[5,16,128]{2,1,0:T(8,128)S(1)}, u32[]{:S(2)}, u32[]{:S(2)}) collective-permute-start(f32[5,16,128]{2,1,0:T(8,128)S(1)} %add_add_fusion.1), channel_id=1, source_target_pairs={{192,0},{193,1},{194,2},{195,3}} | collective-permute-start | bytes 122888 | tf_op jit(solution)/shard_map/ppermute | solution.py:553
  32.0 9.2 %collective-permute-start.10 = (f32[5,16,128]{2,1,0:T(8,128)S(1)}, f32[5,16,128]{2,1,0:T(8,128)S(1)}, u32[]{:S(2)}, u32[]{:S(2)}) collective-permute-start(f32[5,16,128]{2,1,0:T(8,128)S(1)} %add_add_fusion.1), channel_id=1, source_target_pairs={{64,0},{65,1},{66,2},{67,3}} | collective-permute-start | bytes 122888 | tf_op jit(solution)/shard_map/ppermute | solution.py:553
  39.2 2.1 %collective-permute-start.13 = (bf16[5,16,128]{2,1,0:T(8,128)(2,1)S(1)}, bf16[5,16,128]{2,1,0:T(8,128)(2,1)S(1)}, u32[]{:S(2)}, u32[]{:S(2)}) collective-permute-start(bf16[5,16,128]{2,1,0:T(8,128)(2,1)S(1)} %get-tuple-element.58), channel_id=1, source_target_pairs={{0,4},{4,0},{8,12},{12,8},{16,20},{20,16},{24,28},{28,24},{32,36},... | collective-permute-start | bytes 61448 | tf_op jit(solution)/shard_map/ppermute | solution.py:624
  39.3 7.2 %collective-permute-start.14 = (bf16[5,16,128]{2,1,0:T(8,128)(2,1)S(1)}, bf16[5,16,128]{2,1,0:T(8,128)(2,1)S(1)}, u32[]{:S(2)}, u32[]{:S(2)}) collective-permute-start(bf16[5,16,128]{2,1,0:T(8,128)(2,1)S(1)} %get-tuple-element.59), channel_id=1, source_target_pairs={{4,8},{8,4},{12,16},{16,12},{20,24},{24,20},{28,32},{32,28},{36,40... | collective-permute-start | bytes 61448 | tf_op jit(solution)/shard_map/ppermute | solution.py:625
  47.2 6.5 %collective-permute-start.15 = (bf16[5,16,768]{2,1,0:T(8,128)(2,1)S(1)}, bf16[5,16,768]{2,1,0:T(8,128)(2,1)S(1)}, u32[]{:S(2)}, u32[]{:S(2)}) collective-permute-start(bf16[5,16,768]{2,1,0:T(8,128)(2,1)S(1)} %get-tuple-element.65), channel_id=1, source_target_pairs={{0,2},{2,0},{1,3},{3,1},{4,6},{6,4},{5,7},{7,5},{8,10},{10,8},{9,1... | collective-permute-start | bytes 368648 | tf_op jit(solution)/shard_map/ppermute | solution.py:649
  47.9 4.9 %collective-permute-start.16 = (bf16[5,16,128]{2,1,0:T(8,128)(2,1)S(1)}, bf16[5,16,128]{2,1,0:T(8,128)(2,1)S(1)}, u32[]{:S(2)}, u32[]{:S(2)}) collective-permute-start(bf16[5,16,128]{2,1,0:T(8,128)(2,1)S(1)} %get-tuple-element.66), channel_id=1, source_target_pairs={{0,1},{1,0},{2,3},{3,2},{4,5},{5,4},{6,7},{7,6},{8,9},{9,8},{10,11... | collective-permute-start | bytes 61448 | tf_op jit(solution)/shard_map/ppermute | solution.py:650
  (4 other events, 48.0 us)

commit v5 on v4

--- a/solution.py
+++ b/solution.py
@@ -14,7 +14,7 @@
 SPAN_CELLS = 32
 PAIR = 2 * CELLS
 MIXED = 352
-INNER = 224
+INNER = 192
 TIME_STEP = 0.4
 f32 = jnp.float32
 bf16 = jnp.bfloat16
@@ -118,13 +118,13 @@
 
 
 def prepare_kernel(
-    rows_hbm, seeds_hbm, shape_hbm, v_hbm, plane_ref, trace_ref, core_ref, chip_ref, pitch_ref,
+    rows_hbm, seeds_hbm, shape_hbm, v_hbm, plane_ref, core_ref, chip_ref, pitch_ref,
     span_ref, rows_ref, seeds_ref, shape_ref, v_ref, span_held, sems, *, normalizer,
 ):
     copies = [
         pltpu.make_async_copy(source, target, sems.at[i])
         for i, (source, target) in enumerate([
-            (rows_hbm, rows_ref), (seeds_hbm, seeds_ref), (shape_hbm, shape_ref), (v_hbm, v_ref)
+            (rows_hbm, rows_ref), (seeds_hbm, seeds_ref), (shape_hbm, shape_ref), (v_hbm, v_ref),
         ])
     ]
     for copy in copies:
@@ -139,10 +139,10 @@
     copies[3].wait()
     for pair in range(EX // 2):
         at = slice(pair * PAIR, (pair + 1) * PAIR)
-        traces = [dot(pick, v_ref[f, :, at]) for f in range(FIELDS)]
         for f in range(FIELDS):
-            trace_ref[f, :, at] = traces[f].astype(bf16)
-            pack_field(f, traces[f], pair, first_span, lane, pitch_ref, span_held)
+            pack_field(
+                f, dot(pick, v_ref[f, :, at]), pair, first_span, lane, pitch_ref, span_held
+            )
     span_ref[...] = span_held[...].astype(bf16)
     store_stream(
         v_ref[:, 48:64, (EX - 1) * CELLS :], v_ref[:, 0:16, 0:CELLS], core_ref, chip_ref
@@ -306,6 +306,18 @@
     return trial
 
 
+def with_traces(filter_matrix, pick):
+    return jnp.concatenate([filter_matrix, dot(pick, filter_matrix).astype(bf16)], axis=0)
+
+
+def mix_traces(read, pick, own):
+    def run():
+        for f in range(FIELDS):
+            own[f] = dot(pick, read(f, 0, 64)).astype(bf16)
+
+    return [run]
+
+
 def place(pair):
     return slice(pair * PAIR, (pair + 1) * PAIR)
 
@@ -335,19 +347,20 @@
 
 
 def phase_one_kernel(
-    v_ref, trace_ref, from_core_ref, from_chip_ref, near_ref, far_ref, pin_ref, coefs, weights_ref,
-    smooth_ref, out_ref, out_trace_ref, core_ref, chip_ref, pitch_ref, span_ref, mixed, span_held,
+    v_ref, from_core_ref, from_chip_ref, near_ref, far_ref, pin_ref, coefs, weights_ref, filter_ref,
+    out_ref, out_trace_ref, core_ref, chip_ref, pitch_ref, span_ref, mixed, own, span_held,
 ):
     first_span = lax.axis_index("span") == 0
     lane = lanes()
-    weights, smooth = weights_ref[...], smooth_ref[...]
+    pick = trace_selector()
+    weights, smooth = weights_ref[...], with_traces(filter_ref[...], pick)
     span_held[...] = jnp.zeros_like(span_held)
     below, above = from_below(from_core_ref, from_chip_ref), from_above(from_core_ref, from_chip_ref)
     vector, matrix = [], []
 
     def add(pair):
         at = place(pair)
-        rows = mixed.at[pair % 2]
+        rows, held = mixed.at[pair % 2], own.at[pair % 2]
 
         def read(f, r0, r1):
             return v_ref[f, r0:r1, at]
@@ -359,7 +372,8 @@
             pack_field(f, trace, pair, first_span, lane, pitch_ref, span_held)
 
         vector.append(
-            mix_fluxes(read, coefs, rows)
+            mix_traces(read, pick, held)
+            + mix_fluxes(read, coefs, rows)
             + mix_stream(
                 read,
                 lower_pair(v_ref, below, pair),
@@ -367,7 +381,7 @@
                 coefs, rows, 192,
             )
             + mix_sides(
-                lambda f, r0, r1: trace_ref[f, r0:r1, at].astype(f32),
+                lambda f, r0, r1: held[f, r0:r1].astype(f32),
                 lambda f: near_ref[f, :, pair * CELLS : (pair + 1) * CELLS].astype(f32),
                 lambda f: far_ref[f].astype(f32),
                 [2 * pair, 2 * pair + 1], coefs, rows, 224, first_span, lane,
@@ -387,34 +401,18 @@
     )
 
 
-def inner_two_kernel(
-    v_ref, mean_ref, amp_ref, plane_ref, from_core_ref, from_chip_ref, coefs, weights_ref, part_ref,
-    mixed,
-):
-    first_rans = lax.axis_index("rans") == 0
+def inner_two_kernel(v_ref, coefs, weights_ref, part_ref, mixed):
     weights = weights_ref[...]
-    below, above = from_below(from_core_ref, from_chip_ref), from_above(from_core_ref, from_chip_ref)
     vector, matrix = [], []
-
-    def edge(f):
-        return jnp.where(first_rans, inflow_of(mean_ref, amp_ref, plane_ref)(f), below(f))
 
     def add(pair):
         at = place(pair)
         rows = mixed.at[pair % 2]
 
-        def read(f, r0, r1):
-            return v_ref[f, r0:r1, at]
-
         def store(f, value):
             part_ref[f, :, at] = value
 
-        vector.append(
-            mix_fluxes(read, coefs, rows)
-            + mix_stream(
-                read, lower_pair(v_ref, edge, pair), upper_pair(v_ref, above, pair), coefs, rows, 192,
-            )
-        )
+        vector.append(mix_fluxes(lambda f, r0, r1: v_ref[f, r0:r1, at], coefs, rows))
         matrix.append(staggered([lambda f, _: dot(weights, rows[f]), store]))
 
     for pair in range(EX // 2):
@@ -423,13 +421,18 @@
 
 
 def outer_two_kernel(
-    v_ref, trace_ref, base_ref, part_ref, near_ref, far_ref, pin_ref, coefs, weights_ref,
-    smooth_ref, out_ref, mixed,
+    v_ref, trace_ref, base_ref, part_ref, mean_ref, amp_ref, plane_ref, from_core_ref, from_chip_ref,
+    near_ref, far_ref, pin_ref, coefs, weights_ref, smooth_ref, out_ref, mixed,
 ):
     first_span = lax.axis_index("span") == 0
+    first_rans = lax.axis_index("rans") == 0
     lane = lanes()
     weights, smooth = weights_ref[...], smooth_ref[...]
+    below, above = from_below(from_core_ref, from_chip_ref), from_above(from_core_ref, from_chip_ref)
     vector, matrix = [], []
+
+    def edge(f):
+        return jnp.where(first_rans, inflow_of(mean_ref, amp_ref, plane_ref)(f), below(f))
 
     def add(pair):
         at = place(pair)
@@ -442,13 +445,16 @@
             out_ref[f, :, at] = value.astype(bf16)
 
         vector.append(
-            mix_sides(
+            mix_stream(
+                read, lower_pair(v_ref, edge, pair), upper_pair(v_ref, above, pair), coefs, rows, 0
+            )
+            + mix_sides(
                 lambda f, r0, r1: trace_ref[f, r0:r1, at].astype(f32),
                 lambda f: near_ref[f, :, pair * CELLS : (pair + 1) * CELLS].astype(f32),
                 lambda f: far_ref[f].astype(f32),
-                [2 * pair, 2 * pair + 1], coefs, rows, 0, first_span, lane,
+                [2 * pair, 2 * pair + 1], coefs, rows, 32, first_span, lane,
             )
-            + mix_wall(read, lambda: pin_ref[:, at].astype(f32), rows, 64)
+            + mix_wall(read, lambda: pin_ref[:, at].astype(f32), rows, 96)
         )
         matrix.append(
             staggered([
@@ -468,9 +474,9 @@
 
 
 def inflow_kernel(
-    held_ref, held_trace_ref, held_pitch_ref, held_span_ref, v_ref, trace_ref, mean_ref, amp_ref,
-    plane_ref, near_ref, far_ref, pin_ref, coefs, weights_ref, smooth_ref, out_ref, out_trace_ref,
-    pitch_ref, span_ref, mixed,
+    held_ref, held_trace_ref, held_pitch_ref, held_span_ref, v_ref, mean_ref, amp_ref,
+    plane_ref, near_ref, far_ref, pin_ref, coefs, weights_ref, filter_ref, out_ref, out_trace_ref,
+    pitch_ref, span_ref, mixed, own,
 ):
     first_span = lax.axis_index("span") == 0
     first_rans = lax.axis_index("rans") == 0
@@ -478,7 +484,8 @@
 
     @pl.when(first_rans)
     def _():
-        weights, smooth = weights_ref[...], smooth_ref[...]
+        pick = trace_selector()
+        weights, smooth = weights_ref[...], with_traces(filter_ref[...], pick)
 
         def read(f, r0, r1):
             return v_ref[f, r0:r1, 0:CELLS]
@@ -496,14 +503,15 @@
             ).astype(bf16)
 
         vector = (
-            mix_stream(
+            mix_traces(read, pick, own)
+            + mix_stream(
                 read,
                 inflow_of(mean_ref, amp_ref, plane_ref),
                 lambda f: v_ref[f, 0:16, CELLS:PAIR].astype(f32),
                 coefs, mixed, 192,
             )
             + mix_sides(
-                lambda f, r0, r1: trace_ref[f, r0:r1].astype(f32),
+                lambda f, r0, r1: own[f, r0:r1].astype(f32),
                 lambda f: near_ref[f].astype(f32),
                 lambda f: far_ref[f].astype(f32),
                 [0], coefs, mixed, 224, first_span, lane,
@@ -565,11 +573,6 @@
     ).reshape(-1)
     coefs = jnp.concatenate([flux_jacobian.reshape(-1), face_coefs])
     pins = pinched_map.reshape(1, -1)
-    rows = filter_matrix.reshape(4, 4, 4, NODES)
-    smooth = jnp.concatenate(
-        [filter_matrix]
-        + [part.reshape(16, NODES) for part in (rows[:, 0], rows[:, 3], rows[:, :, 0], rows[:, :, 3])]
-    )
     fixed_specs = [VMEM, SMEM, VMEM, VMEM]
     elements = solution.shape[2]
     traces = shape_of(FIELDS, NODES, elements)
@@ -579,13 +582,13 @@
     next_chip = [(a + 1, b + 1) for a, b in same_chip if max(a, b) + 1 < ranks]
 
     span_scratch = pltpu.VMEM((FIELDS, 16, CELLS), f32)
-    plane, trace, core, chip, pitch, span = pl.pallas_call(
+    plane, core, chip, pitch, span = pl.pallas_call(
         functools.partial(
             prepare_kernel, normalizer=float((plane_rows / (eddies * ranks * foot)) ** 0.5)
         ),
-        out_shape=(shape_of(FIELDS, 16, CELLS, dtype=f32), traces) + sends,
+        out_shape=(shape_of(FIELDS, 16, CELLS, dtype=f32),) + sends,
         in_specs=[pl.BlockSpec(memory_space=pltpu.HBM)] * 4,
-        out_specs=(VMEM,) * 6,
+        out_specs=(VMEM,) * 5,
         scratch_shapes=[
             pltpu.VMEM((foot, eddies), jnp.int32),
             pltpu.VMEM((1, eddies), jnp.int32),
@@ -614,17 +617,19 @@
     phase_one, trace_one, core, chip, pitch, span = pl.pallas_call(
         phase_one_kernel,
         out_shape=(traces, traces) + sends,
-        in_specs=[VMEM] * 6 + fixed_specs,
+        in_specs=[VMEM] * 5 + fixed_specs,
         out_specs=(VMEM,) * 6,
-        scratch_shapes=[pltpu.VMEM((2, FIELDS, MIXED, PAIR), bf16), span_scratch],
+        scratch_shapes=[
+            pltpu.VMEM((2, FIELDS, MIXED, PAIR), bf16),
+            pltpu.VMEM((2, FIELDS, NODES, PAIR), bf16),
+            span_scratch,
+        ],
         compiler_params=PARAMS,
         cost_estimate=cost(6),
         name="phase_one",
-    )(solution, trace, from_core, from_chip, near, far, pins, coefs, weights, smooth)
+    )(solution, from_core, from_chip, near, far, pins, coefs, weights, filter_matrix)
     from_core = lax.ppermute(core, "rans", same_chip)
     from_chip = lax.ppermute(chip, "rans", next_chip)
-    plane, from_core, from_chip = lax.optimization_barrier((plane, from_core, from_chip))
-
     mean = mean_inflow.reshape(FIELDS, 16, CELLS)
     amplitude = eddy_amplitude.reshape(FIELDS, 16, CELLS)
     layer = front(FIELDS, NODES, CELLS)
@@ -633,43 +638,46 @@
         inflow_kernel,
         grid=(1,),
         out_shape=(traces, traces, sends[2], sends[3]),
-        in_specs=[layer, layer, face, face, front(FIELDS, NODES, PAIR), layer]
+        in_specs=[layer, layer, face, face, front(FIELDS, NODES, PAIR)]
         + [face] * 5
-        + [front(1, CELLS), SMEM, front(NODES, MIXED), front(2 * NODES, NODES)],
+        + [front(1, CELLS), SMEM, front(NODES, MIXED), front(NODES, NODES)],
         out_specs=(layer, layer, face, face),
-        scratch_shapes=[pltpu.VMEM((FIELDS, MIXED, CELLS), bf16)],
+        scratch_shapes=[
+            pltpu.VMEM((FIELDS, MIXED, CELLS), bf16),
+            pltpu.VMEM((FIELDS, NODES, CELLS), bf16),
+        ],
         input_output_aliases={0: 0, 1: 1, 2: 2, 3: 3},
         compiler_params=PARAMS,
         cost_estimate=cost(1),
         name="inflow_layer",
     )(
-        phase_one, trace_one, pitch, span, solution, trace, mean, amplitude, plane, near, far,
-        pins, coefs, weights, smooth,
+        phase_one, trace_one, pitch, span, solution, mean, amplitude, plane, near, far,
+        pins, coefs, weights, filter_matrix,
     )
     near = lax.ppermute(pitch, "pitch", swap)
     far = lax.ppermute(span, "span", swap)
     part = pl.pallas_call(
         inner_two_kernel,
         out_shape=shape_of(FIELDS, NODES, elements, dtype=f32),
-        in_specs=[VMEM] * 6 + [SMEM, VMEM],
+        in_specs=[VMEM, SMEM, VMEM],
         out_specs=VMEM,
         scratch_shapes=[pltpu.VMEM((2, FIELDS, INNER, PAIR), bf16)],
         compiler_params=PARAMS,
         cost_estimate=cost(3),
         name="inner_two",
-    )(phase_one, mean, amplitude, plane, from_core, from_chip, coefs, weights[:, :INNER])
+    )(phase_one, coefs, weights[:, :INNER])
     return pl.pallas_call(
         outer_two_kernel,
         out_shape=traces,
-        in_specs=[VMEM] * 7 + fixed_specs[1:],
+        in_specs=[VMEM] * 12 + fixed_specs[1:],
         out_specs=VMEM,
         scratch_shapes=[pltpu.VMEM((2, FIELDS, MIXED - INNER, PAIR), bf16)],
         compiler_params=PARAMS,
         cost_estimate=cost(4),
         name="outer_two",
     )(
-        phase_one, trace_one, solution, part, near, far, pins, coefs, weights[:, INNER:],
-        filter_matrix,
+        phase_one, trace_one, solution, part, mean, amplitude, plane, from_core, from_chip, near, far,
+        pins, coefs, weights[:, INNER:], filter_matrix,
     )
 
 

time: 58 us -> 53 us (0.914)
  the two profiles are of different devices: /device:TPU:224 before, /device:TPU:1 now
where the time goes in v5:
time: 53 us; the launch traced here: 52.5 us
  starting transfers between devices  28.6 us (54%)
  Pallas kernels  18.2 us (34%)
  waiting for transfers between devices  2.54 us (5%)
  local copies, waits for them, and re-layouts  1.79 us (3%)
  other arithmetic  1.14 us (2%)
    ppermute x2, starting transfers between devices, body(): from_chip = lax.ppermute(chip, 'rans', next_chip)  9.27 us
    ppermute x9, starting transfers between devices, gather_sum(): lax.ppermute(value, 'rans', [(r + o, r) for r in roots])  8.61 us
    ppermute x2, starting transfers between devices, body(): from_core = lax.ppermute(core, 'rans', same_chip)  5.93 us
    pallas_call x1, Pallas kernels, body(): pl.pallas_call(phase_one_kernel, out_shape=(traces, traces) + sends, in_s...  5.43 us
    pallas_call x1, Pallas kernels, body(): pl.pallas_call(functools.partial(prepare_kernel, normalizer=float((plane_...  4.95 us
    pallas_call x1, Pallas kernels, body(): pl.pallas_call(outer_two_kernel, out_shape=traces, in_specs=[VMEM] * 12 +...  4.3 us
    ppermute x2, starting transfers between devices, body(): near = lax.ppermute(pitch, 'pitch', swap)  3.14 us
    pallas_call x1, Pallas kernels, body(): pl.pallas_call(inner_two_kernel, out_shape=shape_of(FIELDS, NODES, elemen...  2.8 us
  transfers between devices with their start and end apart: 17, of which 2 were waited for; matrix products, arithmetic and copies ran while one was open for 5% of the time, Pallas kernels for 16%

profile of v5, /device:TPU:1, one launch (start us, length us, event | category | flops | bytes accessed | tf_op | source)
XLA Modules:
  0.0 52.5 jit_solution(5744323835725971873)
XLA Ops:
  0.0 5.0 %prepare.1 = (f32[5,16,128]{2,1,0:T(8,128)}, bf16[5,16,128]{2,1,0:T(8,128)(2,1)}, bf16[5,16,128]{2,1,0:T(8,128)(2,1)}, bf16[5,16,768]{2,1,0:T(8,128)(2,1)}, bf16[5,16,128]{2,1,0:T(8,128)(2,1)}) custom-call(s32[64,256]{1,0:T(8,128)} %bitcast.19, s32[1,256]{1,0:T(1,128)} %bitcast.21, f32[64,256]{1,0:T(8,128)} %bitcast.20, bf16[5,64,1536]{2,1,0:T(8,128)(2,1)} %base_ref.1), custom_call_target="tpu_custom_call" | custom-call | flops 500000000 | bytes 15000000 | tf_op jit(solution)/shard_map/prepare/pallas_call | solution.py:585
  5.0 1.4 %collective-permute-start.2 = (f32[5,16,128]{2,1,0:T(8,128)}, f32[5,16,128]{2,1,0:T(8,128)S(1)}, u32[]{:S(2)}, u32[]{:S(2)}) collective-permute-start(f32[5,16,128]{2,1,0:T(8,128)} %get-tuple-element.32), channel_id=1, source_target_pairs={{16,0},{20,4},{48,32},{52,36},{80,64},{84,68},{112,96},{116,100},{... | collective-permute-start | bytes 122888 | tf_op jit(solution)/shard_map/ppermute | solution.py:561
  6.5 1.3 %collective-permute-start.1 = (f32[5,16,128]{2,1,0:T(8,128)}, f32[5,16,128]{2,1,0:T(8,128)S(1)}, u32[]{:S(2)}, u32[]{:S(2)}) collective-permute-start(f32[5,16,128]{2,1,0:T(8,128)} %get-tuple-element.32), channel_id=1, source_target_pairs={{24,0},{28,4},{56,32},{60,36},{88,64},{92,68},{120,96},{124,100},{... | collective-permute-start | bytes 122888 | tf_op jit(solution)/shard_map/ppermute | solution.py:561
  7.8 1.3 %collective-permute-start = (f32[5,16,128]{2,1,0:T(8,128)}, f32[5,16,128]{2,1,0:T(8,128)S(1)}, u32[]{:S(2)}, u32[]{:S(2)}) collective-permute-start(f32[5,16,128]{2,1,0:T(8,128)} %get-tuple-element.32), channel_id=1, source_target_pairs={{8,0},{12,4},{40,32},{44,36},{72,64},{76,68},{104,96},{108,100},{1... | collective-permute-start | bytes 122888 | tf_op jit(solution)/shard_map/ppermute | solution.py:561
  9.1 7.4 %collective-permute-start.7 = (bf16[5,16,128]{2,1,0:T(8,128)(2,1)}, bf16[5,16,128]{2,1,0:T(8,128)(2,1)S(1)}, u32[]{:S(2)}, u32[]{:S(2)}) collective-permute-start(bf16[5,16,128]{2,1,0:T(8,128)(2,1)} %get-tuple-element.39), channel_id=1, source_target_pairs={{4,8},{8,4},{12,16},{16,12},{20,24},{24,20},{28,32},{32,28},{36,40... | collective-permute-start | bytes 61448 | tf_op jit(solution)/shard_map/ppermute | solution.py:606
  16.4 1.1 %collective-permute-start.6 = (bf16[5,16,768]{2,1,0:T(8,128)(2,1)}, bf16[5,16,768]{2,1,0:T(8,128)(2,1)S(1)}, u32[]{:S(2)}, u32[]{:S(2)}) collective-permute-start(bf16[5,16,768]{2,1,0:T(8,128)(2,1)} %get-tuple-element.38), channel_id=1, source_target_pairs={{0,2},{2,0},{1,3},{3,1},{4,6},{6,4},{5,7},{7,5},{8,10},{10,8},{9,1... | collective-permute-start | bytes 368648 | tf_op jit(solution)/shard_map/ppermute | solution.py:605
  17.5 0.7 %copy.20 = f32[3,5,5]{2,1,0:T(8,128)S(1)} copy(f32[3,5,5]{2,0,1:T(4,128)} %param.15) | data formatting | bytes 600 | tf_op args[2]
  18.2 0.8 %slice_bitcast_fusion = (bf16[64,64]{1,0:T(8,128)(2,1)S(1)}, bf16[64,64]{1,0:T(8,128)(2,1)S(1)}, bf16[64,64]{1,0:T(8,128)(2,1)S(1)}) fusion(bf16[3,64,64]{2,1,0:T(8,128)(2,1)} %param.14), kind=kLoop, calls=%fused_computation.6 | loop fusion | bytes 49152 | tf_op jit(solution)/shard_map/squeeze | solution.py:567
  19.4 0.8 %add_add_fusion.2 = f32[5,16,128]{2,1,0:T(8,128)S(1)} fusion(f32[5,16,128]{2,1,0:T(8,128)S(1)} %collective-permute-done.2, f32[5,16,128]{2,1,0:T(8,128)S(1)} %collective-permute-done.1, f32[5,16,128]{2,1,0:T(8,128)} %get-tuple-element.32, f32[5,16,128]{2,1,0:T(8,128)S(1)} %collective-permute-done), kind=kLoop, calls=%fused_computation.2 | loop fusion | flops 30720 | bytes 204800 | tf_op jit(solution)/shard_map/add | solution.py:563
  20.2 0.7 %collective-permute-start.5 = (f32[5,16,128]{2,1,0:T(8,128)S(1)}, f32[5,16,128]{2,1,0:T(8,128)S(1)}, u32[]{:S(2)}, u32[]{:S(2)}) collective-permute-start(f32[5,16,128]{2,1,0:T(8,128)S(1)} %add_add_fusion.2), channel_id=1, source_target_pairs={{36,0},{100,64},{164,128},{228,192},{37,1},{101,65},{165,129},{229... | collective-permute-start | bytes 122888 | tf_op jit(solution)/shard_map/ppermute | solution.py:561
  20.9 0.7 %collective-permute-start.4 = (f32[5,16,128]{2,1,0:T(8,128)S(1)}, f32[5,16,128]{2,1,0:T(8,128)S(1)}, u32[]{:S(2)}, u32[]{:S(2)}) collective-permute-start(f32[5,16,128]{2,1,0:T(8,128)S(1)} %add_add_fusion.2), channel_id=1, source_target_pairs={{32,0},{96,64},{160,128},{224,192},{33,1},{97,65},{161,129},{225,1... | collective-permute-start | bytes 122888 | tf_op jit(solution)/shard_map/ppermute | solution.py:561
  21.5 1.3 %collective-permute-start.3 = (f32[5,16,128]{2,1,0:T(8,128)S(1)}, f32[5,16,128]{2,1,0:T(8,128)S(1)}, u32[]{:S(2)}, u32[]{:S(2)}) collective-permute-start(f32[5,16,128]{2,1,0:T(8,128)S(1)} %add_add_fusion.2), channel_id=1, source_target_pairs={{4,0},{68,64},{132,128},{196,192},{5,1},{69,65},{133,129},{197,193... | collective-permute-start | bytes 122888 | tf_op jit(solution)/shard_map/ppermute | solution.py:561
  23.7 2.3 %collective-permute-done.8.far_ref = bf16[5,16,128]{2,1,0:T(8,128)(2,1)S(1)} collective-permute-done((bf16[5,16,128]{2,1,0:T(8,128)(2,1)}, bf16[5,16,128]{2,1,0:T(8,128)(2,1)S(1)}, u32[]{:S(2)}, u32[]{:S(2)}) %collective-permute-start.8) | collective-permute-done | bytes 20512 | tf_op jit(solution)/shard_map/ppermute | solution.py:610
  26.0 0.7 %collective-permute-start.12 = (f32[5,16,128]{2,1,0:T(8,128)S(1)}, f32[5,16,128]{2,1,0:T(8,128)S(1)}, u32[]{:S(2)}, u32[]{:S(2)}) collective-permute-start(f32[5,16,128]{2,1,0:T(8,128)S(1)} %add_add_fusion.1), channel_id=1, source_target_pairs={{128,0},{129,1},{130,2},{131,3}} | collective-permute-start | bytes 122888 | tf_op jit(solution)/shard_map/ppermute | solution.py:561
  26.6 0.7 %collective-permute-start.11 = (f32[5,16,128]{2,1,0:T(8,128)S(1)}, f32[5,16,128]{2,1,0:T(8,128)S(1)}, u32[]{:S(2)}, u32[]{:S(2)}) collective-permute-start(f32[5,16,128]{2,1,0:T(8,128)S(1)} %add_add_fusion.1), channel_id=1, source_target_pairs={{192,0},{193,1},{194,2},{195,3}} | collective-permute-start | bytes 122888 | tf_op jit(solution)/shard_map/ppermute | solution.py:561
  27.3 0.7 %collective-permute-start.10 = (f32[5,16,128]{2,1,0:T(8,128)S(1)}, f32[5,16,128]{2,1,0:T(8,128)S(1)}, u32[]{:S(2)}, u32[]{:S(2)}) collective-permute-start(f32[5,16,128]{2,1,0:T(8,128)S(1)} %add_add_fusion.1), channel_id=1, source_target_pairs={{64,0},{65,1},{66,2},{67,3}} | collective-permute-start | bytes 122888 | tf_op jit(solution)/shard_map/ppermute | solution.py:561
  28.0 5.4 %phase_one.1 = (bf16[5,64,1536]{2,1,0:T(8,128)(2,1)S(1)}, bf16[5,64,1536]{2,1,0:T(8,128)(2,1)S(1)}, bf16[5,16,128]{2,1,0:T(8,128)(2,1)S(1)}, bf16[5,16,128]{2,1,...) custom-call(bf16[5,64,1536]{2,1,0:T(8,128)(2,1)S(1)} %copy-done, ...), custom_call_target="tpu_custom_call" | custom-call | flops 600000000 | bytes 18000000 | tf_op jit(solution)/shard_map/phase_one/pallas_call | solution.py:617
  33.5 0.7 %inflow_layer.1 = (bf16[5,64,1536]{2,1,0:T(8,128)(2,1)S(1)}, bf16[5,64,1536]{2,1,0:T(8,128)(2,1)S(1)}, bf16[5,16,768]{2,1,0:T(8,128)(2,1)S(1)}, bf16[5,16,128]{2,1,0:T(8,128)(2,1)S(1)}) custom-call(bf16[5,64,1536]{2,1,0:T(8,128)(2,1)S(1)} %get-tuple-element.48.held_ref, ...), custom_call_target="tpu_custom_call", output_to_operand_aliasing={{0}: (0, {}), {1}: (1, {}), {2}: (2, {}), {3}: (3, {})} | custom-call | flops 100000000 | bytes 3000000 | tf_op jit(solution)/shard_map/inflow_layer/pallas_call | solution.py:637
  34.2 2.0 %collective-permute-start.15 = (bf16[5,16,768]{2,1,0:T(8,128)(2,1)S(1)}, bf16[5,16,768]{2,1,0:T(8,128)(2,1)S(1)}, u32[]{:S(2)}, u32[]{:S(2)}) collective-permute-start(bf16[5,16,768]{2,1,0:T(8,128)(2,1)S(1)} %get-tuple-element.57), channel_id=1, source_target_pairs={{0,2},{2,0},{1,3},{3,1},{4,6},{6,4},{5,7},{7,5},{8,10},{10,8},{9,1... | collective-permute-start | bytes 368648 | tf_op jit(solution)/shard_map/ppermute | solution.py:657
  36.3 5.9 %collective-permute-start.13 = (bf16[5,16,128]{2,1,0:T(8,128)(2,1)S(1)}, bf16[5,16,128]{2,1,0:T(8,128)(2,1)S(1)}, u32[]{:S(2)}, u32[]{:S(2)}) collective-permute-start(bf16[5,16,128]{2,1,0:T(8,128)(2,1)S(1)} %get-tuple-element.55), channel_id=1, source_target_pairs={{0,4},{4,0},{8,12},{12,8},{16,20},{20,16},{24,28},{28,24},{32,36},... | collective-permute-start | bytes 61448 | tf_op jit(solution)/shard_map/ppermute | solution.py:631
  42.2 1.9 %collective-permute-start.14 = (bf16[5,16,128]{2,1,0:T(8,128)(2,1)S(1)}, bf16[5,16,128]{2,1,0:T(8,128)(2,1)S(1)}, u32[]{:S(2)}, u32[]{:S(2)}) collective-permute-start(bf16[5,16,128]{2,1,0:T(8,128)(2,1)S(1)} %get-tuple-element.56), channel_id=1, source_target_pairs={{4,8},{8,4},{12,16},{16,12},{20,24},{24,20},{28,32},{32,28},{36,40... | collective-permute-start | bytes 61448 | tf_op jit(solution)/shard_map/ppermute | solution.py:632
  44.2 1.2 %collective-permute-start.16 = (bf16[5,16,128]{2,1,0:T(8,128)(2,1)S(1)}, bf16[5,16,128]{2,1,0:T(8,128)(2,1)S(1)}, u32[]{:S(2)}, u32[]{:S(2)}) collective-permute-start(bf16[5,16,128]{2,1,0:T(8,128)(2,1)S(1)} %get-tuple-element.58), channel_id=1, source_target_pairs={{0,1},{1,0},{2,3},{3,2},{4,5},{5,4},{6,7},{7,6},{8,9},{9,8},{10,11... | collective-permute-start | bytes 61448 | tf_op jit(solution)/shard_map/ppermute | solution.py:658
  45.4 2.8 %inner_two.1.part_ref = f32[5,64,1536]{2,1,0:T(8,128)S(1)} custom-call(bf16[5,64,1536]{2,1,0:T(8,128)(2,1)S(1)} %get-tuple-element.53.v_ref, f32[225]{0:T(256)S(1)} %pad_maximum_fusion.2.coefs, bf16[64,192]{1,0:T(8,128)(2,1)S(1)} %pad_maximum_fusion.weights_ref), custom_call_target="tpu_custom_call" | custom-call | flops 300000000 | bytes 9000000 | tf_op jit(solution)/shard_map/inner_two/pallas_call | solution.py:659
  48.3 4.3 %outer_two.1 = bf16[5,64,1536]{2,1,0:T(8,128)(2,1)} custom-call(bf16[5,64,1536]{2,1,0:T(8,128)(2,1)S(1)} %get-tuple-element.53.v_ref, bf16[5,64,1536]{2,1,0:T(8,128)(2,1)S(1)} %get-tuple-element.54.trace_ref, bf16[5,64,1536]{2,1,0:T(8,128)(2,1)S(1)} %copy-done, f32[5,64,1536]{2,1,0:T(8,128)S(1)} %inner_two.1.part_ref, f32[5,16,128]{2,1,0:T(8,128)S(1)} %bitcast.16, ...), custom_call_target="tpu_custom_call" | custom-call | flops 400000000 | bytes 12000000 | tf_op jit(solution)/shard_map/outer_two/pallas_call | solution.py:669
  (45 shorter events, 1.3 us)
Async XLA Ops:
  0.0 28.0 %copy-start = (bf16[5,64,1536]{2,1,0:T(8,128)(2,1)S(1)}, bf16[5,64,1536]{2,1,0:T(8,128)(2,1)}, u32[]{:S(2)}) copy-start(bf16[5,64,1536]{2,1,0:T(8,128)(2,1)} %base_ref.1) | copy-start | bytes 2949124
  0.0 19.1 %copy-start.5 = (bf16[64,64]{1,0:T(8,128)(2,1)S(1)}, bf16[64,64]{1,0:T(8,128)(2,1)}, u32[]{:S(2)}) copy-start(bf16[64,64]{1,0:T(8,128)(2,1)} %param.18) | copy-start | bytes 24580
  0.0 19.1 %copy-start.4 = (bf16[64,96]{1,0:T(8,128)(2,1)S(1)}, bf16[64,96]{1,0:T(8,128)(2,1)}, u32[]{:S(2)}) copy-start(bf16[64,96]{1,0:T(8,128)(2,1)} %param.16) | copy-start | bytes 36868
  0.0 22.9 %copy-start.6 = (s32[1536]{0:T(1024)S(1)}, s32[1536]{0:T(1024)}, u32[]{:S(2)}) copy-start(s32[1536]{0:T(1024)} %param.19) | copy-start | bytes 18436
  0.0 28.0 %copy-start.3 = (bf16[64,64]{1,0:T(8,128)(2,1)S(1)}, bf16[64,64]{1,0:T(8,128)(2,1)}, u32[]{:S(2)}) copy-start(bf16[64,64]{1,0:T(8,128)(2,1)} %smooth_ref.1) | copy-start | bytes 24580
  5.0 28.5 %copy-start.1 = (f32[1,1,5,2048]{3,1,2,0:T(1,128)S(1)}, f32[1,1,5,2048]{3,1,2,0:T(1,128)}, u32[]{:S(2)}) copy-start(f32[1,1,5,2048]{3,1,2,0:T(1,128)} %param.23) | copy-start | bytes 122884
  5.0 28.5 %copy-start.2 = (f32[1,1,5,2048]{3,1,2,0:T(1,128)S(1)}, f32[1,1,5,2048]{3,1,2,0:T(1,128)}, u32[]{:S(2)}) copy-start(f32[1,1,5,2048]{3,1,2,0:T(1,128)} %param.24) | copy-start | bytes 122884
  5.0 14.3 %collective-permute-start.2 = (f32[5,16,128]{2,1,0:T(8,128)}, f32[5,16,128]{2,1,0:T(8,128)S(1)}, u32[]{:S(2)}, u32[]{:S(2)}) collective-permute-start(f32[5,16,128]{2,1,0:T(8,128)} %get-tuple-element.32), channel_id=1, source_target_pairs={{16,0},{20,4},{48,32},{52,36},{80,64},{84,68},{112,96},{116,100},{... | collective-permute-start | bytes 122888 | tf_op jit(solution)/shard_map/ppermute | solution.py:561
  6.5 12.9 %collective-permute-start.1 = (f32[5,16,128]{2,1,0:T(8,128)}, f32[5,16,128]{2,1,0:T(8,128)S(1)}, u32[]{:S(2)}, u32[]{:S(2)}) collective-permute-start(f32[5,16,128]{2,1,0:T(8,128)} %get-tuple-element.32), channel_id=1, source_target_pairs={{24,0},{28,4},{56,32},{60,36},{88,64},{92,68},{120,96},{124,100},{... | collective-permute-start | bytes 122888 | tf_op jit(solution)/shard_map/ppermute | solution.py:561
  7.8 11.6 %collective-permute-start = (f32[5,16,128]{2,1,0:T(8,128)}, f32[5,16,128]{2,1,0:T(8,128)S(1)}, u32[]{:S(2)}, u32[]{:S(2)}) collective-permute-start(f32[5,16,128]{2,1,0:T(8,128)} %get-tuple-element.32), channel_id=1, source_target_pairs={{8,0},{12,4},{40,32},{44,36},{72,64},{76,68},{104,96},{108,100},{1... | collective-permute-start | bytes 122888 | tf_op jit(solution)/shard_map/ppermute | solution.py:561
  9.1 14.0 %collective-permute-start.7 = (bf16[5,16,128]{2,1,0:T(8,128)(2,1)}, bf16[5,16,128]{2,1,0:T(8,128)(2,1)S(1)}, u32[]{:S(2)}, u32[]{:S(2)}) collective-permute-start(bf16[5,16,128]{2,1,0:T(8,128)(2,1)} %get-tuple-element.39), channel_id=1, source_target_pairs={{4,8},{8,4},{12,16},{16,12},{20,24},{24,20},{28,32},{32,28},{36,40... | collective-permute-start | bytes 61448 | tf_op jit(solution)/shard_map/ppermute | solution.py:606
  16.4 6.6 %collective-permute-start.6 = (bf16[5,16,768]{2,1,0:T(8,128)(2,1)}, bf16[5,16,768]{2,1,0:T(8,128)(2,1)S(1)}, u32[]{:S(2)}, u32[]{:S(2)}) collective-permute-start(bf16[5,16,768]{2,1,0:T(8,128)(2,1)} %get-tuple-element.38), channel_id=1, source_target_pairs={{0,2},{2,0},{1,3},{3,1},{4,6},{6,4},{5,7},{7,5},{8,10},{10,8},{9,1... | collective-permute-start | bytes 368648 | tf_op jit(solution)/shard_map/ppermute | solution.py:605
  20.2 3.3 %collective-permute-start.5 = (f32[5,16,128]{2,1,0:T(8,128)S(1)}, f32[5,16,128]{2,1,0:T(8,128)S(1)}, u32[]{:S(2)}, u32[]{:S(2)}) collective-permute-start(f32[5,16,128]{2,1,0:T(8,128)S(1)} %add_add_fusion.2), channel_id=1, source_target_pairs={{36,0},{100,64},{164,128},{228,192},{37,1},{101,65},{165,129},{229... | collective-permute-start | bytes 122888 | tf_op jit(solution)/shard_map/ppermute | solution.py:561
  20.9 2.6 %collective-permute-start.4 = (f32[5,16,128]{2,1,0:T(8,128)S(1)}, f32[5,16,128]{2,1,0:T(8,128)S(1)}, u32[]{:S(2)}, u32[]{:S(2)}) collective-permute-start(f32[5,16,128]{2,1,0:T(8,128)S(1)} %add_add_fusion.2), channel_id=1, source_target_pairs={{32,0},{96,64},{160,128},{224,192},{33,1},{97,65},{161,129},{225,1... | collective-permute-start | bytes 122888 | tf_op jit(solution)/shard_map/ppermute | solution.py:561
  21.5 2.2 %collective-permute-start.3 = (f32[5,16,128]{2,1,0:T(8,128)S(1)}, f32[5,16,128]{2,1,0:T(8,128)S(1)}, u32[]{:S(2)}, u32[]{:S(2)}) collective-permute-start(f32[5,16,128]{2,1,0:T(8,128)S(1)} %add_add_fusion.2), channel_id=1, source_target_pairs={{4,0},{68,64},{132,128},{196,192},{5,1},{69,65},{133,129},{197,193... | collective-permute-start | bytes 122888 | tf_op jit(solution)/shard_map/ppermute | solution.py:561
  23.1 2.9 %collective-permute-start.8 = (bf16[5,16,128]{2,1,0:T(8,128)(2,1)}, bf16[5,16,128]{2,1,0:T(8,128)(2,1)S(1)}, u32[]{:S(2)}, u32[]{:S(2)}) collective-permute-start(bf16[5,16,128]{2,1,0:T(8,128)(2,1)} %get-tuple-element.41), channel_id=1, source_target_pairs={{0,1},{1,0},{2,3},{3,2},{4,5},{5,4},{6,7},{7,6},{8,9},{9,8},{10,11... | collective-permute-start | bytes 61448 | tf_op jit(solution)/shard_map/ppermute | solution.py:610
  23.5 2.5 %collective-permute-start.9 = (bf16[5,16,128]{2,1,0:T(8,128)(2,1)}, bf16[5,16,128]{2,1,0:T(8,128)(2,1)S(1)}, u32[]{:S(2)}, u32[]{:S(2)}) collective-permute-start(bf16[5,16,128]{2,1,0:T(8,128)(2,1)} %get-tuple-element.42), channel_id=1, source_target_pairs={{0,4},{4,0},{8,12},{12,8},{16,20},{20,16},{24,28},{28,24},{32,36},... | collective-permute-start | bytes 61448 | tf_op jit(solution)/shard_map/ppermute | solution.py:611
  26.0 7.5 %collective-permute-start.12 = (f32[5,16,128]{2,1,0:T(8,128)S(1)}, f32[5,16,128]{2,1,0:T(8,128)S(1)}, u32[]{:S(2)}, u32[]{:S(2)}) collective-permute-start(f32[5,16,128]{2,1,0:T(8,128)S(1)} %add_add_fusion.1), channel_id=1, source_target_pairs={{128,0},{129,1},{130,2},{131,3}} | collective-permute-start | bytes 122888 | tf_op jit(solution)/shard_map/ppermute | solution.py:561
  26.6 6.8 %collective-permute-start.11 = (f32[5,16,128]{2,1,0:T(8,128)S(1)}, f32[5,16,128]{2,1,0:T(8,128)S(1)}, u32[]{:S(2)}, u32[]{:S(2)}) collective-permute-start(f32[5,16,128]{2,1,0:T(8,128)S(1)} %add_add_fusion.1), channel_id=1, source_target_pairs={{192,0},{193,1},{194,2},{195,3}} | collective-permute-start | bytes 122888 | tf_op jit(solution)/shard_map/ppermute | solution.py:561
  27.3 6.1 %collective-permute-start.10 = (f32[5,16,128]{2,1,0:T(8,128)S(1)}, f32[5,16,128]{2,1,0:T(8,128)S(1)}, u32[]{:S(2)}, u32[]{:S(2)}) collective-permute-start(f32[5,16,128]{2,1,0:T(8,128)S(1)} %add_add_fusion.1), channel_id=1, source_target_pairs={{64,0},{65,1},{66,2},{67,3}} | collective-permute-start | bytes 122888 | tf_op jit(solution)/shard_map/ppermute | solution.py:561
  34.2 14.0 %collective-permute-start.15 = (bf16[5,16,768]{2,1,0:T(8,128)(2,1)S(1)}, bf16[5,16,768]{2,1,0:T(8,128)(2,1)S(1)}, u32[]{:S(2)}, u32[]{:S(2)}) collective-permute-start(bf16[5,16,768]{2,1,0:T(8,128)(2,1)S(1)} %get-tuple-element.57), channel_id=1, source_target_pairs={{0,2},{2,0},{1,3},{3,1},{4,6},{6,4},{5,7},{7,5},{8,10},{10,8},{9,1... | collective-permute-start | bytes 368648 | tf_op jit(solution)/shard_map/ppermute | solution.py:657
  36.3 11.9 %collective-permute-start.13 = (bf16[5,16,128]{2,1,0:T(8,128)(2,1)S(1)}, bf16[5,16,128]{2,1,0:T(8,128)(2,1)S(1)}, u32[]{:S(2)}, u32[]{:S(2)}) collective-permute-start(bf16[5,16,128]{2,1,0:T(8,128)(2,1)S(1)} %get-tuple-element.55), channel_id=1, source_target_pairs={{0,4},{4,0},{8,12},{12,8},{16,20},{20,16},{24,28},{28,24},{32,36},... | collective-permute-start | bytes 61448 | tf_op jit(solution)/shard_map/ppermute | solution.py:631
  42.2 6.0 %collective-permute-start.14 = (bf16[5,16,128]{2,1,0:T(8,128)(2,1)S(1)}, bf16[5,16,128]{2,1,0:T(8,128)(2,1)S(1)}, u32[]{:S(2)}, u32[]{:S(2)}) collective-permute-start(bf16[5,16,128]{2,1,0:T(8,128)(2,1)S(1)} %get-tuple-element.56), channel_id=1, source_target_pairs={{4,8},{8,4},{12,16},{16,12},{20,24},{24,20},{28,32},{32,28},{36,40... | collective-permute-start | bytes 61448 | tf_op jit(solution)/shard_map/ppermute | solution.py:632
  44.2 4.1 %collective-permute-start.16 = (bf16[5,16,128]{2,1,0:T(8,128)(2,1)S(1)}, bf16[5,16,128]{2,1,0:T(8,128)(2,1)S(1)}, u32[]{:S(2)}, u32[]{:S(2)}) collective-permute-start(bf16[5,16,128]{2,1,0:T(8,128)(2,1)S(1)} %get-tuple-element.58), channel_id=1, source_target_pairs={{0,1},{1,0},{2,3},{3,2},{4,5},{5,4},{6,7},{7,6},{8,9},{9,8},{10,11... | collective-permute-start | bytes 61448 | tf_op jit(solution)/shard_map/ppermute | solution.py:658
  (1 other events, 19.0 us)

commit v6 on v5

--- a/solution.py
+++ b/solution.py
@@ -149,11 +149,30 @@
     )
 
 
-def mix(coefs, base, arrays):
-    total = coefs[base] * arrays[0]
+def mix(row, arrays):
+    total = row[0] * arrays[0]
     for g in range(1, FIELDS):
-        total = total + coefs[base + g] * arrays[g]
+        total = total + row[g] * arrays[g]
     return total
+
+
+def flux_row(jacobian, d, f):
+    return [jacobian[f, d, g] for g in range(FIELDS)]
+
+
+def face_row(jacobian, t, f):
+    half = 0.5 * (1.0 if t % 2 else -1.0)
+    row = [half * jacobian[f, t // 2, g] for g in range(FIELDS)]
+    row[f] = row[f] - 0.5
+    return row
+
+
+def fill(weights, parts):
+    column = 0
+    for part in parts:
+        weights[:, column : column + part.shape[1]] = part
+        column += part.shape[1]
+    return weights[...]
 
 
 def mix_fluxes(read, coefs, mixed):
@@ -163,7 +182,7 @@
             for d in range(3):
                 for f in range(FIELDS):
                     mixed[f, 64 * d + r : 64 * d + r + 16, :] = mix(
-                        coefs, 25 * d + 5 * f, rows
+                        flux_row(coefs, d, f), rows
                     ).astype(bf16)
 
         return run
@@ -173,7 +192,7 @@
 
 def write_jumps(t, jumps, coefs, mixed, first_row):
     for f in range(FIELDS):
-        mixed[f, first_row : first_row + 16, :] = mix(coefs, 75 + 25 * t + 5 * f, jumps).astype(bf16)
+        mixed[f, first_row : first_row + 16, :] = mix(face_row(coefs, t, f), jumps).astype(bf16)
 
 
 def mix_stream(read, lower, upper, coefs, mixed, row):
@@ -347,13 +366,18 @@
 
 
 def phase_one_kernel(
-    v_ref, from_core_ref, from_chip_ref, near_ref, far_ref, pin_ref, coefs, weights_ref, filter_ref,
-    out_ref, out_trace_ref, core_ref, chip_ref, pitch_ref, span_ref, mixed, own, span_held,
+    v_ref, from_core_ref, from_chip_ref, near_ref, far_ref, pin_ref, coefs, volume_ref, lift_ref,
+    wall_ref, filter_ref,
+    out_ref, out_trace_ref, core_ref, chip_ref, pitch_ref, span_ref, mixed, own, weights_held,
+    span_held,
 ):
     first_span = lax.axis_index("span") == 0
     lane = lanes()
     pick = trace_selector()
-    weights, smooth = weights_ref[...], with_traces(filter_ref[...], pick)
+    smooth = with_traces(filter_ref[...], pick)
+    weights = fill(
+        weights_held, [volume_ref[0], volume_ref[1], volume_ref[2], lift_ref[...], wall_ref[...]]
+    )
     span_held[...] = jnp.zeros_like(span_held)
     below, above = from_below(from_core_ref, from_chip_ref), from_above(from_core_ref, from_chip_ref)
     vector, matrix = [], []
@@ -401,8 +425,8 @@
     )
 
 
-def inner_two_kernel(v_ref, coefs, weights_ref, part_ref, mixed):
-    weights = weights_ref[...]
+def inner_two_kernel(v_ref, coefs, volume_ref, part_ref, mixed, weights_held):
+    weights = fill(weights_held, [volume_ref[d] for d in range(3)])
     vector, matrix = [], []
 
     def add(pair):
@@ -422,12 +446,12 @@
 
 def outer_two_kernel(
     v_ref, trace_ref, base_ref, part_ref, mean_ref, amp_ref, plane_ref, from_core_ref, from_chip_ref,
-    near_ref, far_ref, pin_ref, coefs, weights_ref, smooth_ref, out_ref, mixed,
+    near_ref, far_ref, pin_ref, coefs, lift_ref, wall_ref, smooth_ref, out_ref, mixed, weights_held,
 ):
     first_span = lax.axis_index("span") == 0
     first_rans = lax.axis_index("rans") == 0
     lane = lanes()
-    weights, smooth = weights_ref[...], smooth_ref[...]
+    weights, smooth = fill(weights_held, [lift_ref[...], wall_ref[...]]), smooth_ref[...]
     below, above = from_below(from_core_ref, from_chip_ref), from_above(from_core_ref, from_chip_ref)
     vector, matrix = [], []
 
@@ -475,8 +499,9 @@
 
 def inflow_kernel(
     held_ref, held_trace_ref, held_pitch_ref, held_span_ref, v_ref, mean_ref, amp_ref,
-    plane_ref, near_ref, far_ref, pin_ref, coefs, weights_ref, filter_ref, out_ref, out_trace_ref,
-    pitch_ref, span_ref, mixed, own,
+    plane_ref, near_ref, far_ref, pin_ref, coefs, volume_ref, lift_ref, wall_ref, filter_ref, out_ref,
+    out_trace_ref,
+    pitch_ref, span_ref, mixed, own, weights_held,
 ):
     first_span = lax.axis_index("span") == 0
     first_rans = lax.axis_index("rans") == 0
@@ -485,7 +510,10 @@
     @pl.when(first_rans)
     def _():
         pick = trace_selector()
-        weights, smooth = weights_ref[...], with_traces(filter_ref[...], pick)
+        smooth = with_traces(filter_ref[...], pick)
+        weights = fill(
+            weights_held, [volume_ref[0], volume_ref[1], volume_ref[2], lift_ref[...], wall_ref[...]]
+        )
 
         def read(f, r0, r1):
             return v_ref[f, r0:r1, 0:CELLS]
@@ -563,17 +591,8 @@
             value = value + part
         return value
 
-    weights = jnp.concatenate(
-        [volume_ops[0], volume_ops[1], volume_ops[2], lift_matrix, wall_matrix], axis=1
-    )
-    identity = jnp.eye(FIELDS, dtype=f32)
-    sides = jnp.array([-1.0, 1.0], f32)
-    face_coefs = (
-        0.5 * sides[None, :, None, None] * flux_jacobian[:, None] - 0.5 * identity
-    ).reshape(-1)
-    coefs = jnp.concatenate([flux_jacobian.reshape(-1), face_coefs])
+    jacobian = flux_jacobian.transpose(1, 0, 2)
     pins = pinched_map.reshape(1, -1)
-    fixed_specs = [VMEM, SMEM, VMEM, VMEM]
     elements = solution.shape[2]
     traces = shape_of(FIELDS, NODES, elements)
     sends = (faces, faces, shape_of(FIELDS, 16, EX // 2 * CELLS), faces)
@@ -603,33 +622,37 @@
     )(mode_rows[0, 0].T, mode_seeds.reshape(1, eddies), mode_shape[0, 0].T, solution)
     plane = gather_sum(plane, (2, 6, 4), [8 * z + c for z in range(8) for c in range(2)])
     near = lax.ppermute(pitch, "pitch", swap)
+    plane, chip, core, span = lax.optimization_barrier((plane, chip, core, span))
+    plane = gather_sum(plane, (1, 8, 9), [0, 16, 32, 48])
     from_chip = lax.ppermute(chip, "rans", next_chip)
-    plane, core, span = lax.optimization_barrier((plane, core, span))
-    plane = gather_sum(plane, (1, 8, 9), [0, 16, 32, 48])
-    core, span, near, from_chip = lax.optimization_barrier((core, span, near, from_chip))
+    core, span, near = lax.optimization_barrier((core, span, near))
     far = lax.ppermute(span, "span", swap)
     from_core = lax.ppermute(core, "rans", same_chip)
-    plane, near, far, from_core, from_chip = lax.optimization_barrier(
-        (plane, near, far, from_core, from_chip)
-    )
+    plane, near, far, from_core = lax.optimization_barrier((plane, near, far, from_core))
     plane = gather_sum(plane, (16, 48, 32), [0])
 
     phase_one, trace_one, core, chip, pitch, span = pl.pallas_call(
         phase_one_kernel,
         out_shape=(traces, traces) + sends,
-        in_specs=[VMEM] * 5 + fixed_specs,
+        in_specs=[VMEM] * 6 + [SMEM] + [VMEM] * 4,
         out_specs=(VMEM,) * 6,
         scratch_shapes=[
             pltpu.VMEM((2, FIELDS, MIXED, PAIR), bf16),
             pltpu.VMEM((2, FIELDS, NODES, PAIR), bf16),
+            pltpu.VMEM((NODES, MIXED), bf16),
             span_scratch,
         ],
         compiler_params=PARAMS,
         cost_estimate=cost(6),
         name="phase_one",
-    )(solution, from_core, from_chip, near, far, pins, coefs, weights, filter_matrix)
+    )(
+        solution, from_core, from_chip, near, far, pins, jacobian, volume_ops, lift_matrix, wall_matrix,
+        filter_matrix,
+    )
     from_core = lax.ppermute(core, "rans", same_chip)
     from_chip = lax.ppermute(chip, "rans", next_chip)
+    plane, from_core = lax.optimization_barrier((plane, from_core))
+
     mean = mean_inflow.reshape(FIELDS, 16, CELLS)
     amplitude = eddy_amplitude.reshape(FIELDS, 16, CELLS)
     layer = front(FIELDS, NODES, CELLS)
@@ -640,19 +663,23 @@
         out_shape=(traces, traces, sends[2], sends[3]),
         in_specs=[layer, layer, face, face, front(FIELDS, NODES, PAIR)]
         + [face] * 5
-        + [front(1, CELLS), SMEM, front(NODES, MIXED), front(NODES, NODES)],
+        + [
+            front(1, CELLS), SMEM, front(3, NODES, NODES), front(NODES, 96), front(NODES, NODES),
+            front(NODES, NODES),
+        ],
         out_specs=(layer, layer, face, face),
         scratch_shapes=[
             pltpu.VMEM((FIELDS, MIXED, CELLS), bf16),
             pltpu.VMEM((FIELDS, NODES, CELLS), bf16),
+            pltpu.VMEM((NODES, MIXED), bf16),
         ],
         input_output_aliases={0: 0, 1: 1, 2: 2, 3: 3},
         compiler_params=PARAMS,
-        cost_estimate=cost(1),
+        cost_estimate=cost(0.1),
         name="inflow_layer",
     )(
         phase_one, trace_one, pitch, span, solution, mean, amplitude, plane, near, far,
-        pins, coefs, weights, filter_matrix,
+        pins, jacobian, volume_ops, lift_matrix, wall_matrix, filter_matrix,
     )
     near = lax.ppermute(pitch, "pitch", swap)
     far = lax.ppermute(span, "span", swap)
@@ -661,23 +688,28 @@
         out_shape=shape_of(FIELDS, NODES, elements, dtype=f32),
         in_specs=[VMEM, SMEM, VMEM],
         out_specs=VMEM,
-        scratch_shapes=[pltpu.VMEM((2, FIELDS, INNER, PAIR), bf16)],
+        scratch_shapes=[
+            pltpu.VMEM((2, FIELDS, INNER, PAIR), bf16), pltpu.VMEM((NODES, INNER), bf16)
+        ],
         compiler_params=PARAMS,
-        cost_estimate=cost(3),
+        cost_estimate=cost(0.1),
         name="inner_two",
-    )(phase_one, coefs, weights[:, :INNER])
+    )(phase_one, jacobian, volume_ops)
     return pl.pallas_call(
         outer_two_kernel,
         out_shape=traces,
-        in_specs=[VMEM] * 12 + fixed_specs[1:],
+        in_specs=[VMEM] * 12 + [SMEM] + [VMEM] * 3,
         out_specs=VMEM,
-        scratch_shapes=[pltpu.VMEM((2, FIELDS, MIXED - INNER, PAIR), bf16)],
+        scratch_shapes=[
+            pltpu.VMEM((2, FIELDS, MIXED - INNER, PAIR), bf16),
+            pltpu.VMEM((NODES, MIXED - INNER), bf16),
+        ],
         compiler_params=PARAMS,
         cost_estimate=cost(4),
         name="outer_two",
     )(
         phase_one, trace_one, solution, part, mean, amplitude, plane, from_core, from_chip, near, far,
-        pins, coefs, weights[:, INNER:], filter_matrix,
+        pins, jacobian, lift_matrix, wall_matrix, filter_matrix,
     )
 
 

time: 53 us -> 52.2 us (0.985)
  the two profiles are of different devices: /device:TPU:1 before, /device:TPU:121 now
where the time goes in v6:
time: 52.2 us; the launch traced here: 51.9 us
  starting transfers between devices  28.3 us (54%)
  Pallas kernels  18.8 us (36%)
  waiting for transfers between devices  3.58 us (7%)
  other arithmetic  0.83 us (2%)
    ppermute x2, starting transfers between devices, body(): from_chip = lax.ppermute(chip, 'rans', next_chip)  12.9 us
    ppermute x9, starting transfers between devices, gather_sum(): lax.ppermute(value, 'rans', [(r + o, r) for r in roots])  7.77 us
    ppermute x2, starting transfers between devices, body(): near = lax.ppermute(pitch, 'pitch', swap)  5.66 us
    pallas_call x1, Pallas kernels, body(): pl.pallas_call(phase_one_kernel, out_shape=(traces, traces) + sends, in_s...  5.59 us
    pallas_call x1, Pallas kernels, body(): pl.pallas_call(functools.partial(prepare_kernel, normalizer=float((plane_...  4.92 us
    pallas_call x1, Pallas kernels, body(): pl.pallas_call(outer_two_kernel, out_shape=traces, in_specs=[VMEM] * 12 +...  4.54 us
    pallas_call x1, Pallas kernels, body(): pl.pallas_call(inner_two_kernel, out_shape=shape_of(FIELDS, NODES, elemen...  2.94 us
    ppermute x2, starting transfers between devices, body(): far = lax.ppermute(span, 'span', swap)  1.89 us
  transfers between devices with their start and end apart: 17, of which 3 were waited for; matrix products, arithmetic and copies ran while one was open for 2% of the time, Pallas kernels for 16%

profile of v6, /device:TPU:121, one launch (start us, length us, event | category | flops | bytes accessed | tf_op | source)
XLA Modules:
  0.0 51.9 jit_solution(285279776863801109)
XLA Ops:
  0.1 4.9 %prepare.1 = (f32[5,16,128]{2,1,0:T(8,128)}, bf16[5,16,128]{2,1,0:T(8,128)(2,1)}, bf16[5,16,128]{2,1,0:T(8,128)(2,1)}, bf16[5,16,768]{2,1,0:T(8,128)(2,1)}, bf16[5,16,128]{2,1,0:T(8,128)(2,1)}) custom-call(s32[64,256]{1,0:T(8,128)} %bitcast.18, s32[1,256]{1,0:T(1,128)} %bitcast.20, f32[64,256]{1,0:T(8,128)} %bitcast.19, bf16[5,64,1536]{2,1,0:T(8,128)(2,1)} %base_ref.1), custom_call_target="tpu_custom_call" | custom-call | flops 500000000 | bytes 15000000 | tf_op jit(solution)/shard_map/prepare/pallas_call | solution.py:604
  5.0 0.7 %collective-permute-start.2 = (f32[5,16,128]{2,1,0:T(8,128)}, f32[5,16,128]{2,1,0:T(8,128)S(1)}, u32[]{:S(2)}, u32[]{:S(2)}) collective-permute-start(f32[5,16,128]{2,1,0:T(8,128)} %get-tuple-element.33), channel_id=1, source_target_pairs={{16,0},{20,4},{48,32},{52,36},{80,64},{84,68},{112,96},{116,100},{... | collective-permute-start | bytes 122888 | tf_op jit(solution)/shard_map/ppermute | solution.py:589
  5.7 2.5 %collective-permute-start.1 = (f32[5,16,128]{2,1,0:T(8,128)}, f32[5,16,128]{2,1,0:T(8,128)S(1)}, u32[]{:S(2)}, u32[]{:S(2)}) collective-permute-start(f32[5,16,128]{2,1,0:T(8,128)} %get-tuple-element.33), channel_id=1, source_target_pairs={{24,0},{28,4},{56,32},{60,36},{88,64},{92,68},{120,96},{124,100},{... | collective-permute-start | bytes 122888 | tf_op jit(solution)/shard_map/ppermute | solution.py:589
  8.1 0.7 %collective-permute-start = (f32[5,16,128]{2,1,0:T(8,128)}, f32[5,16,128]{2,1,0:T(8,128)S(1)}, u32[]{:S(2)}, u32[]{:S(2)}) collective-permute-start(f32[5,16,128]{2,1,0:T(8,128)} %get-tuple-element.33), channel_id=1, source_target_pairs={{8,0},{12,4},{40,32},{44,36},{72,64},{76,68},{104,96},{108,100},{1... | collective-permute-start | bytes 122888 | tf_op jit(solution)/shard_map/ppermute | solution.py:589
  8.8 2.8 %collective-permute-start.6 = (bf16[5,16,768]{2,1,0:T(8,128)(2,1)}, bf16[5,16,768]{2,1,0:T(8,128)(2,1)S(1)}, u32[]{:S(2)}, u32[]{:S(2)}) collective-permute-start(bf16[5,16,768]{2,1,0:T(8,128)(2,1)} %get-tuple-element.40), channel_id=1, source_target_pairs={{0,2},{2,0},{1,3},{3,1},{4,6},{6,4},{5,7},{7,5},{8,10},{10,8},{9,1... | collective-permute-start | bytes 368648 | tf_op jit(solution)/shard_map/ppermute | solution.py:624
  11.7 0.8 %add_add_fusion.2 = f32[5,16,128]{2,1,0:T(8,128)S(1)} fusion(f32[5,16,128]{2,1,0:T(8,128)S(1)} %collective-permute-done.2, f32[5,16,128]{2,1,0:T(8,128)S(1)} %collective-permute-done.1, f32[5,16,128]{2,1,0:T(8,128)} %get-tuple-element.33, f32[5,16,128]{2,1,0:T(8,128)S(1)} %collective-permute-done), kind=kLoop, calls=%fused_computation.2 | loop fusion | flops 30720 | bytes 204800 | tf_op jit(solution)/shard_map/add | solution.py:591
  12.5 0.7 %collective-permute-start.5 = (f32[5,16,128]{2,1,0:T(8,128)S(1)}, f32[5,16,128]{2,1,0:T(8,128)S(1)}, u32[]{:S(2)}, u32[]{:S(2)}) collective-permute-start(f32[5,16,128]{2,1,0:T(8,128)S(1)} %add_add_fusion.2), channel_id=1, source_target_pairs={{36,0},{100,64},{164,128},{228,192},{37,1},{101,65},{165,129},{229... | collective-permute-start | bytes 122888 | tf_op jit(solution)/shard_map/ppermute | solution.py:589
  13.1 0.7 %collective-permute-start.4 = (f32[5,16,128]{2,1,0:T(8,128)S(1)}, f32[5,16,128]{2,1,0:T(8,128)S(1)}, u32[]{:S(2)}, u32[]{:S(2)}) collective-permute-start(f32[5,16,128]{2,1,0:T(8,128)S(1)} %add_add_fusion.2), channel_id=1, source_target_pairs={{32,0},{96,64},{160,128},{224,192},{33,1},{97,65},{161,129},{225,1... | collective-permute-start | bytes 122888 | tf_op jit(solution)/shard_map/ppermute | solution.py:589
  13.8 0.7 %collective-permute-start.3 = (f32[5,16,128]{2,1,0:T(8,128)S(1)}, f32[5,16,128]{2,1,0:T(8,128)S(1)}, u32[]{:S(2)}, u32[]{:S(2)}) collective-permute-start(f32[5,16,128]{2,1,0:T(8,128)S(1)} %add_add_fusion.2), channel_id=1, source_target_pairs={{4,0},{68,64},{132,128},{196,192},{5,1},{69,65},{133,129},{197,193... | collective-permute-start | bytes 122888 | tf_op jit(solution)/shard_map/ppermute | solution.py:589
  14.5 8.9 %collective-permute-start.9 = (bf16[5,16,128]{2,1,0:T(8,128)(2,1)}, bf16[5,16,128]{2,1,0:T(8,128)(2,1)S(1)}, u32[]{:S(2)}, u32[]{:S(2)}) collective-permute-start(bf16[5,16,128]{2,1,0:T(8,128)(2,1)} %get-tuple-element.45), channel_id=1, source_target_pairs={{4,8},{8,4},{12,16},{16,12},{20,24},{24,20},{28,32},{32,28},{36,40... | collective-permute-start | bytes 61448 | tf_op jit(solution)/shard_map/ppermute | solution.py:627
  23.4 1.3 %collective-permute-start.7 = (bf16[5,16,128]{2,1,0:T(8,128)(2,1)}, bf16[5,16,128]{2,1,0:T(8,128)(2,1)S(1)}, u32[]{:S(2)}, u32[]{:S(2)}) collective-permute-start(bf16[5,16,128]{2,1,0:T(8,128)(2,1)} %get-tuple-element.42), channel_id=1, source_target_pairs={{0,1},{1,0},{2,3},{3,2},{4,5},{5,4},{6,7},{7,6},{8,9},{9,8},{10,11... | collective-permute-start | bytes 61448 | tf_op jit(solution)/shard_map/ppermute | solution.py:629
  24.8 1.6 %collective-permute-done.7.far_ref = bf16[5,16,128]{2,1,0:T(8,128)(2,1)S(1)} collective-permute-done((bf16[5,16,128]{2,1,0:T(8,128)(2,1)}, bf16[5,16,128]{2,1,0:T(8,128)(2,1)S(1)}, u32[]{:S(2)}, u32[]{:S(2)}) %collective-permute-start.7) | collective-permute-done | bytes 20512 | tf_op jit(solution)/shard_map/ppermute | solution.py:629
  26.3 0.7 %collective-permute-start.12 = (f32[5,16,128]{2,1,0:T(8,128)S(1)}, f32[5,16,128]{2,1,0:T(8,128)S(1)}, u32[]{:S(2)}, u32[]{:S(2)}) collective-permute-start(f32[5,16,128]{2,1,0:T(8,128)S(1)} %add_add_fusion.1), channel_id=1, source_target_pairs={{128,0},{129,1},{130,2},{131,3}} | collective-permute-start | bytes 122888 | tf_op jit(solution)/shard_map/ppermute | solution.py:589
  27.0 0.7 %collective-permute-start.11 = (f32[5,16,128]{2,1,0:T(8,128)S(1)}, f32[5,16,128]{2,1,0:T(8,128)S(1)}, u32[]{:S(2)}, u32[]{:S(2)}) collective-permute-start(f32[5,16,128]{2,1,0:T(8,128)S(1)} %add_add_fusion.1), channel_id=1, source_target_pairs={{192,0},{193,1},{194,2},{195,3}} | collective-permute-start | bytes 122888 | tf_op jit(solution)/shard_map/ppermute | solution.py:589
  27.7 0.7 %collective-permute-start.10 = (f32[5,16,128]{2,1,0:T(8,128)S(1)}, f32[5,16,128]{2,1,0:T(8,128)S(1)}, u32[]{:S(2)}, u32[]{:S(2)}) collective-permute-start(f32[5,16,128]{2,1,0:T(8,128)S(1)} %add_add_fusion.1), channel_id=1, source_target_pairs={{64,0},{65,1},{66,2},{67,3}} | collective-permute-start | bytes 122888 | tf_op jit(solution)/shard_map/ppermute | solution.py:589
  28.4 5.6 %phase_one.1 = (bf16[5,64,1536]{2,1,0:T(8,128)(2,1)S(1)}, bf16[5,64,1536]{2,1,0:T(8,128)(2,1)S(1)}, bf16[5,16,128]{2,1,0:T(8,128)(2,1)S(1)}, bf16[5,16,128]{2,1,...) custom-call(bf16[5,64,1536]{2,1,0:T(8,128)(2,1)S(1)} %copy-done, ...), custom_call_target="tpu_custom_call" | custom-call | flops 600000000 | bytes 18000000 | tf_op jit(solution)/shard_map/phase_one/pallas_call | solution.py:634
  34.2 1.1 %collective-permute-done.13.from_core_ref = bf16[5,16,128]{2,1,0:T(8,128)(2,1)S(1)} collective-permute-done((bf16[5,16,128]{2,1,0:T(8,128)(2,1)S(1)}, bf16[5,16,128]{2,1,0:T(8,128)(2,1)S(1)}, u32[]{:S(2)}, u32[]{:S(2)}) %collective-permute-start.13) | collective-permute-done | bytes 20512 | tf_op jit(solution)/shard_map/ppermute | solution.py:652
  35.3 0.8 %inflow_layer.1 = (bf16[5,64,1536]{2,1,0:T(8,128)(2,1)S(1)}, bf16[5,64,1536]{2,1,0:T(8,128)(2,1)S(1)}, bf16[5,16,768]{2,1,0:T(8,128)(2,1)S(1)}, bf16[5,16,128]{2,1,0:T(8,128)(2,1)S(1)}) custom-call(bf16[5,64,1536]{2,1,0:T(8,128)(2,1)S(1)} %get-tuple-element.48.held_ref, ...), custom_call_target="tpu_custom_call", output_to_operand_aliasing={{0}: (0, {}), {1}: (1, {}), {2}: (2, {}), {3}: (3, {})} | custom-call | flops 10000000 | bytes 300000 | tf_op jit(solution)/shard_map/inflow_layer/pallas_call | solution.py:660
  36.1 2.8 %collective-permute-start.15 = (bf16[5,16,768]{2,1,0:T(8,128)(2,1)S(1)}, bf16[5,16,768]{2,1,0:T(8,128)(2,1)S(1)}, u32[]{:S(2)}, u32[]{:S(2)}) collective-permute-start(bf16[5,16,768]{2,1,0:T(8,128)(2,1)S(1)} %get-tuple-element.59), channel_id=1, source_target_pairs={{0,2},{2,0},{1,3},{3,1},{4,6},{6,4},{5,7},{7,5},{8,10},{10,8},{9,1... | collective-permute-start | bytes 368648 | tf_op jit(solution)/shard_map/ppermute | solution.py:684
  38.9 4.0 %collective-permute-start.14 = (bf16[5,16,128]{2,1,0:T(8,128)(2,1)S(1)}, bf16[5,16,128]{2,1,0:T(8,128)(2,1)S(1)}, u32[]{:S(2)}, u32[]{:S(2)}) collective-permute-start(bf16[5,16,128]{2,1,0:T(8,128)(2,1)S(1)} %get-tuple-element.58), channel_id=1, source_target_pairs={{4,8},{8,4},{12,16},{16,12},{20,24},{24,20},{28,32},{32,28},{36,40... | collective-permute-start | bytes 61448 | tf_op jit(solution)/shard_map/ppermute | solution.py:653
  43.0 0.6 %collective-permute-start.16 = (bf16[5,16,128]{2,1,0:T(8,128)(2,1)S(1)}, bf16[5,16,128]{2,1,0:T(8,128)(2,1)S(1)}, u32[]{:S(2)}, u32[]{:S(2)}) collective-permute-start(bf16[5,16,128]{2,1,0:T(8,128)(2,1)S(1)} %get-tuple-element.60), channel_id=1, source_target_pairs={{0,1},{1,0},{2,3},{3,2},{4,5},{5,4},{6,7},{7,6},{8,9},{9,8},{10,11... | collective-permute-start | bytes 61448 | tf_op jit(solution)/shard_map/ppermute | solution.py:685
  43.6 2.9 %inner_two.1.part_ref = f32[5,64,1536]{2,1,0:T(8,128)S(1)} custom-call(bf16[5,64,1536]{2,1,0:T(8,128)(2,1)S(1)} %get-tuple-element.55.v_ref, f32[5,3,5]{2,1,0:T(4,128)S(1)} %bitcast.16, bf16[3,64,64]{2,1,0:T(8,128)(2,1)S(1)} %copy-done.1), custom_call_target="tpu_custom_call" | custom-call | flops 10000000 | bytes 300000 | tf_op jit(solution)/shard_map/inner_two/pallas_call | solution.py:686
  46.5 0.8 %collective-permute-done.14.from_chip_ref = bf16[5,16,128]{2,1,0:T(8,128)(2,1)S(1)} collective-permute-done((bf16[5,16,128]{2,1,0:T(8,128)(2,1)S(1)}, bf16[5,16,128]{2,1,0:T(8,128)(2,1)S(1)}, u32[]{:S(2)}, u32[]{:S(2)}) %collective-permute-start.14) | collective-permute-done | bytes 20512 | tf_op jit(solution)/shard_map/ppermute | solution.py:653
  47.4 4.5 %outer_two.1 = bf16[5,64,1536]{2,1,0:T(8,128)(2,1)} custom-call(bf16[5,64,1536]{2,1,0:T(8,128)(2,1)S(1)} %get-tuple-element.55.v_ref, bf16[5,64,1536]{2,1,0:T(8,128)(2,1)S(1)} %get-tuple-element.56.trace_ref, bf16[5,64,1536]{2,1,0:T(8,128)(2,1)S(1)} %copy-done, f32[5,64,1536]{2,1,0:T(8,128)S(1)} %inner_two.1.part_ref, f32[5,16,128]{2,1,0:T(8,128)S(1)} %bitcast.11, ...), custom_call_target="tpu_custom_call" | custom-call | flops 400000000 | bytes 12000000 | tf_op jit(solution)/shard_map/outer_two/pallas_call | solution.py:698
  (37 shorter events, 0.2 us)
Async XLA Ops:
  0.0 28.4 %copy-start.6 = (bf16[64,64]{1,0:T(8,128)(2,1)S(1)}, bf16[64,64]{1,0:T(8,128)(2,1)}, u32[]{:S(2)}) copy-start(bf16[64,64]{1,0:T(8,128)(2,1)} %wall_ref.5) | copy-start | bytes 24580
  0.0 28.4 %copy-start.7 = (bf16[64,64]{1,0:T(8,128)(2,1)S(1)}, bf16[64,64]{1,0:T(8,128)(2,1)}, u32[]{:S(2)}) copy-start(bf16[64,64]{1,0:T(8,128)(2,1)} %smooth_ref.1) | copy-start | bytes 24580
  0.0 28.4 %copy-start.5 = (bf16[64,96]{1,0:T(8,128)(2,1)S(1)}, bf16[64,96]{1,0:T(8,128)(2,1)}, u32[]{:S(2)}) copy-start(bf16[64,96]{1,0:T(8,128)(2,1)} %lift_ref.5) | copy-start | bytes 36868
  0.0 28.4 %copy-start.1 = (bf16[3,64,64]{2,1,0:T(8,128)(2,1)S(1)}, bf16[3,64,64]{2,1,0:T(8,128)(2,1)}, u32[]{:S(2)}) copy-start(bf16[3,64,64]{2,1,0:T(8,128)(2,1)} %volume_ref.5) | copy-start | bytes 73732
  0.0 28.4 %copy-start.4 = (f32[3,5,5]{2,0,1:T(4,128)S(1)}, f32[3,5,5]{2,0,1:T(4,128)}, u32[]{:S(2)}) copy-start(f32[3,5,5]{2,0,1:T(4,128)} %param.14) | copy-start | bytes 904
  0.0 35.2 %copy-start.2 = (f32[1,1,5,2048]{3,1,2,0:T(1,128)S(1)}, f32[1,1,5,2048]{3,1,2,0:T(1,128)}, u32[]{:S(2)}) copy-start(f32[1,1,5,2048]{3,1,2,0:T(1,128)} %param.22) | copy-start | bytes 122884
  0.1 35.2 %copy-start.3 = (f32[1,1,5,2048]{3,1,2,0:T(1,128)S(1)}, f32[1,1,5,2048]{3,1,2,0:T(1,128)}, u32[]{:S(2)}) copy-start(f32[1,1,5,2048]{3,1,2,0:T(1,128)} %param.23) | copy-start | bytes 122884
  5.0 6.7 %collective-permute-start.2 = (f32[5,16,128]{2,1,0:T(8,128)}, f32[5,16,128]{2,1,0:T(8,128)S(1)}, u32[]{:S(2)}, u32[]{:S(2)}) collective-permute-start(f32[5,16,128]{2,1,0:T(8,128)} %get-tuple-element.33), channel_id=1, source_target_pairs={{16,0},{20,4},{48,32},{52,36},{80,64},{84,68},{112,96},{116,100},{... | collective-permute-start | bytes 122888 | tf_op jit(solution)/shard_map/ppermute | solution.py:589
  5.7 6.0 %collective-permute-start.1 = (f32[5,16,128]{2,1,0:T(8,128)}, f32[5,16,128]{2,1,0:T(8,128)S(1)}, u32[]{:S(2)}, u32[]{:S(2)}) collective-permute-start(f32[5,16,128]{2,1,0:T(8,128)} %get-tuple-element.33), channel_id=1, source_target_pairs={{24,0},{28,4},{56,32},{60,36},{88,64},{92,68},{120,96},{124,100},{... | collective-permute-start | bytes 122888 | tf_op jit(solution)/shard_map/ppermute | solution.py:589
  8.1 3.5 %collective-permute-start = (f32[5,16,128]{2,1,0:T(8,128)}, f32[5,16,128]{2,1,0:T(8,128)S(1)}, u32[]{:S(2)}, u32[]{:S(2)}) collective-permute-start(f32[5,16,128]{2,1,0:T(8,128)} %get-tuple-element.33), channel_id=1, source_target_pairs={{8,0},{12,4},{40,32},{44,36},{72,64},{76,68},{104,96},{108,100},{1... | collective-permute-start | bytes 122888 | tf_op jit(solution)/shard_map/ppermute | solution.py:589
  8.8 14.6 %collective-permute-start.6 = (bf16[5,16,768]{2,1,0:T(8,128)(2,1)}, bf16[5,16,768]{2,1,0:T(8,128)(2,1)S(1)}, u32[]{:S(2)}, u32[]{:S(2)}) collective-permute-start(bf16[5,16,768]{2,1,0:T(8,128)(2,1)} %get-tuple-element.40), channel_id=1, source_target_pairs={{0,2},{2,0},{1,3},{3,1},{4,6},{6,4},{5,7},{7,5},{8,10},{10,8},{9,1... | collective-permute-start | bytes 368648 | tf_op jit(solution)/shard_map/ppermute | solution.py:624
  12.5 12.3 %collective-permute-start.5 = (f32[5,16,128]{2,1,0:T(8,128)S(1)}, f32[5,16,128]{2,1,0:T(8,128)S(1)}, u32[]{:S(2)}, u32[]{:S(2)}) collective-permute-start(f32[5,16,128]{2,1,0:T(8,128)S(1)} %add_add_fusion.2), channel_id=1, source_target_pairs={{36,0},{100,64},{164,128},{228,192},{37,1},{101,65},{165,129},{229... | collective-permute-start | bytes 122888 | tf_op jit(solution)/shard_map/ppermute | solution.py:589
  13.1 11.6 %collective-permute-start.4 = (f32[5,16,128]{2,1,0:T(8,128)S(1)}, f32[5,16,128]{2,1,0:T(8,128)S(1)}, u32[]{:S(2)}, u32[]{:S(2)}) collective-permute-start(f32[5,16,128]{2,1,0:T(8,128)S(1)} %add_add_fusion.2), channel_id=1, source_target_pairs={{32,0},{96,64},{160,128},{224,192},{33,1},{97,65},{161,129},{225,1... | collective-permute-start | bytes 122888 | tf_op jit(solution)/shard_map/ppermute | solution.py:589
  13.8 10.9 %collective-permute-start.3 = (f32[5,16,128]{2,1,0:T(8,128)S(1)}, f32[5,16,128]{2,1,0:T(8,128)S(1)}, u32[]{:S(2)}, u32[]{:S(2)}) collective-permute-start(f32[5,16,128]{2,1,0:T(8,128)S(1)} %add_add_fusion.2), channel_id=1, source_target_pairs={{4,0},{68,64},{132,128},{196,192},{5,1},{69,65},{133,129},{197,193... | collective-permute-start | bytes 122888 | tf_op jit(solution)/shard_map/ppermute | solution.py:589
  14.5 13.9 %collective-permute-start.9 = (bf16[5,16,128]{2,1,0:T(8,128)(2,1)}, bf16[5,16,128]{2,1,0:T(8,128)(2,1)S(1)}, u32[]{:S(2)}, u32[]{:S(2)}) collective-permute-start(bf16[5,16,128]{2,1,0:T(8,128)(2,1)} %get-tuple-element.45), channel_id=1, source_target_pairs={{4,8},{8,4},{12,16},{16,12},{20,24},{24,20},{28,32},{32,28},{36,40... | collective-permute-start | bytes 61448 | tf_op jit(solution)/shard_map/ppermute | solution.py:627
  23.4 2.9 %collective-permute-start.7 = (bf16[5,16,128]{2,1,0:T(8,128)(2,1)}, bf16[5,16,128]{2,1,0:T(8,128)(2,1)S(1)}, u32[]{:S(2)}, u32[]{:S(2)}) collective-permute-start(bf16[5,16,128]{2,1,0:T(8,128)(2,1)} %get-tuple-element.42), channel_id=1, source_target_pairs={{0,1},{1,0},{2,3},{3,2},{4,5},{5,4},{6,7},{7,6},{8,9},{9,8},{10,11... | collective-permute-start | bytes 61448 | tf_op jit(solution)/shard_map/ppermute | solution.py:629
  24.7 1.6 %collective-permute-start.8 = (bf16[5,16,128]{2,1,0:T(8,128)(2,1)}, bf16[5,16,128]{2,1,0:T(8,128)(2,1)S(1)}, u32[]{:S(2)}, u32[]{:S(2)}) collective-permute-start(bf16[5,16,128]{2,1,0:T(8,128)(2,1)} %get-tuple-element.43), channel_id=1, source_target_pairs={{0,4},{4,0},{8,12},{12,8},{16,20},{20,16},{24,28},{28,24},{32,36},... | collective-permute-start | bytes 61448 | tf_op jit(solution)/shard_map/ppermute | solution.py:630
  26.3 7.8 %collective-permute-start.12 = (f32[5,16,128]{2,1,0:T(8,128)S(1)}, f32[5,16,128]{2,1,0:T(8,128)S(1)}, u32[]{:S(2)}, u32[]{:S(2)}) collective-permute-start(f32[5,16,128]{2,1,0:T(8,128)S(1)} %add_add_fusion.1), channel_id=1, source_target_pairs={{128,0},{129,1},{130,2},{131,3}} | collective-permute-start | bytes 122888 | tf_op jit(solution)/shard_map/ppermute | solution.py:589
  27.0 7.1 %collective-permute-start.11 = (f32[5,16,128]{2,1,0:T(8,128)S(1)}, f32[5,16,128]{2,1,0:T(8,128)S(1)}, u32[]{:S(2)}, u32[]{:S(2)}) collective-permute-start(f32[5,16,128]{2,1,0:T(8,128)S(1)} %add_add_fusion.1), channel_id=1, source_target_pairs={{192,0},{193,1},{194,2},{195,3}} | collective-permute-start | bytes 122888 | tf_op jit(solution)/shard_map/ppermute | solution.py:589
  27.7 6.5 %collective-permute-start.10 = (f32[5,16,128]{2,1,0:T(8,128)S(1)}, f32[5,16,128]{2,1,0:T(8,128)S(1)}, u32[]{:S(2)}, u32[]{:S(2)}) collective-permute-start(f32[5,16,128]{2,1,0:T(8,128)S(1)} %add_add_fusion.1), channel_id=1, source_target_pairs={{64,0},{65,1},{66,2},{67,3}} | collective-permute-start | bytes 122888 | tf_op jit(solution)/shard_map/ppermute | solution.py:589
  34.0 1.3 %collective-permute-start.13 = (bf16[5,16,128]{2,1,0:T(8,128)(2,1)S(1)}, bf16[5,16,128]{2,1,0:T(8,128)(2,1)S(1)}, u32[]{:S(2)}, u32[]{:S(2)}) collective-permute-start(bf16[5,16,128]{2,1,0:T(8,128)(2,1)S(1)} %get-tuple-element.53), channel_id=1, source_target_pairs={{0,4},{4,0},{8,12},{12,8},{16,20},{20,16},{24,28},{28,24},{32,36},... | collective-permute-start | bytes 61448 | tf_op jit(solution)/shard_map/ppermute | solution.py:652
  36.1 11.3 %collective-permute-start.15 = (bf16[5,16,768]{2,1,0:T(8,128)(2,1)S(1)}, bf16[5,16,768]{2,1,0:T(8,128)(2,1)S(1)}, u32[]{:S(2)}, u32[]{:S(2)}) collective-permute-start(bf16[5,16,768]{2,1,0:T(8,128)(2,1)S(1)} %get-tuple-element.59), channel_id=1, source_target_pairs={{0,2},{2,0},{1,3},{3,1},{4,6},{6,4},{5,7},{7,5},{8,10},{10,8},{9,1... | collective-permute-start | bytes 368648 | tf_op jit(solution)/shard_map/ppermute | solution.py:684
  38.9 8.4 %collective-permute-start.14 = (bf16[5,16,128]{2,1,0:T(8,128)(2,1)S(1)}, bf16[5,16,128]{2,1,0:T(8,128)(2,1)S(1)}, u32[]{:S(2)}, u32[]{:S(2)}) collective-permute-start(bf16[5,16,128]{2,1,0:T(8,128)(2,1)S(1)} %get-tuple-element.58), channel_id=1, source_target_pairs={{4,8},{8,4},{12,16},{16,12},{20,24},{24,20},{28,32},{32,28},{36,40... | collective-permute-start | bytes 61448 | tf_op jit(solution)/shard_map/ppermute | solution.py:653
  43.0 4.4 %collective-permute-start.16 = (bf16[5,16,128]{2,1,0:T(8,128)(2,1)S(1)}, bf16[5,16,128]{2,1,0:T(8,128)(2,1)S(1)}, u32[]{:S(2)}, u32[]{:S(2)}) collective-permute-start(bf16[5,16,128]{2,1,0:T(8,128)(2,1)S(1)} %get-tuple-element.60), channel_id=1, source_target_pairs={{0,1},{1,0},{2,3},{3,2},{4,5},{5,4},{6,7},{7,6},{8,9},{9,8},{10,11... | collective-permute-start | bytes 61448 | tf_op jit(solution)/shard_map/ppermute | solution.py:685
  (2 other events, 42.8 us)

commit v7 on v6

--- a/solution.py
+++ b/solution.py
@@ -585,8 +585,30 @@
     eddies, foot = mode_shape.shape[2:]
     plane_rows = mean_inflow.shape[3]
     faces = shape_of(FIELDS, 16, CELLS)
-    def gather_sum(value, offsets, roots):
-        parts = [lax.ppermute(value, "rans", [(r + o, r) for r in roots]) for o in offsets]
+    def slab(z, y, core):
+        return 8 * z + 2 * y + core
+
+    columns = ranks // 8
+    root_y = [0] + [1] * (columns - 1)
+    first_level = [
+        [
+            (slab(z, [y for y in range(4) if y != root_y[z]][turn], core), slab(z, root_y[z], core))
+            for z in range(columns)
+            for core in range(2)
+        ]
+        for turn in range(3)
+    ]
+    second_level = [
+        [
+            (slab(z + up, root_y[z + up], core), slab(z, root_y[z], 0))
+            for z in range(0, columns, 2)
+        ]
+        for up, core in ((0, 1), (1, 0), (1, 1))
+    ]
+    third_level = [[(slab(z, root_y[z], 0), 0)] for z in (2, 6, 4)]
+
+    def gather_sum(value, level):
+        parts = [lax.ppermute(value, "rans", pairs) for pairs in level]
         for part in parts:
             value = value + part
         return value
@@ -620,16 +642,16 @@
         cost_estimate=cost(5),
         name="prepare",
     )(mode_rows[0, 0].T, mode_seeds.reshape(1, eddies), mode_shape[0, 0].T, solution)
-    plane = gather_sum(plane, (2, 6, 4), [8 * z + c for z in range(8) for c in range(2)])
+    plane = gather_sum(plane, first_level)
     near = lax.ppermute(pitch, "pitch", swap)
     plane, chip, core, span = lax.optimization_barrier((plane, chip, core, span))
-    plane = gather_sum(plane, (1, 8, 9), [0, 16, 32, 48])
+    plane = gather_sum(plane, second_level)
     from_chip = lax.ppermute(chip, "rans", next_chip)
     core, span, near = lax.optimization_barrier((core, span, near))
     far = lax.ppermute(span, "span", swap)
     from_core = lax.ppermute(core, "rans", same_chip)
     plane, near, far, from_core = lax.optimization_barrier((plane, near, far, from_core))
-    plane = gather_sum(plane, (16, 48, 32), [0])
+    plane = gather_sum(plane, third_level)
 
     phase_one, trace_one, core, chip, pitch, span = pl.pallas_call(
         phase_one_kernel,

time: 52.2 us -> 51.7 us (level)
  the two profiles are of different devices: /device:TPU:121 before, /device:TPU:1 now
where the time goes in v7:
time: 51.7 us; the launch traced here: 51.4 us
  starting transfers between devices  27.7 us (54%)
  Pallas kernels  18.8 us (36%)
  waiting for transfers between devices  3.72 us (7%)
  other arithmetic  0.82 us (2%)
    ppermute x9, starting transfers between devices, gather_sum(): parts = [lax.ppermute(value, 'rans', pairs) for pairs in level]  14.7 us
    ppermute x2, starting transfers between devices, body(): from_chip = lax.ppermute(chip, 'rans', next_chip)  5.81 us
    pallas_call x1, Pallas kernels, body(): pl.pallas_call(phase_one_kernel, out_shape=(traces, traces) + sends, in_s...  5.59 us
    ppermute x2, starting transfers between devices, body(): near = lax.ppermute(pitch, 'pitch', swap)  5.13 us
    pallas_call x1, Pallas kernels, body(): pl.pallas_call(functools.partial(prepare_kernel, normalizer=float((plane_...  4.91 us
    pallas_call x1, Pallas kernels, body(): pl.pallas_call(outer_two_kernel, out_shape=traces, in_specs=[VMEM] * 12 +...  4.55 us
    pallas_call x1, Pallas kernels, body(): pl.pallas_call(inner_two_kernel, out_shape=shape_of(FIELDS, NODES, elemen...  2.95 us
    ppermute x2, waiting for transfers between devices, body(): far = lax.ppermute(span, 'span', swap)  2.68 us
  transfers between devices with their start and end apart: 17, of which 3 were waited for; matrix products, arithmetic and copies ran while one was open for 2% of the time, Pallas kernels for 17%

profile of v7, /device:TPU:1, one launch (start us, length us, event | category | flops | bytes accessed | tf_op | source)
XLA Modules:
  0.0 51.4 jit_solution(9193575441804229057)
XLA Ops:
  0.1 4.9 %prepare.1 = (f32[5,16,128]{2,1,0:T(8,128)}, bf16[5,16,128]{2,1,0:T(8,128)(2,1)}, bf16[5,16,128]{2,1,0:T(8,128)(2,1)}, bf16[5,16,768]{2,1,0:T(8,128)(2,1)}, bf16[5,16,128]{2,1,0:T(8,128)(2,1)}) custom-call(s32[64,256]{1,0:T(8,128)} %bitcast.18, s32[1,256]{1,0:T(1,128)} %bitcast.20, f32[64,256]{1,0:T(8,128)} %bitcast.19, bf16[5,64,1536]{2,1,0:T(8,128)(2,1)} %base_ref.1), custom_call_target="tpu_custom_call" | custom-call | flops 500000000 | bytes 15000000 | tf_op jit(solution)/shard_map/prepare/pallas_call | solution.py:626
  5.0 1.3 %collective-permute-start.2 = (f32[5,16,128]{2,1,0:T(8,128)}, f32[5,16,128]{2,1,0:T(8,128)S(1)}, u32[]{:S(2)}, u32[]{:S(2)}) collective-permute-start(f32[5,16,128]{2,1,0:T(8,128)} %get-tuple-element.33), channel_id=1, source_target_pairs={{24,0},{28,4},{56,40},{60,44},{88,72},{92,76},{120,104},{124,108},... | collective-permute-start | bytes 122888 | tf_op jit(solution)/shard_map/ppermute | solution.py:611
  6.3 1.3 %collective-permute-start.1 = (f32[5,16,128]{2,1,0:T(8,128)}, f32[5,16,128]{2,1,0:T(8,128)S(1)}, u32[]{:S(2)}, u32[]{:S(2)}) collective-permute-start(f32[5,16,128]{2,1,0:T(8,128)} %get-tuple-element.33), channel_id=1, source_target_pairs={{16,0},{20,4},{48,40},{52,44},{80,72},{84,76},{112,104},{116,108},... | collective-permute-start | bytes 122888 | tf_op jit(solution)/shard_map/ppermute | solution.py:611
  7.6 1.3 %collective-permute-start = (f32[5,16,128]{2,1,0:T(8,128)}, f32[5,16,128]{2,1,0:T(8,128)S(1)}, u32[]{:S(2)}, u32[]{:S(2)}) collective-permute-start(f32[5,16,128]{2,1,0:T(8,128)} %get-tuple-element.33), channel_id=1, source_target_pairs={{8,0},{12,4},{32,40},{36,44},{64,72},{68,76},{96,104},{100,108},{1... | collective-permute-start | bytes 122888 | tf_op jit(solution)/shard_map/ppermute | solution.py:611
  8.9 3.7 %collective-permute-start.6 = (bf16[5,16,768]{2,1,0:T(8,128)(2,1)}, bf16[5,16,768]{2,1,0:T(8,128)(2,1)S(1)}, u32[]{:S(2)}, u32[]{:S(2)}) collective-permute-start(bf16[5,16,768]{2,1,0:T(8,128)(2,1)} %get-tuple-element.40), channel_id=1, source_target_pairs={{0,2},{2,0},{1,3},{3,1},{4,6},{6,4},{5,7},{7,5},{8,10},{10,8},{9,1... | collective-permute-start | bytes 368648 | tf_op jit(solution)/shard_map/ppermute | solution.py:646
  12.6 0.2 collective-permute-done.1
  12.8 0.8 %add_add_fusion.2 = f32[5,16,128]{2,1,0:T(8,128)S(1)} fusion(f32[5,16,128]{2,1,0:T(8,128)S(1)} %collective-permute-done.2, f32[5,16,128]{2,1,0:T(8,128)S(1)} %collective-permute-done.1, f32[5,16,128]{2,1,0:T(8,128)} %get-tuple-element.33, f32[5,16,128]{2,1,0:T(8,128)S(1)} %collective-permute-done), kind=kLoop, calls=%fused_computation.2 | loop fusion | flops 30720 | bytes 204800 | tf_op jit(solution)/shard_map/add | solution.py:613
  13.5 0.7 %collective-permute-start.5 = (f32[5,16,128]{2,1,0:T(8,128)S(1)}, f32[5,16,128]{2,1,0:T(8,128)S(1)}, u32[]{:S(2)}, u32[]{:S(2)}) collective-permute-start(f32[5,16,128]{2,1,0:T(8,128)S(1)} %add_add_fusion.2), channel_id=1, source_target_pairs={{44,0},{108,72},{172,136},{236,200},{45,1},{109,73},{173,137},{237... | collective-permute-start | bytes 122888 | tf_op jit(solution)/shard_map/ppermute | solution.py:611
  14.2 0.7 %collective-permute-start.4 = (f32[5,16,128]{2,1,0:T(8,128)S(1)}, f32[5,16,128]{2,1,0:T(8,128)S(1)}, u32[]{:S(2)}, u32[]{:S(2)}) collective-permute-start(f32[5,16,128]{2,1,0:T(8,128)S(1)} %add_add_fusion.2), channel_id=1, source_target_pairs={{40,0},{104,72},{168,136},{232,200},{41,1},{105,73},{169,137},{233... | collective-permute-start | bytes 122888 | tf_op jit(solution)/shard_map/ppermute | solution.py:611
  14.9 7.5 %collective-permute-start.3 = (f32[5,16,128]{2,1,0:T(8,128)S(1)}, f32[5,16,128]{2,1,0:T(8,128)S(1)}, u32[]{:S(2)}, u32[]{:S(2)}) collective-permute-start(f32[5,16,128]{2,1,0:T(8,128)S(1)} %add_add_fusion.2), channel_id=1, source_target_pairs={{4,0},{76,72},{140,136},{204,200},{5,1},{77,73},{141,137},{205,201... | collective-permute-start | bytes 122888 | tf_op jit(solution)/shard_map/ppermute | solution.py:611
  22.5 1.9 %collective-permute-start.9 = (bf16[5,16,128]{2,1,0:T(8,128)(2,1)}, bf16[5,16,128]{2,1,0:T(8,128)(2,1)S(1)}, u32[]{:S(2)}, u32[]{:S(2)}) collective-permute-start(bf16[5,16,128]{2,1,0:T(8,128)(2,1)} %get-tuple-element.45), channel_id=1, source_target_pairs={{4,8},{8,4},{12,16},{16,12},{20,24},{24,20},{28,32},{32,28},{36,40... | collective-permute-start | bytes 61448 | tf_op jit(solution)/shard_map/ppermute | solution.py:649
  24.7 2.7 %collective-permute-done.7.far_ref = bf16[5,16,128]{2,1,0:T(8,128)(2,1)S(1)} collective-permute-done((bf16[5,16,128]{2,1,0:T(8,128)(2,1)}, bf16[5,16,128]{2,1,0:T(8,128)(2,1)S(1)}, u32[]{:S(2)}, u32[]{:S(2)}) %collective-permute-start.7) | collective-permute-done | bytes 20512 | tf_op jit(solution)/shard_map/ppermute | solution.py:651
  27.3 0.7 %collective-permute-start.12 = (f32[5,16,128]{2,1,0:T(8,128)S(1)}, f32[5,16,128]{2,1,0:T(8,128)S(1)}, u32[]{:S(2)}, u32[]{:S(2)}) collective-permute-start(f32[5,16,128]{2,1,0:T(8,128)S(1)} %add_add_fusion.1), channel_id=1, source_target_pairs={{136,0},{137,1},{138,2},{139,3}} | collective-permute-start | bytes 122888 | tf_op jit(solution)/shard_map/ppermute | solution.py:611
  28.0 0.7 %collective-permute-start.11 = (f32[5,16,128]{2,1,0:T(8,128)S(1)}, f32[5,16,128]{2,1,0:T(8,128)S(1)}, u32[]{:S(2)}, u32[]{:S(2)}) collective-permute-start(f32[5,16,128]{2,1,0:T(8,128)S(1)} %add_add_fusion.1), channel_id=1, source_target_pairs={{200,0},{201,1},{202,2},{203,3}} | collective-permute-start | bytes 122888 | tf_op jit(solution)/shard_map/ppermute | solution.py:611
  28.7 0.7 %collective-permute-start.10 = (f32[5,16,128]{2,1,0:T(8,128)S(1)}, f32[5,16,128]{2,1,0:T(8,128)S(1)}, u32[]{:S(2)}, u32[]{:S(2)}) collective-permute-start(f32[5,16,128]{2,1,0:T(8,128)S(1)} %add_add_fusion.1), channel_id=1, source_target_pairs={{72,0},{73,1},{74,2},{75,3}} | collective-permute-start | bytes 122888 | tf_op jit(solution)/shard_map/ppermute | solution.py:611
  29.4 5.6 %phase_one.1 = (bf16[5,64,1536]{2,1,0:T(8,128)(2,1)S(1)}, bf16[5,64,1536]{2,1,0:T(8,128)(2,1)S(1)}, bf16[5,16,128]{2,1,0:T(8,128)(2,1)S(1)}, bf16[5,16,128]{2,1,...) custom-call(bf16[5,64,1536]{2,1,0:T(8,128)(2,1)S(1)} %copy-done, ...), custom_call_target="tpu_custom_call" | custom-call | flops 600000000 | bytes 18000000 | tf_op jit(solution)/shard_map/phase_one/pallas_call | solution.py:656
  35.0 1.2 %collective-permute-start.13 = (bf16[5,16,128]{2,1,0:T(8,128)(2,1)S(1)}, bf16[5,16,128]{2,1,0:T(8,128)(2,1)S(1)}, u32[]{:S(2)}, u32[]{:S(2)}) collective-permute-start(bf16[5,16,128]{2,1,0:T(8,128)(2,1)S(1)} %get-tuple-element.53), channel_id=1, source_target_pairs={{0,4},{4,0},{8,12},{12,8},{16,20},{20,16},{24,28},{28,24},{32,36},... | collective-permute-start | bytes 61448 | tf_op jit(solution)/shard_map/ppermute | solution.py:674
  36.3 0.8 %collective-permute-done.13.from_core_ref = bf16[5,16,128]{2,1,0:T(8,128)(2,1)S(1)} collective-permute-done((bf16[5,16,128]{2,1,0:T(8,128)(2,1)S(1)}, bf16[5,16,128]{2,1,0:T(8,128)(2,1)S(1)}, u32[]{:S(2)}, u32[]{:S(2)}) %collective-permute-start.13) | collective-permute-done | bytes 20512 | tf_op jit(solution)/shard_map/ppermute | solution.py:674
  37.1 0.8 %inflow_layer.1 = (bf16[5,64,1536]{2,1,0:T(8,128)(2,1)S(1)}, bf16[5,64,1536]{2,1,0:T(8,128)(2,1)S(1)}, bf16[5,16,768]{2,1,0:T(8,128)(2,1)S(1)}, bf16[5,16,128]{2,1,0:T(8,128)(2,1)S(1)}) custom-call(bf16[5,64,1536]{2,1,0:T(8,128)(2,1)S(1)} %get-tuple-element.48.held_ref, ...), custom_call_target="tpu_custom_call", output_to_operand_aliasing={{0}: (0, {}), {1}: (1, {}), {2}: (2, {}), {3}: (3, {})} | custom-call | flops 10000000 | bytes 300000 | tf_op jit(solution)/shard_map/inflow_layer/pallas_call | solution.py:682
  37.9 1.5 %collective-permute-start.15 = (bf16[5,16,768]{2,1,0:T(8,128)(2,1)S(1)}, bf16[5,16,768]{2,1,0:T(8,128)(2,1)S(1)}, u32[]{:S(2)}, u32[]{:S(2)}) collective-permute-start(bf16[5,16,768]{2,1,0:T(8,128)(2,1)S(1)} %get-tuple-element.59), channel_id=1, source_target_pairs={{0,2},{2,0},{1,3},{3,1},{4,6},{6,4},{5,7},{7,5},{8,10},{10,8},{9,1... | collective-permute-start | bytes 368648 | tf_op jit(solution)/shard_map/ppermute | solution.py:706
  39.4 3.9 %collective-permute-start.14 = (bf16[5,16,128]{2,1,0:T(8,128)(2,1)S(1)}, bf16[5,16,128]{2,1,0:T(8,128)(2,1)S(1)}, u32[]{:S(2)}, u32[]{:S(2)}) collective-permute-start(bf16[5,16,128]{2,1,0:T(8,128)(2,1)S(1)} %get-tuple-element.58), channel_id=1, source_target_pairs={{4,8},{8,4},{12,16},{16,12},{20,24},{24,20},{28,32},{32,28},{36,40... | collective-permute-start | bytes 61448 | tf_op jit(solution)/shard_map/ppermute | solution.py:675
  43.3 0.6 %collective-permute-start.16 = (bf16[5,16,128]{2,1,0:T(8,128)(2,1)S(1)}, bf16[5,16,128]{2,1,0:T(8,128)(2,1)S(1)}, u32[]{:S(2)}, u32[]{:S(2)}) collective-permute-start(bf16[5,16,128]{2,1,0:T(8,128)(2,1)S(1)} %get-tuple-element.60), channel_id=1, source_target_pairs={{0,1},{1,0},{2,3},{3,2},{4,5},{5,4},{6,7},{7,6},{8,9},{9,8},{10,11... | collective-permute-start | bytes 61448 | tf_op jit(solution)/shard_map/ppermute | solution.py:707
  43.9 2.9 %inner_two.1.part_ref = f32[5,64,1536]{2,1,0:T(8,128)S(1)} custom-call(bf16[5,64,1536]{2,1,0:T(8,128)(2,1)S(1)} %get-tuple-element.55.v_ref, f32[5,3,5]{2,1,0:T(4,128)S(1)} %bitcast.16, bf16[3,64,64]{2,1,0:T(8,128)(2,1)S(1)} %copy-done.1), custom_call_target="tpu_custom_call" | custom-call | flops 10000000 | bytes 300000 | tf_op jit(solution)/shard_map/inner_two/pallas_call | solution.py:708
  46.9 4.5 %outer_two.1 = bf16[5,64,1536]{2,1,0:T(8,128)(2,1)} custom-call(bf16[5,64,1536]{2,1,0:T(8,128)(2,1)S(1)} %get-tuple-element.55.v_ref, bf16[5,64,1536]{2,1,0:T(8,128)(2,1)S(1)} %get-tuple-element.56.trace_ref, bf16[5,64,1536]{2,1,0:T(8,128)(2,1)S(1)} %copy-done, f32[5,64,1536]{2,1,0:T(8,128)S(1)} %inner_two.1.part_ref, f32[5,16,128]{2,1,0:T(8,128)S(1)} %bitcast.11, ...), custom_call_target="tpu_custom_call" | custom-call | flops 400000000 | bytes 12000000 | tf_op jit(solution)/shard_map/outer_two/pallas_call | solution.py:720
  (37 shorter events, 0.3 us)
Async XLA Ops:
  0.0 29.4 %copy-start.6 = (bf16[64,64]{1,0:T(8,128)(2,1)S(1)}, bf16[64,64]{1,0:T(8,128)(2,1)}, u32[]{:S(2)}) copy-start(bf16[64,64]{1,0:T(8,128)(2,1)} %wall_ref.5) | copy-start | bytes 24580
  0.0 29.4 %copy-start.7 = (bf16[64,64]{1,0:T(8,128)(2,1)S(1)}, bf16[64,64]{1,0:T(8,128)(2,1)}, u32[]{:S(2)}) copy-start(bf16[64,64]{1,0:T(8,128)(2,1)} %smooth_ref.1) | copy-start | bytes 24580
  0.0 29.4 %copy-start.5 = (bf16[64,96]{1,0:T(8,128)(2,1)S(1)}, bf16[64,96]{1,0:T(8,128)(2,1)}, u32[]{:S(2)}) copy-start(bf16[64,96]{1,0:T(8,128)(2,1)} %lift_ref.5) | copy-start | bytes 36868
  0.0 29.4 %copy-start.1 = (bf16[3,64,64]{2,1,0:T(8,128)(2,1)S(1)}, bf16[3,64,64]{2,1,0:T(8,128)(2,1)}, u32[]{:S(2)}) copy-start(bf16[3,64,64]{2,1,0:T(8,128)(2,1)} %volume_ref.5) | copy-start | bytes 73732
  0.0 29.4 %copy-start.4 = (f32[3,5,5]{2,0,1:T(4,128)S(1)}, f32[3,5,5]{2,0,1:T(4,128)}, u32[]{:S(2)}) copy-start(f32[3,5,5]{2,0,1:T(4,128)} %param.14) | copy-start | bytes 904
  0.0 37.1 %copy-start.2 = (f32[1,1,5,2048]{3,1,2,0:T(1,128)S(1)}, f32[1,1,5,2048]{3,1,2,0:T(1,128)}, u32[]{:S(2)}) copy-start(f32[1,1,5,2048]{3,1,2,0:T(1,128)} %param.22) | copy-start | bytes 122884
  0.1 37.0 %copy-start.3 = (f32[1,1,5,2048]{3,1,2,0:T(1,128)S(1)}, f32[1,1,5,2048]{3,1,2,0:T(1,128)}, u32[]{:S(2)}) copy-start(f32[1,1,5,2048]{3,1,2,0:T(1,128)} %param.23) | copy-start | bytes 122884
  5.0 7.6 %collective-permute-start.2 = (f32[5,16,128]{2,1,0:T(8,128)}, f32[5,16,128]{2,1,0:T(8,128)S(1)}, u32[]{:S(2)}, u32[]{:S(2)}) collective-permute-start(f32[5,16,128]{2,1,0:T(8,128)} %get-tuple-element.33), channel_id=1, source_target_pairs={{24,0},{28,4},{56,40},{60,44},{88,72},{92,76},{120,104},{124,108},... | collective-permute-start | bytes 122888 | tf_op jit(solution)/shard_map/ppermute | solution.py:611
  6.3 6.5 %collective-permute-start.1 = (f32[5,16,128]{2,1,0:T(8,128)}, f32[5,16,128]{2,1,0:T(8,128)S(1)}, u32[]{:S(2)}, u32[]{:S(2)}) collective-permute-start(f32[5,16,128]{2,1,0:T(8,128)} %get-tuple-element.33), channel_id=1, source_target_pairs={{16,0},{20,4},{48,40},{52,44},{80,72},{84,76},{112,104},{116,108},... | collective-permute-start | bytes 122888 | tf_op jit(solution)/shard_map/ppermute | solution.py:611
  7.6 5.2 %collective-permute-start = (f32[5,16,128]{2,1,0:T(8,128)}, f32[5,16,128]{2,1,0:T(8,128)S(1)}, u32[]{:S(2)}, u32[]{:S(2)}) collective-permute-start(f32[5,16,128]{2,1,0:T(8,128)} %get-tuple-element.33), channel_id=1, source_target_pairs={{8,0},{12,4},{32,40},{36,44},{64,72},{68,76},{96,104},{100,108},{1... | collective-permute-start | bytes 122888 | tf_op jit(solution)/shard_map/ppermute | solution.py:611
  8.9 15.5 %collective-permute-start.6 = (bf16[5,16,768]{2,1,0:T(8,128)(2,1)}, bf16[5,16,768]{2,1,0:T(8,128)(2,1)S(1)}, u32[]{:S(2)}, u32[]{:S(2)}) collective-permute-start(bf16[5,16,768]{2,1,0:T(8,128)(2,1)} %get-tuple-element.40), channel_id=1, source_target_pairs={{0,2},{2,0},{1,3},{3,1},{4,6},{6,4},{5,7},{7,5},{8,10},{10,8},{9,1... | collective-permute-start | bytes 368648 | tf_op jit(solution)/shard_map/ppermute | solution.py:646
  13.5 11.0 %collective-permute-start.5 = (f32[5,16,128]{2,1,0:T(8,128)S(1)}, f32[5,16,128]{2,1,0:T(8,128)S(1)}, u32[]{:S(2)}, u32[]{:S(2)}) collective-permute-start(f32[5,16,128]{2,1,0:T(8,128)S(1)} %add_add_fusion.2), channel_id=1, source_target_pairs={{44,0},{108,72},{172,136},{236,200},{45,1},{109,73},{173,137},{237... | collective-permute-start | bytes 122888 | tf_op jit(solution)/shard_map/ppermute | solution.py:611
  14.2 10.4 %collective-permute-start.4 = (f32[5,16,128]{2,1,0:T(8,128)S(1)}, f32[5,16,128]{2,1,0:T(8,128)S(1)}, u32[]{:S(2)}, u32[]{:S(2)}) collective-permute-start(f32[5,16,128]{2,1,0:T(8,128)S(1)} %add_add_fusion.2), channel_id=1, source_target_pairs={{40,0},{104,72},{168,136},{232,200},{41,1},{105,73},{169,137},{233... | collective-permute-start | bytes 122888 | tf_op jit(solution)/shard_map/ppermute | solution.py:611
  14.9 9.7 %collective-permute-start.3 = (f32[5,16,128]{2,1,0:T(8,128)S(1)}, f32[5,16,128]{2,1,0:T(8,128)S(1)}, u32[]{:S(2)}, u32[]{:S(2)}) collective-permute-start(f32[5,16,128]{2,1,0:T(8,128)S(1)} %add_add_fusion.2), channel_id=1, source_target_pairs={{4,0},{76,72},{140,136},{204,200},{5,1},{77,73},{141,137},{205,201... | collective-permute-start | bytes 122888 | tf_op jit(solution)/shard_map/ppermute | solution.py:611
  22.5 6.9 %collective-permute-start.9 = (bf16[5,16,128]{2,1,0:T(8,128)(2,1)}, bf16[5,16,128]{2,1,0:T(8,128)(2,1)S(1)}, u32[]{:S(2)}, u32[]{:S(2)}) collective-permute-start(bf16[5,16,128]{2,1,0:T(8,128)(2,1)} %get-tuple-element.45), channel_id=1, source_target_pairs={{4,8},{8,4},{12,16},{16,12},{20,24},{24,20},{28,32},{32,28},{36,40... | collective-permute-start | bytes 61448 | tf_op jit(solution)/shard_map/ppermute | solution.py:649
  24.4 2.9 %collective-permute-start.7 = (bf16[5,16,128]{2,1,0:T(8,128)(2,1)}, bf16[5,16,128]{2,1,0:T(8,128)(2,1)S(1)}, u32[]{:S(2)}, u32[]{:S(2)}) collective-permute-start(bf16[5,16,128]{2,1,0:T(8,128)(2,1)} %get-tuple-element.42), channel_id=1, source_target_pairs={{0,1},{1,0},{2,3},{3,2},{4,5},{5,4},{6,7},{7,6},{8,9},{9,8},{10,11... | collective-permute-start | bytes 61448 | tf_op jit(solution)/shard_map/ppermute | solution.py:651
  24.5 2.8 %collective-permute-start.8 = (bf16[5,16,128]{2,1,0:T(8,128)(2,1)}, bf16[5,16,128]{2,1,0:T(8,128)(2,1)S(1)}, u32[]{:S(2)}, u32[]{:S(2)}) collective-permute-start(bf16[5,16,128]{2,1,0:T(8,128)(2,1)} %get-tuple-element.43), channel_id=1, source_target_pairs={{0,4},{4,0},{8,12},{12,8},{16,20},{20,16},{24,28},{28,24},{32,36},... | collective-permute-start | bytes 61448 | tf_op jit(solution)/shard_map/ppermute | solution.py:652
  27.3 8.9 %collective-permute-start.12 = (f32[5,16,128]{2,1,0:T(8,128)S(1)}, f32[5,16,128]{2,1,0:T(8,128)S(1)}, u32[]{:S(2)}, u32[]{:S(2)}) collective-permute-start(f32[5,16,128]{2,1,0:T(8,128)S(1)} %add_add_fusion.1), channel_id=1, source_target_pairs={{136,0},{137,1},{138,2},{139,3}} | collective-permute-start | bytes 122888 | tf_op jit(solution)/shard_map/ppermute | solution.py:611
  28.0 8.3 %collective-permute-start.11 = (f32[5,16,128]{2,1,0:T(8,128)S(1)}, f32[5,16,128]{2,1,0:T(8,128)S(1)}, u32[]{:S(2)}, u32[]{:S(2)}) collective-permute-start(f32[5,16,128]{2,1,0:T(8,128)S(1)} %add_add_fusion.1), channel_id=1, source_target_pairs={{200,0},{201,1},{202,2},{203,3}} | collective-permute-start | bytes 122888 | tf_op jit(solution)/shard_map/ppermute | solution.py:611
  28.7 7.6 %collective-permute-start.10 = (f32[5,16,128]{2,1,0:T(8,128)S(1)}, f32[5,16,128]{2,1,0:T(8,128)S(1)}, u32[]{:S(2)}, u32[]{:S(2)}) collective-permute-start(f32[5,16,128]{2,1,0:T(8,128)S(1)} %add_add_fusion.1), channel_id=1, source_target_pairs={{72,0},{73,1},{74,2},{75,3}} | collective-permute-start | bytes 122888 | tf_op jit(solution)/shard_map/ppermute | solution.py:611
  35.0 2.1 %collective-permute-start.13 = (bf16[5,16,128]{2,1,0:T(8,128)(2,1)S(1)}, bf16[5,16,128]{2,1,0:T(8,128)(2,1)S(1)}, u32[]{:S(2)}, u32[]{:S(2)}) collective-permute-start(bf16[5,16,128]{2,1,0:T(8,128)(2,1)S(1)} %get-tuple-element.53), channel_id=1, source_target_pairs={{0,4},{4,0},{8,12},{12,8},{16,20},{20,16},{24,28},{28,24},{32,36},... | collective-permute-start | bytes 61448 | tf_op jit(solution)/shard_map/ppermute | solution.py:674
  37.9 8.9 %collective-permute-start.15 = (bf16[5,16,768]{2,1,0:T(8,128)(2,1)S(1)}, bf16[5,16,768]{2,1,0:T(8,128)(2,1)S(1)}, u32[]{:S(2)}, u32[]{:S(2)}) collective-permute-start(bf16[5,16,768]{2,1,0:T(8,128)(2,1)S(1)} %get-tuple-element.59), channel_id=1, source_target_pairs={{0,2},{2,0},{1,3},{3,1},{4,6},{6,4},{5,7},{7,5},{8,10},{10,8},{9,1... | collective-permute-start | bytes 368648 | tf_op jit(solution)/shard_map/ppermute | solution.py:706
  39.4 7.4 %collective-permute-start.14 = (bf16[5,16,128]{2,1,0:T(8,128)(2,1)S(1)}, bf16[5,16,128]{2,1,0:T(8,128)(2,1)S(1)}, u32[]{:S(2)}, u32[]{:S(2)}) collective-permute-start(bf16[5,16,128]{2,1,0:T(8,128)(2,1)S(1)} %get-tuple-element.58), channel_id=1, source_target_pairs={{4,8},{8,4},{12,16},{16,12},{20,24},{24,20},{28,32},{32,28},{36,40... | collective-permute-start | bytes 61448 | tf_op jit(solution)/shard_map/ppermute | solution.py:675
  43.3 3.5 %collective-permute-start.16 = (bf16[5,16,128]{2,1,0:T(8,128)(2,1)S(1)}, bf16[5,16,128]{2,1,0:T(8,128)(2,1)S(1)}, u32[]{:S(2)}, u32[]{:S(2)}) collective-permute-start(bf16[5,16,128]{2,1,0:T(8,128)(2,1)S(1)} %get-tuple-element.60), channel_id=1, source_target_pairs={{0,1},{1,0},{2,3},{3,2},{4,5},{5,4},{6,7},{7,6},{8,9},{9,8},{10,11... | collective-permute-start | bytes 61448 | tf_op jit(solution)/shard_map/ppermute | solution.py:707
  (2 other events, 51.8 us)

commit v8 on v7

--- a/solution.py
+++ b/solution.py
@@ -117,26 +117,30 @@
     return lambda f: jnp.where(even, near_chip_ref[f].astype(f32), far_chip_ref[f].astype(f32))
 
 
-def prepare_kernel(
-    rows_hbm, seeds_hbm, shape_hbm, v_hbm, plane_ref, core_ref, chip_ref, pitch_ref,
-    span_ref, rows_ref, seeds_ref, shape_ref, v_ref, span_held, sems, *, normalizer,
+def plane_kernel(
+    rows_hbm, seeds_hbm, shape_hbm, plane_ref, rows_ref, seeds_ref, shape_ref, sems, *, normalizer
 ):
     copies = [
         pltpu.make_async_copy(source, target, sems.at[i])
         for i, (source, target) in enumerate([
-            (rows_hbm, rows_ref), (seeds_hbm, seeds_ref), (shape_hbm, shape_ref), (v_hbm, v_ref),
+            (rows_hbm, rows_ref), (seeds_hbm, seeds_ref), (shape_hbm, shape_ref)
         ])
     ]
     for copy in copies:
         copy.start()
+    for copy in copies:
+        copy.wait()
+    sum_eddies(rows_ref, seeds_ref, shape_ref, plane_ref, normalizer)
+
+
+def pack_kernel(
+    plane_ref, v_ref, held_plane_ref, core_ref, chip_ref, pitch_ref, span_ref, span_held
+):
     first_span = lax.axis_index("span") == 0
     lane = lanes()
     pick = trace_selector()
+    held_plane_ref[...] = plane_ref[...]
     span_held[...] = jnp.zeros_like(span_held)
-    for copy in copies[:3]:
-        copy.wait()
-    sum_eddies(rows_ref, seeds_ref, shape_ref, plane_ref, normalizer)
-    copies[3].wait()
     for pair in range(EX // 2):
         at = slice(pair * PAIR, (pair + 1) * PAIR)
         for f in range(FIELDS):
@@ -607,8 +611,9 @@
     ]
     third_level = [[(slab(z, root_y[z], 0), 0)] for z in (2, 6, 4)]
 
-    def gather_sum(value, level):
+    def gather_sum(value, level, own=None):
         parts = [lax.ppermute(value, "rans", pairs) for pairs in level]
+        value = value if own is None else own
         for part in parts:
             value = value + part
         return value
@@ -623,26 +628,34 @@
     next_chip = [(a + 1, b + 1) for a, b in same_chip if max(a, b) + 1 < ranks]
 
     span_scratch = pltpu.VMEM((FIELDS, 16, CELLS), f32)
-    plane, core, chip, pitch, span = pl.pallas_call(
+    plane = pl.pallas_call(
         functools.partial(
-            prepare_kernel, normalizer=float((plane_rows / (eddies * ranks * foot)) ** 0.5)
+            plane_kernel, normalizer=float((plane_rows / (eddies * ranks * foot)) ** 0.5)
         ),
-        out_shape=(shape_of(FIELDS, 16, CELLS, dtype=f32),) + sends,
-        in_specs=[pl.BlockSpec(memory_space=pltpu.HBM)] * 4,
-        out_specs=(VMEM,) * 5,
+        out_shape=shape_of(FIELDS, 16, CELLS, dtype=f32),
+        in_specs=[pl.BlockSpec(memory_space=pltpu.HBM)] * 3,
+        out_specs=VMEM,
         scratch_shapes=[
             pltpu.VMEM((foot, eddies), jnp.int32),
             pltpu.VMEM((1, eddies), jnp.int32),
             pltpu.VMEM((foot, eddies), f32),
-            pltpu.VMEM(solution.shape, bf16),
-            span_scratch,
-            pltpu.SemaphoreType.DMA((4,)),
+            pltpu.SemaphoreType.DMA((3,)),
         ],
         compiler_params=pltpu.CompilerParams(vmem_limit_bytes=60 * 2**20),
-        cost_estimate=cost(5),
-        name="prepare",
-    )(mode_rows[0, 0].T, mode_seeds.reshape(1, eddies), mode_shape[0, 0].T, solution)
-    plane = gather_sum(plane, first_level)
+        cost_estimate=cost(4),
+        name="eddy_plane",
+    )(mode_rows[0, 0].T, mode_seeds.reshape(1, eddies), mode_shape[0, 0].T)
+    held_plane, core, chip, pitch, span = pl.pallas_call(
+        pack_kernel,
+        out_shape=(shape_of(FIELDS, 16, CELLS, dtype=f32),) + sends,
+        in_specs=[VMEM] * 2,
+        out_specs=(VMEM,) * 5,
+        scratch_shapes=[span_scratch],
+        compiler_params=PARAMS,
+        cost_estimate=cost(1),
+        name="pack_faces",
+    )(plane, solution)
+    plane = gather_sum(plane, first_level, held_plane)
     near = lax.ppermute(pitch, "pitch", swap)
     plane, chip, core, span = lax.optimization_barrier((plane, chip, core, span))
     plane = gather_sum(plane, second_level)

time: 51.7 us -> 50.4 us (0.975)
  starting transfers between devices: 27.7 us -> 26.7 us
  local copies, waits for them, and re-layouts: 0.04 us -> 0.82 us
  other arithmetic: 0.82 us -> 0.05 us
    ppermute x9, starting transfers between devices: 14.7 us -> 13.8 us  [gather_sum(): parts = [lax.ppermute(value, 'rans', pairs) for pairs in level]]
    unnamed x18 -> x20, local copies, waits for them, and re-layouts: 0.04 us -> 0.81 us
    add x3, other arithmetic: 0.82 us -> 0.05 us  [gather_sum(): value = value + part]
    pallas_call x1 -> x2, Pallas kernels: 4.91 us -> 4.88 us  [the longest x1 4.41 us: body(): pl.pallas_call(functools.partial(plane_kernel, normalizer=float((plane_ro...]
  transfers between devices with their start and end apart: 17 -> 17, of which waited for: 3 -> 2; matrix products, arithmetic and copies ran while one was open for 2% -> 0% of each run, Pallas kernels for 17% -> 18%
where the time goes in v8:
time: 50.4 us; the launch traced here: 50 us
  starting transfers between devices  26.7 us (53%)
  Pallas kernels  18.8 us (37%)
  waiting for transfers between devices  3.32 us (7%)
  local copies, waits for them, and re-layouts  0.82 us (2%)
    ppermute x9, starting transfers between devices, gather_sum(): parts = [lax.ppermute(value, 'rans', pairs) for pairs in level]  13.8 us
    ppermute x2, starting transfers between devices, body(): from_chip = lax.ppermute(chip, 'rans', next_chip)  5.79 us
    pallas_call x1, Pallas kernels, body(): pl.pallas_call(phase_one_kernel, out_shape=(traces, traces) + sends, in_s...  5.59 us
    ppermute x2, starting transfers between devices, body(): near = lax.ppermute(pitch, 'pitch', swap)  5.13 us
    pallas_call x1, Pallas kernels, body(): pl.pallas_call(outer_two_kernel, out_shape=traces, in_specs=[VMEM] * 12 +...  4.56 us
    pallas_call x1, Pallas kernels, body(): pl.pallas_call(functools.partial(plane_kernel, normalizer=float((plane_ro...  4.41 us
    pallas_call x1, Pallas kernels, body(): pl.pallas_call(inner_two_kernel, out_shape=shape_of(FIELDS, NODES, elemen...  2.95 us
    ppermute x2, waiting for transfers between devices, body(): far = lax.ppermute(span, 'span', swap)  2.47 us
  transfers between devices with their start and end apart: 17, of which 2 were waited for; matrix products, arithmetic and copies ran while one was open for 0% of the time, Pallas kernels for 18%

profile of v8, /device:TPU:1, one launch (start us, length us, event | category | flops | bytes accessed | tf_op | source)
XLA Modules:
  0.0 50.0 jit_solution(1262356259170807322)
XLA Ops:
  0.0 4.4 %eddy_plane.1.plane_ref = f32[5,16,128]{2,1,0:T(8,128)} custom-call(s32[64,256]{1,0:T(8,128)} %bitcast.18, s32[1,256]{1,0:T(1,128)} %bitcast.20, f32[64,256]{1,0:T(8,128)} %bitcast.19), custom_call_target="tpu_custom_call" | custom-call | flops 400000000 | bytes 12000000 | tf_op jit(solution)/shard_map/eddy_plane/pallas_call | solution.py:631
  4.5 1.4 %collective-permute-start.2 = (f32[5,16,128]{2,1,0:T(8,128)}, f32[5,16,128]{2,1,0:T(8,128)S(1)}, u32[]{:S(2)}, u32[]{:S(2)}) collective-permute-start(f32[5,16,128]{2,1,0:T(8,128)} %eddy_plane.1.plane_ref), channel_id=1, source_target_pairs={{24,0},{28,4},{56,40},{60,44},{88,72},{92,76},{120,104},{124,108},... | collective-permute-start | bytes 122888 | tf_op jit(solution)/shard_map/ppermute | solution.py:615
  5.9 1.3 %collective-permute-start.1 = (f32[5,16,128]{2,1,0:T(8,128)}, f32[5,16,128]{2,1,0:T(8,128)S(1)}, u32[]{:S(2)}, u32[]{:S(2)}) collective-permute-start(f32[5,16,128]{2,1,0:T(8,128)} %eddy_plane.1.plane_ref), channel_id=1, source_target_pairs={{16,0},{20,4},{48,40},{52,44},{80,72},{84,76},{112,104},{116,108},... | collective-permute-start | bytes 122888 | tf_op jit(solution)/shard_map/ppermute | solution.py:615
  7.2 1.3 %collective-permute-start = (f32[5,16,128]{2,1,0:T(8,128)}, f32[5,16,128]{2,1,0:T(8,128)S(1)}, u32[]{:S(2)}, u32[]{:S(2)}) collective-permute-start(f32[5,16,128]{2,1,0:T(8,128)} %eddy_plane.1.plane_ref), channel_id=1, source_target_pairs={{8,0},{12,4},{32,40},{36,44},{64,72},{68,76},{96,104},{100,108},{1... | collective-permute-start | bytes 122888 | tf_op jit(solution)/shard_map/ppermute | solution.py:615
  8.5 0.8 %copy-done.8 = f32[5,16,128]{2,1,0:T(8,128)S(1)} copy-done((f32[5,16,128]{2,1,0:T(8,128)S(1)}, f32[5,16,128]{2,1,0:T(8,128)}, u32[]{:S(2)}) %copy-start.8) | copy-done | bytes 40984
  9.3 0.5 pack_faces.1
  9.8 3.7 %collective-permute-start.6 = (bf16[5,16,768]{2,1,0:T(8,128)(2,1)S(1)}, bf16[5,16,768]{2,1,0:T(8,128)(2,1)S(1)}, u32[]{:S(2)}, u32[]{:S(2)}) collective-permute-start(bf16[5,16,768]{2,1,0:T(8,128)(2,1)S(1)} %get-tuple-element.40), channel_id=1, source_target_pairs={{0,2},{2,0},{1,3},{3,1},{4,6},{6,4},{5,7},{7,5},{8,10},{10,8},{9,1... | collective-permute-start | bytes 368648 | tf_op jit(solution)/shard_map/ppermute | solution.py:659
  13.5 0.7 %collective-permute-start.5 = (f32[5,16,128]{2,1,0:T(8,128)S(1)}, f32[5,16,128]{2,1,0:T(8,128)S(1)}, u32[]{:S(2)}, u32[]{:S(2)}) collective-permute-start(f32[5,16,128]{2,1,0:T(8,128)S(1)} %add_add_fusion.2), channel_id=1, source_target_pairs={{44,0},{108,72},{172,136},{236,200},{45,1},{109,73},{173,137},{237... | collective-permute-start | bytes 122888 | tf_op jit(solution)/shard_map/ppermute | solution.py:615
  14.2 0.7 %collective-permute-start.4 = (f32[5,16,128]{2,1,0:T(8,128)S(1)}, f32[5,16,128]{2,1,0:T(8,128)S(1)}, u32[]{:S(2)}, u32[]{:S(2)}) collective-permute-start(f32[5,16,128]{2,1,0:T(8,128)S(1)} %add_add_fusion.2), channel_id=1, source_target_pairs={{40,0},{104,72},{168,136},{232,200},{41,1},{105,73},{169,137},{233... | collective-permute-start | bytes 122888 | tf_op jit(solution)/shard_map/ppermute | solution.py:615
  14.8 6.5 %collective-permute-start.3 = (f32[5,16,128]{2,1,0:T(8,128)S(1)}, f32[5,16,128]{2,1,0:T(8,128)S(1)}, u32[]{:S(2)}, u32[]{:S(2)}) collective-permute-start(f32[5,16,128]{2,1,0:T(8,128)S(1)} %add_add_fusion.2), channel_id=1, source_target_pairs={{4,0},{76,72},{140,136},{204,200},{5,1},{77,73},{141,137},{205,201... | collective-permute-start | bytes 122888 | tf_op jit(solution)/shard_map/ppermute | solution.py:615
  21.3 1.9 %collective-permute-start.9 = (bf16[5,16,128]{2,1,0:T(8,128)(2,1)S(1)}, bf16[5,16,128]{2,1,0:T(8,128)(2,1)S(1)}, u32[]{:S(2)}, u32[]{:S(2)}) collective-permute-start(bf16[5,16,128]{2,1,0:T(8,128)(2,1)S(1)} %get-tuple-element.45), channel_id=1, source_target_pairs={{4,8},{8,4},{12,16},{16,12},{20,24},{24,20},{28,32},{32,28},{36,40... | collective-permute-start | bytes 61448 | tf_op jit(solution)/shard_map/ppermute | solution.py:662
  23.5 2.5 %collective-permute-done.7.far_ref = bf16[5,16,128]{2,1,0:T(8,128)(2,1)S(1)} collective-permute-done((bf16[5,16,128]{2,1,0:T(8,128)(2,1)S(1)}, bf16[5,16,128]{2,1,0:T(8,128)(2,1)S(1)}, u32[]{:S(2)}, u32[]{:S(2)}) %collective-permute-start.7) | collective-permute-done | bytes 20512 | tf_op jit(solution)/shard_map/ppermute | solution.py:664
  26.0 0.7 %collective-permute-start.12 = (f32[5,16,128]{2,1,0:T(8,128)S(1)}, f32[5,16,128]{2,1,0:T(8,128)S(1)}, u32[]{:S(2)}, u32[]{:S(2)}) collective-permute-start(f32[5,16,128]{2,1,0:T(8,128)S(1)} %add_add_fusion.1), channel_id=1, source_target_pairs={{136,0},{137,1},{138,2},{139,3}} | collective-permute-start | bytes 122888 | tf_op jit(solution)/shard_map/ppermute | solution.py:615
  26.6 0.7 %collective-permute-start.11 = (f32[5,16,128]{2,1,0:T(8,128)S(1)}, f32[5,16,128]{2,1,0:T(8,128)S(1)}, u32[]{:S(2)}, u32[]{:S(2)}) collective-permute-start(f32[5,16,128]{2,1,0:T(8,128)S(1)} %add_add_fusion.1), channel_id=1, source_target_pairs={{200,0},{201,1},{202,2},{203,3}} | collective-permute-start | bytes 122888 | tf_op jit(solution)/shard_map/ppermute | solution.py:615
  27.3 0.7 %collective-permute-start.10 = (f32[5,16,128]{2,1,0:T(8,128)S(1)}, f32[5,16,128]{2,1,0:T(8,128)S(1)}, u32[]{:S(2)}, u32[]{:S(2)}) collective-permute-start(f32[5,16,128]{2,1,0:T(8,128)S(1)} %add_add_fusion.1), channel_id=1, source_target_pairs={{72,0},{73,1},{74,2},{75,3}} | collective-permute-start | bytes 122888 | tf_op jit(solution)/shard_map/ppermute | solution.py:615
  28.0 5.6 %phase_one.1 = (bf16[5,64,1536]{2,1,0:T(8,128)(2,1)S(1)}, bf16[5,64,1536]{2,1,0:T(8,128)(2,1)S(1)}, bf16[5,16,128]{2,1,0:T(8,128)(2,1)S(1)}, bf16[5,16,128]{2,1,...) custom-call(bf16[5,64,1536]{2,1,0:T(8,128)(2,1)S(1)} %copy-done, ...), custom_call_target="tpu_custom_call" | custom-call | flops 600000000 | bytes 18000000 | tf_op jit(solution)/shard_map/phase_one/pallas_call | solution.py:669
  33.6 1.2 %collective-permute-start.13 = (bf16[5,16,128]{2,1,0:T(8,128)(2,1)S(1)}, bf16[5,16,128]{2,1,0:T(8,128)(2,1)S(1)}, u32[]{:S(2)}, u32[]{:S(2)}) collective-permute-start(bf16[5,16,128]{2,1,0:T(8,128)(2,1)S(1)} %get-tuple-element.53), channel_id=1, source_target_pairs={{0,4},{4,0},{8,12},{12,8},{16,20},{20,16},{24,28},{28,24},{32,36},... | collective-permute-start | bytes 61448 | tf_op jit(solution)/shard_map/ppermute | solution.py:687
  34.9 0.8 %collective-permute-done.13.from_core_ref = bf16[5,16,128]{2,1,0:T(8,128)(2,1)S(1)} collective-permute-done((bf16[5,16,128]{2,1,0:T(8,128)(2,1)S(1)}, bf16[5,16,128]{2,1,0:T(8,128)(2,1)S(1)}, u32[]{:S(2)}, u32[]{:S(2)}) %collective-permute-start.13) | collective-permute-done | bytes 20512 | tf_op jit(solution)/shard_map/ppermute | solution.py:687
  35.7 0.8 %inflow_layer.1 = (bf16[5,64,1536]{2,1,0:T(8,128)(2,1)S(1)}, bf16[5,64,1536]{2,1,0:T(8,128)(2,1)S(1)}, bf16[5,16,768]{2,1,0:T(8,128)(2,1)S(1)}, bf16[5,16,128]{2,1,0:T(8,128)(2,1)S(1)}) custom-call(bf16[5,64,1536]{2,1,0:T(8,128)(2,1)S(1)} %get-tuple-element.48.held_ref, ...), custom_call_target="tpu_custom_call", output_to_operand_aliasing={{0}: (0, {}), {1}: (1, {}), {2}: (2, {}), {3}: (3, {})} | custom-call | flops 10000000 | bytes 300000 | tf_op jit(solution)/shard_map/inflow_layer/pallas_call | solution.py:695
  36.6 1.5 %collective-permute-start.15 = (bf16[5,16,768]{2,1,0:T(8,128)(2,1)S(1)}, bf16[5,16,768]{2,1,0:T(8,128)(2,1)S(1)}, u32[]{:S(2)}, u32[]{:S(2)}) collective-permute-start(bf16[5,16,768]{2,1,0:T(8,128)(2,1)S(1)} %get-tuple-element.59), channel_id=1, source_target_pairs={{0,2},{2,0},{1,3},{3,1},{4,6},{6,4},{5,7},{7,5},{8,10},{10,8},{9,1... | collective-permute-start | bytes 368648 | tf_op jit(solution)/shard_map/ppermute | solution.py:719
  38.0 3.9 %collective-permute-start.14 = (bf16[5,16,128]{2,1,0:T(8,128)(2,1)S(1)}, bf16[5,16,128]{2,1,0:T(8,128)(2,1)S(1)}, u32[]{:S(2)}, u32[]{:S(2)}) collective-permute-start(bf16[5,16,128]{2,1,0:T(8,128)(2,1)S(1)} %get-tuple-element.58), channel_id=1, source_target_pairs={{4,8},{8,4},{12,16},{16,12},{20,24},{24,20},{28,32},{32,28},{36,40... | collective-permute-start | bytes 61448 | tf_op jit(solution)/shard_map/ppermute | solution.py:688
  41.9 0.6 %collective-permute-start.16 = (bf16[5,16,128]{2,1,0:T(8,128)(2,1)S(1)}, bf16[5,16,128]{2,1,0:T(8,128)(2,1)S(1)}, u32[]{:S(2)}, u32[]{:S(2)}) collective-permute-start(bf16[5,16,128]{2,1,0:T(8,128)(2,1)S(1)} %get-tuple-element.60), channel_id=1, source_target_pairs={{0,1},{1,0},{2,3},{3,2},{4,5},{5,4},{6,7},{7,6},{8,9},{9,8},{10,11... | collective-permute-start | bytes 61448 | tf_op jit(solution)/shard_map/ppermute | solution.py:720
  42.5 3.0 %inner_two.1.part_ref = f32[5,64,1536]{2,1,0:T(8,128)S(1)} custom-call(bf16[5,64,1536]{2,1,0:T(8,128)(2,1)S(1)} %get-tuple-element.55.v_ref, f32[5,3,5]{2,1,0:T(4,128)S(1)} %bitcast.16, bf16[3,64,64]{2,1,0:T(8,128)(2,1)S(1)} %copy-done.1), custom_call_target="tpu_custom_call" | custom-call | flops 10000000 | bytes 300000 | tf_op jit(solution)/shard_map/inner_two/pallas_call | solution.py:721
  45.5 4.6 %outer_two.1 = bf16[5,64,1536]{2,1,0:T(8,128)(2,1)} custom-call(bf16[5,64,1536]{2,1,0:T(8,128)(2,1)S(1)} %get-tuple-element.55.v_ref, bf16[5,64,1536]{2,1,0:T(8,128)(2,1)S(1)} %get-tuple-element.56.trace_ref, bf16[5,64,1536]{2,1,0:T(8,128)(2,1)S(1)} %copy-done, f32[5,64,1536]{2,1,0:T(8,128)S(1)} %inner_two.1.part_ref, f32[5,16,128]{2,1,0:T(8,128)S(1)} %bitcast.11, ...), custom_call_target="tpu_custom_call" | custom-call | flops 400000000 | bytes 12000000 | tf_op jit(solution)/shard_map/outer_two/pallas_call | solution.py:733
  (40 shorter events, 0.3 us)
Async XLA Ops:
  0.0 28.0 %copy-start.6 = (bf16[64,64]{1,0:T(8,128)(2,1)S(1)}, bf16[64,64]{1,0:T(8,128)(2,1)}, u32[]{:S(2)}) copy-start(bf16[64,64]{1,0:T(8,128)(2,1)} %wall_ref.5) | copy-start | bytes 24580
  0.0 28.0 %copy-start.7 = (bf16[64,64]{1,0:T(8,128)(2,1)S(1)}, bf16[64,64]{1,0:T(8,128)(2,1)}, u32[]{:S(2)}) copy-start(bf16[64,64]{1,0:T(8,128)(2,1)} %smooth_ref.1) | copy-start | bytes 24580
  0.0 28.0 %copy-start.5 = (bf16[64,96]{1,0:T(8,128)(2,1)S(1)}, bf16[64,96]{1,0:T(8,128)(2,1)}, u32[]{:S(2)}) copy-start(bf16[64,96]{1,0:T(8,128)(2,1)} %lift_ref.5) | copy-start | bytes 36868
  0.0 28.0 %copy-start.1 = (bf16[3,64,64]{2,1,0:T(8,128)(2,1)S(1)}, bf16[3,64,64]{2,1,0:T(8,128)(2,1)}, u32[]{:S(2)}) copy-start(bf16[3,64,64]{2,1,0:T(8,128)(2,1)} %volume_ref.5) | copy-start | bytes 73732
  0.0 28.0 %copy-start.4 = (f32[3,5,5]{2,0,1:T(4,128)S(1)}, f32[3,5,5]{2,0,1:T(4,128)}, u32[]{:S(2)}) copy-start(f32[3,5,5]{2,0,1:T(4,128)} %param.14) | copy-start | bytes 904
  4.5 31.3 %copy-start.2 = (f32[1,1,5,2048]{3,1,2,0:T(1,128)S(1)}, f32[1,1,5,2048]{3,1,2,0:T(1,128)}, u32[]{:S(2)}) copy-start(f32[1,1,5,2048]{3,1,2,0:T(1,128)} %param.22) | copy-start | bytes 122884
  4.5 31.3 %copy-start.3 = (f32[1,1,5,2048]{3,1,2,0:T(1,128)S(1)}, f32[1,1,5,2048]{3,1,2,0:T(1,128)}, u32[]{:S(2)}) copy-start(f32[1,1,5,2048]{3,1,2,0:T(1,128)} %param.23) | copy-start | bytes 122884
  4.5 9.0 %collective-permute-start.2 = (f32[5,16,128]{2,1,0:T(8,128)}, f32[5,16,128]{2,1,0:T(8,128)S(1)}, u32[]{:S(2)}, u32[]{:S(2)}) collective-permute-start(f32[5,16,128]{2,1,0:T(8,128)} %eddy_plane.1.plane_ref), channel_id=1, source_target_pairs={{24,0},{28,4},{56,40},{60,44},{88,72},{92,76},{120,104},{124,108},... | collective-permute-start | bytes 122888 | tf_op jit(solution)/shard_map/ppermute | solution.py:615
  5.9 7.5 %collective-permute-start.1 = (f32[5,16,128]{2,1,0:T(8,128)}, f32[5,16,128]{2,1,0:T(8,128)S(1)}, u32[]{:S(2)}, u32[]{:S(2)}) collective-permute-start(f32[5,16,128]{2,1,0:T(8,128)} %eddy_plane.1.plane_ref), channel_id=1, source_target_pairs={{16,0},{20,4},{48,40},{52,44},{80,72},{84,76},{112,104},{116,108},... | collective-permute-start | bytes 122888 | tf_op jit(solution)/shard_map/ppermute | solution.py:615
  7.2 6.2 %collective-permute-start = (f32[5,16,128]{2,1,0:T(8,128)}, f32[5,16,128]{2,1,0:T(8,128)S(1)}, u32[]{:S(2)}, u32[]{:S(2)}) collective-permute-start(f32[5,16,128]{2,1,0:T(8,128)} %eddy_plane.1.plane_ref), channel_id=1, source_target_pairs={{8,0},{12,4},{32,40},{36,44},{64,72},{68,76},{96,104},{100,108},{1... | collective-permute-start | bytes 122888 | tf_op jit(solution)/shard_map/ppermute | solution.py:615
  9.8 13.5 %collective-permute-start.6 = (bf16[5,16,768]{2,1,0:T(8,128)(2,1)S(1)}, bf16[5,16,768]{2,1,0:T(8,128)(2,1)S(1)}, u32[]{:S(2)}, u32[]{:S(2)}) collective-permute-start(bf16[5,16,768]{2,1,0:T(8,128)(2,1)S(1)} %get-tuple-element.40), channel_id=1, source_target_pairs={{0,2},{2,0},{1,3},{3,1},{4,6},{6,4},{5,7},{7,5},{8,10},{10,8},{9,1... | collective-permute-start | bytes 368648 | tf_op jit(solution)/shard_map/ppermute | solution.py:659
  13.5 9.9 %collective-permute-start.5 = (f32[5,16,128]{2,1,0:T(8,128)S(1)}, f32[5,16,128]{2,1,0:T(8,128)S(1)}, u32[]{:S(2)}, u32[]{:S(2)}) collective-permute-start(f32[5,16,128]{2,1,0:T(8,128)S(1)} %add_add_fusion.2), channel_id=1, source_target_pairs={{44,0},{108,72},{172,136},{236,200},{45,1},{109,73},{173,137},{237... | collective-permute-start | bytes 122888 | tf_op jit(solution)/shard_map/ppermute | solution.py:615
  14.2 9.3 %collective-permute-start.4 = (f32[5,16,128]{2,1,0:T(8,128)S(1)}, f32[5,16,128]{2,1,0:T(8,128)S(1)}, u32[]{:S(2)}, u32[]{:S(2)}) collective-permute-start(f32[5,16,128]{2,1,0:T(8,128)S(1)} %add_add_fusion.2), channel_id=1, source_target_pairs={{40,0},{104,72},{168,136},{232,200},{41,1},{105,73},{169,137},{233... | collective-permute-start | bytes 122888 | tf_op jit(solution)/shard_map/ppermute | solution.py:615
  14.8 8.7 %collective-permute-start.3 = (f32[5,16,128]{2,1,0:T(8,128)S(1)}, f32[5,16,128]{2,1,0:T(8,128)S(1)}, u32[]{:S(2)}, u32[]{:S(2)}) collective-permute-start(f32[5,16,128]{2,1,0:T(8,128)S(1)} %add_add_fusion.2), channel_id=1, source_target_pairs={{4,0},{76,72},{140,136},{204,200},{5,1},{77,73},{141,137},{205,201... | collective-permute-start | bytes 122888 | tf_op jit(solution)/shard_map/ppermute | solution.py:615
  21.3 6.7 %collective-permute-start.9 = (bf16[5,16,128]{2,1,0:T(8,128)(2,1)S(1)}, bf16[5,16,128]{2,1,0:T(8,128)(2,1)S(1)}, u32[]{:S(2)}, u32[]{:S(2)}) collective-permute-start(bf16[5,16,128]{2,1,0:T(8,128)(2,1)S(1)} %get-tuple-element.45), channel_id=1, source_target_pairs={{4,8},{8,4},{12,16},{16,12},{20,24},{24,20},{28,32},{32,28},{36,40... | collective-permute-start | bytes 61448 | tf_op jit(solution)/shard_map/ppermute | solution.py:662
  23.3 2.7 %collective-permute-start.7 = (bf16[5,16,128]{2,1,0:T(8,128)(2,1)S(1)}, bf16[5,16,128]{2,1,0:T(8,128)(2,1)S(1)}, u32[]{:S(2)}, u32[]{:S(2)}) collective-permute-start(bf16[5,16,128]{2,1,0:T(8,128)(2,1)S(1)} %get-tuple-element.42), channel_id=1, source_target_pairs={{0,1},{1,0},{2,3},{3,2},{4,5},{5,4},{6,7},{7,6},{8,9},{9,8},{10,11... | collective-permute-start | bytes 61448 | tf_op jit(solution)/shard_map/ppermute | solution.py:664
  23.4 2.6 %collective-permute-start.8 = (bf16[5,16,128]{2,1,0:T(8,128)(2,1)S(1)}, bf16[5,16,128]{2,1,0:T(8,128)(2,1)S(1)}, u32[]{:S(2)}, u32[]{:S(2)}) collective-permute-start(bf16[5,16,128]{2,1,0:T(8,128)(2,1)S(1)} %get-tuple-element.43), channel_id=1, source_target_pairs={{0,4},{4,0},{8,12},{12,8},{16,20},{20,16},{24,28},{28,24},{32,36},... | collective-permute-start | bytes 61448 | tf_op jit(solution)/shard_map/ppermute | solution.py:665
  26.0 8.9 %collective-permute-start.12 = (f32[5,16,128]{2,1,0:T(8,128)S(1)}, f32[5,16,128]{2,1,0:T(8,128)S(1)}, u32[]{:S(2)}, u32[]{:S(2)}) collective-permute-start(f32[5,16,128]{2,1,0:T(8,128)S(1)} %add_add_fusion.1), channel_id=1, source_target_pairs={{136,0},{137,1},{138,2},{139,3}} | collective-permute-start | bytes 122888 | tf_op jit(solution)/shard_map/ppermute | solution.py:615
  26.6 8.3 %collective-permute-start.11 = (f32[5,16,128]{2,1,0:T(8,128)S(1)}, f32[5,16,128]{2,1,0:T(8,128)S(1)}, u32[]{:S(2)}, u32[]{:S(2)}) collective-permute-start(f32[5,16,128]{2,1,0:T(8,128)S(1)} %add_add_fusion.1), channel_id=1, source_target_pairs={{200,0},{201,1},{202,2},{203,3}} | collective-permute-start | bytes 122888 | tf_op jit(solution)/shard_map/ppermute | solution.py:615
  27.3 7.6 %collective-permute-start.10 = (f32[5,16,128]{2,1,0:T(8,128)S(1)}, f32[5,16,128]{2,1,0:T(8,128)S(1)}, u32[]{:S(2)}, u32[]{:S(2)}) collective-permute-start(f32[5,16,128]{2,1,0:T(8,128)S(1)} %add_add_fusion.1), channel_id=1, source_target_pairs={{72,0},{73,1},{74,2},{75,3}} | collective-permute-start | bytes 122888 | tf_op jit(solution)/shard_map/ppermute | solution.py:615
  33.6 2.1 %collective-permute-start.13 = (bf16[5,16,128]{2,1,0:T(8,128)(2,1)S(1)}, bf16[5,16,128]{2,1,0:T(8,128)(2,1)S(1)}, u32[]{:S(2)}, u32[]{:S(2)}) collective-permute-start(bf16[5,16,128]{2,1,0:T(8,128)(2,1)S(1)} %get-tuple-element.53), channel_id=1, source_target_pairs={{0,4},{4,0},{8,12},{12,8},{16,20},{20,16},{24,28},{28,24},{32,36},... | collective-permute-start | bytes 61448 | tf_op jit(solution)/shard_map/ppermute | solution.py:687
  36.6 8.9 %collective-permute-start.15 = (bf16[5,16,768]{2,1,0:T(8,128)(2,1)S(1)}, bf16[5,16,768]{2,1,0:T(8,128)(2,1)S(1)}, u32[]{:S(2)}, u32[]{:S(2)}) collective-permute-start(bf16[5,16,768]{2,1,0:T(8,128)(2,1)S(1)} %get-tuple-element.59), channel_id=1, source_target_pairs={{0,2},{2,0},{1,3},{3,1},{4,6},{6,4},{5,7},{7,5},{8,10},{10,8},{9,1... | collective-permute-start | bytes 368648 | tf_op jit(solution)/shard_map/ppermute | solution.py:719
  38.0 7.4 %collective-permute-start.14 = (bf16[5,16,128]{2,1,0:T(8,128)(2,1)S(1)}, bf16[5,16,128]{2,1,0:T(8,128)(2,1)S(1)}, u32[]{:S(2)}, u32[]{:S(2)}) collective-permute-start(bf16[5,16,128]{2,1,0:T(8,128)(2,1)S(1)} %get-tuple-element.58), channel_id=1, source_target_pairs={{4,8},{8,4},{12,16},{16,12},{20,24},{24,20},{28,32},{32,28},{36,40... | collective-permute-start | bytes 61448 | tf_op jit(solution)/shard_map/ppermute | solution.py:688
  41.9 3.6 %collective-permute-start.16 = (bf16[5,16,128]{2,1,0:T(8,128)(2,1)S(1)}, bf16[5,16,128]{2,1,0:T(8,128)(2,1)S(1)}, u32[]{:S(2)}, u32[]{:S(2)}) collective-permute-start(bf16[5,16,128]{2,1,0:T(8,128)(2,1)S(1)} %get-tuple-element.60), channel_id=1, source_target_pairs={{0,1},{1,0},{2,3},{3,2},{4,5},{5,4},{6,7},{7,6},{8,9},{9,8},{10,11... | collective-permute-start | bytes 61448 | tf_op jit(solution)/shard_map/ppermute | solution.py:720
  (3 other events, 30.6 us)

commit v9 on v8

--- a/solution.py
+++ b/solution.py
@@ -63,7 +63,9 @@
             )
         return total
 
-    total = lax.fori_loop(0, rows_ref.shape[0] // 8, chunk, jnp.zeros((160, CELLS), f32))
+    total = lax.fori_loop(
+        0, rows_ref.shape[0] // 8, chunk, jnp.zeros((160, CELLS), f32), unroll=True
+    )
     for f in range(FIELDS):
         plane_ref[f] = (total[32 * f : 32 * f + 16] + total[32 * f + 16 : 32 * f + 32]) * normalizer
 

time: 50.4 us -> 49.6 us (0.984)
  Pallas kernels: 18.8 us -> 18 us
    pallas_call x1, Pallas kernels: 4.41 us -> 3.61 us  [body(): pl.pallas_call(functools.partial(plane_kernel, normalizer=float((plane_ro...]
where the time goes in v9:
time: 49.6 us; the launch traced here: 49.3 us
  starting transfers between devices  26.7 us (54%)
  Pallas kernels  18 us (36%)
  waiting for transfers between devices  3.32 us (7%)
  local copies, waits for them, and re-layouts  0.82 us (2%)
    ppermute x9, starting transfers between devices, gather_sum(): parts = [lax.ppermute(value, 'rans', pairs) for pairs in level]  13.8 us
    ppermute x2, starting transfers between devices, body(): from_chip = lax.ppermute(chip, 'rans', next_chip)  5.8 us
    pallas_call x1, Pallas kernels, body(): pl.pallas_call(phase_one_kernel, out_shape=(traces, traces) + sends, in_s...  5.6 us
    ppermute x2, starting transfers between devices, body(): near = lax.ppermute(pitch, 'pitch', swap)  5.13 us
    pallas_call x1, Pallas kernels, body(): pl.pallas_call(outer_two_kernel, out_shape=traces, in_specs=[VMEM] * 12 +...  4.56 us
    pallas_call x1, Pallas kernels, body(): pl.pallas_call(functools.partial(plane_kernel, normalizer=float((plane_ro...  3.61 us
    pallas_call x1, Pallas kernels, body(): pl.pallas_call(inner_two_kernel, out_shape=shape_of(FIELDS, NODES, elemen...  2.95 us
    ppermute x2, waiting for transfers between devices, body(): far = lax.ppermute(span, 'span', swap)  2.47 us
  transfers between devices with their start and end apart: 17, of which 2 were waited for; matrix products, arithmetic and copies ran while one was open for 0% of the time, Pallas kernels for 18%

profile of v9, /device:TPU:1, one launch (start us, length us, event | category | flops | bytes accessed | tf_op | source)
XLA Modules:
  0.0 49.3 jit_solution(1435897567285242678)
XLA Ops:
  0.0 3.6 %eddy_plane.1.plane_ref = f32[5,16,128]{2,1,0:T(8,128)} custom-call(s32[64,256]{1,0:T(8,128)} %bitcast.18, s32[1,256]{1,0:T(1,128)} %bitcast.20, f32[64,256]{1,0:T(8,128)} %bitcast.19), custom_call_target="tpu_custom_call" | custom-call | flops 400000000 | bytes 12000000 | tf_op jit(solution)/shard_map/eddy_plane/pallas_call | solution.py:633
  3.7 1.4 %collective-permute-start.2 = (f32[5,16,128]{2,1,0:T(8,128)}, f32[5,16,128]{2,1,0:T(8,128)S(1)}, u32[]{:S(2)}, u32[]{:S(2)}) collective-permute-start(f32[5,16,128]{2,1,0:T(8,128)} %eddy_plane.1.plane_ref), channel_id=1, source_target_pairs={{24,0},{28,4},{56,40},{60,44},{88,72},{92,76},{120,104},{124,108},... | collective-permute-start | bytes 122888 | tf_op jit(solution)/shard_map/ppermute | solution.py:617
  5.1 1.3 %collective-permute-start.1 = (f32[5,16,128]{2,1,0:T(8,128)}, f32[5,16,128]{2,1,0:T(8,128)S(1)}, u32[]{:S(2)}, u32[]{:S(2)}) collective-permute-start(f32[5,16,128]{2,1,0:T(8,128)} %eddy_plane.1.plane_ref), channel_id=1, source_target_pairs={{16,0},{20,4},{48,40},{52,44},{80,72},{84,76},{112,104},{116,108},... | collective-permute-start | bytes 122888 | tf_op jit(solution)/shard_map/ppermute | solution.py:617
  6.4 1.3 %collective-permute-start = (f32[5,16,128]{2,1,0:T(8,128)}, f32[5,16,128]{2,1,0:T(8,128)S(1)}, u32[]{:S(2)}, u32[]{:S(2)}) collective-permute-start(f32[5,16,128]{2,1,0:T(8,128)} %eddy_plane.1.plane_ref), channel_id=1, source_target_pairs={{8,0},{12,4},{32,40},{36,44},{64,72},{68,76},{96,104},{100,108},{1... | collective-permute-start | bytes 122888 | tf_op jit(solution)/shard_map/ppermute | solution.py:617
  7.7 0.8 %copy-done.8 = f32[5,16,128]{2,1,0:T(8,128)S(1)} copy-done((f32[5,16,128]{2,1,0:T(8,128)S(1)}, f32[5,16,128]{2,1,0:T(8,128)}, u32[]{:S(2)}) %copy-start.8) | copy-done | bytes 40984
  8.5 0.5 pack_faces.1
  9.0 3.7 %collective-permute-start.6 = (bf16[5,16,768]{2,1,0:T(8,128)(2,1)S(1)}, bf16[5,16,768]{2,1,0:T(8,128)(2,1)S(1)}, u32[]{:S(2)}, u32[]{:S(2)}) collective-permute-start(bf16[5,16,768]{2,1,0:T(8,128)(2,1)S(1)} %get-tuple-element.40), channel_id=1, source_target_pairs={{0,2},{2,0},{1,3},{3,1},{4,6},{6,4},{5,7},{7,5},{8,10},{10,8},{9,1... | collective-permute-start | bytes 368648 | tf_op jit(solution)/shard_map/ppermute | solution.py:661
  12.7 0.7 %collective-permute-start.5 = (f32[5,16,128]{2,1,0:T(8,128)S(1)}, f32[5,16,128]{2,1,0:T(8,128)S(1)}, u32[]{:S(2)}, u32[]{:S(2)}) collective-permute-start(f32[5,16,128]{2,1,0:T(8,128)S(1)} %add_add_fusion.2), channel_id=1, source_target_pairs={{44,0},{108,72},{172,136},{236,200},{45,1},{109,73},{173,137},{237... | collective-permute-start | bytes 122888 | tf_op jit(solution)/shard_map/ppermute | solution.py:617
  13.4 0.7 %collective-permute-start.4 = (f32[5,16,128]{2,1,0:T(8,128)S(1)}, f32[5,16,128]{2,1,0:T(8,128)S(1)}, u32[]{:S(2)}, u32[]{:S(2)}) collective-permute-start(f32[5,16,128]{2,1,0:T(8,128)S(1)} %add_add_fusion.2), channel_id=1, source_target_pairs={{40,0},{104,72},{168,136},{232,200},{41,1},{105,73},{169,137},{233... | collective-permute-start | bytes 122888 | tf_op jit(solution)/shard_map/ppermute | solution.py:617
  14.0 6.5 %collective-permute-start.3 = (f32[5,16,128]{2,1,0:T(8,128)S(1)}, f32[5,16,128]{2,1,0:T(8,128)S(1)}, u32[]{:S(2)}, u32[]{:S(2)}) collective-permute-start(f32[5,16,128]{2,1,0:T(8,128)S(1)} %add_add_fusion.2), channel_id=1, source_target_pairs={{4,0},{76,72},{140,136},{204,200},{5,1},{77,73},{141,137},{205,201... | collective-permute-start | bytes 122888 | tf_op jit(solution)/shard_map/ppermute | solution.py:617
  20.5 1.9 %collective-permute-start.9 = (bf16[5,16,128]{2,1,0:T(8,128)(2,1)S(1)}, bf16[5,16,128]{2,1,0:T(8,128)(2,1)S(1)}, u32[]{:S(2)}, u32[]{:S(2)}) collective-permute-start(bf16[5,16,128]{2,1,0:T(8,128)(2,1)S(1)} %get-tuple-element.45), channel_id=1, source_target_pairs={{4,8},{8,4},{12,16},{16,12},{20,24},{24,20},{28,32},{32,28},{36,40... | collective-permute-start | bytes 61448 | tf_op jit(solution)/shard_map/ppermute | solution.py:664
  22.7 2.5 %collective-permute-done.7.far_ref = bf16[5,16,128]{2,1,0:T(8,128)(2,1)S(1)} collective-permute-done((bf16[5,16,128]{2,1,0:T(8,128)(2,1)S(1)}, bf16[5,16,128]{2,1,0:T(8,128)(2,1)S(1)}, u32[]{:S(2)}, u32[]{:S(2)}) %collective-permute-start.7) | collective-permute-done | bytes 20512 | tf_op jit(solution)/shard_map/ppermute | solution.py:666
  25.2 0.7 %collective-permute-start.12 = (f32[5,16,128]{2,1,0:T(8,128)S(1)}, f32[5,16,128]{2,1,0:T(8,128)S(1)}, u32[]{:S(2)}, u32[]{:S(2)}) collective-permute-start(f32[5,16,128]{2,1,0:T(8,128)S(1)} %add_add_fusion.1), channel_id=1, source_target_pairs={{136,0},{137,1},{138,2},{139,3}} | collective-permute-start | bytes 122888 | tf_op jit(solution)/shard_map/ppermute | solution.py:617
  25.8 0.7 %collective-permute-start.11 = (f32[5,16,128]{2,1,0:T(8,128)S(1)}, f32[5,16,128]{2,1,0:T(8,128)S(1)}, u32[]{:S(2)}, u32[]{:S(2)}) collective-permute-start(f32[5,16,128]{2,1,0:T(8,128)S(1)} %add_add_fusion.1), channel_id=1, source_target_pairs={{200,0},{201,1},{202,2},{203,3}} | collective-permute-start | bytes 122888 | tf_op jit(solution)/shard_map/ppermute | solution.py:617
  26.5 0.7 %collective-permute-start.10 = (f32[5,16,128]{2,1,0:T(8,128)S(1)}, f32[5,16,128]{2,1,0:T(8,128)S(1)}, u32[]{:S(2)}, u32[]{:S(2)}) collective-permute-start(f32[5,16,128]{2,1,0:T(8,128)S(1)} %add_add_fusion.1), channel_id=1, source_target_pairs={{72,0},{73,1},{74,2},{75,3}} | collective-permute-start | bytes 122888 | tf_op jit(solution)/shard_map/ppermute | solution.py:617
  27.2 5.6 %phase_one.1 = (bf16[5,64,1536]{2,1,0:T(8,128)(2,1)S(1)}, bf16[5,64,1536]{2,1,0:T(8,128)(2,1)S(1)}, bf16[5,16,128]{2,1,0:T(8,128)(2,1)S(1)}, bf16[5,16,128]{2,1,...) custom-call(bf16[5,64,1536]{2,1,0:T(8,128)(2,1)S(1)} %copy-done, ...), custom_call_target="tpu_custom_call" | custom-call | flops 600000000 | bytes 18000000 | tf_op jit(solution)/shard_map/phase_one/pallas_call | solution.py:671
  32.8 1.2 %collective-permute-start.13 = (bf16[5,16,128]{2,1,0:T(8,128)(2,1)S(1)}, bf16[5,16,128]{2,1,0:T(8,128)(2,1)S(1)}, u32[]{:S(2)}, u32[]{:S(2)}) collective-permute-start(bf16[5,16,128]{2,1,0:T(8,128)(2,1)S(1)} %get-tuple-element.53), channel_id=1, source_target_pairs={{0,4},{4,0},{8,12},{12,8},{16,20},{20,16},{24,28},{28,24},{32,36},... | collective-permute-start | bytes 61448 | tf_op jit(solution)/shard_map/ppermute | solution.py:689
  34.1 0.8 %collective-permute-done.13.from_core_ref = bf16[5,16,128]{2,1,0:T(8,128)(2,1)S(1)} collective-permute-done((bf16[5,16,128]{2,1,0:T(8,128)(2,1)S(1)}, bf16[5,16,128]{2,1,0:T(8,128)(2,1)S(1)}, u32[]{:S(2)}, u32[]{:S(2)}) %collective-permute-start.13) | collective-permute-done | bytes 20512 | tf_op jit(solution)/shard_map/ppermute | solution.py:689
  34.9 0.8 %inflow_layer.1 = (bf16[5,64,1536]{2,1,0:T(8,128)(2,1)S(1)}, bf16[5,64,1536]{2,1,0:T(8,128)(2,1)S(1)}, bf16[5,16,768]{2,1,0:T(8,128)(2,1)S(1)}, bf16[5,16,128]{2,1,0:T(8,128)(2,1)S(1)}) custom-call(bf16[5,64,1536]{2,1,0:T(8,128)(2,1)S(1)} %get-tuple-element.48.held_ref, ...), custom_call_target="tpu_custom_call", output_to_operand_aliasing={{0}: (0, {}), {1}: (1, {}), {2}: (2, {}), {3}: (3, {})} | custom-call | flops 10000000 | bytes 300000 | tf_op jit(solution)/shard_map/inflow_layer/pallas_call | solution.py:697
  35.8 1.5 %collective-permute-start.15 = (bf16[5,16,768]{2,1,0:T(8,128)(2,1)S(1)}, bf16[5,16,768]{2,1,0:T(8,128)(2,1)S(1)}, u32[]{:S(2)}, u32[]{:S(2)}) collective-permute-start(bf16[5,16,768]{2,1,0:T(8,128)(2,1)S(1)} %get-tuple-element.59), channel_id=1, source_target_pairs={{0,2},{2,0},{1,3},{3,1},{4,6},{6,4},{5,7},{7,5},{8,10},{10,8},{9,1... | collective-permute-start | bytes 368648 | tf_op jit(solution)/shard_map/ppermute | solution.py:721
  37.2 3.9 %collective-permute-start.14 = (bf16[5,16,128]{2,1,0:T(8,128)(2,1)S(1)}, bf16[5,16,128]{2,1,0:T(8,128)(2,1)S(1)}, u32[]{:S(2)}, u32[]{:S(2)}) collective-permute-start(bf16[5,16,128]{2,1,0:T(8,128)(2,1)S(1)} %get-tuple-element.58), channel_id=1, source_target_pairs={{4,8},{8,4},{12,16},{16,12},{20,24},{24,20},{28,32},{32,28},{36,40... | collective-permute-start | bytes 61448 | tf_op jit(solution)/shard_map/ppermute | solution.py:690
  41.1 0.6 %collective-permute-start.16 = (bf16[5,16,128]{2,1,0:T(8,128)(2,1)S(1)}, bf16[5,16,128]{2,1,0:T(8,128)(2,1)S(1)}, u32[]{:S(2)}, u32[]{:S(2)}) collective-permute-start(bf16[5,16,128]{2,1,0:T(8,128)(2,1)S(1)} %get-tuple-element.60), channel_id=1, source_target_pairs={{0,1},{1,0},{2,3},{3,2},{4,5},{5,4},{6,7},{7,6},{8,9},{9,8},{10,11... | collective-permute-start | bytes 61448 | tf_op jit(solution)/shard_map/ppermute | solution.py:722
  41.7 3.0 %inner_two.1.part_ref = f32[5,64,1536]{2,1,0:T(8,128)S(1)} custom-call(bf16[5,64,1536]{2,1,0:T(8,128)(2,1)S(1)} %get-tuple-element.55.v_ref, f32[5,3,5]{2,1,0:T(4,128)S(1)} %bitcast.16, bf16[3,64,64]{2,1,0:T(8,128)(2,1)S(1)} %copy-done.1), custom_call_target="tpu_custom_call" | custom-call | flops 10000000 | bytes 300000 | tf_op jit(solution)/shard_map/inner_two/pallas_call | solution.py:723
  44.7 4.6 %outer_two.1 = bf16[5,64,1536]{2,1,0:T(8,128)(2,1)} custom-call(bf16[5,64,1536]{2,1,0:T(8,128)(2,1)S(1)} %get-tuple-element.55.v_ref, bf16[5,64,1536]{2,1,0:T(8,128)(2,1)S(1)} %get-tuple-element.56.trace_ref, bf16[5,64,1536]{2,1,0:T(8,128)(2,1)S(1)} %copy-done, f32[5,64,1536]{2,1,0:T(8,128)S(1)} %inner_two.1.part_ref, f32[5,16,128]{2,1,0:T(8,128)S(1)} %bitcast.11, ...), custom_call_target="tpu_custom_call" | custom-call | flops 400000000 | bytes 12000000 | tf_op jit(solution)/shard_map/outer_two/pallas_call | solution.py:735
  (40 shorter events, 0.3 us)
Async XLA Ops:
  0.0 27.2 %copy-start.6 = (bf16[64,64]{1,0:T(8,128)(2,1)S(1)}, bf16[64,64]{1,0:T(8,128)(2,1)}, u32[]{:S(2)}) copy-start(bf16[64,64]{1,0:T(8,128)(2,1)} %wall_ref.5) | copy-start | bytes 24580
  0.0 27.2 %copy-start.7 = (bf16[64,64]{1,0:T(8,128)(2,1)S(1)}, bf16[64,64]{1,0:T(8,128)(2,1)}, u32[]{:S(2)}) copy-start(bf16[64,64]{1,0:T(8,128)(2,1)} %smooth_ref.1) | copy-start | bytes 24580
  0.0 27.2 %copy-start.5 = (bf16[64,96]{1,0:T(8,128)(2,1)S(1)}, bf16[64,96]{1,0:T(8,128)(2,1)}, u32[]{:S(2)}) copy-start(bf16[64,96]{1,0:T(8,128)(2,1)} %lift_ref.5) | copy-start | bytes 36868
  0.0 27.2 %copy-start.1 = (bf16[3,64,64]{2,1,0:T(8,128)(2,1)S(1)}, bf16[3,64,64]{2,1,0:T(8,128)(2,1)}, u32[]{:S(2)}) copy-start(bf16[3,64,64]{2,1,0:T(8,128)(2,1)} %volume_ref.5) | copy-start | bytes 73732
  0.0 27.2 %copy-start.4 = (f32[3,5,5]{2,0,1:T(4,128)S(1)}, f32[3,5,5]{2,0,1:T(4,128)}, u32[]{:S(2)}) copy-start(f32[3,5,5]{2,0,1:T(4,128)} %param.14) | copy-start | bytes 904
  3.7 31.3 %copy-start.2 = (f32[1,1,5,2048]{3,1,2,0:T(1,128)S(1)}, f32[1,1,5,2048]{3,1,2,0:T(1,128)}, u32[]{:S(2)}) copy-start(f32[1,1,5,2048]{3,1,2,0:T(1,128)} %param.22) | copy-start | bytes 122884
  3.7 31.3 %copy-start.3 = (f32[1,1,5,2048]{3,1,2,0:T(1,128)S(1)}, f32[1,1,5,2048]{3,1,2,0:T(1,128)}, u32[]{:S(2)}) copy-start(f32[1,1,5,2048]{3,1,2,0:T(1,128)} %param.23) | copy-start | bytes 122884
  3.7 9.0 %collective-permute-start.2 = (f32[5,16,128]{2,1,0:T(8,128)}, f32[5,16,128]{2,1,0:T(8,128)S(1)}, u32[]{:S(2)}, u32[]{:S(2)}) collective-permute-start(f32[5,16,128]{2,1,0:T(8,128)} %eddy_plane.1.plane_ref), channel_id=1, source_target_pairs={{24,0},{28,4},{56,40},{60,44},{88,72},{92,76},{120,104},{124,108},... | collective-permute-start | bytes 122888 | tf_op jit(solution)/shard_map/ppermute | solution.py:617
  5.1 7.5 %collective-permute-start.1 = (f32[5,16,128]{2,1,0:T(8,128)}, f32[5,16,128]{2,1,0:T(8,128)S(1)}, u32[]{:S(2)}, u32[]{:S(2)}) collective-permute-start(f32[5,16,128]{2,1,0:T(8,128)} %eddy_plane.1.plane_ref), channel_id=1, source_target_pairs={{16,0},{20,4},{48,40},{52,44},{80,72},{84,76},{112,104},{116,108},... | collective-permute-start | bytes 122888 | tf_op jit(solution)/shard_map/ppermute | solution.py:617
  6.4 6.2 %collective-permute-start = (f32[5,16,128]{2,1,0:T(8,128)}, f32[5,16,128]{2,1,0:T(8,128)S(1)}, u32[]{:S(2)}, u32[]{:S(2)}) collective-permute-start(f32[5,16,128]{2,1,0:T(8,128)} %eddy_plane.1.plane_ref), channel_id=1, source_target_pairs={{8,0},{12,4},{32,40},{36,44},{64,72},{68,76},{96,104},{100,108},{1... | collective-permute-start | bytes 122888 | tf_op jit(solution)/shard_map/ppermute | solution.py:617
  9.0 13.5 %collective-permute-start.6 = (bf16[5,16,768]{2,1,0:T(8,128)(2,1)S(1)}, bf16[5,16,768]{2,1,0:T(8,128)(2,1)S(1)}, u32[]{:S(2)}, u32[]{:S(2)}) collective-permute-start(bf16[5,16,768]{2,1,0:T(8,128)(2,1)S(1)} %get-tuple-element.40), channel_id=1, source_target_pairs={{0,2},{2,0},{1,3},{3,1},{4,6},{6,4},{5,7},{7,5},{8,10},{10,8},{9,1... | collective-permute-start | bytes 368648 | tf_op jit(solution)/shard_map/ppermute | solution.py:661
  12.7 9.9 %collective-permute-start.5 = (f32[5,16,128]{2,1,0:T(8,128)S(1)}, f32[5,16,128]{2,1,0:T(8,128)S(1)}, u32[]{:S(2)}, u32[]{:S(2)}) collective-permute-start(f32[5,16,128]{2,1,0:T(8,128)S(1)} %add_add_fusion.2), channel_id=1, source_target_pairs={{44,0},{108,72},{172,136},{236,200},{45,1},{109,73},{173,137},{237... | collective-permute-start | bytes 122888 | tf_op jit(solution)/shard_map/ppermute | solution.py:617
  13.4 9.3 %collective-permute-start.4 = (f32[5,16,128]{2,1,0:T(8,128)S(1)}, f32[5,16,128]{2,1,0:T(8,128)S(1)}, u32[]{:S(2)}, u32[]{:S(2)}) collective-permute-start(f32[5,16,128]{2,1,0:T(8,128)S(1)} %add_add_fusion.2), channel_id=1, source_target_pairs={{40,0},{104,72},{168,136},{232,200},{41,1},{105,73},{169,137},{233... | collective-permute-start | bytes 122888 | tf_op jit(solution)/shard_map/ppermute | solution.py:617
  14.0 8.7 %collective-permute-start.3 = (f32[5,16,128]{2,1,0:T(8,128)S(1)}, f32[5,16,128]{2,1,0:T(8,128)S(1)}, u32[]{:S(2)}, u32[]{:S(2)}) collective-permute-start(f32[5,16,128]{2,1,0:T(8,128)S(1)} %add_add_fusion.2), channel_id=1, source_target_pairs={{4,0},{76,72},{140,136},{204,200},{5,1},{77,73},{141,137},{205,201... | collective-permute-start | bytes 122888 | tf_op jit(solution)/shard_map/ppermute | solution.py:617
  20.5 6.7 %collective-permute-start.9 = (bf16[5,16,128]{2,1,0:T(8,128)(2,1)S(1)}, bf16[5,16,128]{2,1,0:T(8,128)(2,1)S(1)}, u32[]{:S(2)}, u32[]{:S(2)}) collective-permute-start(bf16[5,16,128]{2,1,0:T(8,128)(2,1)S(1)} %get-tuple-element.45), channel_id=1, source_target_pairs={{4,8},{8,4},{12,16},{16,12},{20,24},{24,20},{28,32},{32,28},{36,40... | collective-permute-start | bytes 61448 | tf_op jit(solution)/shard_map/ppermute | solution.py:664
  22.5 2.7 %collective-permute-start.7 = (bf16[5,16,128]{2,1,0:T(8,128)(2,1)S(1)}, bf16[5,16,128]{2,1,0:T(8,128)(2,1)S(1)}, u32[]{:S(2)}, u32[]{:S(2)}) collective-permute-start(bf16[5,16,128]{2,1,0:T(8,128)(2,1)S(1)} %get-tuple-element.42), channel_id=1, source_target_pairs={{0,1},{1,0},{2,3},{3,2},{4,5},{5,4},{6,7},{7,6},{8,9},{9,8},{10,11... | collective-permute-start | bytes 61448 | tf_op jit(solution)/shard_map/ppermute | solution.py:666
  22.6 2.6 %collective-permute-start.8 = (bf16[5,16,128]{2,1,0:T(8,128)(2,1)S(1)}, bf16[5,16,128]{2,1,0:T(8,128)(2,1)S(1)}, u32[]{:S(2)}, u32[]{:S(2)}) collective-permute-start(bf16[5,16,128]{2,1,0:T(8,128)(2,1)S(1)} %get-tuple-element.43), channel_id=1, source_target_pairs={{0,4},{4,0},{8,12},{12,8},{16,20},{20,16},{24,28},{28,24},{32,36},... | collective-permute-start | bytes 61448 | tf_op jit(solution)/shard_map/ppermute | solution.py:667
  25.2 8.9 %collective-permute-start.12 = (f32[5,16,128]{2,1,0:T(8,128)S(1)}, f32[5,16,128]{2,1,0:T(8,128)S(1)}, u32[]{:S(2)}, u32[]{:S(2)}) collective-permute-start(f32[5,16,128]{2,1,0:T(8,128)S(1)} %add_add_fusion.1), channel_id=1, source_target_pairs={{136,0},{137,1},{138,2},{139,3}} | collective-permute-start | bytes 122888 | tf_op jit(solution)/shard_map/ppermute | solution.py:617
  25.8 8.3 %collective-permute-start.11 = (f32[5,16,128]{2,1,0:T(8,128)S(1)}, f32[5,16,128]{2,1,0:T(8,128)S(1)}, u32[]{:S(2)}, u32[]{:S(2)}) collective-permute-start(f32[5,16,128]{2,1,0:T(8,128)S(1)} %add_add_fusion.1), channel_id=1, source_target_pairs={{200,0},{201,1},{202,2},{203,3}} | collective-permute-start | bytes 122888 | tf_op jit(solution)/shard_map/ppermute | solution.py:617
  26.5 7.6 %collective-permute-start.10 = (f32[5,16,128]{2,1,0:T(8,128)S(1)}, f32[5,16,128]{2,1,0:T(8,128)S(1)}, u32[]{:S(2)}, u32[]{:S(2)}) collective-permute-start(f32[5,16,128]{2,1,0:T(8,128)S(1)} %add_add_fusion.1), channel_id=1, source_target_pairs={{72,0},{73,1},{74,2},{75,3}} | collective-permute-start | bytes 122888 | tf_op jit(solution)/shard_map/ppermute | solution.py:617
  32.8 2.1 %collective-permute-start.13 = (bf16[5,16,128]{2,1,0:T(8,128)(2,1)S(1)}, bf16[5,16,128]{2,1,0:T(8,128)(2,1)S(1)}, u32[]{:S(2)}, u32[]{:S(2)}) collective-permute-start(bf16[5,16,128]{2,1,0:T(8,128)(2,1)S(1)} %get-tuple-element.53), channel_id=1, source_target_pairs={{0,4},{4,0},{8,12},{12,8},{16,20},{20,16},{24,28},{28,24},{32,36},... | collective-permute-start | bytes 61448 | tf_op jit(solution)/shard_map/ppermute | solution.py:689
  35.8 8.9 %collective-permute-start.15 = (bf16[5,16,768]{2,1,0:T(8,128)(2,1)S(1)}, bf16[5,16,768]{2,1,0:T(8,128)(2,1)S(1)}, u32[]{:S(2)}, u32[]{:S(2)}) collective-permute-start(bf16[5,16,768]{2,1,0:T(8,128)(2,1)S(1)} %get-tuple-element.59), channel_id=1, source_target_pairs={{0,2},{2,0},{1,3},{3,1},{4,6},{6,4},{5,7},{7,5},{8,10},{10,8},{9,1... | collective-permute-start | bytes 368648 | tf_op jit(solution)/shard_map/ppermute | solution.py:721
  37.2 7.4 %collective-permute-start.14 = (bf16[5,16,128]{2,1,0:T(8,128)(2,1)S(1)}, bf16[5,16,128]{2,1,0:T(8,128)(2,1)S(1)}, u32[]{:S(2)}, u32[]{:S(2)}) collective-permute-start(bf16[5,16,128]{2,1,0:T(8,128)(2,1)S(1)} %get-tuple-element.58), channel_id=1, source_target_pairs={{4,8},{8,4},{12,16},{16,12},{20,24},{24,20},{28,32},{32,28},{36,40... | collective-permute-start | bytes 61448 | tf_op jit(solution)/shard_map/ppermute | solution.py:690
  41.1 3.5 %collective-permute-start.16 = (bf16[5,16,128]{2,1,0:T(8,128)(2,1)S(1)}, bf16[5,16,128]{2,1,0:T(8,128)(2,1)S(1)}, u32[]{:S(2)}, u32[]{:S(2)}) collective-permute-start(bf16[5,16,128]{2,1,0:T(8,128)(2,1)S(1)} %get-tuple-element.60), channel_id=1, source_target_pairs={{0,1},{1,0},{2,3},{3,2},{4,5},{5,4},{6,7},{7,6},{8,9},{9,8},{10,11... | collective-permute-start | bytes 61448 | tf_op jit(solution)/shard_map/ppermute | solution.py:722
  (3 other events, 29.0 us)

commit v10 on v9

--- a/solution.py
+++ b/solution.py
@@ -504,17 +504,23 @@
 
 
 def inflow_kernel(
-    held_ref, held_trace_ref, held_pitch_ref, held_span_ref, v_ref, mean_ref, amp_ref,
-    plane_ref, near_ref, far_ref, pin_ref, coefs, volume_ref, lift_ref, wall_ref, filter_ref, out_ref,
-    out_trace_ref,
-    pitch_ref, span_ref, mixed, own, weights_held,
+    held_any, held_trace_any, held_pitch_any, held_span_any, v_ref, mean_ref, amp_ref, plane_ref,
+    near_ref, far_ref, pin_ref, coefs, volume_ref, lift_ref, wall_ref, filter_ref, out_any,
+    out_trace_any, pitch_any, span_any, mixed, own, weights_held, edge, edge_trace, edge_pitch,
+    edge_span, sems,
 ):
     first_span = lax.axis_index("span") == 0
-    first_rans = lax.axis_index("rans") == 0
     lane = lanes()
-
-    @pl.when(first_rans)
+    layer = slice(0, CELLS)
+
+    @pl.when(lax.axis_index("rans") == 0)
     def _():
+        loads = [
+            pltpu.make_async_copy(held_pitch_any.at[:, :, layer], edge_pitch, sems.at[0]),
+            pltpu.make_async_copy(held_span_any, edge_span, sems.at[1]),
+        ]
+        for copy in loads:
+            copy.start()
         pick = trace_selector()
         smooth = with_traces(filter_ref[...], pick)
         weights = fill(
@@ -522,18 +528,18 @@
         )
 
         def read(f, r0, r1):
-            return v_ref[f, r0:r1, 0:CELLS]
+            return v_ref[f, r0:r1, layer]
 
         def store(f, value):
-            out_ref[f] = value[0:64].astype(bf16)
+            edge[f] = value[0:64].astype(bf16)
             t = value[64:128]
-            out_trace_ref[f] = t.astype(bf16)
+            edge_trace[f] = t.astype(bf16)
             pitch = jnp.where(lane < 32, t[0:16], pltpu.roll(t[16:32], 96, 1))
-            pitch_ref[f] = jnp.where(
-                (lane & 63) < 32, pitch, held_pitch_ref[f].astype(f32)
+            edge_pitch[f] = jnp.where(
+                (lane & 63) < 32, pitch, edge_pitch[f].astype(f32)
             ).astype(bf16)
-            span_ref[f] = pack_span(
-                held_span_ref[f].astype(f32), t[32:48], t[48:64], 0, first_span, lane
+            edge_span[f] = pack_span(
+                edge_span[f].astype(f32), t[32:48], t[48:64], 0, first_span, lane
             ).astype(bf16)
 
         vector = (
@@ -546,24 +552,31 @@
             )
             + mix_sides(
                 lambda f, r0, r1: own[f, r0:r1].astype(f32),
-                lambda f: near_ref[f].astype(f32),
+                lambda f: near_ref[f, :, layer].astype(f32),
                 lambda f: far_ref[f].astype(f32),
                 [0], coefs, mixed, 224, first_span, lane,
             )
             + mix_fluxes(read, coefs, mixed)
-            + mix_wall(read, lambda: pin_ref[...].astype(f32), mixed, 288)
+            + mix_wall(read, lambda: pin_ref[:, layer].astype(f32), mixed, 288)
         )
-        matrix = staggered(
+        for step in vector:
+            step()
+        for copy in loads:
+            copy.wait()
+        for step in staggered(
             [lambda f, _: dot(weights, mixed[f]), finish(read, None, smooth), store]
-        )
-        pipeline([vector], [matrix])
-
-    @pl.when(jnp.logical_not(first_rans))
-    def _():
-        out_ref[...] = held_ref[...]
-        out_trace_ref[...] = held_trace_ref[...]
-        pitch_ref[...] = held_pitch_ref[...]
-        span_ref[...] = held_span_ref[...]
+        ):
+            step()
+        stores = [
+            pltpu.make_async_copy(edge, out_any.at[:, :, layer], sems.at[2]),
+            pltpu.make_async_copy(edge_trace, out_trace_any.at[:, :, layer], sems.at[3]),
+            pltpu.make_async_copy(edge_pitch, pitch_any.at[:, :, layer], sems.at[4]),
+            pltpu.make_async_copy(edge_span, span_any, sems.at[5]),
+        ]
+        for copy in stores:
+            copy.start()
+        for copy in stores:
+            copy.wait()
 
 
 VMEM = pl.BlockSpec(memory_space=pltpu.VMEM)
@@ -573,10 +586,6 @@
 
 def shape_of(*dims, dtype=bf16):
     return jax.ShapeDtypeStruct(dims, dtype)
-
-
-def front(*dims):
-    return pl.BlockSpec(dims, lambda i: (0,) * len(dims))
 
 
 def cost(us):
@@ -692,31 +701,29 @@
 
     mean = mean_inflow.reshape(FIELDS, 16, CELLS)
     amplitude = eddy_amplitude.reshape(FIELDS, 16, CELLS)
-    layer = front(FIELDS, NODES, CELLS)
-    face = front(FIELDS, 16, CELLS)
+    anywhere = pl.BlockSpec(memory_space=pl.ANY)
     phase_one, trace_one, pitch, span = pl.pallas_call(
         inflow_kernel,
-        grid=(1,),
         out_shape=(traces, traces, sends[2], sends[3]),
-        in_specs=[layer, layer, face, face, front(FIELDS, NODES, PAIR)]
-        + [face] * 5
-        + [
-            front(1, CELLS), SMEM, front(3, NODES, NODES), front(NODES, 96), front(NODES, NODES),
-            front(NODES, NODES),
-        ],
-        out_specs=(layer, layer, face, face),
+        in_specs=[anywhere] * 4 + [VMEM] * 7 + [SMEM] + [VMEM] * 4,
+        out_specs=(anywhere,) * 4,
         scratch_shapes=[
             pltpu.VMEM((FIELDS, MIXED, CELLS), bf16),
             pltpu.VMEM((FIELDS, NODES, CELLS), bf16),
             pltpu.VMEM((NODES, MIXED), bf16),
+            pltpu.VMEM((FIELDS, NODES, CELLS), bf16),
+            pltpu.VMEM((FIELDS, NODES, CELLS), bf16),
+            pltpu.VMEM((FIELDS, 16, CELLS), bf16),
+            pltpu.VMEM((FIELDS, 16, CELLS), bf16),
+            pltpu.SemaphoreType.DMA((6,)),
         ],
         input_output_aliases={0: 0, 1: 1, 2: 2, 3: 3},
         compiler_params=PARAMS,
         cost_estimate=cost(0.1),
         name="inflow_layer",
     )(
-        phase_one, trace_one, pitch, span, solution, mean, amplitude, plane, near, far,
-        pins, jacobian, volume_ops, lift_matrix, wall_matrix, filter_matrix,
+        phase_one, trace_one, pitch, span, solution, mean, amplitude, plane, near, far, pins,
+        jacobian, volume_ops, lift_matrix, wall_matrix, filter_matrix,
     )
     near = lax.ppermute(pitch, "pitch", swap)
     far = lax.ppermute(span, "span", swap)

time: 49.6 us -> 49.6 us (level)
  no operation moved by 1% of the time
where the time goes in v10:
time: 49.6 us; the launch traced here: 49.2 us
  starting transfers between devices  26.7 us (54%)
  Pallas kernels  18 us (36%)
  waiting for transfers between devices  3.32 us (7%)
  local copies, waits for them, and re-layouts  0.82 us (2%)
    ppermute x9, starting transfers between devices, gather_sum(): parts = [lax.ppermute(value, 'rans', pairs) for pairs in level]  13.8 us
    ppermute x2, starting transfers between devices, body(): from_chip = lax.ppermute(chip, 'rans', next_chip)  5.8 us
    pallas_call x1, Pallas kernels, body(): pl.pallas_call(phase_one_kernel, out_shape=(traces, traces) + sends, in_s...  5.6 us
    ppermute x2, starting transfers between devices, body(): near = lax.ppermute(pitch, 'pitch', swap)  5.13 us
    pallas_call x1, Pallas kernels, body(): pl.pallas_call(outer_two_kernel, out_shape=traces, in_specs=[VMEM] * 12 +...  4.56 us
    pallas_call x1, Pallas kernels, body(): pl.pallas_call(functools.partial(plane_kernel, normalizer=float((plane_ro...  3.61 us
    pallas_call x1, Pallas kernels, body(): pl.pallas_call(inner_two_kernel, out_shape=shape_of(FIELDS, NODES, elemen...  2.95 us
    ppermute x2, waiting for transfers between devices, body(): far = lax.ppermute(span, 'span', swap)  2.47 us
  transfers between devices with their start and end apart: 17, of which 2 were waited for; matrix products, arithmetic and copies ran while one was open for 0% of the time, Pallas kernels for 18%

profile of v10, /device:TPU:1, one launch (start us, length us, event | category | flops | bytes accessed | tf_op | source)
XLA Modules:
  0.0 49.2 jit_solution(6294519058758781498)
XLA Ops:
  0.0 3.6 %eddy_plane.1.plane_ref = f32[5,16,128]{2,1,0:T(8,128)} custom-call(s32[64,256]{1,0:T(8,128)} %bitcast.18, s32[1,256]{1,0:T(1,128)} %bitcast.20, f32[64,256]{1,0:T(8,128)} %bitcast.19), custom_call_target="tpu_custom_call" | custom-call | flops 400000000 | bytes 12000000 | tf_op jit(solution)/shard_map/eddy_plane/pallas_call | solution.py:642
  3.7 1.4 %collective-permute-start.2 = (f32[5,16,128]{2,1,0:T(8,128)}, f32[5,16,128]{2,1,0:T(8,128)S(1)}, u32[]{:S(2)}, u32[]{:S(2)}) collective-permute-start(f32[5,16,128]{2,1,0:T(8,128)} %eddy_plane.1.plane_ref), channel_id=1, source_target_pairs={{24,0},{28,4},{56,40},{60,44},{88,72},{92,76},{120,104},{124,108},... | collective-permute-start | bytes 122888 | tf_op jit(solution)/shard_map/ppermute | solution.py:626
  5.1 1.3 %collective-permute-start.1 = (f32[5,16,128]{2,1,0:T(8,128)}, f32[5,16,128]{2,1,0:T(8,128)S(1)}, u32[]{:S(2)}, u32[]{:S(2)}) collective-permute-start(f32[5,16,128]{2,1,0:T(8,128)} %eddy_plane.1.plane_ref), channel_id=1, source_target_pairs={{16,0},{20,4},{48,40},{52,44},{80,72},{84,76},{112,104},{116,108},... | collective-permute-start | bytes 122888 | tf_op jit(solution)/shard_map/ppermute | solution.py:626
  6.4 1.3 %collective-permute-start = (f32[5,16,128]{2,1,0:T(8,128)}, f32[5,16,128]{2,1,0:T(8,128)S(1)}, u32[]{:S(2)}, u32[]{:S(2)}) collective-permute-start(f32[5,16,128]{2,1,0:T(8,128)} %eddy_plane.1.plane_ref), channel_id=1, source_target_pairs={{8,0},{12,4},{32,40},{36,44},{64,72},{68,76},{96,104},{100,108},{1... | collective-permute-start | bytes 122888 | tf_op jit(solution)/shard_map/ppermute | solution.py:626
  7.7 0.8 %copy-done.8 = f32[5,16,128]{2,1,0:T(8,128)S(1)} copy-done((f32[5,16,128]{2,1,0:T(8,128)S(1)}, f32[5,16,128]{2,1,0:T(8,128)}, u32[]{:S(2)}) %copy-start.8) | copy-done | bytes 40984
  8.5 0.5 pack_faces.1
  9.0 3.7 %collective-permute-start.6 = (bf16[5,16,768]{2,1,0:T(8,128)(2,1)S(1)}, bf16[5,16,768]{2,1,0:T(8,128)(2,1)S(1)}, u32[]{:S(2)}, u32[]{:S(2)}) collective-permute-start(bf16[5,16,768]{2,1,0:T(8,128)(2,1)S(1)} %get-tuple-element.40), channel_id=1, source_target_pairs={{0,2},{2,0},{1,3},{3,1},{4,6},{6,4},{5,7},{7,5},{8,10},{10,8},{9,1... | collective-permute-start | bytes 368648 | tf_op jit(solution)/shard_map/ppermute | solution.py:670
  12.7 0.7 %collective-permute-start.5 = (f32[5,16,128]{2,1,0:T(8,128)S(1)}, f32[5,16,128]{2,1,0:T(8,128)S(1)}, u32[]{:S(2)}, u32[]{:S(2)}) collective-permute-start(f32[5,16,128]{2,1,0:T(8,128)S(1)} %add_add_fusion.2), channel_id=1, source_target_pairs={{44,0},{108,72},{172,136},{236,200},{45,1},{109,73},{173,137},{237... | collective-permute-start | bytes 122888 | tf_op jit(solution)/shard_map/ppermute | solution.py:626
  13.4 0.7 %collective-permute-start.4 = (f32[5,16,128]{2,1,0:T(8,128)S(1)}, f32[5,16,128]{2,1,0:T(8,128)S(1)}, u32[]{:S(2)}, u32[]{:S(2)}) collective-permute-start(f32[5,16,128]{2,1,0:T(8,128)S(1)} %add_add_fusion.2), channel_id=1, source_target_pairs={{40,0},{104,72},{168,136},{232,200},{41,1},{105,73},{169,137},{233... | collective-permute-start | bytes 122888 | tf_op jit(solution)/shard_map/ppermute | solution.py:626
  14.0 6.5 %collective-permute-start.3 = (f32[5,16,128]{2,1,0:T(8,128)S(1)}, f32[5,16,128]{2,1,0:T(8,128)S(1)}, u32[]{:S(2)}, u32[]{:S(2)}) collective-permute-start(f32[5,16,128]{2,1,0:T(8,128)S(1)} %add_add_fusion.2), channel_id=1, source_target_pairs={{4,0},{76,72},{140,136},{204,200},{5,1},{77,73},{141,137},{205,201... | collective-permute-start | bytes 122888 | tf_op jit(solution)/shard_map/ppermute | solution.py:626
  20.5 1.9 %collective-permute-start.9 = (bf16[5,16,128]{2,1,0:T(8,128)(2,1)S(1)}, bf16[5,16,128]{2,1,0:T(8,128)(2,1)S(1)}, u32[]{:S(2)}, u32[]{:S(2)}) collective-permute-start(bf16[5,16,128]{2,1,0:T(8,128)(2,1)S(1)} %get-tuple-element.45), channel_id=1, source_target_pairs={{4,8},{8,4},{12,16},{16,12},{20,24},{24,20},{28,32},{32,28},{36,40... | collective-permute-start | bytes 61448 | tf_op jit(solution)/shard_map/ppermute | solution.py:673
  22.7 2.5 %collective-permute-done.7.far_ref = bf16[5,16,128]{2,1,0:T(8,128)(2,1)S(1)} collective-permute-done((bf16[5,16,128]{2,1,0:T(8,128)(2,1)S(1)}, bf16[5,16,128]{2,1,0:T(8,128)(2,1)S(1)}, u32[]{:S(2)}, u32[]{:S(2)}) %collective-permute-start.7) | collective-permute-done | bytes 20512 | tf_op jit(solution)/shard_map/ppermute | solution.py:675
  25.2 0.7 %collective-permute-start.12 = (f32[5,16,128]{2,1,0:T(8,128)S(1)}, f32[5,16,128]{2,1,0:T(8,128)S(1)}, u32[]{:S(2)}, u32[]{:S(2)}) collective-permute-start(f32[5,16,128]{2,1,0:T(8,128)S(1)} %add_add_fusion.1), channel_id=1, source_target_pairs={{136,0},{137,1},{138,2},{139,3}} | collective-permute-start | bytes 122888 | tf_op jit(solution)/shard_map/ppermute | solution.py:626
  25.8 0.7 %collective-permute-start.11 = (f32[5,16,128]{2,1,0:T(8,128)S(1)}, f32[5,16,128]{2,1,0:T(8,128)S(1)}, u32[]{:S(2)}, u32[]{:S(2)}) collective-permute-start(f32[5,16,128]{2,1,0:T(8,128)S(1)} %add_add_fusion.1), channel_id=1, source_target_pairs={{200,0},{201,1},{202,2},{203,3}} | collective-permute-start | bytes 122888 | tf_op jit(solution)/shard_map/ppermute | solution.py:626
  26.5 0.7 %collective-permute-start.10 = (f32[5,16,128]{2,1,0:T(8,128)S(1)}, f32[5,16,128]{2,1,0:T(8,128)S(1)}, u32[]{:S(2)}, u32[]{:S(2)}) collective-permute-start(f32[5,16,128]{2,1,0:T(8,128)S(1)} %add_add_fusion.1), channel_id=1, source_target_pairs={{72,0},{73,1},{74,2},{75,3}} | collective-permute-start | bytes 122888 | tf_op jit(solution)/shard_map/ppermute | solution.py:626
  27.2 5.6 %phase_one.1 = (bf16[5,64,1536]{2,1,0:T(8,128)(2,1)S(1)}, bf16[5,64,1536]{2,1,0:T(8,128)(2,1)S(1)}, bf16[5,16,128]{2,1,0:T(8,128)(2,1)S(1)}, bf16[5,16,128]{2,1,...) custom-call(bf16[5,64,1536]{2,1,0:T(8,128)(2,1)S(1)} %copy-done, ...), custom_call_target="tpu_custom_call" | custom-call | flops 600000000 | bytes 18000000 | tf_op jit(solution)/shard_map/phase_one/pallas_call | solution.py:680
  32.8 1.2 %collective-permute-start.13 = (bf16[5,16,128]{2,1,0:T(8,128)(2,1)S(1)}, bf16[5,16,128]{2,1,0:T(8,128)(2,1)S(1)}, u32[]{:S(2)}, u32[]{:S(2)}) collective-permute-start(bf16[5,16,128]{2,1,0:T(8,128)(2,1)S(1)} %get-tuple-element.53), channel_id=1, source_target_pairs={{0,4},{4,0},{8,12},{12,8},{16,20},{20,16},{24,28},{28,24},{32,36},... | collective-permute-start | bytes 61448 | tf_op jit(solution)/shard_map/ppermute | solution.py:698
  34.1 0.8 %collective-permute-done.13.from_core_ref = bf16[5,16,128]{2,1,0:T(8,128)(2,1)S(1)} collective-permute-done((bf16[5,16,128]{2,1,0:T(8,128)(2,1)S(1)}, bf16[5,16,128]{2,1,0:T(8,128)(2,1)S(1)}, u32[]{:S(2)}, u32[]{:S(2)}) %collective-permute-start.13) | collective-permute-done | bytes 20512 | tf_op jit(solution)/shard_map/ppermute | solution.py:698
  34.9 0.8 %inflow_layer.1 = (bf16[5,64,1536]{2,1,0:T(8,128)(2,1)S(1)}, bf16[5,64,1536]{2,1,0:T(8,128)(2,1)S(1)}, bf16[5,16,768]{2,1,0:T(8,128)(2,1)S(1)}, bf16[5,16,128]{2,1,0:T(8,128)(2,1)S(1)}) custom-call(bf16[5,64,1536]{2,1,0:T(8,128)(2,1)S(1)} %get-tuple-element.48.held_any, ...), custom_call_target="tpu_custom_call", output_to_operand_aliasing={{0}: (0, {}), {1}: (1, {}), {2}: (2, {}), {3}: (3, {})} | custom-call | flops 10000000 | bytes 300000 | tf_op jit(solution)/shard_map/inflow_layer/pallas_call | solution.py:705
  35.7 1.5 %collective-permute-start.15 = (bf16[5,16,768]{2,1,0:T(8,128)(2,1)S(1)}, bf16[5,16,768]{2,1,0:T(8,128)(2,1)S(1)}, u32[]{:S(2)}, u32[]{:S(2)}) collective-permute-start(bf16[5,16,768]{2,1,0:T(8,128)(2,1)S(1)} %get-tuple-element.59), channel_id=1, source_target_pairs={{0,2},{2,0},{1,3},{3,1},{4,6},{6,4},{5,7},{7,5},{8,10},{10,8},{9,1... | collective-permute-start | bytes 368648 | tf_op jit(solution)/shard_map/ppermute | solution.py:728
  37.2 3.9 %collective-permute-start.14 = (bf16[5,16,128]{2,1,0:T(8,128)(2,1)S(1)}, bf16[5,16,128]{2,1,0:T(8,128)(2,1)S(1)}, u32[]{:S(2)}, u32[]{:S(2)}) collective-permute-start(bf16[5,16,128]{2,1,0:T(8,128)(2,1)S(1)} %get-tuple-element.58), channel_id=1, source_target_pairs={{4,8},{8,4},{12,16},{16,12},{20,24},{24,20},{28,32},{32,28},{36,40... | collective-permute-start | bytes 61448 | tf_op jit(solution)/shard_map/ppermute | solution.py:699
  41.1 0.6 %collective-permute-start.16 = (bf16[5,16,128]{2,1,0:T(8,128)(2,1)S(1)}, bf16[5,16,128]{2,1,0:T(8,128)(2,1)S(1)}, u32[]{:S(2)}, u32[]{:S(2)}) collective-permute-start(bf16[5,16,128]{2,1,0:T(8,128)(2,1)S(1)} %get-tuple-element.60), channel_id=1, source_target_pairs={{0,1},{1,0},{2,3},{3,2},{4,5},{5,4},{6,7},{7,6},{8,9},{9,8},{10,11... | collective-permute-start | bytes 61448 | tf_op jit(solution)/shard_map/ppermute | solution.py:729
  41.7 2.9 %inner_two.1.part_ref = f32[5,64,1536]{2,1,0:T(8,128)S(1)} custom-call(bf16[5,64,1536]{2,1,0:T(8,128)(2,1)S(1)} %get-tuple-element.55.v_ref, f32[5,3,5]{2,1,0:T(4,128)S(1)} %bitcast.16, bf16[3,64,64]{2,1,0:T(8,128)(2,1)S(1)} %copy-done.1), custom_call_target="tpu_custom_call" | custom-call | flops 10000000 | bytes 300000 | tf_op jit(solution)/shard_map/inner_two/pallas_call | solution.py:730
  44.6 4.6 %outer_two.1 = bf16[5,64,1536]{2,1,0:T(8,128)(2,1)} custom-call(bf16[5,64,1536]{2,1,0:T(8,128)(2,1)S(1)} %get-tuple-element.55.v_ref, bf16[5,64,1536]{2,1,0:T(8,128)(2,1)S(1)} %get-tuple-element.56.trace_ref, bf16[5,64,1536]{2,1,0:T(8,128)(2,1)S(1)} %copy-done, f32[5,64,1536]{2,1,0:T(8,128)S(1)} %inner_two.1.part_ref, f32[5,16,128]{2,1,0:T(8,128)S(1)} %bitcast.11, ...), custom_call_target="tpu_custom_call" | custom-call | flops 400000000 | bytes 12000000 | tf_op jit(solution)/shard_map/outer_two/pallas_call | solution.py:742
  (40 shorter events, 0.3 us)
Async XLA Ops:
  0.0 27.2 %copy-start.6 = (bf16[64,64]{1,0:T(8,128)(2,1)S(1)}, bf16[64,64]{1,0:T(8,128)(2,1)}, u32[]{:S(2)}) copy-start(bf16[64,64]{1,0:T(8,128)(2,1)} %wall_ref.5) | copy-start | bytes 24580
  0.0 27.2 %copy-start.7 = (bf16[64,64]{1,0:T(8,128)(2,1)S(1)}, bf16[64,64]{1,0:T(8,128)(2,1)}, u32[]{:S(2)}) copy-start(bf16[64,64]{1,0:T(8,128)(2,1)} %smooth_ref.1) | copy-start | bytes 24580
  0.0 27.2 %copy-start.5 = (bf16[64,96]{1,0:T(8,128)(2,1)S(1)}, bf16[64,96]{1,0:T(8,128)(2,1)}, u32[]{:S(2)}) copy-start(bf16[64,96]{1,0:T(8,128)(2,1)} %lift_ref.5) | copy-start | bytes 36868
  0.0 27.2 %copy-start.1 = (bf16[3,64,64]{2,1,0:T(8,128)(2,1)S(1)}, bf16[3,64,64]{2,1,0:T(8,128)(2,1)}, u32[]{:S(2)}) copy-start(bf16[3,64,64]{2,1,0:T(8,128)(2,1)} %volume_ref.5) | copy-start | bytes 73732
  0.0 27.2 %copy-start.4 = (f32[3,5,5]{2,0,1:T(4,128)S(1)}, f32[3,5,5]{2,0,1:T(4,128)}, u32[]{:S(2)}) copy-start(f32[3,5,5]{2,0,1:T(4,128)} %param.14) | copy-start | bytes 904
  3.7 31.3 %copy-start.2 = (f32[1,1,5,2048]{3,1,2,0:T(1,128)S(1)}, f32[1,1,5,2048]{3,1,2,0:T(1,128)}, u32[]{:S(2)}) copy-start(f32[1,1,5,2048]{3,1,2,0:T(1,128)} %param.22) | copy-start | bytes 122884
  3.7 31.3 %copy-start.3 = (f32[1,1,5,2048]{3,1,2,0:T(1,128)S(1)}, f32[1,1,5,2048]{3,1,2,0:T(1,128)}, u32[]{:S(2)}) copy-start(f32[1,1,5,2048]{3,1,2,0:T(1,128)} %param.23) | copy-start | bytes 122884
  3.7 9.0 %collective-permute-start.2 = (f32[5,16,128]{2,1,0:T(8,128)}, f32[5,16,128]{2,1,0:T(8,128)S(1)}, u32[]{:S(2)}, u32[]{:S(2)}) collective-permute-start(f32[5,16,128]{2,1,0:T(8,128)} %eddy_plane.1.plane_ref), channel_id=1, source_target_pairs={{24,0},{28,4},{56,40},{60,44},{88,72},{92,76},{120,104},{124,108},... | collective-permute-start | bytes 122888 | tf_op jit(solution)/shard_map/ppermute | solution.py:626
  5.1 7.5 %collective-permute-start.1 = (f32[5,16,128]{2,1,0:T(8,128)}, f32[5,16,128]{2,1,0:T(8,128)S(1)}, u32[]{:S(2)}, u32[]{:S(2)}) collective-permute-start(f32[5,16,128]{2,1,0:T(8,128)} %eddy_plane.1.plane_ref), channel_id=1, source_target_pairs={{16,0},{20,4},{48,40},{52,44},{80,72},{84,76},{112,104},{116,108},... | collective-permute-start | bytes 122888 | tf_op jit(solution)/shard_map/ppermute | solution.py:626
  6.4 6.2 %collective-permute-start = (f32[5,16,128]{2,1,0:T(8,128)}, f32[5,16,128]{2,1,0:T(8,128)S(1)}, u32[]{:S(2)}, u32[]{:S(2)}) collective-permute-start(f32[5,16,128]{2,1,0:T(8,128)} %eddy_plane.1.plane_ref), channel_id=1, source_target_pairs={{8,0},{12,4},{32,40},{36,44},{64,72},{68,76},{96,104},{100,108},{1... | collective-permute-start | bytes 122888 | tf_op jit(solution)/shard_map/ppermute | solution.py:626
  9.0 13.5 %collective-permute-start.6 = (bf16[5,16,768]{2,1,0:T(8,128)(2,1)S(1)}, bf16[5,16,768]{2,1,0:T(8,128)(2,1)S(1)}, u32[]{:S(2)}, u32[]{:S(2)}) collective-permute-start(bf16[5,16,768]{2,1,0:T(8,128)(2,1)S(1)} %get-tuple-element.40), channel_id=1, source_target_pairs={{0,2},{2,0},{1,3},{3,1},{4,6},{6,4},{5,7},{7,5},{8,10},{10,8},{9,1... | collective-permute-start | bytes 368648 | tf_op jit(solution)/shard_map/ppermute | solution.py:670
  12.7 9.9 %collective-permute-start.5 = (f32[5,16,128]{2,1,0:T(8,128)S(1)}, f32[5,16,128]{2,1,0:T(8,128)S(1)}, u32[]{:S(2)}, u32[]{:S(2)}) collective-permute-start(f32[5,16,128]{2,1,0:T(8,128)S(1)} %add_add_fusion.2), channel_id=1, source_target_pairs={{44,0},{108,72},{172,136},{236,200},{45,1},{109,73},{173,137},{237... | collective-permute-start | bytes 122888 | tf_op jit(solution)/shard_map/ppermute | solution.py:626
  13.4 9.3 %collective-permute-start.4 = (f32[5,16,128]{2,1,0:T(8,128)S(1)}, f32[5,16,128]{2,1,0:T(8,128)S(1)}, u32[]{:S(2)}, u32[]{:S(2)}) collective-permute-start(f32[5,16,128]{2,1,0:T(8,128)S(1)} %add_add_fusion.2), channel_id=1, source_target_pairs={{40,0},{104,72},{168,136},{232,200},{41,1},{105,73},{169,137},{233... | collective-permute-start | bytes 122888 | tf_op jit(solution)/shard_map/ppermute | solution.py:626
  14.0 8.7 %collective-permute-start.3 = (f32[5,16,128]{2,1,0:T(8,128)S(1)}, f32[5,16,128]{2,1,0:T(8,128)S(1)}, u32[]{:S(2)}, u32[]{:S(2)}) collective-permute-start(f32[5,16,128]{2,1,0:T(8,128)S(1)} %add_add_fusion.2), channel_id=1, source_target_pairs={{4,0},{76,72},{140,136},{204,200},{5,1},{77,73},{141,137},{205,201... | collective-permute-start | bytes 122888 | tf_op jit(solution)/shard_map/ppermute | solution.py:626
  20.5 6.7 %collective-permute-start.9 = (bf16[5,16,128]{2,1,0:T(8,128)(2,1)S(1)}, bf16[5,16,128]{2,1,0:T(8,128)(2,1)S(1)}, u32[]{:S(2)}, u32[]{:S(2)}) collective-permute-start(bf16[5,16,128]{2,1,0:T(8,128)(2,1)S(1)} %get-tuple-element.45), channel_id=1, source_target_pairs={{4,8},{8,4},{12,16},{16,12},{20,24},{24,20},{28,32},{32,28},{36,40... | collective-permute-start | bytes 61448 | tf_op jit(solution)/shard_map/ppermute | solution.py:673
  22.5 2.7 %collective-permute-start.7 = (bf16[5,16,128]{2,1,0:T(8,128)(2,1)S(1)}, bf16[5,16,128]{2,1,0:T(8,128)(2,1)S(1)}, u32[]{:S(2)}, u32[]{:S(2)}) collective-permute-start(bf16[5,16,128]{2,1,0:T(8,128)(2,1)S(1)} %get-tuple-element.42), channel_id=1, source_target_pairs={{0,1},{1,0},{2,3},{3,2},{4,5},{5,4},{6,7},{7,6},{8,9},{9,8},{10,11... | collective-permute-start | bytes 61448 | tf_op jit(solution)/shard_map/ppermute | solution.py:675
  22.6 2.6 %collective-permute-start.8 = (bf16[5,16,128]{2,1,0:T(8,128)(2,1)S(1)}, bf16[5,16,128]{2,1,0:T(8,128)(2,1)S(1)}, u32[]{:S(2)}, u32[]{:S(2)}) collective-permute-start(bf16[5,16,128]{2,1,0:T(8,128)(2,1)S(1)} %get-tuple-element.43), channel_id=1, source_target_pairs={{0,4},{4,0},{8,12},{12,8},{16,20},{20,16},{24,28},{28,24},{32,36},... | collective-permute-start | bytes 61448 | tf_op jit(solution)/shard_map/ppermute | solution.py:676
  25.2 8.9 %collective-permute-start.12 = (f32[5,16,128]{2,1,0:T(8,128)S(1)}, f32[5,16,128]{2,1,0:T(8,128)S(1)}, u32[]{:S(2)}, u32[]{:S(2)}) collective-permute-start(f32[5,16,128]{2,1,0:T(8,128)S(1)} %add_add_fusion.1), channel_id=1, source_target_pairs={{136,0},{137,1},{138,2},{139,3}} | collective-permute-start | bytes 122888 | tf_op jit(solution)/shard_map/ppermute | solution.py:626
  25.8 8.3 %collective-permute-start.11 = (f32[5,16,128]{2,1,0:T(8,128)S(1)}, f32[5,16,128]{2,1,0:T(8,128)S(1)}, u32[]{:S(2)}, u32[]{:S(2)}) collective-permute-start(f32[5,16,128]{2,1,0:T(8,128)S(1)} %add_add_fusion.1), channel_id=1, source_target_pairs={{200,0},{201,1},{202,2},{203,3}} | collective-permute-start | bytes 122888 | tf_op jit(solution)/shard_map/ppermute | solution.py:626
  26.5 7.6 %collective-permute-start.10 = (f32[5,16,128]{2,1,0:T(8,128)S(1)}, f32[5,16,128]{2,1,0:T(8,128)S(1)}, u32[]{:S(2)}, u32[]{:S(2)}) collective-permute-start(f32[5,16,128]{2,1,0:T(8,128)S(1)} %add_add_fusion.1), channel_id=1, source_target_pairs={{72,0},{73,1},{74,2},{75,3}} | collective-permute-start | bytes 122888 | tf_op jit(solution)/shard_map/ppermute | solution.py:626
  32.8 2.1 %collective-permute-start.13 = (bf16[5,16,128]{2,1,0:T(8,128)(2,1)S(1)}, bf16[5,16,128]{2,1,0:T(8,128)(2,1)S(1)}, u32[]{:S(2)}, u32[]{:S(2)}) collective-permute-start(bf16[5,16,128]{2,1,0:T(8,128)(2,1)S(1)} %get-tuple-element.53), channel_id=1, source_target_pairs={{0,4},{4,0},{8,12},{12,8},{16,20},{20,16},{24,28},{28,24},{32,36},... | collective-permute-start | bytes 61448 | tf_op jit(solution)/shard_map/ppermute | solution.py:698
  35.7 8.9 %collective-permute-start.15 = (bf16[5,16,768]{2,1,0:T(8,128)(2,1)S(1)}, bf16[5,16,768]{2,1,0:T(8,128)(2,1)S(1)}, u32[]{:S(2)}, u32[]{:S(2)}) collective-permute-start(bf16[5,16,768]{2,1,0:T(8,128)(2,1)S(1)} %get-tuple-element.59), channel_id=1, source_target_pairs={{0,2},{2,0},{1,3},{3,1},{4,6},{6,4},{5,7},{7,5},{8,10},{10,8},{9,1... | collective-permute-start | bytes 368648 | tf_op jit(solution)/shard_map/ppermute | solution.py:728
  37.2 7.4 %collective-permute-start.14 = (bf16[5,16,128]{2,1,0:T(8,128)(2,1)S(1)}, bf16[5,16,128]{2,1,0:T(8,128)(2,1)S(1)}, u32[]{:S(2)}, u32[]{:S(2)}) collective-permute-start(bf16[5,16,128]{2,1,0:T(8,128)(2,1)S(1)} %get-tuple-element.58), channel_id=1, source_target_pairs={{4,8},{8,4},{12,16},{16,12},{20,24},{24,20},{28,32},{32,28},{36,40... | collective-permute-start | bytes 61448 | tf_op jit(solution)/shard_map/ppermute | solution.py:699
  41.1 3.5 %collective-permute-start.16 = (bf16[5,16,128]{2,1,0:T(8,128)(2,1)S(1)}, bf16[5,16,128]{2,1,0:T(8,128)(2,1)S(1)}, u32[]{:S(2)}, u32[]{:S(2)}) collective-permute-start(bf16[5,16,128]{2,1,0:T(8,128)(2,1)S(1)} %get-tuple-element.60), channel_id=1, source_target_pairs={{0,1},{1,0},{2,3},{3,2},{4,5},{5,4},{6,7},{7,6},{8,9},{9,8},{10,11... | collective-permute-start | bytes 61448 | tf_op jit(solution)/shard_map/ppermute | solution.py:729
  (3 other events, 29.0 us)

commit v11 on v10

--- a/solution.py
+++ b/solution.py
@@ -372,11 +372,13 @@
 
 
 def phase_one_kernel(
-    v_ref, from_core_ref, from_chip_ref, near_ref, far_ref, pin_ref, coefs, volume_ref, lift_ref,
+    v_ref, from_core_ref, from_chip_ref, near_ref, far_ref, pin_ref, jacobian_any, volume_ref, lift_ref,
     wall_ref, filter_ref,
     out_ref, out_trace_ref, core_ref, chip_ref, pitch_ref, span_ref, mixed, own, weights_held,
-    span_held,
+    span_held, coefs, sem,
 ):
+    load = pltpu.make_async_copy(jacobian_any, coefs, sem)
+    load.start()
     first_span = lax.axis_index("span") == 0
     lane = lanes()
     pick = trace_selector()
@@ -424,6 +426,7 @@
 
     for pair in range(EX // 2):
         add(pair)
+    load.wait()
     pipeline(vector, matrix)
     span_ref[...] = span_held[...].astype(bf16)
     store_stream(
@@ -431,7 +434,11 @@
     )
 
 
-def inner_two_kernel(v_ref, coefs, volume_ref, part_ref, mixed, weights_held):
+def inner_two_kernel(
+    v_ref, jacobian_any, volume_ref, part_ref, mixed, weights_held, coefs, sem
+):
+    load = pltpu.make_async_copy(jacobian_any, coefs, sem)
+    load.start()
     weights = fill(weights_held, [volume_ref[d] for d in range(3)])
     vector, matrix = [], []
 
@@ -447,13 +454,17 @@
 
     for pair in range(EX // 2):
         add(pair)
+    load.wait()
     pipeline(vector, matrix)
 
 
 def outer_two_kernel(
     v_ref, trace_ref, base_ref, part_ref, mean_ref, amp_ref, plane_ref, from_core_ref, from_chip_ref,
-    near_ref, far_ref, pin_ref, coefs, lift_ref, wall_ref, smooth_ref, out_ref, mixed, weights_held,
+    near_ref, far_ref, pin_ref, jacobian_any, lift_ref, wall_ref, smooth_ref, out_ref, mixed,
+    weights_held, coefs, sem,
 ):
+    load = pltpu.make_async_copy(jacobian_any, coefs, sem)
+    load.start()
     first_span = lax.axis_index("span") == 0
     first_rans = lax.axis_index("rans") == 0
     lane = lanes()
@@ -496,6 +507,7 @@
 
     for pair in range(EX // 2):
         add(pair)
+    load.wait()
     pipeline(vector, matrix)
 
 
@@ -505,9 +517,9 @@
 
 def inflow_kernel(
     held_any, held_trace_any, held_pitch_any, held_span_any, v_ref, mean_ref, amp_ref, plane_ref,
-    near_ref, far_ref, pin_ref, coefs, volume_ref, lift_ref, wall_ref, filter_ref, out_any,
+    near_ref, far_ref, pin_ref, jacobian_any, volume_ref, lift_ref, wall_ref, filter_ref, out_any,
     out_trace_any, pitch_any, span_any, mixed, own, weights_held, edge, edge_trace, edge_pitch,
-    edge_span, sems,
+    edge_span, coefs, sems,
 ):
     first_span = lax.axis_index("span") == 0
     lane = lanes()
@@ -518,6 +530,7 @@
         loads = [
             pltpu.make_async_copy(held_pitch_any.at[:, :, layer], edge_pitch, sems.at[0]),
             pltpu.make_async_copy(held_span_any, edge_span, sems.at[1]),
+            pltpu.make_async_copy(jacobian_any, coefs, sems.at[6]),
         ]
         for copy in loads:
             copy.start()
@@ -559,10 +572,10 @@
             + mix_fluxes(read, coefs, mixed)
             + mix_wall(read, lambda: pin_ref[:, layer].astype(f32), mixed, 288)
         )
+        for copy in loads:
+            copy.wait()
         for step in vector:
             step()
-        for copy in loads:
-            copy.wait()
         for step in staggered(
             [lambda f, _: dot(weights, mixed[f]), finish(read, None, smooth), store]
         ):
@@ -580,7 +593,7 @@
 
 
 VMEM = pl.BlockSpec(memory_space=pltpu.VMEM)
-SMEM = pl.BlockSpec(memory_space=pltpu.SMEM)
+ANY = pl.BlockSpec(memory_space=pl.ANY)
 PARAMS = pltpu.CompilerParams(vmem_limit_bytes=40 * 2**20)
 
 
@@ -630,6 +643,7 @@
         return value
 
     jacobian = flux_jacobian.transpose(1, 0, 2)
+    jacobian_scratch = [pltpu.SMEM(jacobian.shape, f32), pltpu.SemaphoreType.DMA(())]
     pins = pinched_map.reshape(1, -1)
     elements = solution.shape[2]
     traces = shape_of(FIELDS, NODES, elements)
@@ -680,13 +694,14 @@
     phase_one, trace_one, core, chip, pitch, span = pl.pallas_call(
         phase_one_kernel,
         out_shape=(traces, traces) + sends,
-        in_specs=[VMEM] * 6 + [SMEM] + [VMEM] * 4,
+        in_specs=[VMEM] * 6 + [ANY] + [VMEM] * 4,
         out_specs=(VMEM,) * 6,
         scratch_shapes=[
             pltpu.VMEM((2, FIELDS, MIXED, PAIR), bf16),
             pltpu.VMEM((2, FIELDS, NODES, PAIR), bf16),
             pltpu.VMEM((NODES, MIXED), bf16),
             span_scratch,
+            *jacobian_scratch,
         ],
         compiler_params=PARAMS,
         cost_estimate=cost(6),
@@ -701,12 +716,11 @@
 
     mean = mean_inflow.reshape(FIELDS, 16, CELLS)
     amplitude = eddy_amplitude.reshape(FIELDS, 16, CELLS)
-    anywhere = pl.BlockSpec(memory_space=pl.ANY)
     phase_one, trace_one, pitch, span = pl.pallas_call(
         inflow_kernel,
         out_shape=(traces, traces, sends[2], sends[3]),
-        in_specs=[anywhere] * 4 + [VMEM] * 7 + [SMEM] + [VMEM] * 4,
-        out_specs=(anywhere,) * 4,
+        in_specs=[ANY] * 4 + [VMEM] * 7 + [ANY] + [VMEM] * 4,
+        out_specs=(ANY,) * 4,
         scratch_shapes=[
             pltpu.VMEM((FIELDS, MIXED, CELLS), bf16),
             pltpu.VMEM((FIELDS, NODES, CELLS), bf16),
@@ -715,7 +729,8 @@
             pltpu.VMEM((FIELDS, NODES, CELLS), bf16),
             pltpu.VMEM((FIELDS, 16, CELLS), bf16),
             pltpu.VMEM((FIELDS, 16, CELLS), bf16),
-            pltpu.SemaphoreType.DMA((6,)),
+            jacobian_scratch[0],
+            pltpu.SemaphoreType.DMA((7,)),
         ],
         input_output_aliases={0: 0, 1: 1, 2: 2, 3: 3},
         compiler_params=PARAMS,
@@ -730,10 +745,11 @@
     part = pl.pallas_call(
         inner_two_kernel,
         out_shape=shape_of(FIELDS, NODES, elements, dtype=f32),
-        in_specs=[VMEM, SMEM, VMEM],
+        in_specs=[VMEM, ANY, VMEM],
         out_specs=VMEM,
         scratch_shapes=[
-            pltpu.VMEM((2, FIELDS, INNER, PAIR), bf16), pltpu.VMEM((NODES, INNER), bf16)
+            pltpu.VMEM((2, FIELDS, INNER, PAIR), bf16), pltpu.VMEM((NODES, INNER), bf16),
+            *jacobian_scratch,
         ],
         compiler_params=PARAMS,
         cost_estimate=cost(0.1),
@@ -742,11 +758,12 @@
     return pl.pallas_call(
         outer_two_kernel,
         out_shape=traces,
-        in_specs=[VMEM] * 12 + [SMEM] + [VMEM] * 3,
+        in_specs=[VMEM] * 12 + [ANY] + [VMEM] * 3,
         out_specs=VMEM,
         scratch_shapes=[
             pltpu.VMEM((2, FIELDS, MIXED - INNER, PAIR), bf16),
             pltpu.VMEM((NODES, MIXED - INNER), bf16),
+            *jacobian_scratch,
         ],
         compiler_params=PARAMS,
         cost_estimate=cost(4),

time: 49.6 us -> 48.8 us (0.984)
  Pallas kernels: 18 us -> 17 us
    pallas_call x1, Pallas kernels: 0.77 us -> 0.07 us  [body(): pl.pallas_call(inflow_kernel, out_shape=(traces, traces, sends[2], sends[...]
where the time goes in v11:
time: 48.8 us; the launch traced here: 48.4 us
  starting transfers between devices  26.7 us (55%)
  Pallas kernels  17 us (35%)
  waiting for transfers between devices  3.32 us (7%)
  local copies, waits for them, and re-layouts  0.82 us (2%)
  between operations  0.51 us (1%)
    ppermute x9, starting transfers between devices, gather_sum(): parts = [lax.ppermute(value, 'rans', pairs) for pairs in level]  13.8 us
    ppermute x2, starting transfers between devices, body(): from_chip = lax.ppermute(chip, 'rans', next_chip)  5.8 us
    pallas_call x1, Pallas kernels, body(): pl.pallas_call(phase_one_kernel, out_shape=(traces, traces) + sends, in_s...  5.56 us
    ppermute x2, starting transfers between devices, body(): near = lax.ppermute(pitch, 'pitch', swap)  5.12 us
    pallas_call x1, Pallas kernels, body(): pl.pallas_call(outer_two_kernel, out_shape=traces, in_specs=[VMEM] * 12 +...  4.4 us
    pallas_call x1, Pallas kernels, body(): pl.pallas_call(functools.partial(plane_kernel, normalizer=float((plane_ro...  3.61 us
    pallas_call x1, Pallas kernels, body(): pl.pallas_call(inner_two_kernel, out_shape=shape_of(FIELDS, NODES, elemen...  2.92 us
    ppermute x2, waiting for transfers between devices, body(): far = lax.ppermute(span, 'span', swap)  2.47 us
  transfers between devices with their start and end apart: 17, of which 2 were waited for; matrix products, arithmetic and copies ran while one was open for 0% of the time, Pallas kernels for 18%

profile of v11, /device:TPU:1, one launch (start us, length us, event | category | flops | bytes accessed | tf_op | source)
XLA Modules:
  0.0 48.4 jit_solution(1221536294307940514)
XLA Ops:
  0.0 3.6 %eddy_plane.1.plane_ref = f32[5,16,128]{2,1,0:T(8,128)} custom-call(s32[64,256]{1,0:T(8,128)} %bitcast.18, s32[1,256]{1,0:T(1,128)} %bitcast.20, f32[64,256]{1,0:T(8,128)} %bitcast.19), custom_call_target="tpu_custom_call" | custom-call | flops 400000000 | bytes 12000000 | tf_op jit(solution)/shard_map/eddy_plane/pallas_call | solution.py:656
  3.7 1.4 %collective-permute-start.2 = (f32[5,16,128]{2,1,0:T(8,128)}, f32[5,16,128]{2,1,0:T(8,128)S(1)}, u32[]{:S(2)}, u32[]{:S(2)}) collective-permute-start(f32[5,16,128]{2,1,0:T(8,128)} %eddy_plane.1.plane_ref), channel_id=1, source_target_pairs={{24,0},{28,4},{56,40},{60,44},{88,72},{92,76},{120,104},{124,108},... | collective-permute-start | bytes 122888 | tf_op jit(solution)/shard_map/ppermute | solution.py:639
  5.1 1.3 %collective-permute-start.1 = (f32[5,16,128]{2,1,0:T(8,128)}, f32[5,16,128]{2,1,0:T(8,128)S(1)}, u32[]{:S(2)}, u32[]{:S(2)}) collective-permute-start(f32[5,16,128]{2,1,0:T(8,128)} %eddy_plane.1.plane_ref), channel_id=1, source_target_pairs={{16,0},{20,4},{48,40},{52,44},{80,72},{84,76},{112,104},{116,108},... | collective-permute-start | bytes 122888 | tf_op jit(solution)/shard_map/ppermute | solution.py:639
  6.4 1.3 %collective-permute-start = (f32[5,16,128]{2,1,0:T(8,128)}, f32[5,16,128]{2,1,0:T(8,128)S(1)}, u32[]{:S(2)}, u32[]{:S(2)}) collective-permute-start(f32[5,16,128]{2,1,0:T(8,128)} %eddy_plane.1.plane_ref), channel_id=1, source_target_pairs={{8,0},{12,4},{32,40},{36,44},{64,72},{68,76},{96,104},{100,108},{1... | collective-permute-start | bytes 122888 | tf_op jit(solution)/shard_map/ppermute | solution.py:639
  7.7 0.8 %copy-done.8 = f32[5,16,128]{2,1,0:T(8,128)S(1)} copy-done((f32[5,16,128]{2,1,0:T(8,128)S(1)}, f32[5,16,128]{2,1,0:T(8,128)}, u32[]{:S(2)}) %copy-start.8) | copy-done | bytes 40984
  8.5 0.5 pack_faces.1
  9.0 3.7 %collective-permute-start.6 = (bf16[5,16,768]{2,1,0:T(8,128)(2,1)S(1)}, bf16[5,16,768]{2,1,0:T(8,128)(2,1)S(1)}, u32[]{:S(2)}, u32[]{:S(2)}) collective-permute-start(bf16[5,16,768]{2,1,0:T(8,128)(2,1)S(1)} %get-tuple-element.40), channel_id=1, source_target_pairs={{0,2},{2,0},{1,3},{3,1},{4,6},{6,4},{5,7},{7,5},{8,10},{10,8},{9,1... | collective-permute-start | bytes 368648 | tf_op jit(solution)/shard_map/ppermute | solution.py:684
  12.7 0.7 %collective-permute-start.5 = (f32[5,16,128]{2,1,0:T(8,128)S(1)}, f32[5,16,128]{2,1,0:T(8,128)S(1)}, u32[]{:S(2)}, u32[]{:S(2)}) collective-permute-start(f32[5,16,128]{2,1,0:T(8,128)S(1)} %add_add_fusion.2), channel_id=1, source_target_pairs={{44,0},{108,72},{172,136},{236,200},{45,1},{109,73},{173,137},{237... | collective-permute-start | bytes 122888 | tf_op jit(solution)/shard_map/ppermute | solution.py:639
  13.4 0.7 %collective-permute-start.4 = (f32[5,16,128]{2,1,0:T(8,128)S(1)}, f32[5,16,128]{2,1,0:T(8,128)S(1)}, u32[]{:S(2)}, u32[]{:S(2)}) collective-permute-start(f32[5,16,128]{2,1,0:T(8,128)S(1)} %add_add_fusion.2), channel_id=1, source_target_pairs={{40,0},{104,72},{168,136},{232,200},{41,1},{105,73},{169,137},{233... | collective-permute-start | bytes 122888 | tf_op jit(solution)/shard_map/ppermute | solution.py:639
  14.0 6.5 %collective-permute-start.3 = (f32[5,16,128]{2,1,0:T(8,128)S(1)}, f32[5,16,128]{2,1,0:T(8,128)S(1)}, u32[]{:S(2)}, u32[]{:S(2)}) collective-permute-start(f32[5,16,128]{2,1,0:T(8,128)S(1)} %add_add_fusion.2), channel_id=1, source_target_pairs={{4,0},{76,72},{140,136},{204,200},{5,1},{77,73},{141,137},{205,201... | collective-permute-start | bytes 122888 | tf_op jit(solution)/shard_map/ppermute | solution.py:639
  20.5 1.9 %collective-permute-start.9 = (bf16[5,16,128]{2,1,0:T(8,128)(2,1)S(1)}, bf16[5,16,128]{2,1,0:T(8,128)(2,1)S(1)}, u32[]{:S(2)}, u32[]{:S(2)}) collective-permute-start(bf16[5,16,128]{2,1,0:T(8,128)(2,1)S(1)} %get-tuple-element.45), channel_id=1, source_target_pairs={{4,8},{8,4},{12,16},{16,12},{20,24},{24,20},{28,32},{32,28},{36,40... | collective-permute-start | bytes 61448 | tf_op jit(solution)/shard_map/ppermute | solution.py:687
  22.6 0.1 collective-permute-start.8
  22.7 2.5 %collective-permute-done.7.far_ref = bf16[5,16,128]{2,1,0:T(8,128)(2,1)S(1)} collective-permute-done((bf16[5,16,128]{2,1,0:T(8,128)(2,1)S(1)}, bf16[5,16,128]{2,1,0:T(8,128)(2,1)S(1)}, u32[]{:S(2)}, u32[]{:S(2)}) %collective-permute-start.7) | collective-permute-done | bytes 20512 | tf_op jit(solution)/shard_map/ppermute | solution.py:689
  25.2 0.7 %collective-permute-start.12 = (f32[5,16,128]{2,1,0:T(8,128)S(1)}, f32[5,16,128]{2,1,0:T(8,128)S(1)}, u32[]{:S(2)}, u32[]{:S(2)}) collective-permute-start(f32[5,16,128]{2,1,0:T(8,128)S(1)} %add_add_fusion.1), channel_id=1, source_target_pairs={{136,0},{137,1},{138,2},{139,3}} | collective-permute-start | bytes 122888 | tf_op jit(solution)/shard_map/ppermute | solution.py:639
  25.8 0.7 %collective-permute-start.11 = (f32[5,16,128]{2,1,0:T(8,128)S(1)}, f32[5,16,128]{2,1,0:T(8,128)S(1)}, u32[]{:S(2)}, u32[]{:S(2)}) collective-permute-start(f32[5,16,128]{2,1,0:T(8,128)S(1)} %add_add_fusion.1), channel_id=1, source_target_pairs={{200,0},{201,1},{202,2},{203,3}} | collective-permute-start | bytes 122888 | tf_op jit(solution)/shard_map/ppermute | solution.py:639
  26.5 0.7 %collective-permute-start.10 = (f32[5,16,128]{2,1,0:T(8,128)S(1)}, f32[5,16,128]{2,1,0:T(8,128)S(1)}, u32[]{:S(2)}, u32[]{:S(2)}) collective-permute-start(f32[5,16,128]{2,1,0:T(8,128)S(1)} %add_add_fusion.1), channel_id=1, source_target_pairs={{72,0},{73,1},{74,2},{75,3}} | collective-permute-start | bytes 122888 | tf_op jit(solution)/shard_map/ppermute | solution.py:639
  27.2 5.6 %phase_one.1 = (bf16[5,64,1536]{2,1,0:T(8,128)(2,1)S(1)}, bf16[5,64,1536]{2,1,0:T(8,128)(2,1)S(1)}, bf16[5,16,128]{2,1,0:T(8,128)(2,1)S(1)}, bf16[5,16,128]{2,1,...) custom-call(bf16[5,64,1536]{2,1,0:T(8,128)(2,1)S(1)} %copy-done, ...), custom_call_target="tpu_custom_call" | custom-call | flops 600000000 | bytes 18000000 | tf_op jit(solution)/shard_map/phase_one/pallas_call | solution.py:694
  32.8 1.3 %collective-permute-start.13 = (bf16[5,16,128]{2,1,0:T(8,128)(2,1)S(1)}, bf16[5,16,128]{2,1,0:T(8,128)(2,1)S(1)}, u32[]{:S(2)}, u32[]{:S(2)}) collective-permute-start(bf16[5,16,128]{2,1,0:T(8,128)(2,1)S(1)} %get-tuple-element.53), channel_id=1, source_target_pairs={{0,4},{4,0},{8,12},{12,8},{16,20},{20,16},{24,28},{28,24},{32,36},... | collective-permute-start | bytes 61448 | tf_op jit(solution)/shard_map/ppermute | solution.py:713
  34.1 0.8 %collective-permute-done.13.from_core_ref = bf16[5,16,128]{2,1,0:T(8,128)(2,1)S(1)} collective-permute-done((bf16[5,16,128]{2,1,0:T(8,128)(2,1)S(1)}, bf16[5,16,128]{2,1,0:T(8,128)(2,1)S(1)}, u32[]{:S(2)}, u32[]{:S(2)}) %collective-permute-start.13) | collective-permute-done | bytes 20512 | tf_op jit(solution)/shard_map/ppermute | solution.py:713
  35.0 1.5 %collective-permute-start.15 = (bf16[5,16,768]{2,1,0:T(8,128)(2,1)S(1)}, bf16[5,16,768]{2,1,0:T(8,128)(2,1)S(1)}, u32[]{:S(2)}, u32[]{:S(2)}) collective-permute-start(bf16[5,16,768]{2,1,0:T(8,128)(2,1)S(1)} %get-tuple-element.59), channel_id=1, source_target_pairs={{0,2},{2,0},{1,3},{3,1},{4,6},{6,4},{5,7},{7,5},{8,10},{10,8},{9,1... | collective-permute-start | bytes 368648 | tf_op jit(solution)/shard_map/ppermute | solution.py:743
  36.5 3.9 %collective-permute-start.14 = (bf16[5,16,128]{2,1,0:T(8,128)(2,1)S(1)}, bf16[5,16,128]{2,1,0:T(8,128)(2,1)S(1)}, u32[]{:S(2)}, u32[]{:S(2)}) collective-permute-start(bf16[5,16,128]{2,1,0:T(8,128)(2,1)S(1)} %get-tuple-element.58), channel_id=1, source_target_pairs={{4,8},{8,4},{12,16},{16,12},{20,24},{24,20},{28,32},{32,28},{36,40... | collective-permute-start | bytes 61448 | tf_op jit(solution)/shard_map/ppermute | solution.py:714
  40.3 0.6 %collective-permute-start.16 = (bf16[5,16,128]{2,1,0:T(8,128)(2,1)S(1)}, bf16[5,16,128]{2,1,0:T(8,128)(2,1)S(1)}, u32[]{:S(2)}, u32[]{:S(2)}) collective-permute-start(bf16[5,16,128]{2,1,0:T(8,128)(2,1)S(1)} %get-tuple-element.60), channel_id=1, source_target_pairs={{0,1},{1,0},{2,3},{3,2},{4,5},{5,4},{6,7},{7,6},{8,9},{9,8},{10,11... | collective-permute-start | bytes 61448 | tf_op jit(solution)/shard_map/ppermute | solution.py:744
  40.9 2.9 %inner_two.1.part_ref = f32[5,64,1536]{2,1,0:T(8,128)S(1)} custom-call(bf16[5,64,1536]{2,1,0:T(8,128)(2,1)S(1)} %get-tuple-element.55.v_ref, f32[5,3,5]{2,1,0:T(4,128)S(1)} %bitcast.16, bf16[3,64,64]{2,1,0:T(8,128)(2,1)S(1)} %copy-done.1), custom_call_target="tpu_custom_call" | custom-call | flops 10000000 | bytes 300000 | tf_op jit(solution)/shard_map/inner_two/pallas_call | solution.py:745
  43.9 4.4 %outer_two.1 = bf16[5,64,1536]{2,1,0:T(8,128)(2,1)} custom-call(bf16[5,64,1536]{2,1,0:T(8,128)(2,1)S(1)} %get-tuple-element.55.v_ref, bf16[5,64,1536]{2,1,0:T(8,128)(2,1)S(1)} %get-tuple-element.56.trace_ref, bf16[5,64,1536]{2,1,0:T(8,128)(2,1)S(1)} %copy-done, f32[5,64,1536]{2,1,0:T(8,128)S(1)} %inner_two.1.part_ref, f32[5,16,128]{2,1,0:T(8,128)S(1)} %bitcast.11, ...), custom_call_target="tpu_custom_call" | custom-call | flops 400000000 | bytes 12000000 | tf_op jit(solution)/shard_map/outer_two/pallas_call | solution.py:758
  (40 shorter events, 0.3 us)
Async XLA Ops:
  0.0 27.2 %copy-start.6 = (bf16[64,64]{1,0:T(8,128)(2,1)S(1)}, bf16[64,64]{1,0:T(8,128)(2,1)}, u32[]{:S(2)}) copy-start(bf16[64,64]{1,0:T(8,128)(2,1)} %wall_ref.5) | copy-start | bytes 24580
  0.0 27.2 %copy-start.7 = (bf16[64,64]{1,0:T(8,128)(2,1)S(1)}, bf16[64,64]{1,0:T(8,128)(2,1)}, u32[]{:S(2)}) copy-start(bf16[64,64]{1,0:T(8,128)(2,1)} %smooth_ref.1) | copy-start | bytes 24580
  0.0 27.2 %copy-start.5 = (bf16[64,96]{1,0:T(8,128)(2,1)S(1)}, bf16[64,96]{1,0:T(8,128)(2,1)}, u32[]{:S(2)}) copy-start(bf16[64,96]{1,0:T(8,128)(2,1)} %lift_ref.5) | copy-start | bytes 36868
  0.0 27.2 %copy-start.1 = (bf16[3,64,64]{2,1,0:T(8,128)(2,1)S(1)}, bf16[3,64,64]{2,1,0:T(8,128)(2,1)}, u32[]{:S(2)}) copy-start(bf16[3,64,64]{2,1,0:T(8,128)(2,1)} %volume_ref.5) | copy-start | bytes 73732
  0.0 27.2 %copy-start.4 = (f32[3,5,5]{2,0,1:T(4,128)S(1)}, f32[3,5,5]{2,0,1:T(4,128)}, u32[]{:S(2)}) copy-start(f32[3,5,5]{2,0,1:T(4,128)} %param.14) | copy-start | bytes 904
  3.7 31.3 %copy-start.2 = (f32[1,1,5,2048]{3,1,2,0:T(1,128)S(1)}, f32[1,1,5,2048]{3,1,2,0:T(1,128)}, u32[]{:S(2)}) copy-start(f32[1,1,5,2048]{3,1,2,0:T(1,128)} %param.22) | copy-start | bytes 122884
  3.7 31.2 %copy-start.3 = (f32[1,1,5,2048]{3,1,2,0:T(1,128)S(1)}, f32[1,1,5,2048]{3,1,2,0:T(1,128)}, u32[]{:S(2)}) copy-start(f32[1,1,5,2048]{3,1,2,0:T(1,128)} %param.23) | copy-start | bytes 122884
  3.7 9.0 %collective-permute-start.2 = (f32[5,16,128]{2,1,0:T(8,128)}, f32[5,16,128]{2,1,0:T(8,128)S(1)}, u32[]{:S(2)}, u32[]{:S(2)}) collective-permute-start(f32[5,16,128]{2,1,0:T(8,128)} %eddy_plane.1.plane_ref), channel_id=1, source_target_pairs={{24,0},{28,4},{56,40},{60,44},{88,72},{92,76},{120,104},{124,108},... | collective-permute-start | bytes 122888 | tf_op jit(solution)/shard_map/ppermute | solution.py:639
  5.1 7.5 %collective-permute-start.1 = (f32[5,16,128]{2,1,0:T(8,128)}, f32[5,16,128]{2,1,0:T(8,128)S(1)}, u32[]{:S(2)}, u32[]{:S(2)}) collective-permute-start(f32[5,16,128]{2,1,0:T(8,128)} %eddy_plane.1.plane_ref), channel_id=1, source_target_pairs={{16,0},{20,4},{48,40},{52,44},{80,72},{84,76},{112,104},{116,108},... | collective-permute-start | bytes 122888 | tf_op jit(solution)/shard_map/ppermute | solution.py:639
  6.4 6.2 %collective-permute-start = (f32[5,16,128]{2,1,0:T(8,128)}, f32[5,16,128]{2,1,0:T(8,128)S(1)}, u32[]{:S(2)}, u32[]{:S(2)}) collective-permute-start(f32[5,16,128]{2,1,0:T(8,128)} %eddy_plane.1.plane_ref), channel_id=1, source_target_pairs={{8,0},{12,4},{32,40},{36,44},{64,72},{68,76},{96,104},{100,108},{1... | collective-permute-start | bytes 122888 | tf_op jit(solution)/shard_map/ppermute | solution.py:639
  9.0 13.5 %collective-permute-start.6 = (bf16[5,16,768]{2,1,0:T(8,128)(2,1)S(1)}, bf16[5,16,768]{2,1,0:T(8,128)(2,1)S(1)}, u32[]{:S(2)}, u32[]{:S(2)}) collective-permute-start(bf16[5,16,768]{2,1,0:T(8,128)(2,1)S(1)} %get-tuple-element.40), channel_id=1, source_target_pairs={{0,2},{2,0},{1,3},{3,1},{4,6},{6,4},{5,7},{7,5},{8,10},{10,8},{9,1... | collective-permute-start | bytes 368648 | tf_op jit(solution)/shard_map/ppermute | solution.py:684
  12.7 9.9 %collective-permute-start.5 = (f32[5,16,128]{2,1,0:T(8,128)S(1)}, f32[5,16,128]{2,1,0:T(8,128)S(1)}, u32[]{:S(2)}, u32[]{:S(2)}) collective-permute-start(f32[5,16,128]{2,1,0:T(8,128)S(1)} %add_add_fusion.2), channel_id=1, source_target_pairs={{44,0},{108,72},{172,136},{236,200},{45,1},{109,73},{173,137},{237... | collective-permute-start | bytes 122888 | tf_op jit(solution)/shard_map/ppermute | solution.py:639
  13.4 9.3 %collective-permute-start.4 = (f32[5,16,128]{2,1,0:T(8,128)S(1)}, f32[5,16,128]{2,1,0:T(8,128)S(1)}, u32[]{:S(2)}, u32[]{:S(2)}) collective-permute-start(f32[5,16,128]{2,1,0:T(8,128)S(1)} %add_add_fusion.2), channel_id=1, source_target_pairs={{40,0},{104,72},{168,136},{232,200},{41,1},{105,73},{169,137},{233... | collective-permute-start | bytes 122888 | tf_op jit(solution)/shard_map/ppermute | solution.py:639
  14.0 8.7 %collective-permute-start.3 = (f32[5,16,128]{2,1,0:T(8,128)S(1)}, f32[5,16,128]{2,1,0:T(8,128)S(1)}, u32[]{:S(2)}, u32[]{:S(2)}) collective-permute-start(f32[5,16,128]{2,1,0:T(8,128)S(1)} %add_add_fusion.2), channel_id=1, source_target_pairs={{4,0},{76,72},{140,136},{204,200},{5,1},{77,73},{141,137},{205,201... | collective-permute-start | bytes 122888 | tf_op jit(solution)/shard_map/ppermute | solution.py:639
  20.5 6.7 %collective-permute-start.9 = (bf16[5,16,128]{2,1,0:T(8,128)(2,1)S(1)}, bf16[5,16,128]{2,1,0:T(8,128)(2,1)S(1)}, u32[]{:S(2)}, u32[]{:S(2)}) collective-permute-start(bf16[5,16,128]{2,1,0:T(8,128)(2,1)S(1)} %get-tuple-element.45), channel_id=1, source_target_pairs={{4,8},{8,4},{12,16},{16,12},{20,24},{24,20},{28,32},{32,28},{36,40... | collective-permute-start | bytes 61448 | tf_op jit(solution)/shard_map/ppermute | solution.py:687
  22.5 2.7 %collective-permute-start.7 = (bf16[5,16,128]{2,1,0:T(8,128)(2,1)S(1)}, bf16[5,16,128]{2,1,0:T(8,128)(2,1)S(1)}, u32[]{:S(2)}, u32[]{:S(2)}) collective-permute-start(bf16[5,16,128]{2,1,0:T(8,128)(2,1)S(1)} %get-tuple-element.42), channel_id=1, source_target_pairs={{0,1},{1,0},{2,3},{3,2},{4,5},{5,4},{6,7},{7,6},{8,9},{9,8},{10,11... | collective-permute-start | bytes 61448 | tf_op jit(solution)/shard_map/ppermute | solution.py:689
  22.6 2.6 %collective-permute-start.8 = (bf16[5,16,128]{2,1,0:T(8,128)(2,1)S(1)}, bf16[5,16,128]{2,1,0:T(8,128)(2,1)S(1)}, u32[]{:S(2)}, u32[]{:S(2)}) collective-permute-start(bf16[5,16,128]{2,1,0:T(8,128)(2,1)S(1)} %get-tuple-element.43), channel_id=1, source_target_pairs={{0,4},{4,0},{8,12},{12,8},{16,20},{20,16},{24,28},{28,24},{32,36},... | collective-permute-start | bytes 61448 | tf_op jit(solution)/shard_map/ppermute | solution.py:690
  25.2 8.9 %collective-permute-start.12 = (f32[5,16,128]{2,1,0:T(8,128)S(1)}, f32[5,16,128]{2,1,0:T(8,128)S(1)}, u32[]{:S(2)}, u32[]{:S(2)}) collective-permute-start(f32[5,16,128]{2,1,0:T(8,128)S(1)} %add_add_fusion.1), channel_id=1, source_target_pairs={{136,0},{137,1},{138,2},{139,3}} | collective-permute-start | bytes 122888 | tf_op jit(solution)/shard_map/ppermute | solution.py:639
  25.8 8.2 %collective-permute-start.11 = (f32[5,16,128]{2,1,0:T(8,128)S(1)}, f32[5,16,128]{2,1,0:T(8,128)S(1)}, u32[]{:S(2)}, u32[]{:S(2)}) collective-permute-start(f32[5,16,128]{2,1,0:T(8,128)S(1)} %add_add_fusion.1), channel_id=1, source_target_pairs={{200,0},{201,1},{202,2},{203,3}} | collective-permute-start | bytes 122888 | tf_op jit(solution)/shard_map/ppermute | solution.py:639
  26.5 7.6 %collective-permute-start.10 = (f32[5,16,128]{2,1,0:T(8,128)S(1)}, f32[5,16,128]{2,1,0:T(8,128)S(1)}, u32[]{:S(2)}, u32[]{:S(2)}) collective-permute-start(f32[5,16,128]{2,1,0:T(8,128)S(1)} %add_add_fusion.1), channel_id=1, source_target_pairs={{72,0},{73,1},{74,2},{75,3}} | collective-permute-start | bytes 122888 | tf_op jit(solution)/shard_map/ppermute | solution.py:639
  32.8 2.1 %collective-permute-start.13 = (bf16[5,16,128]{2,1,0:T(8,128)(2,1)S(1)}, bf16[5,16,128]{2,1,0:T(8,128)(2,1)S(1)}, u32[]{:S(2)}, u32[]{:S(2)}) collective-permute-start(bf16[5,16,128]{2,1,0:T(8,128)(2,1)S(1)} %get-tuple-element.53), channel_id=1, source_target_pairs={{0,4},{4,0},{8,12},{12,8},{16,20},{20,16},{24,28},{28,24},{32,36},... | collective-permute-start | bytes 61448 | tf_op jit(solution)/shard_map/ppermute | solution.py:713
  35.0 8.9 %collective-permute-start.15 = (bf16[5,16,768]{2,1,0:T(8,128)(2,1)S(1)}, bf16[5,16,768]{2,1,0:T(8,128)(2,1)S(1)}, u32[]{:S(2)}, u32[]{:S(2)}) collective-permute-start(bf16[5,16,768]{2,1,0:T(8,128)(2,1)S(1)} %get-tuple-element.59), channel_id=1, source_target_pairs={{0,2},{2,0},{1,3},{3,1},{4,6},{6,4},{5,7},{7,5},{8,10},{10,8},{9,1... | collective-permute-start | bytes 368648 | tf_op jit(solution)/shard_map/ppermute | solution.py:743
  36.5 7.4 %collective-permute-start.14 = (bf16[5,16,128]{2,1,0:T(8,128)(2,1)S(1)}, bf16[5,16,128]{2,1,0:T(8,128)(2,1)S(1)}, u32[]{:S(2)}, u32[]{:S(2)}) collective-permute-start(bf16[5,16,128]{2,1,0:T(8,128)(2,1)S(1)} %get-tuple-element.58), channel_id=1, source_target_pairs={{4,8},{8,4},{12,16},{16,12},{20,24},{24,20},{28,32},{32,28},{36,40... | collective-permute-start | bytes 61448 | tf_op jit(solution)/shard_map/ppermute | solution.py:714
  40.3 3.5 %collective-permute-start.16 = (bf16[5,16,128]{2,1,0:T(8,128)(2,1)S(1)}, bf16[5,16,128]{2,1,0:T(8,128)(2,1)S(1)}, u32[]{:S(2)}, u32[]{:S(2)}) collective-permute-start(bf16[5,16,128]{2,1,0:T(8,128)(2,1)S(1)} %get-tuple-element.60), channel_id=1, source_target_pairs={{0,1},{1,0},{2,3},{3,2},{4,5},{5,4},{6,7},{7,6},{8,9},{9,8},{10,11... | collective-permute-start | bytes 61448 | tf_op jit(solution)/shard_map/ppermute | solution.py:744
  (3 other events, 29.0 us)
